TPU v7x, 32 devices: a whole 2x2x4 slice. The times are simulated.
32 devices in a mesh: gx: 2 (over x), gy: 4 (over y, core), gz: 4 (over z).
Axes of the slice: x: 2, y: 2, z: 4, core: 2. Of those that a mesh axis runs over, the one named last changes fastest.
Arguments:
- estimate: float32 [32, 64, 1024], P('gx', 'gy', 'gz'), may hold values from 0.5 to 2
- raw_lines: float32 [2, 2, 16, 512, 256], P(None, 'gx', ('gy', 'gz')), may hold values from 0.2 to 3
- line_index: int32 [2, 2, 16, 512], P(None, 'gx', ('gy', 'gz')), may hold values from 0 to 256, as said below
- psf: float32 [2, 3, 33], replicated, may hold values from 0.05 to 1
- view_weight: int32 [2, 2, 4, 4], P(None, 'gx', 'gy', 'gz'), may hold values from 1 to 4
Outputs:
- updated: float32 [32, 64, 1024], P('gx', 'gy', 'gz')
Inputs may be any that keep to these rules, and one draw needn't show every extreme that they name: `line_index`: 256 marks an empty slot; every other entry is a z-line of the destination block, and each z-line of a destination block gets at most one slot per view. In every view and every x-block, some owner sends all 32 slots filled to some destination, and some destination block receives all 16 * 16 z-lines; blocks receive different numbers of z-lines from different numbers of owners.
All inputs are finite; a program needn't handle non-finite values.
Results may differ from a plain program's by a relative error of at most 0.0001.
Values sent between devices are 32-bit elements; how exact they have to be, the bound alone decides.
No kernel may reach another device: no remote copies, remote signals or barrier semaphores. Data moves between devices by JAX's collectives and lax.ppermute only.
A program may use at most 64 MiB of HBM per device.

v0:
```python
import jax
import jax.numpy as jnp
from jax import lax
from jax.sharding import PartitionSpec as P


def padded(block, sides, width):
    for axis, dim in sides:
        count = lax.axis_size(axis)
        forward = [(i, i + 1) for i in range(count - 1)]
        backward = [(target, source) for source, target in forward]
        low = lax.ppermute(
            lax.slice_in_dim(block, block.shape[dim] - width, None, axis=dim), axis, forward
        )
        high = lax.ppermute(lax.slice_in_dim(block, 0, width, axis=dim), axis, backward)
        block = jnp.concatenate([low, block, high], axis=dim)
    return block


def band_matrix(taps, length):
    width = taps.shape[0]
    rows = lax.broadcasted_iota(jnp.int32, (length + width - 1, length), 0)
    cols = lax.broadcasted_iota(jnp.int32, (length + width - 1, length), 1)
    offset = rows - cols
    valid = (offset >= 0) & (offset < width)
    return jnp.where(valid, taps[jnp.clip(offset, 0, width - 1)], 0.0)


def along_x(extended, matrix_x):
    lead, size_y, size_z = extended.shape
    flat = extended.reshape(lead, size_y * size_z)
    result = jnp.dot(matrix_x.T, flat, precision=lax.Precision.HIGHEST)
    return result.reshape(matrix_x.shape[1], size_y, size_z)


def blur(field, taps):
    half_width = (taps.shape[1] - 1) // 2
    size_x, size_y, size_z = field.shape
    matrix_x = band_matrix(taps[0], size_x)
    matrix_y = band_matrix(taps[1], size_y)
    matrix_z = band_matrix(taps[2], size_z)
    highest = lax.Precision.HIGHEST
    extended = padded(field, (("gz", 2),), half_width)
    result = jnp.einsum("abj,jc->abc", extended, matrix_z, precision=highest)
    extended = padded(result, (("gy", 1),), half_width)
    result = jnp.einsum("ajc,jb->abc", extended, matrix_y, precision=highest)
    extended = padded(result, (("gx", 0),), half_width)
    result = along_x(extended, matrix_x)
    return result


def on_device(estimate, raw_lines, line_index, psf, view_weight):
    size_x, size_y, size_z = estimate.shape
    block_lines = size_x * size_y
    views = raw_lines.shape[0]
    group = lax.axis_size(("gy", "gz"))
    slots = line_index.shape[-1]
    capacity = slots // group
    lines = raw_lines.reshape(views, group, capacity, size_z)
    indices = line_index.reshape(views, group, capacity)
    lines, indices = (
        lax.all_to_all(lines, ("gy", "gz"), split_axis=1, concat_axis=1, tiled=True),
        lax.all_to_all(indices, ("gy", "gz"), split_axis=1, concat_axis=1, tiled=True),
    )
    est = estimate
    for view in range(views):
        flat_index = indices[view].reshape(-1)
        flat_lines = lines[view].reshape(-1, size_z)
        volume = (
            jnp.zeros((block_lines, size_z), jnp.float32)
            .at[flat_index]
            .set(flat_lines, mode="drop")
        )
        volume = volume.reshape(size_x, size_y, size_z)
        cover = jnp.zeros((block_lines,), jnp.float32).at[flat_index].set(1.0, mode="drop")
        cover = cover.reshape(size_x, size_y, 1)
        weight = view_weight[view].reshape(()).astype(jnp.float32) * 0.25
        taps = psf[view] / jnp.sum(psf[view], axis=1, keepdims=True)
        blurred = blur(est, taps)
        ratio = 1.0 + weight * cover * (volume / blurred - 1.0)
        est = est * blur(ratio, taps[:, ::-1])
    return est


def solution(mesh):
    placed = (
        P("gx", "gy", "gz"),
        P(None, "gx", ("gy", "gz"), None, None),
        P(None, "gx", ("gy", "gz"), None),
        P(),
        P(None, "gx", "gy", "gz"),
    )
    return jax.shard_map(
        on_device, mesh=mesh, in_specs=placed, out_specs=P("gx", "gy", "gz"), check_vma=False
    )
```

profile of v0, /device:TPU:0, one launch (start us, length us, event | category | flops | bytes accessed | tf_op | source)
XLA Modules:
  0.0 245.3 jit_solution(17900119113289669520)
XLA Ops:
  1.4 7.4 %all-to-all-start = ((s32[2,16,32]{2,0,1:T(2,128)}), s32[2,16,32]{2,0,1:T(2,128)S(1)}, u32[]{:S(2)}, u32[]{:S(2)}) async-start(s32[2,16,32]{2,0,1:T(2,128)} %copy.53), calls=%async_computation | async-start | bytes 32768 | tf_op jit(solution)/shard_map/all_to_all | solution.py:63
  11.2 4.6 %collective-permute-start = (f32[16,16,16]{2,1,0:T(8,128)S(1)}, f32[16,16,16]{2,1,0:T(8,128)S(1)}, u32[]{:S(2)}, u32[]{:S(2)}) collective-permute-start(f32[16,16,16]{2,1,0:T(8,128)S(1)} %get-tuple-element.17), channel_id=1, source_target_pairs={{0,1},{1,2},{2,3},{4,5},{5,6},{6,7},{8,9},{9,10},{10,11},{12,13},{... | collective-permute-start | bytes 49160 | tf_op jit(solution)/shard_map/ppermute | solution.py:12
  15.9 2.3 copy.55
  18.2 5.2 %all-to-all-start.1 = ((f32[2,16,32,256]{3,2,0,1:T(8,128)}), f32[2,16,32,256]{3,2,0,1:T(8,128)S(1)}, u32[]{:S(2)}, u32[]{:S(2)}) async-start(f32[2,16,32,256]{3,2,0,1:T(8,128)} %copy.55), calls=%async_computation.1 | async-start | bytes 2097152 | tf_op jit(solution)/shard_map/all_to_all | solution.py:62
  25.0 21.6 %fusion.34 = f32[16,16,256]{2,1,0:T(8,128)S(1)} fusion(f32[16,16,16]{2,1,0:T(8,128)S(1)} %collective-permute-done.1, f32[16,16,256]{2,1,0:T(8,128)S(1)} %copy-done, f32[16,16,16]{2,1,0:T(8,128)S(1)} %collective-permute-done, f32[]{:T(128)} %bitcast.65, f32[]{:T(128)} %bitcast.66, f32[]{:T(128)} %bitcast.67, f32[]{:T(128)} %bitcast.68, f32[]{:T(128)} %bitcast.69, ...), kind=kOutput, calls=%fused_computation.59 | convolution fusion | flops 232095744 | bytes 557188 | tf_op jit(solution)/shard_map/abj,jc->abc/dot_general | solution.py:44
  47.9 3.0 %collective-permute-start.2 = (f32[16,16,256]{2,1,0:T(8,128)S(1)}, f32[16,16,256]{2,1,0:T(8,128)S(1)}, u32[]{:S(2)}, u32[]{:S(2)}) collective-permute-start(f32[16,16,256]{2,1,0:T(8,128)S(1)} %fusion.34), channel_id=1, source_target_pairs={{0,4},{4,8},{8,12},{1,5},{5,9},{9,13},{2,6},{6,10},{10,14},{3,7},{... | collective-permute-start | bytes 786440 | tf_op jit(solution)/shard_map/ppermute | solution.py:12
  52.3 4.8 %gather_fusion.2 = f32[768]{0:T(1024)S(1)} fusion(f32[33]{0:T(128)S(1)} %get-tuple-element.59, s32[1024]{0:T(1024)S(1)} %pad_clamp_fusion), kind=kCustom, calls=%fused_computation.2 | custom fusion | bytes 9216 | tf_op jit(solution)/shard_map/gather | solution.py:26
  57.1 4.8 %gather_fusion.3 = f32[768]{0:T(1024)S(1)} fusion(f32[33]{0:T(128)S(1)} %get-tuple-element.60, s32[1024]{0:T(1024)S(1)} %pad_clamp_fusion), kind=kCustom, calls=%fused_computation.3 | custom fusion | bytes 9216 | tf_op jit(solution)/shard_map/gather | solution.py:26
  64.0 4.6 %collective-permute-start.4 = (f32[16,16,256]{2,1,0:T(8,128)S(1)}, f32[16,16,256]{2,1,0:T(8,128)S(1)}, u32[]{:S(2)}, u32[]{:S(2)}) collective-permute-start(f32[16,16,256]{2,1,0:T(8,128)S(1)} %convolution_bitcast_fusion.3), channel_id=1, source_target_pairs={{0,16},{1,17},{2,18},{3,19},{4,20},{5,21},{6,22},{7,23},{8,24},{9,... | collective-permute-start | bytes 786440 | tf_op jit(solution)/shard_map/ppermute | solution.py:12
  68.6 2.4 scatter_custom_fusion
  75.1 2.3 scatter_custom_fusion.1
  79.8 4.6 %collective-permute-start.6 = (f32[16,16,16]{2,0,1:T(8,128)S(1)}, f32[16,16,16]{2,0,1:T(8,128)S(1)}, u32[]{:S(2)}, u32[]{:S(2)}) collective-permute-start(f32[16,16,16]{2,0,1:T(8,128)S(1)} %get-tuple-element.15), channel_id=1, source_target_pairs={{0,1},{1,2},{2,3},{4,5},{5,6},{6,7},{8,9},{9,10},{10,11},{12,13},{... | collective-permute-start | bytes 49160 | tf_op jit(solution)/shard_map/ppermute | solution.py:12
  84.5 2.0 collective-permute-done.7
  87.9 21.6 %fusion.44 = f32[16,16,256]{2,1,0:T(8,128)S(1)} fusion(f32[16,16,288]{2,0,1:T(8,128)S(1)} %pad_maximum_fusion.4, f32[]{:T(128)} %bitcast.26, f32[]{:T(128)} %bitcast.24, f32[]{:T(128)} %bitcast.22, f32[]{:T(128)} %bitcast.20, f32[]{:T(128)} %bitcast.18, f32[]{:T(128)} %bitcast.16, f32[]{:T(128)} %bitcast.14, f32[]{:T(128)} %bitcast.28, f32[]{:T(128)} %bitcast.30, ...), kind=kOutput, calls=%fused_computation.72 | convolution fusion | flops 231948288 | bytes 557188 | tf_op jit(solution)/shard_map/abj,jc->abc/dot_general | solution.py:44
  110.8 3.0 %collective-permute-start.8 = (f32[16,16,256]{2,1,0:T(8,128)S(1)}, f32[16,16,256]{2,1,0:T(8,128)S(1)}, u32[]{:S(2)}, u32[]{:S(2)}) collective-permute-start(f32[16,16,256]{2,1,0:T(8,128)S(1)} %fusion.44), channel_id=1, source_target_pairs={{0,4},{4,8},{8,12},{1,5},{5,9},{9,13},{2,6},{6,10},{10,14},{3,7},{... | collective-permute-start | bytes 786440 | tf_op jit(solution)/shard_map/ppermute | solution.py:12
  113.9 4.8 %gather_fusion.1 = f32[768]{0:T(1024)S(1)} fusion(f32[33]{0:T(128)S(1)} %bitcast.718, s32[1024]{0:T(1024)S(1)} %pad_clamp_fusion), kind=kCustom, calls=%fused_computation.1 | custom fusion | bytes 9216 | tf_op jit(solution)/shard_map/gather | solution.py:26
  120.6 4.8 %collective-permute-start.10 = (f32[16,16,256]{2,1,0:T(8,128)S(1)}, f32[16,16,256]{2,1,0:T(8,128)S(1)}, u32[]{:S(2)}, u32[]{:S(2)}) collective-permute-start(f32[16,16,256]{2,1,0:T(8,128)S(1)} %convolution_bitcast_fusion.2), channel_id=1, source_target_pairs={{0,16},{1,17},{2,18},{3,19},{4,20},{5,21},{6,22},{7,23},{8,24},{9,... | collective-permute-start | bytes 786440 | tf_op jit(solution)/shard_map/ppermute | solution.py:12
  125.5 4.8 %gather_fusion = f32[768]{0:T(1024)S(1)} fusion(f32[33]{0:T(128)S(1)} %bitcast.719, s32[1024]{0:T(1024)S(1)} %pad_clamp_fusion), kind=kCustom, calls=%fused_computation | custom fusion | bytes 9216 | tf_op jit(solution)/shard_map/gather | solution.py:26
  133.8 5.0 %collective-permute-start.12 = (f32[16,16,16]{2,0,1:T(8,128)S(1)}, f32[16,16,16]{2,0,1:T(8,128)S(1)}, u32[]{:S(2)}, u32[]{:S(2)}) collective-permute-start(f32[16,16,16]{2,0,1:T(8,128)S(1)} %get-tuple-element.13), channel_id=1, source_target_pairs={{0,1},{1,2},{2,3},{4,5},{5,6},{6,7},{8,9},{9,10},{10,11},{12,13},{... | collective-permute-start | bytes 49160 | tf_op jit(solution)/shard_map/ppermute | solution.py:12
  141.8 21.5 %fusion.42 = f32[16,16,256]{2,1,0:T(8,128)S(1)} fusion(f32[16,16,288]{2,0,1:T(8,128)S(1)} %pad_maximum_fusion.5, f32[]{:T(128)} %bitcast.118, f32[]{:T(128)} %bitcast.119, f32[]{:T(128)} %bitcast.120, f32[]{:T(128)} %bitcast.121, f32[]{:T(128)} %bitcast.122, f32[]{:T(128)} %bitcast.124, f32[]{:T(128)} %bitcast.123, f32[]{:T(128)} %bitcast.92, f32[]{:T(128)} %bitcast.93, ...), kind=kOutput, calls=%fused_computation.70 | convolution fusion | flops 231948288 | bytes 557188 | tf_op jit(solution)/shard_map/abj,jc->abc/dot_general | solution.py:44
  164.7 3.0 %collective-permute-start.14 = (f32[16,16,256]{2,1,0:T(8,128)S(1)}, f32[16,16,256]{2,1,0:T(8,128)S(1)}, u32[]{:S(2)}, u32[]{:S(2)}) collective-permute-start(f32[16,16,256]{2,1,0:T(8,128)S(1)} %fusion.42), channel_id=1, source_target_pairs={{0,4},{4,8},{8,12},{1,5},{5,9},{9,13},{2,6},{6,10},{10,14},{3,7},{... | collective-permute-start | bytes 786440 | tf_op jit(solution)/shard_map/ppermute | solution.py:12
  168.4 4.8 %gather_fusion.6 = f32[768]{0:T(1024)S(1)} fusion(f32[33]{0:T(128)S(1)} %get-tuple-element.22, s32[1024]{0:T(1024)S(1)} %pad_clamp_fusion), kind=kCustom, calls=%fused_computation.6 | custom fusion | bytes 9216 | tf_op jit(solution)/shard_map/gather | solution.py:26
  173.3 4.8 %gather_fusion.7 = f32[768]{0:T(1024)S(1)} fusion(f32[33]{0:T(128)S(1)} %get-tuple-element.23, s32[1024]{0:T(1024)S(1)} %pad_clamp_fusion), kind=kCustom, calls=%fused_computation.7 | custom fusion | bytes 9216 | tf_op jit(solution)/shard_map/gather | solution.py:26
  180.0 4.6 %collective-permute-start.16 = (f32[16,16,256]{2,1,0:T(8,128)S(1)}, f32[16,16,256]{2,1,0:T(8,128)S(1)}, u32[]{:S(2)}, u32[]{:S(2)}) collective-permute-start(f32[16,16,256]{2,1,0:T(8,128)S(1)} %convolution_bitcast_fusion.1), channel_id=1, source_target_pairs={{0,16},{1,17},{2,18},{3,19},{4,20},{5,21},{6,22},{7,23},{8,24},{9,... | collective-permute-start | bytes 786440 | tf_op jit(solution)/shard_map/ppermute | solution.py:12
  184.6 2.4 scatter_custom_fusion.2
  187.2 2.3 scatter_custom_fusion.3
  193.0 5.0 %collective-permute-start.18 = (f32[16,16,16]{2,0,1:T(8,128)S(1)}, f32[16,16,16]{2,0,1:T(8,128)S(1)}, u32[]{:S(2)}, u32[]{:S(2)}) collective-permute-start(f32[16,16,16]{2,0,1:T(8,128)S(1)} %get-tuple-element.11), channel_id=1, source_target_pairs={{0,1},{1,2},{2,3},{4,5},{5,6},{6,7},{8,9},{9,10},{10,11},{12,13},{... | collective-permute-start | bytes 49160 | tf_op jit(solution)/shard_map/ppermute | solution.py:12
  200.7 21.5 %fusion.40 = f32[16,16,256]{2,1,0:T(8,128)S(1)} fusion(f32[16,16,288]{2,0,1:T(8,128)S(1)} %pad_maximum_fusion.6, f32[]{:T(128)} %bitcast.98, f32[]{:T(128)} %bitcast.97, f32[]{:T(128)} %bitcast.96, f32[]{:T(128)} %bitcast.95, f32[]{:T(128)} %bitcast.94, f32[]{:T(128)} %bitcast.93, f32[]{:T(128)} %bitcast.92, f32[]{:T(128)} %bitcast.99, f32[]{:T(128)} %bitcast.100, ...), kind=kOutput, calls=%fused_computation.68 | convolution fusion | flops 231948288 | bytes 557188 | tf_op jit(solution)/shard_map/abj,jc->abc/dot_general | solution.py:44
  223.5 3.0 %collective-permute-start.20 = (f32[16,16,256]{2,1,0:T(8,128)S(1)}, f32[16,16,256]{2,1,0:T(8,128)S(1)}, u32[]{:S(2)}, u32[]{:S(2)}) collective-permute-start(f32[16,16,256]{2,1,0:T(8,128)S(1)} %fusion.40), channel_id=1, source_target_pairs={{0,4},{4,8},{8,12},{1,5},{5,9},{9,13},{2,6},{6,10},{10,14},{3,7},{... | collective-permute-start | bytes 786440 | tf_op jit(solution)/shard_map/ppermute | solution.py:12
  226.7 4.8 %gather_fusion.5 = f32[768]{0:T(1024)S(1)} fusion(f32[33]{0:T(128)S(1)} %bitcast.720, s32[1024]{0:T(1024)S(1)} %pad_clamp_fusion), kind=kCustom, calls=%fused_computation.5 | custom fusion | bytes 9216 | tf_op jit(solution)/shard_map/gather | solution.py:26
  233.4 4.6 %collective-permute-start.22 = (f32[16,16,256]{2,1,0:T(8,128)S(1)}, f32[16,16,256]{2,1,0:T(8,128)S(1)}, u32[]{:S(2)}, u32[]{:S(2)}) collective-permute-start(f32[16,16,256]{2,1,0:T(8,128)S(1)} %convolution_bitcast_fusion), channel_id=1, source_target_pairs={{0,16},{1,17},{2,18},{3,19},{4,20},{5,21},{6,22},{7,23},{8,24},{9,... | collective-permute-start | bytes 786440 | tf_op jit(solution)/shard_map/ppermute | solution.py:12
  238.0 4.8 %gather_fusion.4 = f32[768]{0:T(1024)S(1)} fusion(f32[33]{0:T(128)S(1)} %bitcast.717, s32[1024]{0:T(1024)S(1)} %pad_clamp_fusion), kind=kCustom, calls=%fused_computation.4 | custom fusion | bytes 9216 | tf_op jit(solution)/shard_map/gather | solution.py:26
  (103 shorter events, 42.6 us)
Async XLA Ops:
  1.4 16.8 %all-to-all-start = ((s32[2,16,32]{2,0,1:T(2,128)}), s32[2,16,32]{2,0,1:T(2,128)S(1)}, u32[]{:S(2)}, u32[]{:S(2)}) async-start(s32[2,16,32]{2,0,1:T(2,128)} %copy.53), calls=%async_computation | async-start | bytes 32768 | tf_op jit(solution)/shard_map/all_to_all | solution.py:63
  9.9 5.9 %copy-start.1 = (f32[2,3,33]{2,0,1:T(2,128)S(1)}, f32[2,3,33]{2,0,1:T(2,128)}, u32[]{:S(2)}) copy-start(f32[2,3,33]{2,0,1:T(2,128)} %param.8) | copy-start | bytes 2380
  9.9 15.1 %collective-permute-start.1 = (f32[16,16,16]{2,1,0:T(8,128)S(1)}, f32[16,16,16]{2,1,0:T(8,128)S(1)}, u32[]{:S(2)}, u32[]{:S(2)}) collective-permute-start(f32[16,16,16]{2,1,0:T(8,128)S(1)} %get-tuple-element.18), channel_id=1, source_target_pairs={{1,0},{2,1},{3,2},{5,4},{6,5},{7,6},{9,8},{10,9},{11,10},{13,12},{... | collective-permute-start | bytes 49160 | tf_op jit(solution)/shard_map/ppermute | solution.py:15
  11.2 13.8 %collective-permute-start = (f32[16,16,16]{2,1,0:T(8,128)S(1)}, f32[16,16,16]{2,1,0:T(8,128)S(1)}, u32[]{:S(2)}, u32[]{:S(2)}) collective-permute-start(f32[16,16,16]{2,1,0:T(8,128)S(1)} %get-tuple-element.17), channel_id=1, source_target_pairs={{0,1},{1,2},{2,3},{4,5},{5,6},{6,7},{8,9},{9,10},{10,11},{12,13},{... | collective-permute-start | bytes 49160 | tf_op jit(solution)/shard_map/ppermute | solution.py:12
  18.2 6.8 %copy-start = (f32[16,16,256]{2,1,0:T(8,128)S(1)}, f32[16,16,256]{2,1,0:T(8,128)}, u32[]{:S(2)}) copy-start(f32[16,16,256]{2,1,0:T(8,128)} %param.5) | copy-start | bytes 786436
  18.2 56.8 %all-to-all-start.1 = ((f32[2,16,32,256]{3,2,0,1:T(8,128)}), f32[2,16,32,256]{3,2,0,1:T(8,128)S(1)}, u32[]{:S(2)}, u32[]{:S(2)}) async-start(f32[2,16,32,256]{3,2,0,1:T(8,128)} %copy.55), calls=%async_computation.1 | async-start | bytes 2097152 | tf_op jit(solution)/shard_map/all_to_all | solution.py:62
  25.0 25.9 %copy-start.2 = (s32[2,1,1,1]{0,3,2,1:T(1,128)S(1)}, s32[2,1,1,1]{0,3,2,1:T(1,128)}, u32[]{:S(2)}) copy-start(s32[2,1,1,1]{0,3,2,1:T(1,128)} %param.9) | copy-start | bytes 28
  46.6 15.5 %collective-permute-start.3 = (f32[16,16,256]{2,1,0:T(8,128)S(1)}, f32[16,16,256]{2,1,0:T(8,128)S(1)}, u32[]{:S(2)}, u32[]{:S(2)}) collective-permute-start(f32[16,16,256]{2,1,0:T(8,128)S(1)} %fusion.34), channel_id=1, source_target_pairs={{4,0},{8,4},{12,8},{5,1},{9,5},{13,9},{6,2},{10,6},{14,10},{7,3},{... | collective-permute-start | bytes 786440 | tf_op jit(solution)/shard_map/ppermute | solution.py:15
  47.9 14.2 %collective-permute-start.2 = (f32[16,16,256]{2,1,0:T(8,128)S(1)}, f32[16,16,256]{2,1,0:T(8,128)S(1)}, u32[]{:S(2)}, u32[]{:S(2)}) collective-permute-start(f32[16,16,256]{2,1,0:T(8,128)S(1)} %fusion.34), channel_id=1, source_target_pairs={{0,4},{4,8},{8,12},{1,5},{5,9},{9,13},{2,6},{6,10},{10,14},{3,7},{... | collective-permute-start | bytes 786440 | tf_op jit(solution)/shard_map/ppermute | solution.py:12
  62.7 10.5 %collective-permute-start.5 = (f32[16,16,256]{2,1,0:T(8,128)S(1)}, f32[16,16,256]{2,1,0:T(8,128)S(1)}, u32[]{:S(2)}, u32[]{:S(2)}) collective-permute-start(f32[16,16,256]{2,1,0:T(8,128)S(1)} %convolution_bitcast_fusion.3), channel_id=1, source_target_pairs={{16,0},{17,1},{18,2},{19,3},{20,4},{21,5},{22,6},{23,7},{24,8},{25... | collective-permute-start | bytes 786440 | tf_op jit(solution)/shard_map/ppermute | solution.py:15
  64.0 10.9 %collective-permute-start.4 = (f32[16,16,256]{2,1,0:T(8,128)S(1)}, f32[16,16,256]{2,1,0:T(8,128)S(1)}, u32[]{:S(2)}, u32[]{:S(2)}) collective-permute-start(f32[16,16,256]{2,1,0:T(8,128)S(1)} %convolution_bitcast_fusion.3), channel_id=1, source_target_pairs={{0,16},{1,17},{2,18},{3,19},{4,20},{5,21},{6,22},{7,23},{8,24},{9,... | collective-permute-start | bytes 786440 | tf_op jit(solution)/shard_map/ppermute | solution.py:12
  78.5 8.0 %collective-permute-start.7 = (f32[16,16,16]{2,0,1:T(8,128)S(1)}, f32[16,16,16]{2,0,1:T(8,128)S(1)}, u32[]{:S(2)}, u32[]{:S(2)}) collective-permute-start(f32[16,16,16]{2,0,1:T(8,128)S(1)} %get-tuple-element.16), channel_id=1, source_target_pairs={{1,0},{2,1},{3,2},{5,4},{6,5},{7,6},{9,8},{10,9},{11,10},{13,12},{... | collective-permute-start | bytes 49160 | tf_op jit(solution)/shard_map/ppermute | solution.py:15
  79.8 7.8 %collective-permute-start.6 = (f32[16,16,16]{2,0,1:T(8,128)S(1)}, f32[16,16,16]{2,0,1:T(8,128)S(1)}, u32[]{:S(2)}, u32[]{:S(2)}) collective-permute-start(f32[16,16,16]{2,0,1:T(8,128)S(1)} %get-tuple-element.15), channel_id=1, source_target_pairs={{0,1},{1,2},{2,3},{4,5},{5,6},{6,7},{8,9},{9,10},{10,11},{12,13},{... | collective-permute-start | bytes 49160 | tf_op jit(solution)/shard_map/ppermute | solution.py:12
  109.5 9.3 %collective-permute-start.9 = (f32[16,16,256]{2,1,0:T(8,128)S(1)}, f32[16,16,256]{2,1,0:T(8,128)S(1)}, u32[]{:S(2)}, u32[]{:S(2)}) collective-permute-start(f32[16,16,256]{2,1,0:T(8,128)S(1)} %fusion.44), channel_id=1, source_target_pairs={{4,0},{8,4},{12,8},{5,1},{9,5},{13,9},{6,2},{10,6},{14,10},{7,3},{... | collective-permute-start | bytes 786440 | tf_op jit(solution)/shard_map/ppermute | solution.py:15
  110.8 8.0 %collective-permute-start.8 = (f32[16,16,256]{2,1,0:T(8,128)S(1)}, f32[16,16,256]{2,1,0:T(8,128)S(1)}, u32[]{:S(2)}, u32[]{:S(2)}) collective-permute-start(f32[16,16,256]{2,1,0:T(8,128)S(1)} %fusion.44), channel_id=1, source_target_pairs={{0,4},{4,8},{8,12},{1,5},{5,9},{9,13},{2,6},{6,10},{10,14},{3,7},{... | collective-permute-start | bytes 786440 | tf_op jit(solution)/shard_map/ppermute | solution.py:12
  119.3 11.8 %collective-permute-start.11 = (f32[16,16,256]{2,1,0:T(8,128)S(1)}, f32[16,16,256]{2,1,0:T(8,128)S(1)}, u32[]{:S(2)}, u32[]{:S(2)}) collective-permute-start(f32[16,16,256]{2,1,0:T(8,128)S(1)} %convolution_bitcast_fusion.2), channel_id=1, source_target_pairs={{16,0},{17,1},{18,2},{19,3},{20,4},{21,5},{22,6},{23,7},{24,8},{25... | collective-permute-start | bytes 786440 | tf_op jit(solution)/shard_map/ppermute | solution.py:15
  120.6 10.7 %collective-permute-start.10 = (f32[16,16,256]{2,1,0:T(8,128)S(1)}, f32[16,16,256]{2,1,0:T(8,128)S(1)}, u32[]{:S(2)}, u32[]{:S(2)}) collective-permute-start(f32[16,16,256]{2,1,0:T(8,128)S(1)} %convolution_bitcast_fusion.2), channel_id=1, source_target_pairs={{0,16},{1,17},{2,18},{3,19},{4,20},{5,21},{6,22},{7,23},{8,24},{9,... | collective-permute-start | bytes 786440 | tf_op jit(solution)/shard_map/ppermute | solution.py:12
  132.5 8.0 %collective-permute-start.13 = (f32[16,16,16]{2,0,1:T(8,128)S(1)}, f32[16,16,16]{2,0,1:T(8,128)S(1)}, u32[]{:S(2)}, u32[]{:S(2)}) collective-permute-start(f32[16,16,16]{2,0,1:T(8,128)S(1)} %get-tuple-element.14), channel_id=1, source_target_pairs={{1,0},{2,1},{3,2},{5,4},{6,5},{7,6},{9,8},{10,9},{11,10},{13,12},{... | collective-permute-start | bytes 49160 | tf_op jit(solution)/shard_map/ppermute | solution.py:15
  133.8 7.8 %collective-permute-start.12 = (f32[16,16,16]{2,0,1:T(8,128)S(1)}, f32[16,16,16]{2,0,1:T(8,128)S(1)}, u32[]{:S(2)}, u32[]{:S(2)}) collective-permute-start(f32[16,16,16]{2,0,1:T(8,128)S(1)} %get-tuple-element.13), channel_id=1, source_target_pairs={{0,1},{1,2},{2,3},{4,5},{5,6},{6,7},{8,9},{9,10},{10,11},{12,13},{... | collective-permute-start | bytes 49160 | tf_op jit(solution)/shard_map/ppermute | solution.py:12
  163.4 14.8 %collective-permute-start.15 = (f32[16,16,256]{2,1,0:T(8,128)S(1)}, f32[16,16,256]{2,1,0:T(8,128)S(1)}, u32[]{:S(2)}, u32[]{:S(2)}) collective-permute-start(f32[16,16,256]{2,1,0:T(8,128)S(1)} %fusion.42), channel_id=1, source_target_pairs={{4,0},{8,4},{12,8},{5,1},{9,5},{13,9},{6,2},{10,6},{14,10},{7,3},{... | collective-permute-start | bytes 786440 | tf_op jit(solution)/shard_map/ppermute | solution.py:15
  164.7 13.5 %collective-permute-start.14 = (f32[16,16,256]{2,1,0:T(8,128)S(1)}, f32[16,16,256]{2,1,0:T(8,128)S(1)}, u32[]{:S(2)}, u32[]{:S(2)}) collective-permute-start(f32[16,16,256]{2,1,0:T(8,128)S(1)} %fusion.42), channel_id=1, source_target_pairs={{0,4},{4,8},{8,12},{1,5},{5,9},{9,13},{2,6},{6,10},{10,14},{3,7},{... | collective-permute-start | bytes 786440 | tf_op jit(solution)/shard_map/ppermute | solution.py:12
  178.7 10.8 %collective-permute-start.17 = (f32[16,16,256]{2,1,0:T(8,128)S(1)}, f32[16,16,256]{2,1,0:T(8,128)S(1)}, u32[]{:S(2)}, u32[]{:S(2)}) collective-permute-start(f32[16,16,256]{2,1,0:T(8,128)S(1)} %convolution_bitcast_fusion.1), channel_id=1, source_target_pairs={{16,0},{17,1},{18,2},{19,3},{20,4},{21,5},{22,6},{23,7},{24,8},{25... | collective-permute-start | bytes 786440 | tf_op jit(solution)/shard_map/ppermute | solution.py:15
  180.0 10.5 %collective-permute-start.16 = (f32[16,16,256]{2,1,0:T(8,128)S(1)}, f32[16,16,256]{2,1,0:T(8,128)S(1)}, u32[]{:S(2)}, u32[]{:S(2)}) collective-permute-start(f32[16,16,256]{2,1,0:T(8,128)S(1)} %convolution_bitcast_fusion.1), channel_id=1, source_target_pairs={{0,16},{1,17},{2,18},{3,19},{4,20},{5,21},{6,22},{7,23},{8,24},{9,... | collective-permute-start | bytes 786440 | tf_op jit(solution)/shard_map/ppermute | solution.py:12
  191.7 7.3 %collective-permute-start.19 = (f32[16,16,16]{2,0,1:T(8,128)S(1)}, f32[16,16,16]{2,0,1:T(8,128)S(1)}, u32[]{:S(2)}, u32[]{:S(2)}) collective-permute-start(f32[16,16,16]{2,0,1:T(8,128)S(1)} %get-tuple-element.12), channel_id=1, source_target_pairs={{1,0},{2,1},{3,2},{5,4},{6,5},{7,6},{9,8},{10,9},{11,10},{13,12},{... | collective-permute-start | bytes 49160 | tf_op jit(solution)/shard_map/ppermute | solution.py:15
  193.0 7.5 %collective-permute-start.18 = (f32[16,16,16]{2,0,1:T(8,128)S(1)}, f32[16,16,16]{2,0,1:T(8,128)S(1)}, u32[]{:S(2)}, u32[]{:S(2)}) collective-permute-start(f32[16,16,16]{2,0,1:T(8,128)S(1)} %get-tuple-element.11), channel_id=1, source_target_pairs={{0,1},{1,2},{2,3},{4,5},{5,6},{6,7},{8,9},{9,10},{10,11},{12,13},{... | collective-permute-start | bytes 49160 | tf_op jit(solution)/shard_map/ppermute | solution.py:12
  222.2 9.3 %collective-permute-start.21 = (f32[16,16,256]{2,1,0:T(8,128)S(1)}, f32[16,16,256]{2,1,0:T(8,128)S(1)}, u32[]{:S(2)}, u32[]{:S(2)}) collective-permute-start(f32[16,16,256]{2,1,0:T(8,128)S(1)} %fusion.40), channel_id=1, source_target_pairs={{4,0},{8,4},{12,8},{5,1},{9,5},{13,9},{6,2},{10,6},{14,10},{7,3},{... | collective-permute-start | bytes 786440 | tf_op jit(solution)/shard_map/ppermute | solution.py:15
  223.5 8.0 %collective-permute-start.20 = (f32[16,16,256]{2,1,0:T(8,128)S(1)}, f32[16,16,256]{2,1,0:T(8,128)S(1)}, u32[]{:S(2)}, u32[]{:S(2)}) collective-permute-start(f32[16,16,256]{2,1,0:T(8,128)S(1)} %fusion.40), channel_id=1, source_target_pairs={{0,4},{4,8},{8,12},{1,5},{5,9},{9,13},{2,6},{6,10},{10,14},{3,7},{... | collective-permute-start | bytes 786440 | tf_op jit(solution)/shard_map/ppermute | solution.py:12
  232.1 10.8 %collective-permute-start.23 = (f32[16,16,256]{2,1,0:T(8,128)S(1)}, f32[16,16,256]{2,1,0:T(8,128)S(1)}, u32[]{:S(2)}, u32[]{:S(2)}) collective-permute-start(f32[16,16,256]{2,1,0:T(8,128)S(1)} %convolution_bitcast_fusion), channel_id=1, source_target_pairs={{16,0},{17,1},{18,2},{19,3},{20,4},{21,5},{22,6},{23,7},{24,8},{25... | collective-permute-start | bytes 786440 | tf_op jit(solution)/shard_map/ppermute | solution.py:15
  233.4 10.1 %collective-permute-start.22 = (f32[16,16,256]{2,1,0:T(8,128)S(1)}, f32[16,16,256]{2,1,0:T(8,128)S(1)}, u32[]{:S(2)}, u32[]{:S(2)}) collective-permute-start(f32[16,16,256]{2,1,0:T(8,128)S(1)} %convolution_bitcast_fusion), channel_id=1, source_target_pairs={{0,16},{1,17},{2,18},{3,19},{4,20},{5,21},{6,22},{7,23},{8,24},{9,... | collective-permute-start | bytes 786440 | tf_op jit(solution)/shard_map/ppermute | solution.py:12
where the time goes:
time: 249 us; the launch traced here: 245 us
  matrix products  92.2 us (37%)
  starting transfers between devices  78 us (31%)
  local copies, waits for them, and re-layouts  58.1 us (23%)
  waiting for transfers between devices  13.3 us (5%)
    dot_general x4, matrix products, blur(): result = jnp.einsum('abj,jc->abc', extended, matrix_z, precision=highest)  86.2 us
    ppermute x12, starting transfers between devices, padded(): lax.ppermute(lax.slice_in_dim(block, block.shape[dim] - width, None, axis...  49.9 us
    gather x20, local copies, waits for them, and re-layouts, band_matrix(): return jnp.where(valid, taps[jnp.clip(offset, 0, width - 1)], 0.0)  41.7 us
    ppermute x12, starting transfers between devices, padded(): lax.ppermute(lax.slice_in_dim(block, 0, width, axis=dim), axis, backward)  15.5 us
    all_to_all x1, starting transfers between devices, on_device(): lax.all_to_all(indices, ('gy', 'gz'), split_axis=1, concat_axis=1, tiled=...  7.39 us
    ppermute x12, waiting for transfers between devices, padded(): lax.ppermute(lax.slice_in_dim(block, block.shape[dim] - width, None, axis...  7.38 us
    ppermute x12, waiting for transfers between devices, padded(): lax.ppermute(lax.slice_in_dim(block, 0, width, axis=dim), axis, backward)  5.95 us
    all_to_all x1, starting transfers between devices, on_device(): lax.all_to_all(lines, ('gy', 'gz'), split_axis=1, concat_axis=1, tiled=True)  5.24 us
  transfers between devices with their start and end apart: 26, of which 11 were waited for; matrix products, arithmetic and copies ran while one was open for 31% of the time, Pallas kernels for 0%

commit v1 on v0

--- a/solution.py
+++ b/solution.py
@@ -1,7 +1,327 @@
+import functools
+
 import jax
 import jax.numpy as jnp
 from jax import lax
+from jax.experimental import pallas as pl
+from jax.experimental.pallas import tpu as pltpu
 from jax.sharding import PartitionSpec as P
+
+F32, BF16 = jnp.float32, jnp.bfloat16
+VMEM = pl.BlockSpec(memory_space=pltpu.VMEM)
+SMEM = pl.BlockSpec(memory_space=pltpu.SMEM)
+ALL = ("gx", "gy", "gz")
+PLANE = ("gx", "gy")
+
+
+def ring_place(x, y, z):
+    place = 2 * x + (x ^ y)
+    return place if z % 2 == 0 else 3 - place
+
+
+def slab_of(device, z):
+    x, gy = device // 4, device % 4
+    place = ring_place(x, gy // 2, z)
+    return 2 * place + ((gy % 2) ^ (place % 2))
+
+
+def chain_pairs(planes):
+    order = []
+    for z in range(planes):
+        by_slab = sorted(range(8), key=lambda device: slab_of(device, z))
+        order += [device * planes + z for device in by_slab]
+    far, near = [], []
+    for k in range(len(order) - 1):
+        pair = (order[k], order[k + 1])
+        (near if k % 2 == 0 else far).extend([pair, pair[::-1]])
+    return far, near
+
+
+def split2(value):
+    high = value.astype(BF16)
+    return high, (value - high.astype(F32)).astype(BF16)
+
+
+def split3(value):
+    high = value.astype(BF16)
+    rest = value - high.astype(F32)
+    middle = rest.astype(BF16)
+    return high, middle, (rest - middle.astype(F32)).astype(BF16)
+
+
+def dot_nn(a, b):
+    return lax.dot_general(a, b, (((1,), (0,)), ((), ())), preferred_element_type=F32)
+
+
+def dot_nt(a, b):
+    return lax.dot_general(a, b, (((1,), (1,)), ((), ())), preferred_element_type=F32)
+
+
+def call(kernel, out_shapes, in_specs, scratch=(), flops=0, **kwargs):
+    return pl.pallas_call(
+        kernel,
+        out_shape=out_shapes,
+        in_specs=in_specs,
+        out_specs=jax.tree.map(lambda _: VMEM, out_shapes),
+        scratch_shapes=list(scratch),
+        compiler_params=pltpu.CompilerParams(vmem_limit_bytes=40 * 1024 * 1024),
+        cost_estimate=pl.CostEstimate(flops=flops, bytes_accessed=1 << 20, transcendentals=0),
+        **kwargs,
+    )
+
+
+def est_kernel(planes, here, weight, est, out):
+    turned = est[...].T
+    z_odd = here[2] % 2
+    rows = lax.broadcasted_iota(jnp.int32, (8, 256), 0)
+    weights = jnp.where(
+        rows == 0,
+        weight[0, 0].astype(F32) * 0.25,
+        jnp.where(rows == 1, weight[1, 0].astype(F32) * 0.25, 0.0),
+    )
+    for parity in range(2):
+        @pl.when(z_odd == parity)
+        def _():
+            for device in range(8):
+                slab = slab_of(device, parity)
+                out[device, 0:32, :] = turned[slab * 32 : slab * 32 + 32, :]
+    for device in range(8):
+        out[device, 32:40, :] = weights
+
+
+def lines_kernel(planes, here, raw, index, out0, out1):
+    mine = here[2]
+    chunk = lax.broadcasted_iota(jnp.int32, (8, 128), 1) // 32
+    for z in range(planes):
+        numbers = [jnp.zeros((8, 128), F32)] * 2
+        rows = lax.broadcasted_iota(jnp.int32, (8, 128), 0)
+        for place in range(4):
+            block = lax.rem(place - mine + 4, 4)
+            for view in range(2):
+                row = index[pl.ds(view * 4 + block, 1), :].astype(F32)
+                row = pltpu.roll(jnp.broadcast_to(row, (8, 128)), (32 * (place - z)) % 128, 1)
+                numbers[view] = jnp.where(chunk == place, row, numbers[view])
+        both = jnp.where(rows == 0, numbers[0], jnp.where(rows == 1, numbers[1], 0.0))
+        for view, out in enumerate((out0, out1)):
+            parts = []
+            for place in range(4):
+                block = lax.rem(place - mine + 4, 4)
+                start = pl.multiple_of((block * planes + z) * 32, 32)
+                parts.append(raw[view, pl.ds(start, 32), :])
+            turned = jnp.concatenate(parts, axis=0).T
+            for device in range(8):
+                slab = slab_of(device, z)
+                out[device * planes + z, 0:32, :] = turned[slab * 32 : slab * 32 + 32, :]
+                if view == 0:
+                    out[device * planes + z, 32:40, :] = both
+
+
+def taps_kernel(psf, big_high, big_low, band, held):
+    held[...] = jnp.zeros_like(held)
+    held[0:3, 0:33] = psf[...]
+    taps = held[...]
+    total = jnp.sum(taps, axis=1, keepdims=True)
+    taps = taps / jnp.where(total == 0.0, 1.0, total)
+
+    def toeplitz(row, size):
+        wide = jnp.broadcast_to(row, (size, 128))
+        return pltpu.roll(wide, 0, 1, stride=1, stride_axis=0)
+
+    lane_r = lax.broadcasted_iota(jnp.int32, (128, 128), 0)
+    lane_c = lax.broadcasted_iota(jnp.int32, (128, 128), 1)
+    turn = (lane_r + lane_c == 32).astype(BF16)
+    pieces = split3(taps)
+    reversed_taps = sum(dot_nn(piece, turn) for piece in pieces)
+    for way, source in enumerate((taps, reversed_taps)):
+        high, low = split2(toeplitz(source[2:3, :], 32))
+        twice = high.astype(F32) + pltpu.roll(high.astype(F32), 64, 1)
+        band[way, :, 0:128] = twice.astype(BF16)
+        band[way, :, 128:256] = low
+    tall_x = jnp.broadcast_to(toeplitz(taps[0:1, :], 16)[:, None, :], (16, 16, 128)).reshape(256, 128)
+    tall_y = jnp.broadcast_to(toeplitz(taps[1:2, :], 16)[None], (16, 16, 128)).reshape(256, 128)
+    from_row = lax.broadcasted_iota(jnp.int32, (128, 256), 0)
+    to_lane = lax.broadcasted_iota(jnp.int32, (128, 256), 1)
+    wide_x, wide_y = [], []
+    for offset in range(3):
+        pick_x = (from_row == to_lane // 16 + 16 * offset).astype(BF16)
+        pick_y = (from_row == lax.rem(to_lane, 16) + 16 * offset).astype(BF16)
+        wide_x.append(sum(dot_nn(piece, pick_x) for piece in split3(tall_x)))
+        wide_y.append(sum(dot_nn(piece, pick_y) for piece in split3(tall_y)))
+    for dx in range(3):
+        for dy in range(3):
+            high, low = split2(wide_x[dx] * wide_y[dy])
+            big_high[dx * 3 + dy] = high
+            big_low[dx * 3 + dy] = low
+
+
+def scatter_kernel(view, recv0, recv1, slab, data, cover):
+    chunk = lax.broadcasted_iota(jnp.int32, (40, 128), 1) // 32
+    line = lax.broadcasted_iota(jnp.int32, (256, 512), 0).astype(F32)
+    recv = recv1 if view else recv0
+    ones = jnp.ones((16, 512), BF16)
+    for x in range(2):
+        for block in range(4):
+            column = x * 4 + block
+            numbers, values = [], []
+            for t in range(4):
+                tile = jnp.zeros((32, 128), F32)
+                number = jnp.zeros((8, 128), F32)
+                for place in range(4):
+                    source = x * 16 + 4 * t + (place - block) % 4
+                    tile = jnp.where(chunk[0:32] == place, recv[source, 0:32, :], tile)
+                    number = jnp.where(chunk[0:8] == place, recv0[source, 32:40, :], number)
+                values.append(tile)
+                numbers.append(number)
+            value = jnp.concatenate(values, axis=1)
+            number = jnp.concatenate(numbers, axis=1)[view : view + 1, :]
+            hot = (line == number).astype(BF16)
+            left = jnp.concatenate([*split3(value), ones], axis=0)
+            result = dot_nt(left, hot)
+            data[column] = result[0:32] + result[32:64] + result[64:96]
+            weight = slab[column, 32 + view : 33 + view, :]
+            cover[column] = result[96:104] * weight
+
+
+def payloads(here, value, far, near):
+    upper = here[3]
+    far[...] = value[:, pl.ds(pl.multiple_of(16 * upper, 16), 16), :]
+    near[...] = value[:, pl.ds(pl.multiple_of(16 - 16 * upper, 16), 16), :]
+
+
+def send_kernel(here, slab, far, near):
+    payloads(here, slab, far, near)
+
+
+def blurred_into(here, way, value, far, near, band, big_high, big_low, wide, flat, total):
+    upper = here[3]
+    wide[:, 16:48, :] = value[:, 0:32, :]
+    wide[:, pl.ds(pl.multiple_of(48 * upper, 16), 16), :] = far[...]
+    wide[:, pl.ds(pl.multiple_of(48 - 48 * upper, 16), 16), :] = near[...]
+    weights = band[way]
+    for column in range(8):
+        high, low = split2(wide[column])
+        stacked = jnp.concatenate([high, low, high, high], axis=0)
+        flat[column * 32 : column * 32 + 32, :] = dot_nn(weights, stacked)
+    high, low = split2(flat[...])
+
+    def product(start, stop, dx, dy):
+        if way == 0:
+            at, dot = (dx + 1) * 3 + dy + 1, dot_nt
+        else:
+            at, dot = (1 - dx) * 3 + 1 - dy, dot_nn
+        rows = stop - start
+        both = dot(jnp.concatenate([high[start:stop], low[start:stop]], axis=0), big_high[at])
+        return both[:rows] + both[rows:] + dot(high[start:stop], big_low[at])
+
+    total[...] = product(0, 256, 0, 0)
+    for dx in (-1, 0, 1):
+        for dy in (-1, 0, 1):
+            if dx == 0 and dy == 0:
+                continue
+            for x in range(2):
+                if not 0 <= x + dx < 2:
+                    continue
+                first, last = max(0, -dy), min(4, 4 - dy)
+                out = (x * 4 + first) * 32, (x * 4 + last) * 32
+                shift = (dx * 4 + dy) * 32
+                total[out[0] : out[1], :] += product(out[0] + shift, out[1] + shift, dx, dy)
+
+
+def ratio_kernel(here, est, far, near, band, big_high, big_low, data, cover, ratio, next_far, next_near, wide, flat, total):
+    blurred_into(here, 0, est, far, near, band, big_high, big_low, wide, flat, total)
+    for column in range(8):
+        blurred = total[column * 32 : column * 32 + 32, :]
+        ratio[column] = 1.0 + cover[column, 0:1, :] * (data[column] / blurred - 1.0)
+    payloads(here, ratio, next_far, next_near)
+
+
+def update_kernel(here, ratio, far, near, band, big_high, big_low, est, new, next_far, next_near, wide, flat, total):
+    blurred_into(here, 1, ratio, far, near, band, big_high, big_low, wide, flat, total)
+    for column in range(8):
+        new[column] = est[column, 0:32, :] * total[column * 32 : column * 32 + 32, :]
+    if next_far is not None:
+        payloads(here, new, next_far, next_near)
+
+
+def last_kernel(here, ratio, far, near, band, big_high, big_low, est, new, wide, flat, total):
+    update_kernel(here, ratio, far, near, band, big_high, big_low, est, new, None, None, wide, flat, total)
+
+
+def join_kernel(here, parts, out, held):
+    z_odd = here[2] % 2
+    for parity in range(2):
+        @pl.when(z_odd == parity)
+        def _():
+            for device in range(8):
+                slab = slab_of(device, parity)
+                held[slab * 32 : slab * 32 + 32, :] = parts[device]
+    out[...] = held[...].T
+
+
+def shape(*dims, dtype=F32):
+    return jax.ShapeDtypeStruct(dims, dtype)
+
+
+def slab_sweep(planes, estimate, raw_lines, line_index, psf, view_weight):
+    x, gy, z = (lax.axis_index(axis) for axis in ALL)
+    y, core = gy // 2, gy % 2
+    place = 2 * x + (x ^ y)
+    place = jnp.where(z % 2 == 0, place, 3 - place)
+    here = jnp.stack([x, gy, z, core ^ (place % 2)]).astype(jnp.int32)
+    far_pairs, near_pairs = chain_pairs(planes)
+
+    def exchange(far, near):
+        return (
+            lax.ppermute(far, ALL, far_pairs),
+            lax.ppermute(near, ALL, near_pairs),
+        )
+
+    pieces = call(
+        functools.partial(est_kernel, planes),
+        shape(8, 40, 256),
+        [SMEM, SMEM, VMEM],
+    )(here, view_weight.reshape(2, 1), estimate.reshape(256, 256))
+    slab = lax.all_to_all(pieces, PLANE, split_axis=0, concat_axis=0, tiled=True)
+    lines0, lines1 = call(
+        functools.partial(lines_kernel, planes),
+        (shape(8 * planes, 40, 128), shape(8 * planes, 32, 128)),
+        [SMEM, VMEM, VMEM],
+    )(here, raw_lines.reshape(2, 4 * planes * 32, 256), line_index.reshape(8, 128))
+    lines0 = lax.all_to_all(lines0, ALL, split_axis=0, concat_axis=0, tiled=True)
+    lines1 = lax.all_to_all(lines1, ALL, split_axis=0, concat_axis=0, tiled=True)
+    half = shape(8, 16, 256)
+    scratch = [pltpu.VMEM((8, 64, 256), F32), pltpu.VMEM((256, 256), F32), pltpu.VMEM((256, 256), F32)]
+    far, near = call(send_kernel, (half, half), [SMEM, VMEM])(here, slab)
+    est = slab
+    for view in range(2):
+        big_high, big_low, band = call(
+            taps_kernel,
+            (shape(9, 256, 256, dtype=BF16), shape(9, 256, 256, dtype=BF16), shape(2, 32, 256, dtype=BF16)),
+            [VMEM],
+            [pltpu.VMEM((8, 128), F32)],
+            flops=1 << 30,
+        )(psf[view])
+        data, cover = call(
+            functools.partial(scatter_kernel, view),
+            (shape(8, 32, 256), shape(8, 8, 256)),
+            [VMEM] * 3,
+            flops=1 << 30,
+        )(lines0, lines1, slab)
+        mats = (band, big_high, big_low)
+        ratio, far, near = call(
+            ratio_kernel, (shape(8, 32, 256), half, half), [SMEM] + [VMEM] * 8, scratch, flops=1 << 30
+        )(here, est, *exchange(far, near), *mats, data, cover)
+        if view == 0:
+            est, far, near = call(
+                update_kernel, (shape(8, 32, 256), half, half), [SMEM] + [VMEM] * 7, scratch, flops=1 << 30
+            )(here, ratio, *exchange(far, near), *mats, est)
+        else:
+            est = call(last_kernel, shape(8, 32, 256), [SMEM] + [VMEM] * 7, scratch, flops=1 << 30)(
+                here, ratio, *exchange(far, near), *mats, est
+            )
+    parts = lax.all_to_all(est, PLANE, split_axis=0, concat_axis=0, tiled=True)
+    out = call(join_kernel, shape(256, 256), [SMEM, VMEM], [pltpu.VMEM((256, 256), F32)])(here, parts)
+    return out.reshape(16, 16, 256)
 
 
 def padded(block, sides, width):
@@ -49,7 +369,7 @@
     return result
 
 
-def on_device(estimate, raw_lines, line_index, psf, view_weight):
+def block_sweep(estimate, raw_lines, line_index, psf, view_weight):
     size_x, size_y, size_z = estimate.shape
     block_lines = size_x * size_y
     views = raw_lines.shape[0]
@@ -90,6 +410,20 @@
         P(),
         P(None, "gx", "gy", "gz"),
     )
+    sizes = tuple(mesh.shape[axis] for axis in ALL)
+
+    def on_device(estimate, raw_lines, line_index, psf, view_weight):
+        capacity = line_index.shape[-1] // (sizes[1] * sizes[2])
+        fits = (
+            sizes == (2, 4, 4)
+            and estimate.shape == (16, 16, 256)
+            and raw_lines.shape[0] == 2
+            and capacity == 32
+            and psf.shape == (2, 3, 33)
+        )
+        plan = functools.partial(slab_sweep, sizes[2]) if fits else block_sweep
+        return plan(estimate, raw_lines, line_index, psf, view_weight)
+
     return jax.shard_map(
         on_device, mesh=mesh, in_specs=placed, out_specs=P("gx", "gy", "gz"), check_vma=False
     )

time: 249 us -> 95.2 us (0.38); the launches traced: 245 us -> 94.7 us
  matrix products: 92.2 us -> 0 us
  local copies, waits for them, and re-layouts: 58.1 us -> 3.25 us
  starting transfers between devices: 78 us -> 26.2 us
  blocking collectives: 0 us -> 31.9 us
  Pallas kernels: 0 us -> 15.5 us
  waiting for transfers between devices: 13.3 us -> 17.6 us
    dot_general x12 -> x0, matrix products: 92.2 us -> none  [the longest x4 86.2 us: blur(): result = jnp.einsum('abj,jc->abc', extended, matrix_z, precision=highest)]
    ppermute x24 -> x8, starting transfers between devices: 65.4 us -> 17 us  [the longest x4 14.3 us: exchange(): lax.ppermute(near, ALL, near_pairs)]
    gather x20 -> x0, local copies, waits for them, and re-layouts: 41.7 us -> none  [band_matrix(): return jnp.where(valid, taps[jnp.clip(offset, 0, width - 1)], 0.0)]
    all_to_all x0 -> x2, blocking collectives: none -> 31.9 us  [the longest x1 19.1 us: slab_sweep(): lax.all_to_all(lines1, ALL, split_axis=0, concat_axis=0, tiled=True)]
    all_to_all x2, waiting for transfers between devices: 0.01 us -> 15.6 us  [the longest x1 10.6 us: slab_sweep(): lax.all_to_all(lines0, ALL, split_axis=0, concat_axis=0, tiled=True)]
    pallas_call x0 -> x12, Pallas kernels: none -> 15.5 us  [the longest x2 3.58 us: slab_sweep(): call(ratio_kernel, (shape(8, 32, 256), half, half), [SMEM] + [VMEM] * 8,...]
    ppermute x24 -> x8, waiting for transfers between devices: 13.3 us -> 1.98 us  [the longest x4 1.97 us: exchange(): lax.ppermute(near, ALL, near_pairs)]
    scatter x4 -> x0, local copies, waits for them, and re-layouts: 9.51 us -> none  [the longest x2 4.87 us: on_device(): jnp.zeros((block_lines,), jnp.float32).at[flat_index].set(1.0, mode='drop')]
  transfers between devices with their start and end apart: 26 -> 10, of which waited for: 11 -> 4; matrix products, arithmetic and copies ran while one was open for 31% -> 0% of each run, Pallas kernels for 0% -> 6%
where the time goes in v1:
time: 95.2 us; the launch traced here: 94.7 us
  blocking collectives  31.9 us (34%)
  starting transfers between devices  26.2 us (28%)
  waiting for transfers between devices  17.6 us (18%)
  Pallas kernels  15.5 us (16%)
  local copies, waits for them, and re-layouts  3.25 us (3%)
    all_to_all x1, blocking collectives, slab_sweep(): lax.all_to_all(lines1, ALL, split_axis=0, concat_axis=0, tiled=True)  19.1 us
    ppermute x4, starting transfers between devices, exchange(): lax.ppermute(near, ALL, near_pairs)  14.3 us
    all_to_all x1, blocking collectives, slab_sweep(): parts = lax.all_to_all(est, PLANE, split_axis=0, concat_axis=0, tiled=True)  12.8 us
    all_to_all x1, waiting for transfers between devices, slab_sweep(): lax.all_to_all(lines0, ALL, split_axis=0, concat_axis=0, tiled=True)  10.6 us
    all_to_all x1, starting transfers between devices, slab_sweep(): lax.all_to_all(pieces, PLANE, split_axis=0, concat_axis=0, tiled=True)  5.17 us
    all_to_all x1, waiting for transfers between devices, slab_sweep(): lax.all_to_all(pieces, PLANE, split_axis=0, concat_axis=0, tiled=True)  5.02 us
    all_to_all x1, starting transfers between devices, slab_sweep(): lax.all_to_all(lines0, ALL, split_axis=0, concat_axis=0, tiled=True)  4.07 us
    pallas_call x2, Pallas kernels, slab_sweep(): call(ratio_kernel, (shape(8, 32, 256), half, half), [SMEM] + [VMEM] * 8,...  3.58 us
  transfers between devices with their start and end apart: 10, of which 4 were waited for; matrix products, arithmetic and copies ran while one was open for 0% of the time, Pallas kernels for 6%

profile of v1, /device:TPU:0, one launch (start us, length us, event | category | flops | bytes accessed | tf_op | source)
XLA Modules:
  0.0 94.7 jit_solution(9107184276755789242)
XLA Ops:
  0.0 0.8 copy.7.weight
  0.9 0.9 %copy-done.1 = f32[16,16,256]{2,1,0:T(8,128)S(1)} copy-done((f32[16,16,256]{2,1,0:T(8,128)S(1)}, f32[16,16,256]{2,1,0:T(8,128)}, u32[]{:S(2)}) %copy-start.1) | copy-done | bytes 262168
  1.9 1.4 %shard_map.55 = f32[8,40,256]{2,1,0:T(8,128)} custom-call(s32[4]{0:T(128)S(1)} %pad_add_fusion.here, s32[2,1]{1,0:T(2,128)S(1)} %copy.7.weight, f32[256,256]{1,0:T(8,128)S(1)} %bitcast.14), custom_call_target="tpu_custom_call" | custom-call | bytes 1048576 | tf_op jit(solution)/shard_map/pallas_call | solution.py:279
  3.3 5.2 %all-to-all-start = ((f32[8,40,256]{2,1,0:T(8,128)}), f32[8,40,256]{2,1,0:T(8,128)S(1)}, u32[]{:S(2)}, u32[]{:S(2)}) async-start(f32[8,40,256]{2,1,0:T(8,128)} %shard_map.55), calls=%async_computation | async-start | bytes 655360 | tf_op jit(solution)/shard_map/all_to_all | solution.py:284
  8.5 1.7 %shard_map.58 = (f32[32,40,128]{2,1,0:T(8,128)}, f32[32,32,128]{2,1,0:T(8,128)S(1)}) custom-call(s32[4]{0:T(128)S(1)} %pad_add_fusion.here, f32[2,512,256]{2,1,0:T(8,128)S(1)} %bitcast.13, s32[8,128]{1,0:T(8,128)S(1)} %bitcast.15), custom_call_target="tpu_custom_call" | custom-call | bytes 1048576 | tf_op jit(solution)/shard_map/pallas_call | solution.py:285
  10.2 5.0 %all-to-all-done.slab.est = f32[8,40,256]{2,1,0:T(8,128)S(1)} async-done(((f32[8,40,256]{2,1,0:T(8,128)}), f32[8,40,256]{2,1,0:T(8,128)S(1)}, u32[]{:S(2)}, u32[]{:S(2)}) %all-to-all-start) | async-done | bytes 327712 | tf_op jit(solution)/shard_map/all_to_all | solution.py:284
  15.2 19.1 %all_to_all.20.recv1 = f32[32,32,128]{2,1,0:T(8,128)S(1)} all-to-all(f32[32,32,128]{2,1,0:T(8,128)S(1)} %get-tuple-element.34), channel_id=1, replica_groups=mesh['gx'=2,'gy'=4,'gz'=4] {'gx','gy','gz'}, dimensions={0} | all-to-all | bytes 1048576 | tf_op jit(solution)/shard_map/all_to_all | solution.py:291
  34.3 4.1 %all-to-all-start.1 = ((f32[32,40,128]{2,1,0:T(8,128)}), f32[32,40,128]{2,1,0:T(8,128)S(1)}, u32[]{:S(2)}, u32[]{:S(2)}) async-start(f32[32,40,128]{2,1,0:T(8,128)} %get-tuple-element.33), calls=%async_computation.1 | async-start | bytes 1310720 | tf_op jit(solution)/shard_map/all_to_all | solution.py:290
  38.4 0.6 shard_map.56
  39.0 0.7 collective-permute-start
  39.7 2.9 %collective-permute-start.1 = (f32[8,16,256]{2,1,0:T(8,128)S(1)}, f32[8,16,256]{2,1,0:T(8,128)S(1)}, u32[]{:S(2)}, u32[]{:S(2)}) collective-permute-start(f32[8,16,256]{2,1,0:T(8,128)S(1)} %get-tuple-element.29), channel_id=1, source_target_pairs={{0,4},{4,0},{12,8},{8,12},{24,28},{28,24},{20,16},{16,20},{17,21},... | collective-permute-start | bytes 393224 | tf_op jit(solution)/shard_map/ppermute | solution.py:276
  42.6 1.1 %shard_map.57 = (bf16[9,256,256]{2,1,0:T(8,128)(2,1)S(1)}, bf16[9,256,256]{2,1,0:T(8,128)(2,1)S(1)}, bf16[2,32,256]{2,1,0:T(8,128)(2,1)S(1)}) custom-call(f32[3,33]{1,0:T(4,128)S(1)} %get-tuple-element.54.psf), custom_call_target="tpu_custom_call" | custom-call | flops 1073741824 | bytes 1048576 | tf_op jit(solution)/shard_map/pallas_call | solution.py:297
  43.7 1.0 %copy-done.3 = bf16[9,256,256]{2,1,0:T(8,128)(2,1)} copy-done((bf16[9,256,256]{2,1,0:T(8,128)(2,1)}, bf16[9,256,256]{2,1,0:T(8,128)(2,1)S(1)}, u32[]{:S(2)}) %copy-start.3) | copy-done | bytes 1179672
  44.7 10.6 %all-to-all-done.1.recv0 = f32[32,40,128]{2,1,0:T(8,128)S(1)} async-done(((f32[32,40,128]{2,1,0:T(8,128)}), f32[32,40,128]{2,1,0:T(8,128)S(1)}, u32[]{:S(2)}, u32[]{:S(2)}) %all-to-all-start.1) | async-done | bytes 655392 | tf_op jit(solution)/shard_map/all_to_all | solution.py:290
  55.3 0.8 shard_map.59
  56.2 0.4 copy-done.4
  56.6 1.8 %shard_map.60 = (f32[8,32,256]{2,1,0:T(8,128)S(1)}, f32[8,16,256]{2,1,0:T(8,128)S(1)}, f32[8,16,256]{2,1,0:T(8,128)S(1)}) custom-call(s32[4]{0:T(128)S(1)} %pad_add_fusion.here, f32[8,40,256]{2,1,0:T(8,128)S(1)} %all-to-all-done.slab.est, f32[8,16,256]{2,1,0:T(8,128)S(1)} %collective-permute-done.far, f32[8,16,256]{2,1,0:T(8,128)S(1)} %collective-permute-done.1.near, ...), custom_call_target="tpu_custom_call" | custom-call | flops 1073741824 | bytes 1048576 | tf_op jit(solution)/shard_map/pallas_call | solution.py:311
  58.4 0.7 collective-permute-start.2
  59.1 3.9 %collective-permute-start.3 = (f32[8,16,256]{2,1,0:T(8,128)S(1)}, f32[8,16,256]{2,1,0:T(8,128)S(1)}, u32[]{:S(2)}, u32[]{:S(2)}) collective-permute-start(f32[8,16,256]{2,1,0:T(8,128)S(1)} %get-tuple-element.39), channel_id=1, source_target_pairs={{0,4},{4,0},{12,8},{8,12},{24,28},{28,24},{20,16},{16,20},{17,21},... | collective-permute-start | bytes 393224 | tf_op jit(solution)/shard_map/ppermute | solution.py:276
  62.9 1.0 %collective-permute-done.3.near = f32[8,16,256]{2,1,0:T(8,128)S(1)} collective-permute-done((f32[8,16,256]{2,1,0:T(8,128)S(1)}, f32[8,16,256]{2,1,0:T(8,128)S(1)}, u32[]{:S(2)}, u32[]{:S(2)}) %collective-permute-start.3) | collective-permute-done | bytes 131104 | tf_op jit(solution)/shard_map/ppermute | solution.py:276
  63.9 1.5 %shard_map.61 = (f32[8,32,256]{2,1,0:T(8,128)S(1)}, f32[8,16,256]{2,1,0:T(8,128)S(1)}, f32[8,16,256]{2,1,0:T(8,128)S(1)}) custom-call(s32[4]{0:T(128)S(1)} %pad_add_fusion.here, f32[8,32,256]{2,1,0:T(8,128)S(1)} %get-tuple-element.37.ratio, f32[8,16,256]{2,1,0:T(8,128)S(1)} %collective-permute-done.2.far, f32[8,16,256]{2,1,0:T(8,128)S(1)} %collective-permute-done.3.near, ...), custom_call_target="tpu_custom_call" | custom-call | flops 1073741824 | bytes 1048576 | tf_op jit(solution)/shard_map/pallas_call | solution.py:315
  65.4 0.7 collective-permute-start.4
  66.1 4.1 %collective-permute-start.5 = (f32[8,16,256]{2,1,0:T(8,128)S(1)}, f32[8,16,256]{2,1,0:T(8,128)S(1)}, u32[]{:S(2)}, u32[]{:S(2)}) collective-permute-start(f32[8,16,256]{2,1,0:T(8,128)S(1)} %get-tuple-element.42), channel_id=1, source_target_pairs={{0,4},{4,0},{12,8},{8,12},{24,28},{28,24},{20,16},{16,20},{17,21},... | collective-permute-start | bytes 393224 | tf_op jit(solution)/shard_map/ppermute | solution.py:276
  70.2 1.0 %shard_map.62 = (bf16[9,256,256]{2,1,0:T(8,128)(2,1)S(1)}, bf16[9,256,256]{2,1,0:T(8,128)(2,1)S(1)}, bf16[2,32,256]{2,1,0:T(8,128)(2,1)S(1)}) custom-call(f32[3,33]{1,0:T(4,128)S(1)} %get-tuple-element.53.psf), custom_call_target="tpu_custom_call" | custom-call | flops 1073741824 | bytes 1048576 | tf_op jit(solution)/shard_map/pallas_call | solution.py:297
  71.2 0.8 shard_map.63
  72.1 1.8 %shard_map.64 = (f32[8,32,256]{2,1,0:T(8,128)S(1)}, f32[8,16,256]{2,1,0:T(8,128)S(1)}, f32[8,16,256]{2,1,0:T(8,128)S(1)}) custom-call(s32[4]{0:T(128)S(1)} %pad_add_fusion.here, f32[8,32,256]{2,1,0:T(8,128)S(1)} %get-tuple-element.40.est, f32[8,16,256]{2,1,0:T(8,128)S(1)} %collective-permute-done.4.far, f32[8,16,256]{2,1,0:T(8,128)S(1)} %collective-permute-done.5.near, ...), custom_call_target="tpu_custom_call" | custom-call | flops 1073741824 | bytes 1048576 | tf_op jit(solution)/shard_map/pallas_call | solution.py:311
  73.9 0.7 collective-permute-start.6
  74.6 3.4 %collective-permute-start.7 = (f32[8,16,256]{2,1,0:T(8,128)S(1)}, f32[8,16,256]{2,1,0:T(8,128)S(1)}, u32[]{:S(2)}, u32[]{:S(2)}) collective-permute-start(f32[8,16,256]{2,1,0:T(8,128)S(1)} %get-tuple-element.50), channel_id=1, source_target_pairs={{0,4},{4,0},{12,8},{8,12},{24,28},{28,24},{20,16},{16,20},{17,21},... | collective-permute-start | bytes 393224 | tf_op jit(solution)/shard_map/ppermute | solution.py:276
  78.0 1.0 %collective-permute-done.7.near = f32[8,16,256]{2,1,0:T(8,128)S(1)} collective-permute-done((f32[8,16,256]{2,1,0:T(8,128)S(1)}, f32[8,16,256]{2,1,0:T(8,128)S(1)}, u32[]{:S(2)}, u32[]{:S(2)}) %collective-permute-start.7) | collective-permute-done | bytes 131104 | tf_op jit(solution)/shard_map/ppermute | solution.py:276
  79.0 1.5 %shard_map.65 = f32[8,32,256]{2,1,0:T(8,128)S(1)} custom-call(s32[4]{0:T(128)S(1)} %pad_add_fusion.here, f32[8,32,256]{2,1,0:T(8,128)S(1)} %get-tuple-element.48.ratio, f32[8,16,256]{2,1,0:T(8,128)S(1)} %collective-permute-done.6.far, f32[8,16,256]{2,1,0:T(8,128)S(1)} %collective-permute-done.7.near, bf16[2,32,256]{2,1,0:T(8,128)(2,1)S(1)} %get-tuple-element.43.band, ...), custom_call_target="tpu_custom_call" | custom-call | flops 1073741824 | bytes 1048576 | tf_op jit(solution)/shard_map/pallas_call | solution.py:319
  80.5 12.8 %all_to_all.21.parts = f32[8,32,256]{2,1,0:T(8,128)S(1)} all-to-all(f32[8,32,256]{2,1,0:T(8,128)S(1)} %shard_map.65), channel_id=1, replica_groups=mesh['gx'=2,'gy'=4,'gz'=4] {'gx','gy'}, dimensions={0} | all-to-all | bytes 524288 | tf_op jit(solution)/shard_map/all_to_all | solution.py:322
  93.3 1.4 %shard_map.66 = f32[256,256]{1,0:T(8,128)} custom-call(s32[4]{0:T(128)S(1)} %pad_add_fusion.here, f32[8,32,256]{2,1,0:T(8,128)S(1)} %all_to_all.21.parts), custom_call_target="tpu_custom_call" | custom-call | bytes 1048576 | tf_op jit(solution)/shard_map/pallas_call | solution.py:323
  (18 shorter events, 0.1 us)
Async XLA Ops:
  0.0 8.5 %copy-start = (f32[2,1,1,512,256]{4,3,2,1,0:T(8,128)S(1)}, f32[2,1,1,512,256]{4,3,2,1,0:T(8,128)}, u32[]{:S(2)}) copy-start(f32[2,1,1,512,256]{4,3,2,1,0:T(8,128)} %param.6) | copy-start | bytes 3145732
  0.9 1.0 %copy-start.1 = (f32[16,16,256]{2,1,0:T(8,128)S(1)}, f32[16,16,256]{2,1,0:T(8,128)}, u32[]{:S(2)}) copy-start(f32[16,16,256]{2,1,0:T(8,128)} %param.5) | copy-start | bytes 786436
  1.9 6.6 %copy-start.2 = (s32[2,1,1,512]{3,2,1,0:T(1,128)S(1)}, s32[2,1,1,512]{3,2,1,0:T(1,128)}, u32[]{:S(2)}) copy-start(s32[2,1,1,512]{3,2,1,0:T(1,128)} %param.7) | copy-start | bytes 12292
  3.3 12.0 %all-to-all-start = ((f32[8,40,256]{2,1,0:T(8,128)}), f32[8,40,256]{2,1,0:T(8,128)S(1)}, u32[]{:S(2)}, u32[]{:S(2)}) async-start(f32[8,40,256]{2,1,0:T(8,128)} %shard_map.55), calls=%async_computation | async-start | bytes 655360 | tf_op jit(solution)/shard_map/all_to_all | solution.py:284
  15.2 23.1 %copy-start.5 = (f32[2,3,33]{2,0,1:T(2,128)S(1)}, f32[2,3,33]{2,0,1:T(2,128)}, u32[]{:S(2)}) copy-start(f32[2,3,33]{2,0,1:T(2,128)} %param.8) | copy-start | bytes 2380
  34.3 21.0 %all-to-all-start.1 = ((f32[32,40,128]{2,1,0:T(8,128)}), f32[32,40,128]{2,1,0:T(8,128)S(1)}, u32[]{:S(2)}, u32[]{:S(2)}) async-start(f32[32,40,128]{2,1,0:T(8,128)} %get-tuple-element.33), calls=%async_computation.1 | async-start | bytes 1310720 | tf_op jit(solution)/shard_map/all_to_all | solution.py:290
  39.0 17.2 %collective-permute-start = (f32[8,16,256]{2,1,0:T(8,128)S(1)}, f32[8,16,256]{2,1,0:T(8,128)S(1)}, u32[]{:S(2)}, u32[]{:S(2)}) collective-permute-start(f32[8,16,256]{2,1,0:T(8,128)S(1)} %get-tuple-element.28), channel_id=1, source_target_pairs={{4,12},{12,4},{8,24},{24,8},{28,20},{20,28},{16,17},{17,16},{21,29... | collective-permute-start | bytes 393224 | tf_op jit(solution)/shard_map/ppermute | solution.py:275
  39.7 16.5 %collective-permute-start.1 = (f32[8,16,256]{2,1,0:T(8,128)S(1)}, f32[8,16,256]{2,1,0:T(8,128)S(1)}, u32[]{:S(2)}, u32[]{:S(2)}) collective-permute-start(f32[8,16,256]{2,1,0:T(8,128)S(1)} %get-tuple-element.29), channel_id=1, source_target_pairs={{0,4},{4,0},{12,8},{8,12},{24,28},{28,24},{20,16},{16,20},{17,21},... | collective-permute-start | bytes 393224 | tf_op jit(solution)/shard_map/ppermute | solution.py:276
  43.7 1.0 %copy-start.3 = (bf16[9,256,256]{2,1,0:T(8,128)(2,1)}, bf16[9,256,256]{2,1,0:T(8,128)(2,1)S(1)}, u32[]{:S(2)}) copy-start(bf16[9,256,256]{2,1,0:T(8,128)(2,1)S(1)} %get-tuple-element.32.big_low) | copy-start | bytes 3538948
  55.3 1.3 %copy-start.4 = (bf16[9,256,256]{2,1,0:T(8,128)(2,1)S(1)}, bf16[9,256,256]{2,1,0:T(8,128)(2,1)}, u32[]{:S(2)}) copy-start(bf16[9,256,256]{2,1,0:T(8,128)(2,1)} %copy-done.3) | copy-start | bytes 3538948
  58.4 4.5 %collective-permute-start.2 = (f32[8,16,256]{2,1,0:T(8,128)S(1)}, f32[8,16,256]{2,1,0:T(8,128)S(1)}, u32[]{:S(2)}, u32[]{:S(2)}) collective-permute-start(f32[8,16,256]{2,1,0:T(8,128)S(1)} %get-tuple-element.38), channel_id=1, source_target_pairs={{4,12},{12,4},{8,24},{24,8},{28,20},{20,28},{16,17},{17,16},{21,29... | collective-permute-start | bytes 393224 | tf_op jit(solution)/shard_map/ppermute | solution.py:275
  59.1 4.9 %collective-permute-start.3 = (f32[8,16,256]{2,1,0:T(8,128)S(1)}, f32[8,16,256]{2,1,0:T(8,128)S(1)}, u32[]{:S(2)}, u32[]{:S(2)}) collective-permute-start(f32[8,16,256]{2,1,0:T(8,128)S(1)} %get-tuple-element.39), channel_id=1, source_target_pairs={{0,4},{4,0},{12,8},{8,12},{24,28},{28,24},{20,16},{16,20},{17,21},... | collective-permute-start | bytes 393224 | tf_op jit(solution)/shard_map/ppermute | solution.py:276
  65.4 6.6 %collective-permute-start.4 = (f32[8,16,256]{2,1,0:T(8,128)S(1)}, f32[8,16,256]{2,1,0:T(8,128)S(1)}, u32[]{:S(2)}, u32[]{:S(2)}) collective-permute-start(f32[8,16,256]{2,1,0:T(8,128)S(1)} %get-tuple-element.41), channel_id=1, source_target_pairs={{4,12},{12,4},{8,24},{24,8},{28,20},{20,28},{16,17},{17,16},{21,29... | collective-permute-start | bytes 393224 | tf_op jit(solution)/shard_map/ppermute | solution.py:275
  66.1 6.0 %collective-permute-start.5 = (f32[8,16,256]{2,1,0:T(8,128)S(1)}, f32[8,16,256]{2,1,0:T(8,128)S(1)}, u32[]{:S(2)}, u32[]{:S(2)}) collective-permute-start(f32[8,16,256]{2,1,0:T(8,128)S(1)} %get-tuple-element.42), channel_id=1, source_target_pairs={{0,4},{4,0},{12,8},{8,12},{24,28},{28,24},{20,16},{16,20},{17,21},... | collective-permute-start | bytes 393224 | tf_op jit(solution)/shard_map/ppermute | solution.py:276
  73.9 4.1 %collective-permute-start.6 = (f32[8,16,256]{2,1,0:T(8,128)S(1)}, f32[8,16,256]{2,1,0:T(8,128)S(1)}, u32[]{:S(2)}, u32[]{:S(2)}) collective-permute-start(f32[8,16,256]{2,1,0:T(8,128)S(1)} %get-tuple-element.49), channel_id=1, source_target_pairs={{4,12},{12,4},{8,24},{24,8},{28,20},{20,28},{16,17},{17,16},{21,29... | collective-permute-start | bytes 393224 | tf_op jit(solution)/shard_map/ppermute | solution.py:275
  74.6 4.4 %collective-permute-start.7 = (f32[8,16,256]{2,1,0:T(8,128)S(1)}, f32[8,16,256]{2,1,0:T(8,128)S(1)}, u32[]{:S(2)}, u32[]{:S(2)}) collective-permute-start(f32[8,16,256]{2,1,0:T(8,128)S(1)} %get-tuple-element.50), channel_id=1, source_target_pairs={{0,4},{4,0},{12,8},{8,12},{24,28},{28,24},{20,16},{16,20},{17,21},... | collective-permute-start | bytes 393224 | tf_op jit(solution)/shard_map/ppermute | solution.py:276

commit v2 on v1

--- a/solution.py
+++ b/solution.py
@@ -11,7 +11,6 @@
 VMEM = pl.BlockSpec(memory_space=pltpu.VMEM)
 SMEM = pl.BlockSpec(memory_space=pltpu.SMEM)
 ALL = ("gx", "gy", "gz")
-PLANE = ("gx", "gy")
 
 
 def ring_place(x, y, z):
@@ -64,61 +63,90 @@
         in_specs=in_specs,
         out_specs=jax.tree.map(lambda _: VMEM, out_shapes),
         scratch_shapes=list(scratch),
-        compiler_params=pltpu.CompilerParams(vmem_limit_bytes=40 * 1024 * 1024),
+        compiler_params=pltpu.CompilerParams(vmem_limit_bytes=16 * 1024 * 1024),
         cost_estimate=pl.CostEstimate(flops=flops, bytes_accessed=1 << 20, transcendentals=0),
         **kwargs,
     )
 
 
-def est_kernel(planes, here, weight, est, out):
-    turned = est[...].T
-    z_odd = here[2] % 2
+def coordinates():
+    x, gy, z = (lax.axis_index(axis) for axis in ALL)
+    y, core = gy // 2, lax.rem(gy, 2)
+    return x, y, core, z
+
+
+def place_on_ring(x, y, z):
+    place = 2 * x + lax.rem(x + y, 2)
+    return jnp.where(lax.rem(z, 2) == 0, place, 3 - place)
+
+
+def upper_half():
+    x, y, core, z = coordinates()
+    return lax.rem(core + place_on_ring(x, y, z), 2)
+
+
+def chips():
+    x, y, _, z = coordinates()
+    for flip in range(4):
+        other_x = 1 - x if flip // 2 else x
+        other_y = 1 - y if flip % 2 else y
+        yield flip, other_x, other_y, place_on_ring(other_x, other_y, z)
+
+
+def est_kernel(weight, est, *refs):
+    pieces, turned = refs[:4], refs[4]
+    turned[...] = est[...].T
     rows = lax.broadcasted_iota(jnp.int32, (8, 256), 0)
     weights = jnp.where(
         rows == 0,
-        weight[0, 0].astype(F32) * 0.25,
-        jnp.where(rows == 1, weight[1, 0].astype(F32) * 0.25, 0.0),
-    )
-    for parity in range(2):
-        @pl.when(z_odd == parity)
-        def _():
-            for device in range(8):
-                slab = slab_of(device, parity)
-                out[device, 0:32, :] = turned[slab * 32 : slab * 32 + 32, :]
-    for device in range(8):
-        out[device, 32:40, :] = weights
-
-
-def lines_kernel(planes, here, raw, index, out0, out1):
-    mine = here[2]
+        weight[0].astype(F32) * 0.25,
+        jnp.where(rows == 1, weight[1].astype(F32) * 0.25, 0.0),
+    )
+    for flip, _, _, place in chips():
+        pieces[flip][0:64, :] = turned[pl.ds(pl.multiple_of(place * 64, 64), 64), :]
+        pieces[flip][64:72, :] = weights
+
+
+def slab_kernel(*refs):
+    pieces, (slab, weights, far, near) = refs[:8], refs[8:]
+    _, _, core, _ = coordinates()
+    upper = upper_half()
+    for flip, x, y, _ in chips():
+        for turn in range(2):
+            piece = pieces[4 * turn + flip]
+            column = 4 * x + 2 * y + (core if turn == 0 else 1 - core)
+            slab[column] = piece[pl.ds(pl.multiple_of(32 * upper, 32), 32), :]
+            weights[column] = piece[64:72, :]
+            far[column] = piece[pl.ds(pl.multiple_of(48 * upper, 16), 16), :]
+            near[column] = piece[pl.ds(pl.multiple_of(32 - 16 * upper, 16), 16), :]
+
+
+def lines_kernel(planes, raw, index, out):
+    mine = lax.axis_index("gz")
     chunk = lax.broadcasted_iota(jnp.int32, (8, 128), 1) // 32
+    rows = lax.broadcasted_iota(jnp.int32, (8, 128), 0)
     for z in range(planes):
-        numbers = [jnp.zeros((8, 128), F32)] * 2
-        rows = lax.broadcasted_iota(jnp.int32, (8, 128), 0)
-        for place in range(4):
-            block = lax.rem(place - mine + 4, 4)
-            for view in range(2):
-                row = index[pl.ds(view * 4 + block, 1), :].astype(F32)
-                row = pltpu.roll(jnp.broadcast_to(row, (8, 128)), (32 * (place - z)) % 128, 1)
-                numbers[view] = jnp.where(chunk == place, row, numbers[view])
-        both = jnp.where(rows == 0, numbers[0], jnp.where(rows == 1, numbers[1], 0.0))
-        for view, out in enumerate((out0, out1)):
+        both = jnp.zeros((8, 128), F32)
+        for view in range(2):
             parts = []
             for place in range(4):
                 block = lax.rem(place - mine + 4, 4)
                 start = pl.multiple_of((block * planes + z) * 32, 32)
                 parts.append(raw[view, pl.ds(start, 32), :])
+                row = index[pl.ds(view * 4 + block, 1), :].astype(F32)
+                row = pltpu.roll(jnp.broadcast_to(row, (8, 128)), (32 * (place - z)) % 128, 1)
+                both = jnp.where((chunk == place) & (rows == view), row, both)
             turned = jnp.concatenate(parts, axis=0).T
             for device in range(8):
                 slab = slab_of(device, z)
-                out[device * planes + z, 0:32, :] = turned[slab * 32 : slab * 32 + 32, :]
-                if view == 0:
-                    out[device * planes + z, 32:40, :] = both
-
-
-def taps_kernel(psf, big_high, big_low, band, held):
+                out[device * planes + z, 32 * view : 32 * view + 32, :] = turned[slab * 32 : slab * 32 + 32, :]
+        for device in range(8):
+            out[device * planes + z, 64:72, :] = both
+
+
+def taps_kernel(view, psf, big_high, big_low, band, held):
     held[...] = jnp.zeros_like(held)
-    held[0:3, 0:33] = psf[...]
+    held[0:3, 0:33] = psf[:, view, :]
     taps = held[...]
     total = jnp.sum(taps, axis=1, keepdims=True)
     taps = taps / jnp.where(total == 0.0, 1.0, total)
@@ -154,47 +182,44 @@
             big_low[dx * 3 + dy] = low
 
 
-def scatter_kernel(view, recv0, recv1, slab, data, cover):
-    chunk = lax.broadcasted_iota(jnp.int32, (40, 128), 1) // 32
+def scattered(view, slots, weights, column):
+    chunk = lax.broadcasted_iota(jnp.int32, (32, 128), 1) // 32
     line = lax.broadcasted_iota(jnp.int32, (256, 512), 0).astype(F32)
-    recv = recv1 if view else recv0
-    ones = jnp.ones((16, 512), BF16)
-    for x in range(2):
-        for block in range(4):
-            column = x * 4 + block
-            numbers, values = [], []
-            for t in range(4):
-                tile = jnp.zeros((32, 128), F32)
-                number = jnp.zeros((8, 128), F32)
-                for place in range(4):
-                    source = x * 16 + 4 * t + (place - block) % 4
-                    tile = jnp.where(chunk[0:32] == place, recv[source, 0:32, :], tile)
-                    number = jnp.where(chunk[0:8] == place, recv0[source, 32:40, :], number)
-                values.append(tile)
-                numbers.append(number)
-            value = jnp.concatenate(values, axis=1)
-            number = jnp.concatenate(numbers, axis=1)[view : view + 1, :]
-            hot = (line == number).astype(BF16)
-            left = jnp.concatenate([*split3(value), ones], axis=0)
-            result = dot_nt(left, hot)
-            data[column] = result[0:32] + result[32:64] + result[64:96]
-            weight = slab[column, 32 + view : 33 + view, :]
-            cover[column] = result[96:104] * weight
-
-
-def payloads(here, value, far, near):
-    upper = here[3]
+    x, block = column // 4, column % 4
+    numbers, values = [], []
+    for t in range(4):
+        tile = jnp.zeros((32, 128), F32)
+        number = jnp.zeros((8, 128), F32)
+        for place in range(4):
+            source = x * 16 + 4 * t + (place - block) % 4
+            tile = jnp.where(chunk == place, slots[source, 32 * view : 32 * view + 32, :], tile)
+            number = jnp.where(chunk[0:8] == place, slots[source, 64:72, :], number)
+        values.append(tile)
+        numbers.append(number)
+    value = jnp.concatenate(values, axis=1)
+    number = jnp.concatenate(numbers, axis=1)[view : view + 1, :]
+    hot = (line == number).astype(BF16)
+    left = jnp.concatenate([*split3(value), jnp.ones((16, 512), BF16)], axis=0)
+    result = dot_nt(left, hot)
+    data = result[0:32] + result[32:64] + result[64:96]
+    return data, result[96:97] * weights[column, view : view + 1, :]
+
+
+def scatter_kernel(slots, weights, data, cover):
+    for column in range(8):
+        data[column], row = scattered(1, slots, weights, column)
+        cover[column] = jnp.broadcast_to(row, (8, 256))
+
+
+def payloads(value, far, near):
+    upper = upper_half()
     far[...] = value[:, pl.ds(pl.multiple_of(16 * upper, 16), 16), :]
     near[...] = value[:, pl.ds(pl.multiple_of(16 - 16 * upper, 16), 16), :]
 
 
-def send_kernel(here, slab, far, near):
-    payloads(here, slab, far, near)
-
-
-def blurred_into(here, way, value, far, near, band, big_high, big_low, wide, flat, total):
-    upper = here[3]
-    wide[:, 16:48, :] = value[:, 0:32, :]
+def blurred_into(way, value, far, near, band, big_high, big_low, wide, flat, total):
+    upper = upper_half()
+    wide[:, 16:48, :] = value[...]
     wide[:, pl.ds(pl.multiple_of(48 * upper, 16), 16), :] = far[...]
     wide[:, pl.ds(pl.multiple_of(48 - 48 * upper, 16), 16), :] = near[...]
     weights = band[way]
@@ -227,34 +252,53 @@
                 total[out[0] : out[1], :] += product(out[0] + shift, out[1] + shift, dx, dy)
 
 
-def ratio_kernel(here, est, far, near, band, big_high, big_low, data, cover, ratio, next_far, next_near, wide, flat, total):
-    blurred_into(here, 0, est, far, near, band, big_high, big_low, wide, flat, total)
+def blur_kernel(est, far, near, band, big_high, big_low, blurred, wide, flat):
+    blurred_into(0, est, far, near, band, big_high, big_low, wide, flat, blurred)
+
+
+def scatter_ratio_kernel(slots, weights, blurred, ratio, far, near):
+    for column in range(8):
+        data, cover = scattered(0, slots, weights, column)
+        ratio[column] = 1.0 + cover * (data / blurred[column * 32 : column * 32 + 32, :] - 1.0)
+    payloads(ratio, far, near)
+
+
+def ratio_kernel(est, far, near, band, big_high, big_low, data, cover, ratio, next_far, next_near, wide, flat, total):
+    blurred_into(0, est, far, near, band, big_high, big_low, wide, flat, total)
     for column in range(8):
         blurred = total[column * 32 : column * 32 + 32, :]
         ratio[column] = 1.0 + cover[column, 0:1, :] * (data[column] / blurred - 1.0)
-    payloads(here, ratio, next_far, next_near)
-
-
-def update_kernel(here, ratio, far, near, band, big_high, big_low, est, new, next_far, next_near, wide, flat, total):
-    blurred_into(here, 1, ratio, far, near, band, big_high, big_low, wide, flat, total)
+    payloads(ratio, next_far, next_near)
+
+
+def update_kernel(ratio, far, near, band, big_high, big_low, est, new, next_far, next_near, wide, flat, total):
+    blurred_into(1, ratio, far, near, band, big_high, big_low, wide, flat, total)
     for column in range(8):
-        new[column] = est[column, 0:32, :] * total[column * 32 : column * 32 + 32, :]
-    if next_far is not None:
-        payloads(here, new, next_far, next_near)
-
-
-def last_kernel(here, ratio, far, near, band, big_high, big_low, est, new, wide, flat, total):
-    update_kernel(here, ratio, far, near, band, big_high, big_low, est, new, None, None, wide, flat, total)
-
-
-def join_kernel(here, parts, out, held):
-    z_odd = here[2] % 2
-    for parity in range(2):
-        @pl.when(z_odd == parity)
-        def _():
-            for device in range(8):
-                slab = slab_of(device, parity)
-                held[slab * 32 : slab * 32 + 32, :] = parts[device]
+        new[column] = est[column] * total[column * 32 : column * 32 + 32, :]
+    payloads(new, next_far, next_near)
+
+
+def last_kernel(ratio, far, near, band, big_high, big_low, est, keep, give, wide, flat, total):
+    blurred_into(1, ratio, far, near, band, big_high, big_low, wide, flat, total)
+    _, _, core, _ = coordinates()
+    for flip, x, y, _ in chips():
+        for turn, out in enumerate((keep, give)):
+            column = 4 * x + 2 * y + (core if turn == 0 else 1 - core)
+            start = pl.multiple_of(column * 32, 32)
+            out[flip] = est[column] * total[pl.ds(start, 32), :]
+
+
+def merge_kernel(keep, got, *pieces):
+    upper = upper_half()
+    for flip in range(4):
+        pieces[flip][pl.ds(pl.multiple_of(32 * upper, 32), 32), :] = keep[flip]
+        pieces[flip][pl.ds(pl.multiple_of(32 - 32 * upper, 32), 32), :] = got[flip]
+
+
+def join_kernel(*refs):
+    pieces, (out, held) = refs[:4], refs[4:]
+    for flip, _, _, place in chips():
+        held[pl.ds(pl.multiple_of(64 * place, 64), 64), :] = pieces[flip][...]
     out[...] = held[...].T
 
 
@@ -262,13 +306,16 @@
     return jax.ShapeDtypeStruct(dims, dtype)
 
 
+def swaps(planes):
+    def flipped(by):
+        return [(d * planes + z, (d ^ by) * planes + z) for d in range(8) for z in range(planes)]
+
+    return [flipped(by) for by in (2, 4, 6)], flipped(1)
+
+
 def slab_sweep(planes, estimate, raw_lines, line_index, psf, view_weight):
-    x, gy, z = (lax.axis_index(axis) for axis in ALL)
-    y, core = gy // 2, gy % 2
-    place = 2 * x + (x ^ y)
-    place = jnp.where(z % 2 == 0, place, 3 - place)
-    here = jnp.stack([x, gy, z, core ^ (place % 2)]).astype(jnp.int32)
     far_pairs, near_pairs = chain_pairs(planes)
+    to_chips, to_core = swaps(planes)
 
     def exchange(far, near):
         return (
@@ -276,51 +323,54 @@
             lax.ppermute(near, ALL, near_pairs),
         )
 
-    pieces = call(
-        functools.partial(est_kernel, planes),
-        shape(8, 40, 256),
-        [SMEM, SMEM, VMEM],
-    )(here, view_weight.reshape(2, 1), estimate.reshape(256, 256))
-    slab = lax.all_to_all(pieces, PLANE, split_axis=0, concat_axis=0, tiled=True)
-    lines0, lines1 = call(
-        functools.partial(lines_kernel, planes),
-        (shape(8 * planes, 40, 128), shape(8 * planes, 32, 128)),
-        [SMEM, VMEM, VMEM],
-    )(here, raw_lines.reshape(2, 4 * planes * 32, 256), line_index.reshape(8, 128))
-    lines0 = lax.all_to_all(lines0, ALL, split_axis=0, concat_axis=0, tiled=True)
-    lines1 = lax.all_to_all(lines1, ALL, split_axis=0, concat_axis=0, tiled=True)
-    half = shape(8, 16, 256)
-    scratch = [pltpu.VMEM((8, 64, 256), F32), pltpu.VMEM((256, 256), F32), pltpu.VMEM((256, 256), F32)]
-    far, near = call(send_kernel, (half, half), [SMEM, VMEM])(here, slab)
-    est = slab
+    own, *away = call(
+        est_kernel, (shape(72, 256),) * 4, [SMEM, VMEM], [pltpu.VMEM((256, 256), F32)]
+    )(view_weight.reshape(2), estimate.reshape(256, 256))
+    here = [own] + [lax.ppermute(piece, ALL, pairs) for piece, pairs in zip(away, to_chips)]
+    there = [lax.ppermute(piece, ALL, to_core) for piece in here]
+
+    slots = call(functools.partial(lines_kernel, planes), shape(8 * planes, 72, 128), [VMEM, VMEM])(
+        raw_lines.reshape(2, 4 * planes * 32, 256), line_index.reshape(8, 128)
+    )
+    slots = lax.all_to_all(slots, ALL, split_axis=0, concat_axis=0, tiled=True)
+    half, full = shape(8, 16, 256), shape(8, 32, 256)
+    work = [pltpu.VMEM((8, 64, 256), F32), pltpu.VMEM((256, 256), F32)]
+    total = pltpu.VMEM((256, 256), F32)
+    est, weights, far, near = call(slab_kernel, (full, shape(8, 8, 256), half, half), [VMEM] * 8)(
+        *here, *there
+    )
+    far = lax.ppermute(far, ALL, far_pairs)
+    mats = []
     for view in range(2):
         big_high, big_low, band = call(
-            taps_kernel,
+            functools.partial(taps_kernel, view),
             (shape(9, 256, 256, dtype=BF16), shape(9, 256, 256, dtype=BF16), shape(2, 32, 256, dtype=BF16)),
             [VMEM],
             [pltpu.VMEM((8, 128), F32)],
             flops=1 << 30,
-        )(psf[view])
-        data, cover = call(
-            functools.partial(scatter_kernel, view),
-            (shape(8, 32, 256), shape(8, 8, 256)),
-            [VMEM] * 3,
-            flops=1 << 30,
-        )(lines0, lines1, slab)
-        mats = (band, big_high, big_low)
-        ratio, far, near = call(
-            ratio_kernel, (shape(8, 32, 256), half, half), [SMEM] + [VMEM] * 8, scratch, flops=1 << 30
-        )(here, est, *exchange(far, near), *mats, data, cover)
-        if view == 0:
-            est, far, near = call(
-                update_kernel, (shape(8, 32, 256), half, half), [SMEM] + [VMEM] * 7, scratch, flops=1 << 30
-            )(here, ratio, *exchange(far, near), *mats, est)
-        else:
-            est = call(last_kernel, shape(8, 32, 256), [SMEM] + [VMEM] * 7, scratch, flops=1 << 30)(
-                here, ratio, *exchange(far, near), *mats, est
-            )
-    parts = lax.all_to_all(est, PLANE, split_axis=0, concat_axis=0, tiled=True)
-    out = call(join_kernel, shape(256, 256), [SMEM, VMEM], [pltpu.VMEM((256, 256), F32)])(here, parts)
+        )(psf.transpose(1, 0, 2))
+        mats.append((band, big_high, big_low))
+    blurred = call(blur_kernel, shape(256, 256), [VMEM] * 6, work, flops=1 << 30)(est, far, near, *mats[0])
+    ratio, far, near = call(scatter_ratio_kernel, (full, half, half), [VMEM] * 3, flops=1 << 30)(
+        slots, weights, blurred
+    )
+    est, far, near = call(update_kernel, (full, half, half), [VMEM] * 7, work + [total], flops=1 << 30)(
+        ratio, *exchange(far, near), *mats[0], est
+    )
+    data, cover = call(scatter_kernel, (full, shape(8, 8, 256)), [VMEM] * 2, flops=1 << 30)(
+        slots, weights
+    )
+    ratio, far, near = call(ratio_kernel, (full, half, half), [VMEM] * 8, work + [total], flops=1 << 30)(
+        est, *exchange(far, near), *mats[1], data, cover
+    )
+    quarter = shape(4, 32, 256)
+    keep, give = call(last_kernel, (quarter, quarter), [VMEM] * 7, work + [total], flops=1 << 30)(
+        ratio, *exchange(far, near), *mats[1], est
+    )
+    got = lax.ppermute(give, ALL, to_core)
+    own, *away = call(merge_kernel, (shape(64, 256),) * 4, [VMEM] * 2)(keep, got)
+    parts = [own] + [lax.ppermute(piece, ALL, pairs) for piece, pairs in zip(away, to_chips)]
+    out = call(join_kernel, shape(256, 256), [VMEM] * 4, [pltpu.VMEM((256, 256), F32)])(*parts)
     return out.reshape(16, 16, 256)
 
 

time: 95.2 us -> 75.1 us (0.79)
  blocking collectives: 31.9 us -> 0 us
  waiting for transfers between devices: 17.6 us -> 27.2 us
  starting transfers between devices: 26.2 us -> 31.9 us
  Pallas kernels: 15.5 us -> 11.4 us
    all_to_all x2 -> x0, blocking collectives: 31.9 us -> none  [the longest x1 19.1 us: slab_sweep(): lax.all_to_all(lines1, ALL, split_axis=0, concat_axis=0, tiled=True)]
    ppermute x0 -> x12, waiting for transfers between devices: none -> 19.7 us  [the longest x6 17.5 us: slab_sweep(): lax.ppermute(piece, ALL, pairs)]
    ppermute x0 -> x12, starting transfers between devices: none -> 11.1 us  [the longest x6 9.04 us: slab_sweep(): lax.ppermute(piece, ALL, pairs)]
    all_to_all x2 -> x1, waiting for transfers between devices: 15.6 us -> 5.51 us  [slab_sweep(): slots = lax.all_to_all(slots, ALL, split_axis=0, concat_axis=0, tiled=True)]
    pallas_call x12 -> x13, Pallas kernels: 15.5 us -> 11.4 us  [the longest x2 2.11 us: slab_sweep(): call(functools.partial(taps_kernel, view), (shape(9, 256, 256, dtype=BF16...]
    ppermute x4 -> x3, starting transfers between devices: 14.3 us -> 11.5 us  [exchange(): lax.ppermute(near, ALL, near_pairs)]
    all_to_all x2 -> x1, starting transfers between devices: 9.24 us -> 7.3 us  [slab_sweep(): slots = lax.all_to_all(slots, ALL, split_axis=0, concat_axis=0, tiled=True)]
    ppermute x4 -> x3, starting transfers between devices: 2.68 us -> 2.01 us  [exchange(): lax.ppermute(far, ALL, far_pairs)]
  transfers between devices with their start and end apart: 10 -> 19, of which waited for: 4 -> 11; matrix products, arithmetic and copies ran while one was open for 0% -> 0% of each run, Pallas kernels for 6% -> 7%
where the time goes in v2:
time: 75.1 us; the launch traced here: 73.7 us
  starting transfers between devices  31.9 us (42%)
  waiting for transfers between devices  27.2 us (36%)
  Pallas kernels  11.4 us (15%)
  local copies, waits for them, and re-layouts  2.94 us (4%)
    ppermute x6, waiting for transfers between devices, slab_sweep(): lax.ppermute(piece, ALL, pairs)  17.5 us
    ppermute x3, starting transfers between devices, exchange(): lax.ppermute(near, ALL, near_pairs)  11.5 us
    ppermute x6, starting transfers between devices, slab_sweep(): lax.ppermute(piece, ALL, pairs)  9.04 us
    all_to_all x1, starting transfers between devices, slab_sweep(): slots = lax.all_to_all(slots, ALL, split_axis=0, concat_axis=0, tiled=True)  7.3 us
    all_to_all x1, waiting for transfers between devices, slab_sweep(): slots = lax.all_to_all(slots, ALL, split_axis=0, concat_axis=0, tiled=True)  5.51 us
    unnamed x14, local copies, waits for them, and re-layouts  2.94 us
    pallas_call x2, Pallas kernels, slab_sweep(): call(functools.partial(taps_kernel, view), (shape(9, 256, 256, dtype=BF16...  2.11 us
    ppermute x3, starting transfers between devices, exchange(): lax.ppermute(far, ALL, far_pairs)  2.01 us
  transfers between devices with their start and end apart: 19, of which 11 were waited for; matrix products, arithmetic and copies ran while one was open for 0% of the time, Pallas kernels for 7%

profile of v2, /device:TPU:0, one launch (start us, length us, event | category | flops | bytes accessed | tf_op | source)
XLA Modules:
  0.0 73.7 jit_solution(12793166645556000263)
XLA Ops:
  0.0 1.2 %copy-done = f32[2,1,1,512,256]{4,3,2,1,0:T(8,128)S(1)} copy-done((f32[2,1,1,512,256]{4,3,2,1,0:T(8,128)S(1)}, f32[2,1,1,512,256]{4,3,2,1,0:T(8,128)}, u32[]{:S(2)}) %copy-start) | copy-done | bytes 1048600
  1.9 1.4 %shard_map.55 = f32[32,72,128]{2,1,0:T(8,128)} custom-call(f32[2,512,256]{2,1,0:T(8,128)S(1)} %bitcast.6, s32[8,128]{1,0:T(8,128)S(1)} %bitcast.8), custom_call_target="tpu_custom_call" | custom-call | bytes 1048576 | tf_op jit(solution)/shard_map/pallas_call | solution.py:332
  3.3 7.3 %all-to-all-start = ((f32[32,72,128]{2,1,0:T(8,128)}), f32[32,72,128]{2,1,0:T(8,128)S(1)}, u32[]{:S(2)}, u32[]{:S(2)}) async-start(f32[32,72,128]{2,1,0:T(8,128)} %shard_map.55), calls=%async_computation | async-start | bytes 2359296 | tf_op jit(solution)/shard_map/all_to_all | solution.py:335
  10.7 0.7 shard_map.56
  11.4 1.8 %collective-permute-start = (f32[72,256]{1,0:T(8,128)S(1)}, f32[72,256]{1,0:T(8,128)S(1)}, u32[]{:S(2)}, u32[]{:S(2)}) collective-permute-start(f32[72,256]{1,0:T(8,128)S(1)} %get-tuple-element.37), channel_id=1, source_target_pairs={{0,8},{1,9},{2,10},{3,11},{4,12},{5,13},{6,14},{7,15},{8,0},{9,1},... | collective-permute-start | bytes 221192 | tf_op jit(solution)/shard_map/ppermute | solution.py:329
  13.2 1.5 %collective-permute-start.1 = (f32[72,256]{1,0:T(8,128)S(1)}, f32[72,256]{1,0:T(8,128)S(1)}, u32[]{:S(2)}, u32[]{:S(2)}) collective-permute-start(f32[72,256]{1,0:T(8,128)S(1)} %get-tuple-element.38), channel_id=1, source_target_pairs={{0,16},{1,17},{2,18},{3,19},{4,20},{5,21},{6,22},{7,23},{8,24},{9,... | collective-permute-start | bytes 221192 | tf_op jit(solution)/shard_map/ppermute | solution.py:329
  14.9 6.9 %collective-permute-done.refs_1_ = f32[72,256]{1,0:T(8,128)S(1)} collective-permute-done((f32[72,256]{1,0:T(8,128)S(1)}, f32[72,256]{1,0:T(8,128)S(1)}, u32[]{:S(2)}, u32[]{:S(2)}) %collective-permute-start) | collective-permute-done | bytes 73760 | tf_op jit(solution)/shard_map/ppermute | solution.py:329
  21.8 0.8 %collective-permute-done.1.refs_2_ = f32[72,256]{1,0:T(8,128)S(1)} collective-permute-done((f32[72,256]{1,0:T(8,128)S(1)}, f32[72,256]{1,0:T(8,128)S(1)}, u32[]{:S(2)}, u32[]{:S(2)}) %collective-permute-start.1) | collective-permute-done | bytes 73760 | tf_op jit(solution)/shard_map/ppermute | solution.py:329
  22.6 4.9 %collective-permute-done.2.refs_3_ = f32[72,256]{1,0:T(8,128)S(1)} collective-permute-done((f32[72,256]{1,0:T(8,128)S(1)}, f32[72,256]{1,0:T(8,128)S(1)}, u32[]{:S(2)}, u32[]{:S(2)}) %collective-permute-start.2) | collective-permute-done | bytes 73760 | tf_op jit(solution)/shard_map/ppermute | solution.py:329
  27.6 1.2 %collective-permute-done.6.refs_7_ = f32[72,256]{1,0:T(8,128)S(1)} collective-permute-done((f32[72,256]{1,0:T(8,128)S(1)}, f32[72,256]{1,0:T(8,128)S(1)}, u32[]{:S(2)}, u32[]{:S(2)}) %collective-permute-start.6) | collective-permute-done | bytes 73760 | tf_op jit(solution)/shard_map/ppermute | solution.py:330
  29.6 1.1 %shard_map.58 = (bf16[9,256,256]{2,1,0:T(8,128)(2,1)S(1)}, bf16[9,256,256]{2,1,0:T(8,128)(2,1)S(1)}, bf16[2,32,256]{2,1,0:T(8,128)(2,1)S(1)}) custom-call(f32[3,2,33]{2,1,0:T(2,128)S(1)} %bitcast.10), custom_call_target="tpu_custom_call" | custom-call | flops 1073741824 | bytes 1048576 | tf_op jit(solution)/shard_map/pallas_call | solution.py:345
  30.6 1.2 %shard_map.59.blurred = f32[256,256]{1,0:T(8,128)S(1)} custom-call(f32[8,32,256]{2,1,0:T(8,128)S(1)} %get-tuple-element.41.est, f32[8,16,256]{2,1,0:T(8,128)S(1)} %collective-permute-done.7.far, f32[8,16,256]{2,1,0:T(8,128)S(1)} %get-tuple-element.43.near, bf16[2,32,256]{2,1,0:T(8,128)(2,1)S(1)} %get-tuple-element.44.band, ...), custom_call_target="tpu_custom_call" | custom-call | flops 1073741824 | bytes 1048576 | tf_op jit(solution)/shard_map/pallas_call | solution.py:353
  31.9 1.0 %copy-done.5 = bf16[9,256,256]{2,1,0:T(8,128)(2,1)} copy-done((bf16[9,256,256]{2,1,0:T(8,128)(2,1)}, bf16[9,256,256]{2,1,0:T(8,128)(2,1)S(1)}, u32[]{:S(2)}) %copy-start.5) | copy-done | bytes 1179672
  32.9 5.5 %all-to-all-done.slots = f32[32,72,128]{2,1,0:T(8,128)S(1)} async-done(((f32[32,72,128]{2,1,0:T(8,128)}), f32[32,72,128]{2,1,0:T(8,128)S(1)}, u32[]{:S(2)}, u32[]{:S(2)}) %all-to-all-start) | async-done | bytes 1179680 | tf_op jit(solution)/shard_map/all_to_all | solution.py:335
  38.4 0.9 %shard_map.60 = (f32[8,32,256]{2,1,0:T(8,128)S(1)}, f32[8,16,256]{2,1,0:T(8,128)S(1)}, f32[8,16,256]{2,1,0:T(8,128)S(1)}) custom-call(f32[32,72,128]{2,1,0:T(8,128)S(1)} %all-to-all-done.slots, f32[8,8,256]{2,1,0:T(8,128)S(1)} %get-tuple-element.40.weights, f32[256,256]{1,0:T(8,128)S(1)} %shard_map.59.blurred), custom_call_target="tpu_custom_call" | custom-call | flops 1073741824 | bytes 1048576 | tf_op jit(solution)/shard_map/pallas_call | solution.py:354
  40.0 4.1 %collective-permute-start.9 = (f32[8,16,256]{2,1,0:T(8,128)S(1)}, f32[8,16,256]{2,1,0:T(8,128)S(1)}, u32[]{:S(2)}, u32[]{:S(2)}) collective-permute-start(f32[8,16,256]{2,1,0:T(8,128)S(1)} %get-tuple-element.49), channel_id=1, source_target_pairs={{0,4},{4,0},{12,8},{8,12},{24,28},{28,24},{20,16},{16,20},{17,21},... | collective-permute-start | bytes 393224 | tf_op jit(solution)/shard_map/ppermute | solution.py:323
  44.1 1.0 %collective-permute-done.9.near = f32[8,16,256]{2,1,0:T(8,128)S(1)} collective-permute-done((f32[8,16,256]{2,1,0:T(8,128)S(1)}, f32[8,16,256]{2,1,0:T(8,128)S(1)}, u32[]{:S(2)}, u32[]{:S(2)}) %collective-permute-start.9) | collective-permute-done | bytes 131104 | tf_op jit(solution)/shard_map/ppermute | solution.py:323
  45.1 1.0 %shard_map.61 = (f32[8,32,256]{2,1,0:T(8,128)S(1)}, f32[8,16,256]{2,1,0:T(8,128)S(1)}, f32[8,16,256]{2,1,0:T(8,128)S(1)}) custom-call(f32[8,32,256]{2,1,0:T(8,128)S(1)} %get-tuple-element.47.ratio, f32[8,16,256]{2,1,0:T(8,128)S(1)} %collective-permute-done.8.far, f32[8,16,256]{2,1,0:T(8,128)S(1)} %collective-permute-done.9.near, ...), custom_call_target="tpu_custom_call" | custom-call | flops 1073741824 | bytes 1048576 | tf_op jit(solution)/shard_map/pallas_call | solution.py:357
  46.8 4.1 %collective-permute-start.11 = (f32[8,16,256]{2,1,0:T(8,128)S(1)}, f32[8,16,256]{2,1,0:T(8,128)S(1)}, u32[]{:S(2)}, u32[]{:S(2)}) collective-permute-start(f32[8,16,256]{2,1,0:T(8,128)S(1)} %get-tuple-element.52), channel_id=1, source_target_pairs={{0,4},{4,0},{12,8},{8,12},{24,28},{28,24},{20,16},{16,20},{17,21},... | collective-permute-start | bytes 393224 | tf_op jit(solution)/shard_map/ppermute | solution.py:323
  50.8 1.1 %shard_map.62 = (bf16[9,256,256]{2,1,0:T(8,128)(2,1)S(1)}, bf16[9,256,256]{2,1,0:T(8,128)(2,1)S(1)}, bf16[2,32,256]{2,1,0:T(8,128)(2,1)S(1)}) custom-call(f32[3,2,33]{2,1,0:T(2,128)S(1)} %bitcast.11), custom_call_target="tpu_custom_call" | custom-call | flops 1073741824 | bytes 1048576 | tf_op jit(solution)/shard_map/pallas_call | solution.py:345
  51.9 0.8 %shard_map.63 = (f32[8,32,256]{2,1,0:T(8,128)S(1)}, f32[8,8,256]{2,1,0:T(8,128)S(1)}) custom-call(f32[32,72,128]{2,1,0:T(8,128)S(1)} %all-to-all-done.slots, f32[8,8,256]{2,1,0:T(8,128)S(1)} %get-tuple-element.40.weights), custom_call_target="tpu_custom_call" | custom-call | flops 1073741824 | bytes 1048576 | tf_op jit(solution)/shard_map/pallas_call | solution.py:360
  52.7 1.3 %shard_map.64 = (f32[8,32,256]{2,1,0:T(8,128)S(1)}, f32[8,16,256]{2,1,0:T(8,128)S(1)}, f32[8,16,256]{2,1,0:T(8,128)S(1)}) custom-call(f32[8,32,256]{2,1,0:T(8,128)S(1)} %get-tuple-element.50.est, f32[8,16,256]{2,1,0:T(8,128)S(1)} %collective-permute-done.10.far, f32[8,16,256]{2,1,0:T(8,128)S(1)} %collective-permute-done.11.near, ...), custom_call_target="tpu_custom_call" | custom-call | flops 1073741824 | bytes 1048576 | tf_op jit(solution)/shard_map/pallas_call | solution.py:363
  54.7 3.4 %collective-permute-start.13 = (f32[8,16,256]{2,1,0:T(8,128)S(1)}, f32[8,16,256]{2,1,0:T(8,128)S(1)}, u32[]{:S(2)}, u32[]{:S(2)}) collective-permute-start(f32[8,16,256]{2,1,0:T(8,128)S(1)} %get-tuple-element.60), channel_id=1, source_target_pairs={{0,4},{4,0},{12,8},{8,12},{24,28},{28,24},{20,16},{16,20},{17,21},... | collective-permute-start | bytes 393224 | tf_op jit(solution)/shard_map/ppermute | solution.py:323
  58.1 1.0 %collective-permute-done.13.near = f32[8,16,256]{2,1,0:T(8,128)S(1)} collective-permute-done((f32[8,16,256]{2,1,0:T(8,128)S(1)}, f32[8,16,256]{2,1,0:T(8,128)S(1)}, u32[]{:S(2)}, u32[]{:S(2)}) %collective-permute-start.13) | collective-permute-done | bytes 131104 | tf_op jit(solution)/shard_map/ppermute | solution.py:323
  59.1 1.0 %shard_map.65 = (f32[4,32,256]{2,1,0:T(8,128)S(1)}, f32[4,32,256]{2,1,0:T(8,128)S(1)}) custom-call(f32[8,32,256]{2,1,0:T(8,128)S(1)} %get-tuple-element.58.ratio, f32[8,16,256]{2,1,0:T(8,128)S(1)} %collective-permute-done.12.far, f32[8,16,256]{2,1,0:T(8,128)S(1)} %collective-permute-done.13.near, bf16[2,32,256]{2,1,0:T(8,128)(2,1)S(1)} %get-tuple-element.53.band, ...), custom_call_target="tpu_custom_call" | custom-call | flops 1073741824 | bytes 1048576 | tf_op jit(solution)/shard_map/pallas_call | solution.py:367
  60.1 1.4 %collective-permute-start.14 = (f32[4,32,256]{2,1,0:T(8,128)S(1)}, f32[4,32,256]{2,1,0:T(8,128)S(1)}, u32[]{:S(2)}, u32[]{:S(2)}) collective-permute-start(f32[4,32,256]{2,1,0:T(8,128)S(1)} %get-tuple-element.62), channel_id=1, source_target_pairs={{0,4},{1,5},{2,6},{3,7},{4,0},{5,1},{6,2},{7,3},{8,12},{9,13},{10,... | collective-permute-start | bytes 393224 | tf_op jit(solution)/shard_map/ppermute | solution.py:370
  61.5 1.0 %collective-permute-done.14.got = f32[4,32,256]{2,1,0:T(8,128)S(1)} collective-permute-done((f32[4,32,256]{2,1,0:T(8,128)S(1)}, f32[4,32,256]{2,1,0:T(8,128)S(1)}, u32[]{:S(2)}, u32[]{:S(2)}) %collective-permute-start.14) | collective-permute-done | bytes 131104 | tf_op jit(solution)/shard_map/ppermute | solution.py:370
  62.5 3.7 %collective-permute-start.15 = (f32[64,256]{1,0:T(8,128)S(1)}, f32[64,256]{1,0:T(8,128)S(1)}, u32[]{:S(2)}, u32[]{:S(2)}) collective-permute-start(f32[64,256]{1,0:T(8,128)S(1)} %get-tuple-element.64), channel_id=1, source_target_pairs={{0,8},{1,9},{2,10},{3,11},{4,12},{5,13},{6,14},{7,15},{8,0},{9,1},... | collective-permute-start | bytes 196616 | tf_op jit(solution)/shard_map/ppermute | solution.py:372
  66.2 1.5 %collective-permute-start.16 = (f32[64,256]{1,0:T(8,128)S(1)}, f32[64,256]{1,0:T(8,128)S(1)}, u32[]{:S(2)}, u32[]{:S(2)}) collective-permute-start(f32[64,256]{1,0:T(8,128)S(1)} %get-tuple-element.65), channel_id=1, source_target_pairs={{0,16},{1,17},{2,18},{3,19},{4,20},{5,21},{6,22},{7,23},{8,24},{9,... | collective-permute-start | bytes 196616 | tf_op jit(solution)/shard_map/ppermute | solution.py:372
  68.6 2.3 %collective-permute-done.16.refs_2_ = f32[64,256]{1,0:T(8,128)S(1)} collective-permute-done((f32[64,256]{1,0:T(8,128)S(1)}, f32[64,256]{1,0:T(8,128)S(1)}, u32[]{:S(2)}, u32[]{:S(2)}) %collective-permute-start.16) | collective-permute-done | bytes 65568 | tf_op jit(solution)/shard_map/ppermute | solution.py:372
  70.9 2.0 %collective-permute-done.17.refs_3_ = f32[64,256]{1,0:T(8,128)S(1)} collective-permute-done((f32[64,256]{1,0:T(8,128)S(1)}, f32[64,256]{1,0:T(8,128)S(1)}, u32[]{:S(2)}, u32[]{:S(2)}) %collective-permute-start.17) | collective-permute-done | bytes 65568 | tf_op jit(solution)/shard_map/ppermute | solution.py:372
  72.9 0.9 %shard_map.67 = f32[256,256]{1,0:T(8,128)} custom-call(f32[64,256]{1,0:T(8,128)S(1)} %get-tuple-element.63.refs_0_, f32[64,256]{1,0:T(8,128)S(1)} %collective-permute-done.15.refs_1_, f32[64,256]{1,0:T(8,128)S(1)} %collective-permute-done.16.refs_2_, f32[64,256]{1,0:T(8,128)S(1)} %collective-permute-done.17.refs_3_), custom_call_target="tpu_custom_call" | custom-call | bytes 1048576 | tf_op jit(solution)/shard_map/pallas_call | solution.py:373
  (33 shorter events, 4.7 us)
Async XLA Ops:
  0.0 1.2 %copy-start = (f32[2,1,1,512,256]{4,3,2,1,0:T(8,128)S(1)}, f32[2,1,1,512,256]{4,3,2,1,0:T(8,128)}, u32[]{:S(2)}) copy-start(f32[2,1,1,512,256]{4,3,2,1,0:T(8,128)} %param.6) | copy-start | bytes 3145732
  1.2 0.7 copy-start.2
  3.3 7.3 %copy-start.1 = (f32[16,16,256]{2,1,0:T(8,128)S(1)}, f32[16,16,256]{2,1,0:T(8,128)}, u32[]{:S(2)}) copy-start(f32[16,16,256]{2,1,0:T(8,128)} %param.5) | copy-start | bytes 786436
  3.3 7.3 %copy-start.3 = (s32[2,1,1,1]{0,3,2,1:T(1,128)S(1)}, s32[2,1,1,1]{0,3,2,1:T(1,128)}, u32[]{:S(2)}) copy-start(s32[2,1,1,1]{0,3,2,1:T(1,128)} %param.9) | copy-start | bytes 28
  3.3 26.2 %copy-start.4 = (f32[2,3,33]{2,0,1:T(2,128)S(1)}, f32[2,3,33]{2,0,1:T(2,128)}, u32[]{:S(2)}) copy-start(f32[2,3,33]{2,0,1:T(2,128)} %param.8) | copy-start | bytes 2380
  3.3 35.1 %all-to-all-start = ((f32[32,72,128]{2,1,0:T(8,128)}), f32[32,72,128]{2,1,0:T(8,128)S(1)}, u32[]{:S(2)}, u32[]{:S(2)}) async-start(f32[32,72,128]{2,1,0:T(8,128)} %shard_map.55), calls=%async_computation | async-start | bytes 2359296 | tf_op jit(solution)/shard_map/all_to_all | solution.py:335
  11.4 10.4 %collective-permute-start = (f32[72,256]{1,0:T(8,128)S(1)}, f32[72,256]{1,0:T(8,128)S(1)}, u32[]{:S(2)}, u32[]{:S(2)}) collective-permute-start(f32[72,256]{1,0:T(8,128)S(1)} %get-tuple-element.37), channel_id=1, source_target_pairs={{0,8},{1,9},{2,10},{3,11},{4,12},{5,13},{6,14},{7,15},{8,0},{9,1},... | collective-permute-start | bytes 221192 | tf_op jit(solution)/shard_map/ppermute | solution.py:329
  13.2 9.4 %collective-permute-start.1 = (f32[72,256]{1,0:T(8,128)S(1)}, f32[72,256]{1,0:T(8,128)S(1)}, u32[]{:S(2)}, u32[]{:S(2)}) collective-permute-start(f32[72,256]{1,0:T(8,128)S(1)} %get-tuple-element.38), channel_id=1, source_target_pairs={{0,16},{1,17},{2,18},{3,19},{4,20},{5,21},{6,22},{7,23},{8,24},{9,... | collective-permute-start | bytes 221192 | tf_op jit(solution)/shard_map/ppermute | solution.py:329
  14.7 12.9 %collective-permute-start.2 = (f32[72,256]{1,0:T(8,128)S(1)}, f32[72,256]{1,0:T(8,128)S(1)}, u32[]{:S(2)}, u32[]{:S(2)}) collective-permute-start(f32[72,256]{1,0:T(8,128)S(1)} %get-tuple-element.39), channel_id=1, source_target_pairs={{0,24},{1,25},{2,26},{3,27},{4,28},{5,29},{6,30},{7,31},{8,16},{9,... | collective-permute-start | bytes 221192 | tf_op jit(solution)/shard_map/ppermute | solution.py:329
  14.9 12.6 %collective-permute-start.3 = (f32[72,256]{1,0:T(8,128)S(1)}, f32[72,256]{1,0:T(8,128)S(1)}, u32[]{:S(2)}, u32[]{:S(2)}) collective-permute-start(f32[72,256]{1,0:T(8,128)S(1)} %get-tuple-element.36.refs_0_), channel_id=1, source_target_pairs={{0,4},{1,5},{2,6},{3,7},{4,0},{5,1},{6,2},{7,3},{8,12},{9,13},{10,... | collective-permute-start | bytes 221192 | tf_op jit(solution)/shard_map/ppermute | solution.py:330
  21.8 5.8 %collective-permute-start.4 = (f32[72,256]{1,0:T(8,128)S(1)}, f32[72,256]{1,0:T(8,128)S(1)}, u32[]{:S(2)}, u32[]{:S(2)}) collective-permute-start(f32[72,256]{1,0:T(8,128)S(1)} %collective-permute-done.refs_1_), channel_id=1, source_target_pairs={{0,4},{1,5},{2,6},{3,7},{4,0},{5,1},{6,2},{7,3},{8,12},{9,13},{10,... | collective-permute-start | bytes 221192 | tf_op jit(solution)/shard_map/ppermute | solution.py:330
  22.6 5.0 %collective-permute-start.5 = (f32[72,256]{1,0:T(8,128)S(1)}, f32[72,256]{1,0:T(8,128)S(1)}, u32[]{:S(2)}, u32[]{:S(2)}) collective-permute-start(f32[72,256]{1,0:T(8,128)S(1)} %collective-permute-done.1.refs_2_), channel_id=1, source_target_pairs={{0,4},{1,5},{2,6},{3,7},{4,0},{5,1},{6,2},{7,3},{8,12},{9,13},{10,... | collective-permute-start | bytes 221192 | tf_op jit(solution)/shard_map/ppermute | solution.py:330
  27.6 1.3 %collective-permute-start.6 = (f32[72,256]{1,0:T(8,128)S(1)}, f32[72,256]{1,0:T(8,128)S(1)}, u32[]{:S(2)}, u32[]{:S(2)}) collective-permute-start(f32[72,256]{1,0:T(8,128)S(1)} %collective-permute-done.2.refs_3_), channel_id=1, source_target_pairs={{0,4},{1,5},{2,6},{3,7},{4,0},{5,1},{6,2},{7,3},{8,12},{9,13},{10,... | collective-permute-start | bytes 221192 | tf_op jit(solution)/shard_map/ppermute | solution.py:330
  28.9 1.8 %collective-permute-start.7 = (f32[8,16,256]{2,1,0:T(8,128)S(1)}, f32[8,16,256]{2,1,0:T(8,128)S(1)}, u32[]{:S(2)}, u32[]{:S(2)}) collective-permute-start(f32[8,16,256]{2,1,0:T(8,128)S(1)} %get-tuple-element.42), channel_id=1, source_target_pairs={{4,12},{12,4},{8,24},{24,8},{28,20},{20,28},{16,17},{17,16},{21,29... | collective-permute-start | bytes 393224 | tf_op jit(solution)/shard_map/ppermute | solution.py:342
  31.9 1.0 %copy-start.5 = (bf16[9,256,256]{2,1,0:T(8,128)(2,1)}, bf16[9,256,256]{2,1,0:T(8,128)(2,1)S(1)}, u32[]{:S(2)}) copy-start(bf16[9,256,256]{2,1,0:T(8,128)(2,1)S(1)} %get-tuple-element.46.big_low) | copy-start | bytes 3538948
  38.4 6.6 %copy-start.6 = (bf16[9,256,256]{2,1,0:T(8,128)(2,1)S(1)}, bf16[9,256,256]{2,1,0:T(8,128)(2,1)}, u32[]{:S(2)}) copy-start(bf16[9,256,256]{2,1,0:T(8,128)(2,1)} %copy-done.5) | copy-start | bytes 3538948
  39.3 4.8 %collective-permute-start.8 = (f32[8,16,256]{2,1,0:T(8,128)S(1)}, f32[8,16,256]{2,1,0:T(8,128)S(1)}, u32[]{:S(2)}, u32[]{:S(2)}) collective-permute-start(f32[8,16,256]{2,1,0:T(8,128)S(1)} %get-tuple-element.48), channel_id=1, source_target_pairs={{4,12},{12,4},{8,24},{24,8},{28,20},{20,28},{16,17},{17,16},{21,29... | collective-permute-start | bytes 393224 | tf_op jit(solution)/shard_map/ppermute | solution.py:322
  40.0 5.1 %collective-permute-start.9 = (f32[8,16,256]{2,1,0:T(8,128)S(1)}, f32[8,16,256]{2,1,0:T(8,128)S(1)}, u32[]{:S(2)}, u32[]{:S(2)}) collective-permute-start(f32[8,16,256]{2,1,0:T(8,128)S(1)} %get-tuple-element.49), channel_id=1, source_target_pairs={{0,4},{4,0},{12,8},{8,12},{24,28},{28,24},{20,16},{16,20},{17,21},... | collective-permute-start | bytes 393224 | tf_op jit(solution)/shard_map/ppermute | solution.py:323
  46.1 6.6 %collective-permute-start.10 = (f32[8,16,256]{2,1,0:T(8,128)S(1)}, f32[8,16,256]{2,1,0:T(8,128)S(1)}, u32[]{:S(2)}, u32[]{:S(2)}) collective-permute-start(f32[8,16,256]{2,1,0:T(8,128)S(1)} %get-tuple-element.51), channel_id=1, source_target_pairs={{4,12},{12,4},{8,24},{24,8},{28,20},{20,28},{16,17},{17,16},{21,29... | collective-permute-start | bytes 393224 | tf_op jit(solution)/shard_map/ppermute | solution.py:322
  46.8 6.0 %collective-permute-start.11 = (f32[8,16,256]{2,1,0:T(8,128)S(1)}, f32[8,16,256]{2,1,0:T(8,128)S(1)}, u32[]{:S(2)}, u32[]{:S(2)}) collective-permute-start(f32[8,16,256]{2,1,0:T(8,128)S(1)} %get-tuple-element.52), channel_id=1, source_target_pairs={{0,4},{4,0},{12,8},{8,12},{24,28},{28,24},{20,16},{16,20},{17,21},... | collective-permute-start | bytes 393224 | tf_op jit(solution)/shard_map/ppermute | solution.py:323
  54.0 4.1 %collective-permute-start.12 = (f32[8,16,256]{2,1,0:T(8,128)S(1)}, f32[8,16,256]{2,1,0:T(8,128)S(1)}, u32[]{:S(2)}, u32[]{:S(2)}) collective-permute-start(f32[8,16,256]{2,1,0:T(8,128)S(1)} %get-tuple-element.59), channel_id=1, source_target_pairs={{4,12},{12,4},{8,24},{24,8},{28,20},{20,28},{16,17},{17,16},{21,29... | collective-permute-start | bytes 393224 | tf_op jit(solution)/shard_map/ppermute | solution.py:322
  54.7 4.4 %collective-permute-start.13 = (f32[8,16,256]{2,1,0:T(8,128)S(1)}, f32[8,16,256]{2,1,0:T(8,128)S(1)}, u32[]{:S(2)}, u32[]{:S(2)}) collective-permute-start(f32[8,16,256]{2,1,0:T(8,128)S(1)} %get-tuple-element.60), channel_id=1, source_target_pairs={{0,4},{4,0},{12,8},{8,12},{24,28},{28,24},{20,16},{16,20},{17,21},... | collective-permute-start | bytes 393224 | tf_op jit(solution)/shard_map/ppermute | solution.py:323
  60.1 2.4 %collective-permute-start.14 = (f32[4,32,256]{2,1,0:T(8,128)S(1)}, f32[4,32,256]{2,1,0:T(8,128)S(1)}, u32[]{:S(2)}, u32[]{:S(2)}) collective-permute-start(f32[4,32,256]{2,1,0:T(8,128)S(1)} %get-tuple-element.62), channel_id=1, source_target_pairs={{0,4},{1,5},{2,6},{3,7},{4,0},{5,1},{6,2},{7,3},{8,12},{9,13},{10,... | collective-permute-start | bytes 393224 | tf_op jit(solution)/shard_map/ppermute | solution.py:370
  62.5 6.1 %collective-permute-start.15 = (f32[64,256]{1,0:T(8,128)S(1)}, f32[64,256]{1,0:T(8,128)S(1)}, u32[]{:S(2)}, u32[]{:S(2)}) collective-permute-start(f32[64,256]{1,0:T(8,128)S(1)} %get-tuple-element.64), channel_id=1, source_target_pairs={{0,8},{1,9},{2,10},{3,11},{4,12},{5,13},{6,14},{7,15},{8,0},{9,1},... | collective-permute-start | bytes 196616 | tf_op jit(solution)/shard_map/ppermute | solution.py:372
  66.2 4.7 %collective-permute-start.16 = (f32[64,256]{1,0:T(8,128)S(1)}, f32[64,256]{1,0:T(8,128)S(1)}, u32[]{:S(2)}, u32[]{:S(2)}) collective-permute-start(f32[64,256]{1,0:T(8,128)S(1)} %get-tuple-element.65), channel_id=1, source_target_pairs={{0,16},{1,17},{2,18},{3,19},{4,20},{5,21},{6,22},{7,23},{8,24},{9,... | collective-permute-start | bytes 196616 | tf_op jit(solution)/shard_map/ppermute | solution.py:372
  67.7 5.2 %collective-permute-start.17 = (f32[64,256]{1,0:T(8,128)S(1)}, f32[64,256]{1,0:T(8,128)S(1)}, u32[]{:S(2)}, u32[]{:S(2)}) collective-permute-start(f32[64,256]{1,0:T(8,128)S(1)} %get-tuple-element.66), channel_id=1, source_target_pairs={{0,24},{1,25},{2,26},{3,27},{4,28},{5,29},{6,30},{7,31},{8,16},{9,... | collective-permute-start | bytes 196616 | tf_op jit(solution)/shard_map/ppermute | solution.py:372

commit v3 on v2

--- a/solution.py
+++ b/solution.py
@@ -144,7 +144,7 @@
             out[device * planes + z, 64:72, :] = both
 
 
-def taps_kernel(view, psf, big_high, big_low, band, held):
+def taps_kernel(view, way, psf, _, big_high, big_low, band, held):
     held[...] = jnp.zeros_like(held)
     held[0:3, 0:33] = psf[:, view, :]
     taps = held[...]
@@ -155,18 +155,17 @@
         wide = jnp.broadcast_to(row, (size, 128))
         return pltpu.roll(wide, 0, 1, stride=1, stride_axis=0)
 
-    lane_r = lax.broadcasted_iota(jnp.int32, (128, 128), 0)
-    lane_c = lax.broadcasted_iota(jnp.int32, (128, 128), 1)
-    turn = (lane_r + lane_c == 32).astype(BF16)
-    pieces = split3(taps)
-    reversed_taps = sum(dot_nn(piece, turn) for piece in pieces)
-    for way, source in enumerate((taps, reversed_taps)):
-        high, low = split2(toeplitz(source[2:3, :], 32))
-        twice = high.astype(F32) + pltpu.roll(high.astype(F32), 64, 1)
-        band[way, :, 0:128] = twice.astype(BF16)
-        band[way, :, 128:256] = low
-    tall_x = jnp.broadcast_to(toeplitz(taps[0:1, :], 16)[:, None, :], (16, 16, 128)).reshape(256, 128)
-    tall_y = jnp.broadcast_to(toeplitz(taps[1:2, :], 16)[None], (16, 16, 128)).reshape(256, 128)
+    from_lane = lax.broadcasted_iota(jnp.int32, (128, 128), 0)
+    to_lane = lax.broadcasted_iota(jnp.int32, (128, 128), 1)
+    turn = (from_lane + to_lane == 32).astype(BF16)
+    turned = sum(dot_nn(piece, turn) for piece in split3(taps))
+    along_z, along_xy = (taps, turned) if way == 0 else (turned, taps)
+    high, low = split2(toeplitz(along_z[2:3, :], 32))
+    twice = high.astype(F32) + pltpu.roll(high.astype(F32), 64, 1)
+    band[:, 0:128] = twice.astype(BF16)
+    band[:, 128:256] = low
+    tall_x = jnp.broadcast_to(toeplitz(along_xy[0:1, :], 16)[:, None, :], (16, 16, 128)).reshape(256, 128)
+    tall_y = jnp.broadcast_to(toeplitz(along_xy[1:2, :], 16)[None], (16, 16, 128)).reshape(256, 128)
     from_row = lax.broadcasted_iota(jnp.int32, (128, 256), 0)
     to_lane = lax.broadcasted_iota(jnp.int32, (128, 256), 1)
     wide_x, wide_y = [], []
@@ -178,8 +177,8 @@
     for dx in range(3):
         for dy in range(3):
             high, low = split2(wide_x[dx] * wide_y[dy])
-            big_high[dx * 3 + dy] = high
-            big_low[dx * 3 + dy] = low
+            big_high[8 - dx * 3 - dy] = high
+            big_low[8 - dx * 3 - dy] = low
 
 
 def scattered(view, slots, weights, column):
@@ -217,28 +216,32 @@
     near[...] = value[:, pl.ds(pl.multiple_of(16 - 16 * upper, 16), 16), :]
 
 
-def blurred_into(way, value, far, near, band, big_high, big_low, wide, flat, total):
-    upper = upper_half()
-    wide[:, 16:48, :] = value[...]
-    wide[:, pl.ds(pl.multiple_of(48 * upper, 16), 16), :] = far[...]
-    wide[:, pl.ds(pl.multiple_of(48 - 48 * upper, 16), 16), :] = near[...]
-    weights = band[way]
+def widened(wide, value, far, near, margin):
+    rows, upper = value.shape[1], upper_half()
+    wide[:, margin : margin + rows, :] = value[...]
+    side = margin + rows
+    wide[:, pl.ds(pl.multiple_of(side * upper, 16), margin), :] = far[...]
+    wide[:, pl.ds(pl.multiple_of(side - side * upper, 16), margin), :] = near[...]
+
+
+def blurred_into(wide, band, big_high, big_low, flat, total):
+    rows = wide.shape[1] - 32
+    weights = band[...]
     for column in range(8):
-        high, low = split2(wide[column])
-        stacked = jnp.concatenate([high, low, high, high], axis=0)
-        flat[column * 32 : column * 32 + 32, :] = dot_nn(weights, stacked)
+        for start in range(0, rows, 32):
+            high, low = split2(wide[column, start : start + 64, :])
+            stacked = jnp.concatenate([high, low, high, high], axis=0)
+            at = column * rows + start
+            flat[at : at + 32, :] = dot_nn(weights, stacked)
     high, low = split2(flat[...])
 
     def product(start, stop, dx, dy):
-        if way == 0:
-            at, dot = (dx + 1) * 3 + dy + 1, dot_nt
-        else:
-            at, dot = (1 - dx) * 3 + 1 - dy, dot_nn
-        rows = stop - start
-        both = dot(jnp.concatenate([high[start:stop], low[start:stop]], axis=0), big_high[at])
-        return both[:rows] + both[rows:] + dot(high[start:stop], big_low[at])
-
-    total[...] = product(0, 256, 0, 0)
+        at = (dx + 1) * 3 + dy + 1
+        size = stop - start
+        both = dot_nn(jnp.concatenate([high[start:stop], low[start:stop]], axis=0), big_high[at])
+        return both[:size] + both[size:] + dot_nn(high[start:stop], big_low[at])
+
+    total[...] = product(0, 8 * rows, 0, 0)
     for dx in (-1, 0, 1):
         for dy in (-1, 0, 1):
             if dx == 0 and dy == 0:
@@ -247,39 +250,47 @@
                 if not 0 <= x + dx < 2:
                     continue
                 first, last = max(0, -dy), min(4, 4 - dy)
-                out = (x * 4 + first) * 32, (x * 4 + last) * 32
-                shift = (dx * 4 + dy) * 32
-                total[out[0] : out[1], :] += product(out[0] + shift, out[1] + shift, dx, dy)
+                start, stop = (x * 4 + first) * rows, (x * 4 + last) * rows
+                shift = (dx * 4 + dy) * rows
+                total[start:stop, :] += product(start + shift, stop + shift, dx, dy)
 
 
 def blur_kernel(est, far, near, band, big_high, big_low, blurred, wide, flat):
-    blurred_into(0, est, far, near, band, big_high, big_low, wide, flat, blurred)
-
-
-def scatter_ratio_kernel(slots, weights, blurred, ratio, far, near):
+    widened(wide, est, far, near, 16)
+    blurred_into(wide, band, big_high, big_low, flat, blurred)
+
+
+def ratio_from(ratio, data, cover, blurred):
+    for column in range(8):
+        here = blurred[column * 32 : column * 32 + 32, :]
+        ratio[column] = 1.0 + cover[column, 0:1, :] * (data[column] / here - 1.0)
+
+
+def scatter_ratio_kernel(slots, weights, blurred, ratio):
     for column in range(8):
         data, cover = scattered(0, slots, weights, column)
         ratio[column] = 1.0 + cover * (data / blurred[column * 32 : column * 32 + 32, :] - 1.0)
-    payloads(ratio, far, near)
-
-
-def ratio_kernel(est, far, near, band, big_high, big_low, data, cover, ratio, next_far, next_near, wide, flat, total):
-    blurred_into(0, est, far, near, band, big_high, big_low, wide, flat, total)
+
+
+def middle_kernel(
+    ratio, ratio_far, ratio_near, est, est_far, est_near, band0, high0, low0, band1, high1, low1,
+    data, cover, new, next_ratio, far, near, wide, tall, flat, total, short,
+):
+    widened(wide, ratio, ratio_far, ratio_near, 32)
+    widened(tall, est, est_far, est_near, 16)
+    blurred_into(wide, band0, high0, low0, flat, total)
     for column in range(8):
-        blurred = total[column * 32 : column * 32 + 32, :]
-        ratio[column] = 1.0 + cover[column, 0:1, :] * (data[column] / blurred - 1.0)
-    payloads(ratio, next_far, next_near)
-
-
-def update_kernel(ratio, far, near, band, big_high, big_low, est, new, next_far, next_near, wide, flat, total):
-    blurred_into(1, ratio, far, near, band, big_high, big_low, wide, flat, total)
-    for column in range(8):
-        new[column] = est[column] * total[column * 32 : column * 32 + 32, :]
-    payloads(new, next_far, next_near)
+        tall[column] = tall[column] * total[column * 64 : column * 64 + 64, :]
+    new[...] = tall[:, 16:48, :]
+    out = total.at[0:256, :]
+    blurred_into(tall, band1, high1, low1, short, out)
+    ratio_from(next_ratio, data, cover, out)
+    payloads(next_ratio, far, near)
 
 
 def last_kernel(ratio, far, near, band, big_high, big_low, est, keep, give, wide, flat, total):
-    blurred_into(1, ratio, far, near, band, big_high, big_low, wide, flat, total)
+    widened(wide, ratio, far, near, 16)
+    blurred_into(wide, band, big_high, big_low, flat, total)
     _, _, core, _ = coordinates()
     for flip, x, y, _ in chips():
         for turn, out in enumerate((keep, give)):
@@ -334,39 +345,47 @@
     )
     slots = lax.all_to_all(slots, ALL, split_axis=0, concat_axis=0, tiled=True)
     half, full = shape(8, 16, 256), shape(8, 32, 256)
-    work = [pltpu.VMEM((8, 64, 256), F32), pltpu.VMEM((256, 256), F32)]
-    total = pltpu.VMEM((256, 256), F32)
-    est, weights, far, near = call(slab_kernel, (full, shape(8, 8, 256), half, half), [VMEM] * 8)(
+
+    def work(*dims):
+        return pltpu.VMEM(dims, F32)
+
+    est, weights, est_far, est_near = call(slab_kernel, (full, shape(8, 8, 256), half, half), [VMEM] * 8)(
         *here, *there
     )
-    far = lax.ppermute(far, ALL, far_pairs)
-    mats = []
-    for view in range(2):
+    est_far = lax.ppermute(est_far, ALL, far_pairs)
+    anywhere = pl.BlockSpec(memory_space=pl.ANY)
+
+    def matrices(view, way, after):
+        big = shape(9, 256, 256, dtype=BF16)
         big_high, big_low, band = call(
-            functools.partial(taps_kernel, view),
-            (shape(9, 256, 256, dtype=BF16), shape(9, 256, 256, dtype=BF16), shape(2, 32, 256, dtype=BF16)),
-            [VMEM],
-            [pltpu.VMEM((8, 128), F32)],
+            functools.partial(taps_kernel, view, way),
+            (big, big, shape(32, 256, dtype=BF16)),
+            [VMEM, anywhere],
+            [work(8, 128)],
             flops=1 << 30,
-        )(psf.transpose(1, 0, 2))
-        mats.append((band, big_high, big_low))
-    blurred = call(blur_kernel, shape(256, 256), [VMEM] * 6, work, flops=1 << 30)(est, far, near, *mats[0])
-    ratio, far, near = call(scatter_ratio_kernel, (full, half, half), [VMEM] * 3, flops=1 << 30)(
-        slots, weights, blurred
-    )
-    est, far, near = call(update_kernel, (full, half, half), [VMEM] * 7, work + [total], flops=1 << 30)(
-        ratio, *exchange(far, near), *mats[0], est
-    )
-    data, cover = call(scatter_kernel, (full, shape(8, 8, 256)), [VMEM] * 2, flops=1 << 30)(
-        slots, weights
-    )
-    ratio, far, near = call(ratio_kernel, (full, half, half), [VMEM] * 8, work + [total], flops=1 << 30)(
-        est, *exchange(far, near), *mats[1], data, cover
-    )
+        )(psf.transpose(1, 0, 2), after)
+        return band, big_high, big_low
+
+    blurred = call(
+        blur_kernel, shape(256, 256), [VMEM] * 6, [work(8, 64, 256), work(256, 256)], flops=1 << 30
+    )(est, est_far, est_near, *matrices(0, 0, est))
+    ratio = call(scatter_ratio_kernel, full, [VMEM] * 3, flops=1 << 30)(slots, weights, blurred)
+    data, cover = call(scatter_kernel, (full, shape(8, 8, 256)), [VMEM] * 2, flops=1 << 30)(slots, weights)
+    est, ratio, far, near = call(
+        middle_kernel,
+        (full, full, half, half),
+        [VMEM] * 14,
+        [work(8, 96, 256), work(8, 64, 256), work(512, 256), work(512, 256), work(256, 256)],
+        flops=1 << 30,
+    )(ratio, *exchange(ratio, ratio), est, est_far, est_near, *matrices(0, 1, slots), *matrices(1, 0, slots), data, cover)
     quarter = shape(4, 32, 256)
-    keep, give = call(last_kernel, (quarter, quarter), [VMEM] * 7, work + [total], flops=1 << 30)(
-        ratio, *exchange(far, near), *mats[1], est
-    )
+    keep, give = call(
+        last_kernel,
+        (quarter, quarter),
+        [VMEM] * 7,
+        [work(8, 64, 256), work(256, 256), work(256, 256)],
+        flops=1 << 30,
+    )(ratio, *exchange(far, near), *matrices(1, 1, ratio), est)
     got = lax.ppermute(give, ALL, to_core)
     own, *away = call(merge_kernel, (shape(64, 256),) * 4, [VMEM] * 2)(keep, got)
     parts = [own] + [lax.ppermute(piece, ALL, pairs) for piece, pairs in zip(away, to_chips)]

time: 75.1 us -> 70.1 us (0.933); the launches traced: 73.7 us -> 69.8 us
  starting transfers between devices: 31.9 us -> 26.1 us
  Pallas kernels: 11.4 us -> 15.1 us
  local copies, waits for them, and re-layouts: 2.94 us -> 1.92 us
    ppermute x3 -> x2, starting transfers between devices: 11.5 us -> 7.39 us  [exchange(): lax.ppermute(near, ALL, near_pairs)]
    pallas_call x7 -> x8, Pallas kernels: 7.52 us -> 11.2 us  [the longest x4 4.48 us: matrices(): call(functools.partial(taps_kernel, view, way), (big, big, shape(32, 256,...]
    ppermute x3 -> x2, waiting for transfers between devices: 1.97 us -> 0.01 us  [exchange(): lax.ppermute(near, ALL, near_pairs)]
    ppermute x6, starting transfers between devices: 9.04 us -> 7.86 us  [slab_sweep(): lax.ppermute(piece, ALL, pairs)]
    all_to_all x1, waiting for transfers between devices: 5.51 us -> 6.66 us  [slab_sweep(): slots = lax.all_to_all(slots, ALL, split_axis=0, concat_axis=0, tiled=True)]
    unnamed x14 -> x10, local copies, waits for them, and re-layouts: 2.94 us -> 1.92 us
    ppermute x3 -> x2, starting transfers between devices: 2.01 us -> 1.35 us  [exchange(): lax.ppermute(far, ALL, far_pairs)]
  transfers between devices with their start and end apart: 19 -> 17, of which waited for: 11 -> 9; matrix products, arithmetic and copies ran while one was open for 0% -> 0% of each run, Pallas kernels for 7% -> 10%
where the time goes in v3:
time: 70.1 us; the launch traced here: 69.8 us
  waiting for transfers between devices  26.5 us (38%)
  starting transfers between devices  26.1 us (37%)
  Pallas kernels  15.1 us (22%)
  local copies, waits for them, and re-layouts  1.92 us (3%)
    ppermute x6, waiting for transfers between devices, slab_sweep(): lax.ppermute(piece, ALL, pairs)  17.5 us
    ppermute x6, starting transfers between devices, slab_sweep(): lax.ppermute(piece, ALL, pairs)  7.86 us
    ppermute x2, starting transfers between devices, exchange(): lax.ppermute(near, ALL, near_pairs)  7.39 us
    all_to_all x1, starting transfers between devices, slab_sweep(): slots = lax.all_to_all(slots, ALL, split_axis=0, concat_axis=0, tiled=True)  7.3 us
    all_to_all x1, waiting for transfers between devices, slab_sweep(): slots = lax.all_to_all(slots, ALL, split_axis=0, concat_axis=0, tiled=True)  6.66 us
    pallas_call x4, Pallas kernels, matrices(): call(functools.partial(taps_kernel, view, way), (big, big, shape(32, 256,...  4.48 us
    pallas_call x1, Pallas kernels, slab_sweep(): call(middle_kernel, (full, full, half, half), [VMEM] * 14, [work(8, 96, 2...  3.83 us
    unnamed x10, local copies, waits for them, and re-layouts  1.92 us
  transfers between devices with their start and end apart: 17, of which 9 were waited for; matrix products, arithmetic and copies ran while one was open for 0% of the time, Pallas kernels for 10%

profile of v3, /device:TPU:0, one launch (start us, length us, event | category | flops | bytes accessed | tf_op | source)
XLA Modules:
  0.0 69.8 jit_solution(2170773584888810910)
XLA Ops:
  0.0 1.2 %copy-done = f32[2,1,1,512,256]{4,3,2,1,0:T(8,128)S(1)} copy-done((f32[2,1,1,512,256]{4,3,2,1,0:T(8,128)S(1)}, f32[2,1,1,512,256]{4,3,2,1,0:T(8,128)}, u32[]{:S(2)}) %copy-start) | copy-done | bytes 1048600
  1.2 0.7 copy-done.2
  1.9 1.4 %shard_map.55 = f32[32,72,128]{2,1,0:T(8,128)} custom-call(f32[2,512,256]{2,1,0:T(8,128)S(1)} %bitcast.6, s32[8,128]{1,0:T(8,128)S(1)} %bitcast.8), custom_call_target="tpu_custom_call" | custom-call | bytes 1048576 | tf_op jit(solution)/shard_map/pallas_call | solution.py:343
  3.3 7.3 %all-to-all-start = ((f32[32,72,128]{2,1,0:T(8,128)}), f32[32,72,128]{2,1,0:T(8,128)S(1)}, u32[]{:S(2)}, u32[]{:S(2)}) async-start(f32[32,72,128]{2,1,0:T(8,128)} %shard_map.55), calls=%async_computation | async-start | bytes 2359296 | tf_op jit(solution)/shard_map/all_to_all | solution.py:346
  10.7 0.7 %shard_map.56 = (f32[72,256]{1,0:T(8,128)S(1)}, f32[72,256]{1,0:T(8,128)S(1)}, f32[72,256]{1,0:T(8,128)S(1)}, f32[72,256]{1,0:T(8,128)S(1)}) custom-call(s32[2]{0:T(128)S(1)} %bitcast.9, f32[256,256]{1,0:T(8,128)S(1)} %bitcast.7), custom_call_target="tpu_custom_call" | custom-call | bytes 1048576 | tf_op jit(solution)/shard_map/pallas_call | solution.py:337
  11.4 1.8 %collective-permute-start = (f32[72,256]{1,0:T(8,128)S(1)}, f32[72,256]{1,0:T(8,128)S(1)}, u32[]{:S(2)}, u32[]{:S(2)}) collective-permute-start(f32[72,256]{1,0:T(8,128)S(1)} %get-tuple-element.38), channel_id=1, source_target_pairs={{0,8},{1,9},{2,10},{3,11},{4,12},{5,13},{6,14},{7,15},{8,0},{9,1},... | collective-permute-start | bytes 221192 | tf_op jit(solution)/shard_map/ppermute | solution.py:340
  13.2 1.5 %collective-permute-start.1 = (f32[72,256]{1,0:T(8,128)S(1)}, f32[72,256]{1,0:T(8,128)S(1)}, u32[]{:S(2)}, u32[]{:S(2)}) collective-permute-start(f32[72,256]{1,0:T(8,128)S(1)} %get-tuple-element.39), channel_id=1, source_target_pairs={{0,16},{1,17},{2,18},{3,19},{4,20},{5,21},{6,22},{7,23},{8,24},{9,... | collective-permute-start | bytes 221192 | tf_op jit(solution)/shard_map/ppermute | solution.py:340
  14.9 6.9 %collective-permute-done.refs_1_ = f32[72,256]{1,0:T(8,128)S(1)} collective-permute-done((f32[72,256]{1,0:T(8,128)S(1)}, f32[72,256]{1,0:T(8,128)S(1)}, u32[]{:S(2)}, u32[]{:S(2)}) %collective-permute-start) | collective-permute-done | bytes 73760 | tf_op jit(solution)/shard_map/ppermute | solution.py:340
  21.8 0.8 %collective-permute-done.1.refs_2_ = f32[72,256]{1,0:T(8,128)S(1)} collective-permute-done((f32[72,256]{1,0:T(8,128)S(1)}, f32[72,256]{1,0:T(8,128)S(1)}, u32[]{:S(2)}, u32[]{:S(2)}) %collective-permute-start.1) | collective-permute-done | bytes 73760 | tf_op jit(solution)/shard_map/ppermute | solution.py:340
  22.6 4.9 %collective-permute-done.2.refs_3_ = f32[72,256]{1,0:T(8,128)S(1)} collective-permute-done((f32[72,256]{1,0:T(8,128)S(1)}, f32[72,256]{1,0:T(8,128)S(1)}, u32[]{:S(2)}, u32[]{:S(2)}) %collective-permute-start.2) | collective-permute-done | bytes 73760 | tf_op jit(solution)/shard_map/ppermute | solution.py:340
  27.6 1.2 %collective-permute-done.6.refs_7_ = f32[72,256]{1,0:T(8,128)S(1)} collective-permute-done((f32[72,256]{1,0:T(8,128)S(1)}, f32[72,256]{1,0:T(8,128)S(1)}, u32[]{:S(2)}, u32[]{:S(2)}) %collective-permute-start.6) | collective-permute-done | bytes 73760 | tf_op jit(solution)/shard_map/ppermute | solution.py:341
  29.6 1.2 %shard_map.58 = (bf16[9,256,256]{2,1,0:T(8,128)(2,1)S(1)}, bf16[9,256,256]{2,1,0:T(8,128)(2,1)S(1)}, bf16[32,256]{1,0:T(8,128)(2,1)S(1)}) custom-call(f32[3,2,33]{2,1,0:T(2,128)S(1)} %bitcast.10, f32[8,32,256]{2,1,0:T(8,128)S(1)} %get-tuple-element.42._.est), custom_call_target="tpu_custom_call" | custom-call | flops 1073741824 | bytes 1048576 | tf_op jit(solution)/shard_map/pallas_call | solution.py:360
  30.8 1.0 %shard_map.59.blurred = f32[256,256]{1,0:T(8,128)S(1)} custom-call(f32[8,32,256]{2,1,0:T(8,128)S(1)} %get-tuple-element.42._.est, f32[8,16,256]{2,1,0:T(8,128)S(1)} %collective-permute-done.7.far.est_far, f32[8,16,256]{2,1,0:T(8,128)S(1)} %get-tuple-element.44.near.est_near, bf16[32,256]{1,0:T(8,128)(2,1)S(1)} %get-tuple-element.45.band, ...), custom_call_target="tpu_custom_call" | custom-call | flops 1073741824 | bytes 1048576 | tf_op jit(solution)/shard_map/pallas_call | solution.py:369
  31.8 6.7 %all-to-all-done.slots._ = f32[32,72,128]{2,1,0:T(8,128)S(1)} async-done(((f32[32,72,128]{2,1,0:T(8,128)}), f32[32,72,128]{2,1,0:T(8,128)S(1)}, u32[]{:S(2)}, u32[]{:S(2)}) %all-to-all-start) | async-done | bytes 1179680 | tf_op jit(solution)/shard_map/all_to_all | solution.py:346
  38.4 0.9 %shard_map.60.ratio = f32[8,32,256]{2,1,0:T(8,128)S(1)} custom-call(f32[32,72,128]{2,1,0:T(8,128)S(1)} %all-to-all-done.slots._, f32[8,8,256]{2,1,0:T(8,128)S(1)} %get-tuple-element.41.weights, f32[256,256]{1,0:T(8,128)S(1)} %shard_map.59.blurred), custom_call_target="tpu_custom_call" | custom-call | flops 1073741824 | bytes 1048576 | tf_op jit(solution)/shard_map/pallas_call | solution.py:372
  39.3 0.7 collective-permute-start.8
  40.0 4.1 %collective-permute-start.9 = (f32[8,32,256]{2,1,0:T(8,128)S(1)}, f32[8,32,256]{2,1,0:T(8,128)S(1)}, u32[]{:S(2)}, u32[]{:S(2)}) collective-permute-start(f32[8,32,256]{2,1,0:T(8,128)S(1)} %shard_map.60.ratio), channel_id=1, source_target_pairs={{0,4},{4,0},{12,8},{8,12},{24,28},{28,24},{20,16},{16,20},{17,21},... | collective-permute-start | bytes 786440 | tf_op jit(solution)/shard_map/ppermute | solution.py:334
  44.0 0.8 %shard_map.63 = (f32[8,32,256]{2,1,0:T(8,128)S(1)}, f32[8,8,256]{2,1,0:T(8,128)S(1)}) custom-call(f32[32,72,128]{2,1,0:T(8,128)S(1)} %all-to-all-done.slots._, f32[8,8,256]{2,1,0:T(8,128)S(1)} %get-tuple-element.41.weights), custom_call_target="tpu_custom_call" | custom-call | flops 1073741824 | bytes 1048576 | tf_op jit(solution)/shard_map/pallas_call | solution.py:373
  44.9 1.1 %shard_map.61 = (bf16[9,256,256]{2,1,0:T(8,128)(2,1)S(1)}, bf16[9,256,256]{2,1,0:T(8,128)(2,1)S(1)}, bf16[32,256]{1,0:T(8,128)(2,1)S(1)}) custom-call(f32[3,2,33]{2,1,0:T(2,128)S(1)} %bitcast.11, f32[32,72,128]{2,1,0:T(8,128)S(1)} %all-to-all-done.slots._), custom_call_target="tpu_custom_call" | custom-call | flops 1073741824 | bytes 1048576 | tf_op jit(solution)/shard_map/pallas_call | solution.py:360
  45.9 1.2 %shard_map.62 = (bf16[9,256,256]{2,1,0:T(8,128)(2,1)S(1)}, bf16[9,256,256]{2,1,0:T(8,128)(2,1)S(1)}, bf16[32,256]{1,0:T(8,128)(2,1)S(1)}) custom-call(f32[3,2,33]{2,1,0:T(2,128)S(1)} %bitcast.12, f32[32,72,128]{2,1,0:T(8,128)S(1)} %all-to-all-done.slots._), custom_call_target="tpu_custom_call" | custom-call | flops 1073741824 | bytes 1048576 | tf_op jit(solution)/shard_map/pallas_call | solution.py:360
  47.2 3.8 %shard_map.64 = (f32[8,32,256]{2,1,0:T(8,128)S(1)}, f32[8,32,256]{2,1,0:T(8,128)S(1)}, f32[8,16,256]{2,1,0:T(8,128)S(1)}, f32[8,16,256]{2,1,0:T(8,128)S(1)}) custom-call(f32[8,32,256]{2,1,0:T(8,128)S(1)} %shard_map.60.ratio, f32[8,32,256]{2,1,0:T(8,128)S(1)} %collective-permute-done.8.ratio_far, f32[8,32,256]{2,1,0:T(8,128)S(1)} %collective-permute-done.9.ratio_near, ...), custom_call_target="tpu_custom_call" | custom-call | flops 1073741824 | bytes 1048576 | tf_op jit(solution)/shard_map/pallas_call | solution.py:374
  51.7 3.3 %collective-permute-start.11 = (f32[8,16,256]{2,1,0:T(8,128)S(1)}, f32[8,16,256]{2,1,0:T(8,128)S(1)}, u32[]{:S(2)}, u32[]{:S(2)}) collective-permute-start(f32[8,16,256]{2,1,0:T(8,128)S(1)} %get-tuple-element.58), channel_id=1, source_target_pairs={{0,4},{4,0},{12,8},{8,12},{24,28},{28,24},{20,16},{16,20},{17,21},... | collective-permute-start | bytes 393224 | tf_op jit(solution)/shard_map/ppermute | solution.py:334
  55.0 1.1 %shard_map.65 = (bf16[9,256,256]{2,1,0:T(8,128)(2,1)S(1)}, bf16[9,256,256]{2,1,0:T(8,128)(2,1)S(1)}, bf16[32,256]{1,0:T(8,128)(2,1)S(1)}) custom-call(f32[3,2,33]{2,1,0:T(2,128)S(1)} %bitcast.13, f32[8,32,256]{2,1,0:T(8,128)S(1)} %get-tuple-element.56._.ratio), custom_call_target="tpu_custom_call" | custom-call | flops 1073741824 | bytes 1048576 | tf_op jit(solution)/shard_map/pallas_call | solution.py:360
  56.1 1.0 %shard_map.66 = (f32[4,32,256]{2,1,0:T(8,128)S(1)}, f32[4,32,256]{2,1,0:T(8,128)S(1)}) custom-call(f32[8,32,256]{2,1,0:T(8,128)S(1)} %get-tuple-element.56._.ratio, f32[8,16,256]{2,1,0:T(8,128)S(1)} %collective-permute-done.10.far, f32[8,16,256]{2,1,0:T(8,128)S(1)} %collective-permute-done.11.near, bf16[32,256]{1,0:T(8,128)(2,1)S(1)} %get-tuple-element.59.band, ...), custom_call_target="tpu_custom_call" | custom-call | flops 1073741824 | bytes 1048576 | tf_op jit(solution)/shard_map/pallas_call | solution.py:382
  57.1 1.5 %collective-permute-start.12 = (f32[4,32,256]{2,1,0:T(8,128)S(1)}, f32[4,32,256]{2,1,0:T(8,128)S(1)}, u32[]{:S(2)}, u32[]{:S(2)}) collective-permute-start(f32[4,32,256]{2,1,0:T(8,128)S(1)} %get-tuple-element.64), channel_id=1, source_target_pairs={{0,4},{1,5},{2,6},{3,7},{4,0},{5,1},{6,2},{7,3},{8,12},{9,13},{10,... | collective-permute-start | bytes 393224 | tf_op jit(solution)/shard_map/ppermute | solution.py:389
  58.6 1.0 %collective-permute-done.12.got = f32[4,32,256]{2,1,0:T(8,128)S(1)} collective-permute-done((f32[4,32,256]{2,1,0:T(8,128)S(1)}, f32[4,32,256]{2,1,0:T(8,128)S(1)}, u32[]{:S(2)}, u32[]{:S(2)}) %collective-permute-start.12) | collective-permute-done | bytes 131104 | tf_op jit(solution)/shard_map/ppermute | solution.py:389
  59.7 2.6 %collective-permute-start.13 = (f32[64,256]{1,0:T(8,128)S(1)}, f32[64,256]{1,0:T(8,128)S(1)}, u32[]{:S(2)}, u32[]{:S(2)}) collective-permute-start(f32[64,256]{1,0:T(8,128)S(1)} %get-tuple-element.66), channel_id=1, source_target_pairs={{0,8},{1,9},{2,10},{3,11},{4,12},{5,13},{6,14},{7,15},{8,0},{9,1},... | collective-permute-start | bytes 196616 | tf_op jit(solution)/shard_map/ppermute | solution.py:391
  62.3 1.5 %collective-permute-start.14 = (f32[64,256]{1,0:T(8,128)S(1)}, f32[64,256]{1,0:T(8,128)S(1)}, u32[]{:S(2)}, u32[]{:S(2)}) collective-permute-start(f32[64,256]{1,0:T(8,128)S(1)} %get-tuple-element.67), channel_id=1, source_target_pairs={{0,16},{1,17},{2,18},{3,19},{4,20},{5,21},{6,22},{7,23},{8,24},{9,... | collective-permute-start | bytes 196616 | tf_op jit(solution)/shard_map/ppermute | solution.py:391
  64.0 0.7 %collective-permute-done.13.refs_1_ = f32[64,256]{1,0:T(8,128)S(1)} collective-permute-done((f32[64,256]{1,0:T(8,128)S(1)}, f32[64,256]{1,0:T(8,128)S(1)}, u32[]{:S(2)}, u32[]{:S(2)}) %collective-permute-start.13) | collective-permute-done | bytes 65568 | tf_op jit(solution)/shard_map/ppermute | solution.py:391
  64.7 2.2 %collective-permute-done.14.refs_2_ = f32[64,256]{1,0:T(8,128)S(1)} collective-permute-done((f32[64,256]{1,0:T(8,128)S(1)}, f32[64,256]{1,0:T(8,128)S(1)}, u32[]{:S(2)}, u32[]{:S(2)}) %collective-permute-start.14) | collective-permute-done | bytes 65568 | tf_op jit(solution)/shard_map/ppermute | solution.py:391
  66.9 2.0 %collective-permute-done.15.refs_3_ = f32[64,256]{1,0:T(8,128)S(1)} collective-permute-done((f32[64,256]{1,0:T(8,128)S(1)}, f32[64,256]{1,0:T(8,128)S(1)}, u32[]{:S(2)}, u32[]{:S(2)}) %collective-permute-start.15) | collective-permute-done | bytes 65568 | tf_op jit(solution)/shard_map/ppermute | solution.py:391
  68.9 0.9 %shard_map.68 = f32[256,256]{1,0:T(8,128)} custom-call(f32[64,256]{1,0:T(8,128)S(1)} %get-tuple-element.65.refs_0_, f32[64,256]{1,0:T(8,128)S(1)} %collective-permute-done.13.refs_1_, f32[64,256]{1,0:T(8,128)S(1)} %collective-permute-done.14.refs_2_, f32[64,256]{1,0:T(8,128)S(1)} %collective-permute-done.15.refs_3_), custom_call_target="tpu_custom_call" | custom-call | bytes 1048576 | tf_op jit(solution)/shard_map/pallas_call | solution.py:392
  (26 shorter events, 2.0 us)
Async XLA Ops:
  0.0 1.2 %copy-start = (f32[2,1,1,512,256]{4,3,2,1,0:T(8,128)S(1)}, f32[2,1,1,512,256]{4,3,2,1,0:T(8,128)}, u32[]{:S(2)}) copy-start(f32[2,1,1,512,256]{4,3,2,1,0:T(8,128)} %param.6) | copy-start | bytes 3145732
  1.2 0.7 copy-start.2
  3.3 7.3 %copy-start.1 = (f32[16,16,256]{2,1,0:T(8,128)S(1)}, f32[16,16,256]{2,1,0:T(8,128)}, u32[]{:S(2)}) copy-start(f32[16,16,256]{2,1,0:T(8,128)} %param.5) | copy-start | bytes 786436
  3.3 7.3 %copy-start.3 = (s32[2,1,1,1]{0,3,2,1:T(1,128)S(1)}, s32[2,1,1,1]{0,3,2,1:T(1,128)}, u32[]{:S(2)}) copy-start(s32[2,1,1,1]{0,3,2,1:T(1,128)} %param.9) | copy-start | bytes 28
  3.3 26.2 %copy-start.4 = (f32[2,3,33]{2,0,1:T(2,128)S(1)}, f32[2,3,33]{2,0,1:T(2,128)}, u32[]{:S(2)}) copy-start(f32[2,3,33]{2,0,1:T(2,128)} %param.8) | copy-start | bytes 2380
  3.3 35.1 %all-to-all-start = ((f32[32,72,128]{2,1,0:T(8,128)}), f32[32,72,128]{2,1,0:T(8,128)S(1)}, u32[]{:S(2)}, u32[]{:S(2)}) async-start(f32[32,72,128]{2,1,0:T(8,128)} %shard_map.55), calls=%async_computation | async-start | bytes 2359296 | tf_op jit(solution)/shard_map/all_to_all | solution.py:346
  11.4 10.4 %collective-permute-start = (f32[72,256]{1,0:T(8,128)S(1)}, f32[72,256]{1,0:T(8,128)S(1)}, u32[]{:S(2)}, u32[]{:S(2)}) collective-permute-start(f32[72,256]{1,0:T(8,128)S(1)} %get-tuple-element.38), channel_id=1, source_target_pairs={{0,8},{1,9},{2,10},{3,11},{4,12},{5,13},{6,14},{7,15},{8,0},{9,1},... | collective-permute-start | bytes 221192 | tf_op jit(solution)/shard_map/ppermute | solution.py:340
  13.2 9.4 %collective-permute-start.1 = (f32[72,256]{1,0:T(8,128)S(1)}, f32[72,256]{1,0:T(8,128)S(1)}, u32[]{:S(2)}, u32[]{:S(2)}) collective-permute-start(f32[72,256]{1,0:T(8,128)S(1)} %get-tuple-element.39), channel_id=1, source_target_pairs={{0,16},{1,17},{2,18},{3,19},{4,20},{5,21},{6,22},{7,23},{8,24},{9,... | collective-permute-start | bytes 221192 | tf_op jit(solution)/shard_map/ppermute | solution.py:340
  14.7 12.9 %collective-permute-start.2 = (f32[72,256]{1,0:T(8,128)S(1)}, f32[72,256]{1,0:T(8,128)S(1)}, u32[]{:S(2)}, u32[]{:S(2)}) collective-permute-start(f32[72,256]{1,0:T(8,128)S(1)} %get-tuple-element.40), channel_id=1, source_target_pairs={{0,24},{1,25},{2,26},{3,27},{4,28},{5,29},{6,30},{7,31},{8,16},{9,... | collective-permute-start | bytes 221192 | tf_op jit(solution)/shard_map/ppermute | solution.py:340
  14.9 12.6 %collective-permute-start.3 = (f32[72,256]{1,0:T(8,128)S(1)}, f32[72,256]{1,0:T(8,128)S(1)}, u32[]{:S(2)}, u32[]{:S(2)}) collective-permute-start(f32[72,256]{1,0:T(8,128)S(1)} %get-tuple-element.37.refs_0_), channel_id=1, source_target_pairs={{0,4},{1,5},{2,6},{3,7},{4,0},{5,1},{6,2},{7,3},{8,12},{9,13},{10,... | collective-permute-start | bytes 221192 | tf_op jit(solution)/shard_map/ppermute | solution.py:341
  21.8 5.8 %collective-permute-start.4 = (f32[72,256]{1,0:T(8,128)S(1)}, f32[72,256]{1,0:T(8,128)S(1)}, u32[]{:S(2)}, u32[]{:S(2)}) collective-permute-start(f32[72,256]{1,0:T(8,128)S(1)} %collective-permute-done.refs_1_), channel_id=1, source_target_pairs={{0,4},{1,5},{2,6},{3,7},{4,0},{5,1},{6,2},{7,3},{8,12},{9,13},{10,... | collective-permute-start | bytes 221192 | tf_op jit(solution)/shard_map/ppermute | solution.py:341
  22.6 5.0 %collective-permute-start.5 = (f32[72,256]{1,0:T(8,128)S(1)}, f32[72,256]{1,0:T(8,128)S(1)}, u32[]{:S(2)}, u32[]{:S(2)}) collective-permute-start(f32[72,256]{1,0:T(8,128)S(1)} %collective-permute-done.1.refs_2_), channel_id=1, source_target_pairs={{0,4},{1,5},{2,6},{3,7},{4,0},{5,1},{6,2},{7,3},{8,12},{9,13},{10,... | collective-permute-start | bytes 221192 | tf_op jit(solution)/shard_map/ppermute | solution.py:341
  27.5 1.3 %collective-permute-start.6 = (f32[72,256]{1,0:T(8,128)S(1)}, f32[72,256]{1,0:T(8,128)S(1)}, u32[]{:S(2)}, u32[]{:S(2)}) collective-permute-start(f32[72,256]{1,0:T(8,128)S(1)} %collective-permute-done.2.refs_3_), channel_id=1, source_target_pairs={{0,4},{1,5},{2,6},{3,7},{4,0},{5,1},{6,2},{7,3},{8,12},{9,13},{10,... | collective-permute-start | bytes 221192 | tf_op jit(solution)/shard_map/ppermute | solution.py:341
  28.9 1.9 %collective-permute-start.7 = (f32[8,16,256]{2,1,0:T(8,128)S(1)}, f32[8,16,256]{2,1,0:T(8,128)S(1)}, u32[]{:S(2)}, u32[]{:S(2)}) collective-permute-start(f32[8,16,256]{2,1,0:T(8,128)S(1)} %get-tuple-element.43), channel_id=1, source_target_pairs={{4,12},{12,4},{8,24},{24,8},{28,20},{20,28},{16,17},{17,16},{21,29... | collective-permute-start | bytes 393224 | tf_op jit(solution)/shard_map/ppermute | solution.py:355
  39.3 7.9 %collective-permute-start.8 = (f32[8,32,256]{2,1,0:T(8,128)S(1)}, f32[8,32,256]{2,1,0:T(8,128)S(1)}, u32[]{:S(2)}, u32[]{:S(2)}) collective-permute-start(f32[8,32,256]{2,1,0:T(8,128)S(1)} %shard_map.60.ratio), channel_id=1, source_target_pairs={{4,12},{12,4},{8,24},{24,8},{28,20},{20,28},{16,17},{17,16},{21,29... | collective-permute-start | bytes 786440 | tf_op jit(solution)/shard_map/ppermute | solution.py:333
  40.0 7.2 %collective-permute-start.9 = (f32[8,32,256]{2,1,0:T(8,128)S(1)}, f32[8,32,256]{2,1,0:T(8,128)S(1)}, u32[]{:S(2)}, u32[]{:S(2)}) collective-permute-start(f32[8,32,256]{2,1,0:T(8,128)S(1)} %shard_map.60.ratio), channel_id=1, source_target_pairs={{0,4},{4,0},{12,8},{8,12},{24,28},{28,24},{20,16},{16,20},{17,21},... | collective-permute-start | bytes 786440 | tf_op jit(solution)/shard_map/ppermute | solution.py:334
  51.0 5.1 %collective-permute-start.10 = (f32[8,16,256]{2,1,0:T(8,128)S(1)}, f32[8,16,256]{2,1,0:T(8,128)S(1)}, u32[]{:S(2)}, u32[]{:S(2)}) collective-permute-start(f32[8,16,256]{2,1,0:T(8,128)S(1)} %get-tuple-element.57), channel_id=1, source_target_pairs={{4,12},{12,4},{8,24},{24,8},{28,20},{20,28},{16,17},{17,16},{21,29... | collective-permute-start | bytes 393224 | tf_op jit(solution)/shard_map/ppermute | solution.py:333
  51.7 4.4 %collective-permute-start.11 = (f32[8,16,256]{2,1,0:T(8,128)S(1)}, f32[8,16,256]{2,1,0:T(8,128)S(1)}, u32[]{:S(2)}, u32[]{:S(2)}) collective-permute-start(f32[8,16,256]{2,1,0:T(8,128)S(1)} %get-tuple-element.58), channel_id=1, source_target_pairs={{0,4},{4,0},{12,8},{8,12},{24,28},{28,24},{20,16},{16,20},{17,21},... | collective-permute-start | bytes 393224 | tf_op jit(solution)/shard_map/ppermute | solution.py:334
  57.1 2.5 %collective-permute-start.12 = (f32[4,32,256]{2,1,0:T(8,128)S(1)}, f32[4,32,256]{2,1,0:T(8,128)S(1)}, u32[]{:S(2)}, u32[]{:S(2)}) collective-permute-start(f32[4,32,256]{2,1,0:T(8,128)S(1)} %get-tuple-element.64), channel_id=1, source_target_pairs={{0,4},{1,5},{2,6},{3,7},{4,0},{5,1},{6,2},{7,3},{8,12},{9,13},{10,... | collective-permute-start | bytes 393224 | tf_op jit(solution)/shard_map/ppermute | solution.py:389
  59.7 5.0 %collective-permute-start.13 = (f32[64,256]{1,0:T(8,128)S(1)}, f32[64,256]{1,0:T(8,128)S(1)}, u32[]{:S(2)}, u32[]{:S(2)}) collective-permute-start(f32[64,256]{1,0:T(8,128)S(1)} %get-tuple-element.66), channel_id=1, source_target_pairs={{0,8},{1,9},{2,10},{3,11},{4,12},{5,13},{6,14},{7,15},{8,0},{9,1},... | collective-permute-start | bytes 196616 | tf_op jit(solution)/shard_map/ppermute | solution.py:391
  62.3 4.6 %collective-permute-start.14 = (f32[64,256]{1,0:T(8,128)S(1)}, f32[64,256]{1,0:T(8,128)S(1)}, u32[]{:S(2)}, u32[]{:S(2)}) collective-permute-start(f32[64,256]{1,0:T(8,128)S(1)} %get-tuple-element.67), channel_id=1, source_target_pairs={{0,16},{1,17},{2,18},{3,19},{4,20},{5,21},{6,22},{7,23},{8,24},{9,... | collective-permute-start | bytes 196616 | tf_op jit(solution)/shard_map/ppermute | solution.py:391
  63.8 5.2 %collective-permute-start.15 = (f32[64,256]{1,0:T(8,128)S(1)}, f32[64,256]{1,0:T(8,128)S(1)}, u32[]{:S(2)}, u32[]{:S(2)}) collective-permute-start(f32[64,256]{1,0:T(8,128)S(1)} %get-tuple-element.68), channel_id=1, source_target_pairs={{0,24},{1,25},{2,26},{3,27},{4,28},{5,29},{6,30},{7,31},{8,16},{9,... | collective-permute-start | bytes 196616 | tf_op jit(solution)/shard_map/ppermute | solution.py:391

commit v4 on v3

--- a/solution.py
+++ b/solution.py
@@ -21,7 +21,7 @@
 def slab_of(device, z):
     x, gy = device // 4, device % 4
     place = ring_place(x, gy // 2, z)
-    return 2 * place + ((gy % 2) ^ (place % 2))
+    return 2 * place + gy % 2
 
 
 def chain_pairs(planes):
@@ -56,16 +56,15 @@
     return lax.dot_general(a, b, (((1,), (1,)), ((), ())), preferred_element_type=F32)
 
 
-def call(kernel, out_shapes, in_specs, scratch=(), flops=0, **kwargs):
+def call(kernel, out_shapes, in_specs, scratch=(), flops=0, out_specs=None, vmem=16):
     return pl.pallas_call(
         kernel,
         out_shape=out_shapes,
         in_specs=in_specs,
-        out_specs=jax.tree.map(lambda _: VMEM, out_shapes),
+        out_specs=out_specs or jax.tree.map(lambda _: VMEM, out_shapes),
         scratch_shapes=list(scratch),
-        compiler_params=pltpu.CompilerParams(vmem_limit_bytes=16 * 1024 * 1024),
+        compiler_params=pltpu.CompilerParams(vmem_limit_bytes=vmem * 1024 * 1024),
         cost_estimate=pl.CostEstimate(flops=flops, bytes_accessed=1 << 20, transcendentals=0),
-        **kwargs,
     )
 
 
@@ -81,8 +80,7 @@
 
 
 def upper_half():
-    x, y, core, z = coordinates()
-    return lax.rem(core + place_on_ring(x, y, z), 2)
+    return coordinates()[2]
 
 
 def chips():
@@ -121,27 +119,43 @@
             near[column] = piece[pl.ds(pl.multiple_of(32 - 16 * upper, 16), 16), :]
 
 
-def lines_kernel(planes, raw, index, out):
+def lines_kernel(planes, raw, index, out, held, numbers, made, arrived, numbered, left):
     mine = lax.axis_index("gz")
+    blocks = [lax.rem(place - mine + 4, 4) for place in range(4)]
     chunk = lax.broadcasted_iota(jnp.int32, (8, 128), 1) // 32
     rows = lax.broadcasted_iota(jnp.int32, (8, 128), 0)
+
+    def load(z):
+        return pltpu.make_async_copy(raw.at[:, :, z], held.at[z], arrived.at[z])
+
+    def store(z):
+        return pltpu.make_async_copy(made.at[z], out.at[:, z], left.at[z])
+
+    load_numbers = pltpu.make_async_copy(index, numbers, numbered.at[0])
     for z in range(planes):
+        load(z).start()
+    load_numbers.start()
+    for z in range(planes):
+        load(z).wait()
+        for view in range(2):
+            lines = jnp.concatenate([held[z, view, block] for block in blocks], axis=0)
+            turned = lines.T
+            for device in range(8):
+                slab = slab_of(device, z)
+                made[z, device, 32 * view : 32 * view + 32, :] = turned[slab * 32 : slab * 32 + 32, :]
+        if z == 0:
+            load_numbers.wait()
         both = jnp.zeros((8, 128), F32)
-        for view in range(2):
-            parts = []
-            for place in range(4):
-                block = lax.rem(place - mine + 4, 4)
-                start = pl.multiple_of((block * planes + z) * 32, 32)
-                parts.append(raw[view, pl.ds(start, 32), :])
-                row = index[pl.ds(view * 4 + block, 1), :].astype(F32)
+        for place, block in enumerate(blocks):
+            for view in range(2):
+                row = numbers[pl.ds(view * 4 + block, 1), :].astype(F32)
                 row = pltpu.roll(jnp.broadcast_to(row, (8, 128)), (32 * (place - z)) % 128, 1)
                 both = jnp.where((chunk == place) & (rows == view), row, both)
-            turned = jnp.concatenate(parts, axis=0).T
-            for device in range(8):
-                slab = slab_of(device, z)
-                out[device * planes + z, 32 * view : 32 * view + 32, :] = turned[slab * 32 : slab * 32 + 32, :]
         for device in range(8):
-            out[device * planes + z, 64:72, :] = both
+            made[z, device, 64:72, :] = both
+        store(z).start()
+    for z in range(planes):
+        store(z).wait()
 
 
 def taps_kernel(view, way, psf, _, big_high, big_low, band, held):
@@ -160,10 +174,9 @@
     turn = (from_lane + to_lane == 32).astype(BF16)
     turned = sum(dot_nn(piece, turn) for piece in split3(taps))
     along_z, along_xy = (taps, turned) if way == 0 else (turned, taps)
-    high, low = split2(toeplitz(along_z[2:3, :], 32))
-    twice = high.astype(F32) + pltpu.roll(high.astype(F32), 64, 1)
-    band[:, 0:128] = twice.astype(BF16)
-    band[:, 128:256] = low
+    high, low = (part.astype(F32) for part in split2(toeplitz(along_z[2:3, :], 32)))
+    band[0:32, :] = (high + pltpu.roll(high, 64, 1)).astype(BF16)
+    band[32:64, :] = low.astype(BF16)
     tall_x = jnp.broadcast_to(toeplitz(along_xy[0:1, :], 16)[:, None, :], (16, 16, 128)).reshape(256, 128)
     tall_y = jnp.broadcast_to(toeplitz(along_xy[1:2, :], 16)[None], (16, 16, 128)).reshape(256, 128)
     from_row = lax.broadcasted_iota(jnp.int32, (128, 256), 0)
@@ -229,10 +242,10 @@
     weights = band[...]
     for column in range(8):
         for start in range(0, rows, 32):
-            high, low = split2(wide[column, start : start + 64, :])
-            stacked = jnp.concatenate([high, low, high, high], axis=0)
+            stacked = jnp.concatenate(split2(wide[column, start : start + 64, :]), axis=0)
+            both = dot_nn(weights, stacked)
             at = column * rows + start
-            flat[at : at + 32, :] = dot_nn(weights, stacked)
+            flat[at : at + 32, :] = both[0:32] + both[32:64]
     high, low = split2(flat[...])
 
     def product(start, stop, dx, dy):
@@ -340,9 +353,23 @@
     here = [own] + [lax.ppermute(piece, ALL, pairs) for piece, pairs in zip(away, to_chips)]
     there = [lax.ppermute(piece, ALL, to_core) for piece in here]
 
-    slots = call(functools.partial(lines_kernel, planes), shape(8 * planes, 72, 128), [VMEM, VMEM])(
-        raw_lines.reshape(2, 4 * planes * 32, 256), line_index.reshape(8, 128)
-    )
+    anywhere = pl.BlockSpec(memory_space=pl.ANY)
+    slots = call(
+        functools.partial(lines_kernel, planes),
+        shape(8, planes, 72, 128),
+        [anywhere, anywhere],
+        [
+            pltpu.VMEM((planes, 2, 4, 32, 256), F32),
+            pltpu.VMEM((8, 128), jnp.int32),
+            pltpu.VMEM((planes, 8, 72, 128), F32),
+            pltpu.SemaphoreType.DMA((planes,)),
+            pltpu.SemaphoreType.DMA((1,)),
+            pltpu.SemaphoreType.DMA((planes,)),
+        ],
+        out_specs=anywhere,
+        vmem=56,
+    )(raw_lines.reshape(2, 4, planes, 32, 256), line_index.reshape(8, 128))
+    slots = slots.reshape(8 * planes, 72, 128)
     slots = lax.all_to_all(slots, ALL, split_axis=0, concat_axis=0, tiled=True)
     half, full = shape(8, 16, 256), shape(8, 32, 256)
 
@@ -353,13 +380,11 @@
         *here, *there
     )
     est_far = lax.ppermute(est_far, ALL, far_pairs)
-    anywhere = pl.BlockSpec(memory_space=pl.ANY)
-
     def matrices(view, way, after):
         big = shape(9, 256, 256, dtype=BF16)
         big_high, big_low, band = call(
             functools.partial(taps_kernel, view, way),
-            (big, big, shape(32, 256, dtype=BF16)),
+            (big, big, shape(64, 128, dtype=BF16)),
             [VMEM, anywhere],
             [work(8, 128)],
             flops=1 << 30,

time: 70.1 us -> 67.9 us (0.969)
  local copies, waits for them, and re-layouts: 1.92 us -> 0.02 us
  waiting for transfers between devices: 26.5 us -> 25.3 us
    unnamed x10 -> x6, local copies, waits for them, and re-layouts: 1.92 us -> 0.02 us
    ppermute x1, starting transfers between devices: 1.54 us -> 3.28 us  [slab_sweep(): got = lax.ppermute(give, ALL, to_core)]
    ppermute x6, waiting for transfers between devices: 17.5 us -> 16.3 us  [slab_sweep(): lax.ppermute(piece, ALL, pairs)]
    pallas_call x5, Pallas kernels: 5.89 us -> 6.97 us  [the longest x4 4.48 us: matrices(): call(functools.partial(taps_kernel, view, way), (big, big, shape(64, 128,...]
    ppermute x6, starting transfers between devices: 7.86 us -> 7.12 us  [slab_sweep(): lax.ppermute(piece, ALL, pairs)]
where the time goes in v4:
time: 67.9 us; the launch traced here: 67.7 us
  starting transfers between devices  26.5 us (39%)
  waiting for transfers between devices  25.3 us (37%)
  Pallas kernels  15.6 us (23%)
    ppermute x6, waiting for transfers between devices, slab_sweep(): lax.ppermute(piece, ALL, pairs)  16.3 us
    all_to_all x1, starting transfers between devices, slab_sweep(): slots = lax.all_to_all(slots, ALL, split_axis=0, concat_axis=0, tiled=True)  7.3 us
    ppermute x6, starting transfers between devices, slab_sweep(): lax.ppermute(piece, ALL, pairs)  7.12 us
    ppermute x2, starting transfers between devices, exchange(): lax.ppermute(near, ALL, near_pairs)  6.81 us
    all_to_all x1, waiting for transfers between devices, slab_sweep(): slots = lax.all_to_all(slots, ALL, split_axis=0, concat_axis=0, tiled=True)  6.77 us
    pallas_call x4, Pallas kernels, matrices(): call(functools.partial(taps_kernel, view, way), (big, big, shape(64, 128,...  4.48 us
    pallas_call x1, Pallas kernels, slab_sweep(): call(middle_kernel, (full, full, half, half), [VMEM] * 14, [work(8, 96, 2...  3.47 us
    ppermute x1, starting transfers between devices, slab_sweep(): got = lax.ppermute(give, ALL, to_core)  3.28 us
  transfers between devices with their start and end apart: 17, of which 9 were waited for; matrix products, arithmetic and copies ran while one was open for 0% of the time, Pallas kernels for 10%

profile of v4, /device:TPU:0, one launch (start us, length us, event | category | flops | bytes accessed | tf_op | source)
XLA Modules:
  0.0 67.7 jit_solution(11850539489573703501)
XLA Ops:
  0.0 2.5 %shard_map.55 = f32[8,4,72,128]{3,2,1,0:T(8,128)} custom-call(f32[2,4,4,32,256]{4,3,2,1,0:T(8,128)} %bitcast.14, s32[8,128]{1,0:T(8,128)} %bitcast.15), custom_call_target="tpu_custom_call" | custom-call | bytes 1048576 | tf_op jit(solution)/shard_map/pallas_call | solution.py:357
  2.5 7.3 %all-to-all-start = ((f32[32,72,128]{2,1,0:T(8,128)}), f32[32,72,128]{2,1,0:T(8,128)S(1)}, u32[]{:S(2)}, u32[]{:S(2)}) async-start(f32[32,72,128]{2,1,0:T(8,128)} %bitcast.13), calls=%async_computation | async-start | bytes 2359296 | tf_op jit(solution)/shard_map/all_to_all | solution.py:373
  9.9 0.7 %shard_map.56 = (f32[72,256]{1,0:T(8,128)S(1)}, f32[72,256]{1,0:T(8,128)S(1)}, f32[72,256]{1,0:T(8,128)S(1)}, f32[72,256]{1,0:T(8,128)S(1)}) custom-call(s32[2]{0:T(128)S(1)} %bitcast.8, f32[256,256]{1,0:T(8,128)S(1)} %bitcast.7), custom_call_target="tpu_custom_call" | custom-call | bytes 1048576 | tf_op jit(solution)/shard_map/pallas_call | solution.py:350
  10.6 1.8 %collective-permute-start = (f32[72,256]{1,0:T(8,128)S(1)}, f32[72,256]{1,0:T(8,128)S(1)}, u32[]{:S(2)}, u32[]{:S(2)}) collective-permute-start(f32[72,256]{1,0:T(8,128)S(1)} %get-tuple-element.38), channel_id=1, source_target_pairs={{0,8},{1,9},{2,10},{3,11},{4,12},{5,13},{6,14},{7,15},{8,0},{9,1},... | collective-permute-start | bytes 221192 | tf_op jit(solution)/shard_map/ppermute | solution.py:353
  12.4 1.5 %collective-permute-start.1 = (f32[72,256]{1,0:T(8,128)S(1)}, f32[72,256]{1,0:T(8,128)S(1)}, u32[]{:S(2)}, u32[]{:S(2)}) collective-permute-start(f32[72,256]{1,0:T(8,128)S(1)} %get-tuple-element.39), channel_id=1, source_target_pairs={{0,16},{1,17},{2,18},{3,19},{4,20},{5,21},{6,22},{7,23},{8,24},{9,... | collective-permute-start | bytes 221192 | tf_op jit(solution)/shard_map/ppermute | solution.py:353
  14.1 6.9 %collective-permute-done.refs_1_ = f32[72,256]{1,0:T(8,128)S(1)} collective-permute-done((f32[72,256]{1,0:T(8,128)S(1)}, f32[72,256]{1,0:T(8,128)S(1)}, u32[]{:S(2)}, u32[]{:S(2)}) %collective-permute-start) | collective-permute-done | bytes 73760 | tf_op jit(solution)/shard_map/ppermute | solution.py:353
  21.0 0.8 %collective-permute-done.1.refs_2_ = f32[72,256]{1,0:T(8,128)S(1)} collective-permute-done((f32[72,256]{1,0:T(8,128)S(1)}, f32[72,256]{1,0:T(8,128)S(1)}, u32[]{:S(2)}, u32[]{:S(2)}) %collective-permute-start.1) | collective-permute-done | bytes 73760 | tf_op jit(solution)/shard_map/ppermute | solution.py:353
  21.8 4.9 %collective-permute-done.2.refs_3_ = f32[72,256]{1,0:T(8,128)S(1)} collective-permute-done((f32[72,256]{1,0:T(8,128)S(1)}, f32[72,256]{1,0:T(8,128)S(1)}, u32[]{:S(2)}, u32[]{:S(2)}) %collective-permute-start.2) | collective-permute-done | bytes 73760 | tf_op jit(solution)/shard_map/ppermute | solution.py:353
  26.8 1.2 %collective-permute-done.6.refs_7_ = f32[72,256]{1,0:T(8,128)S(1)} collective-permute-done((f32[72,256]{1,0:T(8,128)S(1)}, f32[72,256]{1,0:T(8,128)S(1)}, u32[]{:S(2)}, u32[]{:S(2)}) %collective-permute-start.6) | collective-permute-done | bytes 73760 | tf_op jit(solution)/shard_map/ppermute | solution.py:354
  28.1 0.7 collective-permute-start.7
  28.8 1.2 %shard_map.58 = (bf16[9,256,256]{2,1,0:T(8,128)(2,1)S(1)}, bf16[9,256,256]{2,1,0:T(8,128)(2,1)S(1)}, bf16[64,128]{1,0:T(8,128)(2,1)S(1)}) custom-call(f32[3,2,33]{2,1,0:T(2,128)S(1)} %bitcast.9, f32[8,32,256]{2,1,0:T(8,128)S(1)} %get-tuple-element.42._.est), custom_call_target="tpu_custom_call" | custom-call | flops 1073741824 | bytes 1048576 | tf_op jit(solution)/shard_map/pallas_call | solution.py:385
  30.0 0.9 %shard_map.59.blurred = f32[256,256]{1,0:T(8,128)S(1)} custom-call(f32[8,32,256]{2,1,0:T(8,128)S(1)} %get-tuple-element.42._.est, f32[8,16,256]{2,1,0:T(8,128)S(1)} %collective-permute-done.7.far.est_far, f32[8,16,256]{2,1,0:T(8,128)S(1)} %get-tuple-element.44.near.est_near, bf16[64,128]{1,0:T(8,128)(2,1)S(1)} %get-tuple-element.45.band, ...), custom_call_target="tpu_custom_call" | custom-call | flops 1073741824 | bytes 1048576 | tf_op jit(solution)/shard_map/pallas_call | solution.py:394
  30.9 6.8 %all-to-all-done.slots._ = f32[32,72,128]{2,1,0:T(8,128)S(1)} async-done(((f32[32,72,128]{2,1,0:T(8,128)}), f32[32,72,128]{2,1,0:T(8,128)S(1)}, u32[]{:S(2)}, u32[]{:S(2)}) %all-to-all-start) | async-done | bytes 1179680 | tf_op jit(solution)/shard_map/all_to_all | solution.py:373
  37.6 0.9 %shard_map.60.ratio = f32[8,32,256]{2,1,0:T(8,128)S(1)} custom-call(f32[32,72,128]{2,1,0:T(8,128)S(1)} %all-to-all-done.slots._, f32[8,8,256]{2,1,0:T(8,128)S(1)} %get-tuple-element.41.weights, f32[256,256]{1,0:T(8,128)S(1)} %shard_map.59.blurred), custom_call_target="tpu_custom_call" | custom-call | flops 1073741824 | bytes 1048576 | tf_op jit(solution)/shard_map/pallas_call | solution.py:397
  38.5 0.7 %collective-permute-start.8 = (f32[8,32,256]{2,1,0:T(8,128)S(1)}, f32[8,32,256]{2,1,0:T(8,128)S(1)}, u32[]{:S(2)}, u32[]{:S(2)}) collective-permute-start(f32[8,32,256]{2,1,0:T(8,128)S(1)} %shard_map.60.ratio), channel_id=1, source_target_pairs={{4,8},{8,4},{12,24},{24,12},{28,16},{16,28},{20,17},{17,20},{21,25... | collective-permute-start | bytes 786440 | tf_op jit(solution)/shard_map/ppermute | solution.py:346
  39.2 2.9 %collective-permute-start.9 = (f32[8,32,256]{2,1,0:T(8,128)S(1)}, f32[8,32,256]{2,1,0:T(8,128)S(1)}, u32[]{:S(2)}, u32[]{:S(2)}) collective-permute-start(f32[8,32,256]{2,1,0:T(8,128)S(1)} %shard_map.60.ratio), channel_id=1, source_target_pairs={{0,4},{4,0},{8,12},{12,8},{24,28},{28,24},{16,20},{20,16},{17,21},... | collective-permute-start | bytes 786440 | tf_op jit(solution)/shard_map/ppermute | solution.py:347
  42.1 0.8 %shard_map.63 = (f32[8,32,256]{2,1,0:T(8,128)S(1)}, f32[8,8,256]{2,1,0:T(8,128)S(1)}) custom-call(f32[32,72,128]{2,1,0:T(8,128)S(1)} %all-to-all-done.slots._, f32[8,8,256]{2,1,0:T(8,128)S(1)} %get-tuple-element.41.weights), custom_call_target="tpu_custom_call" | custom-call | flops 1073741824 | bytes 1048576 | tf_op jit(solution)/shard_map/pallas_call | solution.py:398
  42.9 1.1 %shard_map.61 = (bf16[9,256,256]{2,1,0:T(8,128)(2,1)S(1)}, bf16[9,256,256]{2,1,0:T(8,128)(2,1)S(1)}, bf16[64,128]{1,0:T(8,128)(2,1)S(1)}) custom-call(f32[3,2,33]{2,1,0:T(2,128)S(1)} %bitcast.10, f32[32,72,128]{2,1,0:T(8,128)S(1)} %all-to-all-done.slots._), custom_call_target="tpu_custom_call" | custom-call | flops 1073741824 | bytes 1048576 | tf_op jit(solution)/shard_map/pallas_call | solution.py:385
  44.0 1.2 %shard_map.62 = (bf16[9,256,256]{2,1,0:T(8,128)(2,1)S(1)}, bf16[9,256,256]{2,1,0:T(8,128)(2,1)S(1)}, bf16[64,128]{1,0:T(8,128)(2,1)S(1)}) custom-call(f32[3,2,33]{2,1,0:T(2,128)S(1)} %bitcast.11, f32[32,72,128]{2,1,0:T(8,128)S(1)} %all-to-all-done.slots._), custom_call_target="tpu_custom_call" | custom-call | flops 1073741824 | bytes 1048576 | tf_op jit(solution)/shard_map/pallas_call | solution.py:385
  45.2 3.5 %shard_map.64 = (f32[8,32,256]{2,1,0:T(8,128)S(1)}, f32[8,32,256]{2,1,0:T(8,128)S(1)}, f32[8,16,256]{2,1,0:T(8,128)S(1)}, f32[8,16,256]{2,1,0:T(8,128)S(1)}) custom-call(f32[8,32,256]{2,1,0:T(8,128)S(1)} %shard_map.60.ratio, f32[8,32,256]{2,1,0:T(8,128)S(1)} %collective-permute-done.8.ratio_far, f32[8,32,256]{2,1,0:T(8,128)S(1)} %collective-permute-done.9.ratio_near, ...), custom_call_target="tpu_custom_call" | custom-call | flops 1073741824 | bytes 1048576 | tf_op jit(solution)/shard_map/pallas_call | solution.py:399
  48.7 0.7 collective-permute-start.10
  49.4 3.9 %collective-permute-start.11 = (f32[8,16,256]{2,1,0:T(8,128)S(1)}, f32[8,16,256]{2,1,0:T(8,128)S(1)}, u32[]{:S(2)}, u32[]{:S(2)}) collective-permute-start(f32[8,16,256]{2,1,0:T(8,128)S(1)} %get-tuple-element.58), channel_id=1, source_target_pairs={{0,4},{4,0},{8,12},{12,8},{24,28},{28,24},{16,20},{20,16},{17,21},... | collective-permute-start | bytes 393224 | tf_op jit(solution)/shard_map/ppermute | solution.py:347
  53.3 1.1 %shard_map.65 = (bf16[9,256,256]{2,1,0:T(8,128)(2,1)S(1)}, bf16[9,256,256]{2,1,0:T(8,128)(2,1)S(1)}, bf16[64,128]{1,0:T(8,128)(2,1)S(1)}) custom-call(f32[3,2,33]{2,1,0:T(2,128)S(1)} %bitcast.12, f32[8,32,256]{2,1,0:T(8,128)S(1)} %get-tuple-element.56._.ratio), custom_call_target="tpu_custom_call" | custom-call | flops 1073741824 | bytes 1048576 | tf_op jit(solution)/shard_map/pallas_call | solution.py:385
  54.3 0.9 %shard_map.66 = (f32[4,32,256]{2,1,0:T(8,128)S(1)}, f32[4,32,256]{2,1,0:T(8,128)S(1)}) custom-call(f32[8,32,256]{2,1,0:T(8,128)S(1)} %get-tuple-element.56._.ratio, f32[8,16,256]{2,1,0:T(8,128)S(1)} %collective-permute-done.10.far, f32[8,16,256]{2,1,0:T(8,128)S(1)} %collective-permute-done.11.near, bf16[64,128]{1,0:T(8,128)(2,1)S(1)} %get-tuple-element.59.band, ...), custom_call_target="tpu_custom_call" | custom-call | flops 1073741824 | bytes 1048576 | tf_op jit(solution)/shard_map/pallas_call | solution.py:407
  55.2 3.3 %collective-permute-start.12 = (f32[4,32,256]{2,1,0:T(8,128)S(1)}, f32[4,32,256]{2,1,0:T(8,128)S(1)}, u32[]{:S(2)}, u32[]{:S(2)}) collective-permute-start(f32[4,32,256]{2,1,0:T(8,128)S(1)} %get-tuple-element.64), channel_id=1, source_target_pairs={{0,4},{1,5},{2,6},{3,7},{4,0},{5,1},{6,2},{7,3},{8,12},{9,13},{10,... | collective-permute-start | bytes 393224 | tf_op jit(solution)/shard_map/ppermute | solution.py:414
  58.5 1.0 %collective-permute-done.12.got = f32[4,32,256]{2,1,0:T(8,128)S(1)} collective-permute-done((f32[4,32,256]{2,1,0:T(8,128)S(1)}, f32[4,32,256]{2,1,0:T(8,128)S(1)}, u32[]{:S(2)}, u32[]{:S(2)}) %collective-permute-start.12) | collective-permute-done | bytes 131104 | tf_op jit(solution)/shard_map/ppermute | solution.py:414
  59.5 1.5 %collective-permute-start.13 = (f32[64,256]{1,0:T(8,128)S(1)}, f32[64,256]{1,0:T(8,128)S(1)}, u32[]{:S(2)}, u32[]{:S(2)}) collective-permute-start(f32[64,256]{1,0:T(8,128)S(1)} %get-tuple-element.66), channel_id=1, source_target_pairs={{0,8},{1,9},{2,10},{3,11},{4,12},{5,13},{6,14},{7,15},{8,0},{9,1},... | collective-permute-start | bytes 196616 | tf_op jit(solution)/shard_map/ppermute | solution.py:416
  61.6 1.5 %collective-permute-start.15 = (f32[64,256]{1,0:T(8,128)S(1)}, f32[64,256]{1,0:T(8,128)S(1)}, u32[]{:S(2)}, u32[]{:S(2)}) collective-permute-start(f32[64,256]{1,0:T(8,128)S(1)} %get-tuple-element.68), channel_id=1, source_target_pairs={{0,24},{1,25},{2,26},{3,27},{4,28},{5,29},{6,30},{7,31},{8,16},{9,... | collective-permute-start | bytes 196616 | tf_op jit(solution)/shard_map/ppermute | solution.py:416
  63.1 0.9 %collective-permute-done.13.refs_1_ = f32[64,256]{1,0:T(8,128)S(1)} collective-permute-done((f32[64,256]{1,0:T(8,128)S(1)}, f32[64,256]{1,0:T(8,128)S(1)}, u32[]{:S(2)}, u32[]{:S(2)}) %collective-permute-start.13) | collective-permute-done | bytes 65568 | tf_op jit(solution)/shard_map/ppermute | solution.py:416
  64.0 1.8 %collective-permute-done.14.refs_2_ = f32[64,256]{1,0:T(8,128)S(1)} collective-permute-done((f32[64,256]{1,0:T(8,128)S(1)}, f32[64,256]{1,0:T(8,128)S(1)}, u32[]{:S(2)}, u32[]{:S(2)}) %collective-permute-start.14) | collective-permute-done | bytes 65568 | tf_op jit(solution)/shard_map/ppermute | solution.py:416
  65.7 1.1 %collective-permute-done.15.refs_3_ = f32[64,256]{1,0:T(8,128)S(1)} collective-permute-done((f32[64,256]{1,0:T(8,128)S(1)}, f32[64,256]{1,0:T(8,128)S(1)}, u32[]{:S(2)}, u32[]{:S(2)}) %collective-permute-start.15) | collective-permute-done | bytes 65568 | tf_op jit(solution)/shard_map/ppermute | solution.py:416
  66.8 0.9 %shard_map.68 = f32[256,256]{1,0:T(8,128)} custom-call(f32[64,256]{1,0:T(8,128)S(1)} %get-tuple-element.65.refs_0_, f32[64,256]{1,0:T(8,128)S(1)} %collective-permute-done.13.refs_1_, f32[64,256]{1,0:T(8,128)S(1)} %collective-permute-done.14.refs_2_, f32[64,256]{1,0:T(8,128)S(1)} %collective-permute-done.15.refs_3_), custom_call_target="tpu_custom_call" | custom-call | bytes 1048576 | tf_op jit(solution)/shard_map/pallas_call | solution.py:417
  (22 shorter events, 0.9 us)
Async XLA Ops:
  2.5 7.3 %copy-start = (f32[16,16,256]{2,1,0:T(8,128)S(1)}, f32[16,16,256]{2,1,0:T(8,128)}, u32[]{:S(2)}) copy-start(f32[16,16,256]{2,1,0:T(8,128)} %param.5) | copy-start | bytes 786436
  2.5 7.3 %copy-start.1 = (s32[2,1,1,1]{0,3,2,1:T(1,128)S(1)}, s32[2,1,1,1]{0,3,2,1:T(1,128)}, u32[]{:S(2)}) copy-start(s32[2,1,1,1]{0,3,2,1:T(1,128)} %param.9) | copy-start | bytes 28
  2.5 26.2 %copy-start.2 = (f32[2,3,33]{2,0,1:T(2,128)S(1)}, f32[2,3,33]{2,0,1:T(2,128)}, u32[]{:S(2)}) copy-start(f32[2,3,33]{2,0,1:T(2,128)} %param.8) | copy-start | bytes 2380
  2.5 35.1 %all-to-all-start = ((f32[32,72,128]{2,1,0:T(8,128)}), f32[32,72,128]{2,1,0:T(8,128)S(1)}, u32[]{:S(2)}, u32[]{:S(2)}) async-start(f32[32,72,128]{2,1,0:T(8,128)} %bitcast.13), calls=%async_computation | async-start | bytes 2359296 | tf_op jit(solution)/shard_map/all_to_all | solution.py:373
  10.6 10.4 %collective-permute-start = (f32[72,256]{1,0:T(8,128)S(1)}, f32[72,256]{1,0:T(8,128)S(1)}, u32[]{:S(2)}, u32[]{:S(2)}) collective-permute-start(f32[72,256]{1,0:T(8,128)S(1)} %get-tuple-element.38), channel_id=1, source_target_pairs={{0,8},{1,9},{2,10},{3,11},{4,12},{5,13},{6,14},{7,15},{8,0},{9,1},... | collective-permute-start | bytes 221192 | tf_op jit(solution)/shard_map/ppermute | solution.py:353
  12.4 9.4 %collective-permute-start.1 = (f32[72,256]{1,0:T(8,128)S(1)}, f32[72,256]{1,0:T(8,128)S(1)}, u32[]{:S(2)}, u32[]{:S(2)}) collective-permute-start(f32[72,256]{1,0:T(8,128)S(1)} %get-tuple-element.39), channel_id=1, source_target_pairs={{0,16},{1,17},{2,18},{3,19},{4,20},{5,21},{6,22},{7,23},{8,24},{9,... | collective-permute-start | bytes 221192 | tf_op jit(solution)/shard_map/ppermute | solution.py:353
  13.9 12.9 %collective-permute-start.2 = (f32[72,256]{1,0:T(8,128)S(1)}, f32[72,256]{1,0:T(8,128)S(1)}, u32[]{:S(2)}, u32[]{:S(2)}) collective-permute-start(f32[72,256]{1,0:T(8,128)S(1)} %get-tuple-element.40), channel_id=1, source_target_pairs={{0,24},{1,25},{2,26},{3,27},{4,28},{5,29},{6,30},{7,31},{8,16},{9,... | collective-permute-start | bytes 221192 | tf_op jit(solution)/shard_map/ppermute | solution.py:353
  14.1 12.6 %collective-permute-start.3 = (f32[72,256]{1,0:T(8,128)S(1)}, f32[72,256]{1,0:T(8,128)S(1)}, u32[]{:S(2)}, u32[]{:S(2)}) collective-permute-start(f32[72,256]{1,0:T(8,128)S(1)} %get-tuple-element.37.refs_0_), channel_id=1, source_target_pairs={{0,4},{1,5},{2,6},{3,7},{4,0},{5,1},{6,2},{7,3},{8,12},{9,13},{10,... | collective-permute-start | bytes 221192 | tf_op jit(solution)/shard_map/ppermute | solution.py:354
  21.0 5.8 %collective-permute-start.4 = (f32[72,256]{1,0:T(8,128)S(1)}, f32[72,256]{1,0:T(8,128)S(1)}, u32[]{:S(2)}, u32[]{:S(2)}) collective-permute-start(f32[72,256]{1,0:T(8,128)S(1)} %collective-permute-done.refs_1_), channel_id=1, source_target_pairs={{0,4},{1,5},{2,6},{3,7},{4,0},{5,1},{6,2},{7,3},{8,12},{9,13},{10,... | collective-permute-start | bytes 221192 | tf_op jit(solution)/shard_map/ppermute | solution.py:354
  21.8 5.0 %collective-permute-start.5 = (f32[72,256]{1,0:T(8,128)S(1)}, f32[72,256]{1,0:T(8,128)S(1)}, u32[]{:S(2)}, u32[]{:S(2)}) collective-permute-start(f32[72,256]{1,0:T(8,128)S(1)} %collective-permute-done.1.refs_2_), channel_id=1, source_target_pairs={{0,4},{1,5},{2,6},{3,7},{4,0},{5,1},{6,2},{7,3},{8,12},{9,13},{10,... | collective-permute-start | bytes 221192 | tf_op jit(solution)/shard_map/ppermute | solution.py:354
  26.8 1.3 %collective-permute-start.6 = (f32[72,256]{1,0:T(8,128)S(1)}, f32[72,256]{1,0:T(8,128)S(1)}, u32[]{:S(2)}, u32[]{:S(2)}) collective-permute-start(f32[72,256]{1,0:T(8,128)S(1)} %collective-permute-done.2.refs_3_), channel_id=1, source_target_pairs={{0,4},{1,5},{2,6},{3,7},{4,0},{5,1},{6,2},{7,3},{8,12},{9,13},{10,... | collective-permute-start | bytes 221192 | tf_op jit(solution)/shard_map/ppermute | solution.py:354
  28.1 1.9 %collective-permute-start.7 = (f32[8,16,256]{2,1,0:T(8,128)S(1)}, f32[8,16,256]{2,1,0:T(8,128)S(1)}, u32[]{:S(2)}, u32[]{:S(2)}) collective-permute-start(f32[8,16,256]{2,1,0:T(8,128)S(1)} %get-tuple-element.43), channel_id=1, source_target_pairs={{4,8},{8,4},{12,24},{24,12},{28,16},{16,28},{20,17},{17,20},{21,25... | collective-permute-start | bytes 393224 | tf_op jit(solution)/shard_map/ppermute | solution.py:382
  38.5 6.7 %collective-permute-start.8 = (f32[8,32,256]{2,1,0:T(8,128)S(1)}, f32[8,32,256]{2,1,0:T(8,128)S(1)}, u32[]{:S(2)}, u32[]{:S(2)}) collective-permute-start(f32[8,32,256]{2,1,0:T(8,128)S(1)} %shard_map.60.ratio), channel_id=1, source_target_pairs={{4,8},{8,4},{12,24},{24,12},{28,16},{16,28},{20,17},{17,20},{21,25... | collective-permute-start | bytes 786440 | tf_op jit(solution)/shard_map/ppermute | solution.py:346
  39.2 6.0 %collective-permute-start.9 = (f32[8,32,256]{2,1,0:T(8,128)S(1)}, f32[8,32,256]{2,1,0:T(8,128)S(1)}, u32[]{:S(2)}, u32[]{:S(2)}) collective-permute-start(f32[8,32,256]{2,1,0:T(8,128)S(1)} %shard_map.60.ratio), channel_id=1, source_target_pairs={{0,4},{4,0},{8,12},{12,8},{24,28},{28,24},{16,20},{20,16},{17,21},... | collective-permute-start | bytes 786440 | tf_op jit(solution)/shard_map/ppermute | solution.py:347
  48.7 5.6 %collective-permute-start.10 = (f32[8,16,256]{2,1,0:T(8,128)S(1)}, f32[8,16,256]{2,1,0:T(8,128)S(1)}, u32[]{:S(2)}, u32[]{:S(2)}) collective-permute-start(f32[8,16,256]{2,1,0:T(8,128)S(1)} %get-tuple-element.57), channel_id=1, source_target_pairs={{4,8},{8,4},{12,24},{24,12},{28,16},{16,28},{20,17},{17,20},{21,25... | collective-permute-start | bytes 393224 | tf_op jit(solution)/shard_map/ppermute | solution.py:346
  49.4 5.0 %collective-permute-start.11 = (f32[8,16,256]{2,1,0:T(8,128)S(1)}, f32[8,16,256]{2,1,0:T(8,128)S(1)}, u32[]{:S(2)}, u32[]{:S(2)}) collective-permute-start(f32[8,16,256]{2,1,0:T(8,128)S(1)} %get-tuple-element.58), channel_id=1, source_target_pairs={{0,4},{4,0},{8,12},{12,8},{24,28},{28,24},{16,20},{20,16},{17,21},... | collective-permute-start | bytes 393224 | tf_op jit(solution)/shard_map/ppermute | solution.py:347
  55.2 4.3 %collective-permute-start.12 = (f32[4,32,256]{2,1,0:T(8,128)S(1)}, f32[4,32,256]{2,1,0:T(8,128)S(1)}, u32[]{:S(2)}, u32[]{:S(2)}) collective-permute-start(f32[4,32,256]{2,1,0:T(8,128)S(1)} %get-tuple-element.64), channel_id=1, source_target_pairs={{0,4},{1,5},{2,6},{3,7},{4,0},{5,1},{6,2},{7,3},{8,12},{9,13},{10,... | collective-permute-start | bytes 393224 | tf_op jit(solution)/shard_map/ppermute | solution.py:414
  59.5 4.4 %collective-permute-start.13 = (f32[64,256]{1,0:T(8,128)S(1)}, f32[64,256]{1,0:T(8,128)S(1)}, u32[]{:S(2)}, u32[]{:S(2)}) collective-permute-start(f32[64,256]{1,0:T(8,128)S(1)} %get-tuple-element.66), channel_id=1, source_target_pairs={{0,8},{1,9},{2,10},{3,11},{4,12},{5,13},{6,14},{7,15},{8,0},{9,1},... | collective-permute-start | bytes 196616 | tf_op jit(solution)/shard_map/ppermute | solution.py:416
  61.1 4.7 %collective-permute-start.14 = (f32[64,256]{1,0:T(8,128)S(1)}, f32[64,256]{1,0:T(8,128)S(1)}, u32[]{:S(2)}, u32[]{:S(2)}) collective-permute-start(f32[64,256]{1,0:T(8,128)S(1)} %get-tuple-element.67), channel_id=1, source_target_pairs={{0,16},{1,17},{2,18},{3,19},{4,20},{5,21},{6,22},{7,23},{8,24},{9,... | collective-permute-start | bytes 196616 | tf_op jit(solution)/shard_map/ppermute | solution.py:416
  61.6 5.2 %collective-permute-start.15 = (f32[64,256]{1,0:T(8,128)S(1)}, f32[64,256]{1,0:T(8,128)S(1)}, u32[]{:S(2)}, u32[]{:S(2)}) collective-permute-start(f32[64,256]{1,0:T(8,128)S(1)} %get-tuple-element.68), channel_id=1, source_target_pairs={{0,24},{1,25},{2,26},{3,27},{4,28},{5,29},{6,30},{7,31},{8,16},{9,... | collective-permute-start | bytes 196616 | tf_op jit(solution)/shard_map/ppermute | solution.py:416

commit v5 on v4

--- a/solution.py
+++ b/solution.py
@@ -129,7 +129,8 @@
         return pltpu.make_async_copy(raw.at[:, :, z], held.at[z], arrived.at[z])
 
     def store(z):
-        return pltpu.make_async_copy(made.at[z], out.at[:, z], left.at[z])
+        rows = pl.ds(64 * z, 64 if z < planes - 1 else 64 + 2 * planes)
+        return pltpu.make_async_copy(made.at[:, rows], out.at[:, rows], left.at[z])
 
     load_numbers = pltpu.make_async_copy(index, numbers, numbered.at[0])
     for z in range(planes):
@@ -142,7 +143,8 @@
             turned = lines.T
             for device in range(8):
                 slab = slab_of(device, z)
-                made[z, device, 32 * view : 32 * view + 32, :] = turned[slab * 32 : slab * 32 + 32, :]
+                at = 66 * z + 32 * view
+                made[device, at : at + 32, :] = turned[slab * 32 : slab * 32 + 32, :]
         if z == 0:
             load_numbers.wait()
         both = jnp.zeros((8, 128), F32)
@@ -152,7 +154,7 @@
                 row = pltpu.roll(jnp.broadcast_to(row, (8, 128)), (32 * (place - z)) % 128, 1)
                 both = jnp.where((chunk == place) & (rows == view), row, both)
         for device in range(8):
-            made[z, device, 64:72, :] = both
+            made[device, 66 * z + 64 : 66 * z + 66, :] = both[0:2, :]
         store(z).start()
     for z in range(planes):
         store(z).wait()
@@ -201,15 +203,16 @@
     numbers, values = [], []
     for t in range(4):
         tile = jnp.zeros((32, 128), F32)
-        number = jnp.zeros((8, 128), F32)
+        number = jnp.zeros((1, 128), F32)
         for place in range(4):
-            source = x * 16 + 4 * t + (place - block) % 4
-            tile = jnp.where(chunk == place, slots[source, 32 * view : 32 * view + 32, :], tile)
-            number = jnp.where(chunk[0:8] == place, slots[source, 64:72, :], number)
+            device, at = 4 * x + t, 66 * ((place - block) % 4)
+            tile = jnp.where(chunk == place, slots[device, at + 32 * view : at + 32 * view + 32, :], tile)
+            row = slots[device, at + 64 + view : at + 65 + view, :]
+            number = jnp.where(chunk[0:1] == place, row, number)
         values.append(tile)
         numbers.append(number)
     value = jnp.concatenate(values, axis=1)
-    number = jnp.concatenate(numbers, axis=1)[view : view + 1, :]
+    number = jnp.concatenate(numbers, axis=1)
     hot = (line == number).astype(BF16)
     left = jnp.concatenate([*split3(value), jnp.ones((16, 512), BF16)], axis=0)
     result = dot_nt(left, hot)
@@ -356,12 +359,12 @@
     anywhere = pl.BlockSpec(memory_space=pl.ANY)
     slots = call(
         functools.partial(lines_kernel, planes),
-        shape(8, planes, 72, 128),
+        shape(8, 66 * planes, 128),
         [anywhere, anywhere],
         [
             pltpu.VMEM((planes, 2, 4, 32, 256), F32),
             pltpu.VMEM((8, 128), jnp.int32),
-            pltpu.VMEM((planes, 8, 72, 128), F32),
+            pltpu.VMEM((8, 66 * planes, 128), F32),
             pltpu.SemaphoreType.DMA((planes,)),
             pltpu.SemaphoreType.DMA((1,)),
             pltpu.SemaphoreType.DMA((planes,)),
@@ -369,8 +372,9 @@
         out_specs=anywhere,
         vmem=56,
     )(raw_lines.reshape(2, 4, planes, 32, 256), line_index.reshape(8, 128))
-    slots = slots.reshape(8 * planes, 72, 128)
+    slots = slots.reshape(8 * planes, 1, 66 * 128)
     slots = lax.all_to_all(slots, ALL, split_axis=0, concat_axis=0, tiled=True)
+    slots = slots.reshape(8, 66 * planes, 128)
     half, full = shape(8, 16, 256), shape(8, 32, 256)
 
     def work(*dims):

time: 67.9 us -> 65.8 us (0.969)
  waiting for transfers between devices: 25.3 us -> 23.3 us
    all_to_all x1, waiting for transfers between devices: 6.77 us -> 5.65 us  [slab_sweep(): slots = lax.all_to_all(slots, ALL, split_axis=0, concat_axis=0, tiled=True)]
    ppermute x6, waiting for transfers between devices: 16.3 us -> 15.4 us  [slab_sweep(): lax.ppermute(piece, ALL, pairs)]
  transfers between devices with their start and end apart: 17 -> 17, of which waited for: 9 -> 9; matrix products, arithmetic and copies ran while one was open for 0% -> 0% of each run, Pallas kernels for 10% -> 11%
where the time goes in v5:
time: 65.8 us; the launch traced here: 65.6 us
  starting transfers between devices  26.5 us (40%)
  waiting for transfers between devices  23.3 us (35%)
  Pallas kernels  15.5 us (24%)
    ppermute x6, waiting for transfers between devices, slab_sweep(): lax.ppermute(piece, ALL, pairs)  15.4 us
    all_to_all x1, starting transfers between devices, slab_sweep(): slots = lax.all_to_all(slots, ALL, split_axis=0, concat_axis=0, tiled=True)  7.3 us
    ppermute x6, starting transfers between devices, slab_sweep(): lax.ppermute(piece, ALL, pairs)  7.12 us
    ppermute x2, starting transfers between devices, exchange(): lax.ppermute(near, ALL, near_pairs)  6.78 us
    all_to_all x1, waiting for transfers between devices, slab_sweep(): slots = lax.all_to_all(slots, ALL, split_axis=0, concat_axis=0, tiled=True)  5.65 us
    pallas_call x4, Pallas kernels, matrices(): call(functools.partial(taps_kernel, view, way), (big, big, shape(64, 128,...  4.49 us
    pallas_call x1, Pallas kernels, slab_sweep(): call(middle_kernel, (full, full, half, half), [VMEM] * 14, [work(8, 96, 2...  3.47 us
    ppermute x1, starting transfers between devices, slab_sweep(): got = lax.ppermute(give, ALL, to_core)  3.27 us
  transfers between devices with their start and end apart: 17, of which 9 were waited for; matrix products, arithmetic and copies ran while one was open for 0% of the time, Pallas kernels for 11%

profile of v5, /device:TPU:0, one launch (start us, length us, event | category | flops | bytes accessed | tf_op | source)
XLA Modules:
  0.0 65.6 jit_solution(1830071994082179673)
XLA Ops:
  0.0 2.5 %shard_map.55 = f32[8,264,128]{2,1,0:T(8,128)} custom-call(f32[2,4,4,32,256]{4,3,2,1,0:T(8,128)} %bitcast.19, s32[8,128]{1,0:T(8,128)} %bitcast.20), custom_call_target="tpu_custom_call" | custom-call | bytes 1048576 | tf_op jit(solution)/shard_map/pallas_call | solution.py:360
  2.5 7.3 %all-to-all-start = ((f32[32,1,8448]{2,1,0:T(1,128)}), f32[32,1,8448]{2,1,0:T(1,128)S(1)}, u32[]{:S(2)}, u32[]{:S(2)}) async-start(f32[32,1,8448]{2,1,0:T(1,128)} %bitcast.18), calls=%async_computation | async-start | bytes 2162688 | tf_op jit(solution)/shard_map/all_to_all | solution.py:376
  9.8 0.7 %shard_map.56 = (f32[72,256]{1,0:T(8,128)S(1)}, f32[72,256]{1,0:T(8,128)S(1)}, f32[72,256]{1,0:T(8,128)S(1)}, f32[72,256]{1,0:T(8,128)S(1)}) custom-call(s32[2]{0:T(128)S(1)} %bitcast.13, f32[256,256]{1,0:T(8,128)S(1)} %bitcast.12), custom_call_target="tpu_custom_call" | custom-call | bytes 1048576 | tf_op jit(solution)/shard_map/pallas_call | solution.py:353
  10.6 1.8 %collective-permute-start = (f32[72,256]{1,0:T(8,128)S(1)}, f32[72,256]{1,0:T(8,128)S(1)}, u32[]{:S(2)}, u32[]{:S(2)}) collective-permute-start(f32[72,256]{1,0:T(8,128)S(1)} %get-tuple-element.38), channel_id=1, source_target_pairs={{0,8},{1,9},{2,10},{3,11},{4,12},{5,13},{6,14},{7,15},{8,0},{9,1},... | collective-permute-start | bytes 221192 | tf_op jit(solution)/shard_map/ppermute | solution.py:356
  12.4 1.5 %collective-permute-start.1 = (f32[72,256]{1,0:T(8,128)S(1)}, f32[72,256]{1,0:T(8,128)S(1)}, u32[]{:S(2)}, u32[]{:S(2)}) collective-permute-start(f32[72,256]{1,0:T(8,128)S(1)} %get-tuple-element.39), channel_id=1, source_target_pairs={{0,16},{1,17},{2,18},{3,19},{4,20},{5,21},{6,22},{7,23},{8,24},{9,... | collective-permute-start | bytes 221192 | tf_op jit(solution)/shard_map/ppermute | solution.py:356
  14.1 6.3 %collective-permute-done.refs_1_ = f32[72,256]{1,0:T(8,128)S(1)} collective-permute-done((f32[72,256]{1,0:T(8,128)S(1)}, f32[72,256]{1,0:T(8,128)S(1)}, u32[]{:S(2)}, u32[]{:S(2)}) %collective-permute-start) | collective-permute-done | bytes 73760 | tf_op jit(solution)/shard_map/ppermute | solution.py:356
  20.4 0.9 %collective-permute-done.1.refs_2_ = f32[72,256]{1,0:T(8,128)S(1)} collective-permute-done((f32[72,256]{1,0:T(8,128)S(1)}, f32[72,256]{1,0:T(8,128)S(1)}, u32[]{:S(2)}, u32[]{:S(2)}) %collective-permute-start.1) | collective-permute-done | bytes 73760 | tf_op jit(solution)/shard_map/ppermute | solution.py:356
  21.3 4.5 %collective-permute-done.2.refs_3_ = f32[72,256]{1,0:T(8,128)S(1)} collective-permute-done((f32[72,256]{1,0:T(8,128)S(1)}, f32[72,256]{1,0:T(8,128)S(1)}, u32[]{:S(2)}, u32[]{:S(2)}) %collective-permute-start.2) | collective-permute-done | bytes 73760 | tf_op jit(solution)/shard_map/ppermute | solution.py:356
  25.8 1.2 %collective-permute-done.6.refs_7_ = f32[72,256]{1,0:T(8,128)S(1)} collective-permute-done((f32[72,256]{1,0:T(8,128)S(1)}, f32[72,256]{1,0:T(8,128)S(1)}, u32[]{:S(2)}, u32[]{:S(2)}) %collective-permute-start.6) | collective-permute-done | bytes 73760 | tf_op jit(solution)/shard_map/ppermute | solution.py:357
  27.1 0.7 %collective-permute-start.7 = (f32[8,16,256]{2,1,0:T(8,128)S(1)}, f32[8,16,256]{2,1,0:T(8,128)S(1)}, u32[]{:S(2)}, u32[]{:S(2)}) collective-permute-start(f32[8,16,256]{2,1,0:T(8,128)S(1)} %get-tuple-element.43), channel_id=1, source_target_pairs={{4,8},{8,4},{12,24},{24,12},{28,16},{16,28},{20,17},{17,20},{21,25... | collective-permute-start | bytes 393224 | tf_op jit(solution)/shard_map/ppermute | solution.py:386
  27.8 1.2 %shard_map.58 = (bf16[9,256,256]{2,1,0:T(8,128)(2,1)S(1)}, bf16[9,256,256]{2,1,0:T(8,128)(2,1)S(1)}, bf16[64,128]{1,0:T(8,128)(2,1)S(1)}) custom-call(f32[3,2,33]{2,1,0:T(2,128)S(1)} %bitcast.14, f32[8,32,256]{2,1,0:T(8,128)S(1)} %get-tuple-element.42._.est), custom_call_target="tpu_custom_call" | custom-call | flops 1073741824 | bytes 1048576 | tf_op jit(solution)/shard_map/pallas_call | solution.py:389
  29.0 0.9 %shard_map.59.blurred = f32[256,256]{1,0:T(8,128)S(1)} custom-call(f32[8,32,256]{2,1,0:T(8,128)S(1)} %get-tuple-element.42._.est, f32[8,16,256]{2,1,0:T(8,128)S(1)} %collective-permute-done.7.far.est_far, f32[8,16,256]{2,1,0:T(8,128)S(1)} %get-tuple-element.44.near.est_near, bf16[64,128]{1,0:T(8,128)(2,1)S(1)} %get-tuple-element.45.band, ...), custom_call_target="tpu_custom_call" | custom-call | flops 1073741824 | bytes 1048576 | tf_op jit(solution)/shard_map/pallas_call | solution.py:398
  29.9 5.7 %all-to-all-done = f32[32,1,8448]{2,1,0:T(1,128)S(1)} async-done(((f32[32,1,8448]{2,1,0:T(1,128)}), f32[32,1,8448]{2,1,0:T(1,128)S(1)}, u32[]{:S(2)}, u32[]{:S(2)}) %all-to-all-start) | async-done | bytes 1081376 | tf_op jit(solution)/shard_map/all_to_all | solution.py:376
  35.6 0.9 %shard_map.60.ratio = f32[8,32,256]{2,1,0:T(8,128)S(1)} custom-call(f32[8,264,128]{2,1,0:T(8,128)S(1)} %bitcast.8, f32[8,8,256]{2,1,0:T(8,128)S(1)} %get-tuple-element.41.weights, f32[256,256]{1,0:T(8,128)S(1)} %shard_map.59.blurred), custom_call_target="tpu_custom_call" | custom-call | flops 1073741824 | bytes 1048576 | tf_op jit(solution)/shard_map/pallas_call | solution.py:401
  36.4 0.7 %collective-permute-start.8 = (f32[8,32,256]{2,1,0:T(8,128)S(1)}, f32[8,32,256]{2,1,0:T(8,128)S(1)}, u32[]{:S(2)}, u32[]{:S(2)}) collective-permute-start(f32[8,32,256]{2,1,0:T(8,128)S(1)} %shard_map.60.ratio), channel_id=1, source_target_pairs={{4,8},{8,4},{12,24},{24,12},{28,16},{16,28},{20,17},{17,20},{21,25... | collective-permute-start | bytes 786440 | tf_op jit(solution)/shard_map/ppermute | solution.py:349
  37.1 2.9 %collective-permute-start.9 = (f32[8,32,256]{2,1,0:T(8,128)S(1)}, f32[8,32,256]{2,1,0:T(8,128)S(1)}, u32[]{:S(2)}, u32[]{:S(2)}) collective-permute-start(f32[8,32,256]{2,1,0:T(8,128)S(1)} %shard_map.60.ratio), channel_id=1, source_target_pairs={{0,4},{4,0},{8,12},{12,8},{24,28},{28,24},{16,20},{20,16},{17,21},... | collective-permute-start | bytes 786440 | tf_op jit(solution)/shard_map/ppermute | solution.py:350
  40.0 0.8 %shard_map.63 = (f32[8,32,256]{2,1,0:T(8,128)S(1)}, f32[8,8,256]{2,1,0:T(8,128)S(1)}) custom-call(f32[8,264,128]{2,1,0:T(8,128)S(1)} %bitcast.9, f32[8,8,256]{2,1,0:T(8,128)S(1)} %get-tuple-element.41.weights), custom_call_target="tpu_custom_call" | custom-call | flops 1073741824 | bytes 1048576 | tf_op jit(solution)/shard_map/pallas_call | solution.py:402
  40.9 1.1 %shard_map.61 = (bf16[9,256,256]{2,1,0:T(8,128)(2,1)S(1)}, bf16[9,256,256]{2,1,0:T(8,128)(2,1)S(1)}, bf16[64,128]{1,0:T(8,128)(2,1)S(1)}) custom-call(f32[3,2,33]{2,1,0:T(2,128)S(1)} %bitcast.15, f32[8,264,128]{2,1,0:T(8,128)S(1)} %bitcast.10), custom_call_target="tpu_custom_call" | custom-call | flops 1073741824 | bytes 1048576 | tf_op jit(solution)/shard_map/pallas_call | solution.py:389
  41.9 1.2 %shard_map.62 = (bf16[9,256,256]{2,1,0:T(8,128)(2,1)S(1)}, bf16[9,256,256]{2,1,0:T(8,128)(2,1)S(1)}, bf16[64,128]{1,0:T(8,128)(2,1)S(1)}) custom-call(f32[3,2,33]{2,1,0:T(2,128)S(1)} %bitcast.16, f32[8,264,128]{2,1,0:T(8,128)S(1)} %bitcast.11), custom_call_target="tpu_custom_call" | custom-call | flops 1073741824 | bytes 1048576 | tf_op jit(solution)/shard_map/pallas_call | solution.py:389
  43.1 3.5 %shard_map.64 = (f32[8,32,256]{2,1,0:T(8,128)S(1)}, f32[8,32,256]{2,1,0:T(8,128)S(1)}, f32[8,16,256]{2,1,0:T(8,128)S(1)}, f32[8,16,256]{2,1,0:T(8,128)S(1)}) custom-call(f32[8,32,256]{2,1,0:T(8,128)S(1)} %shard_map.60.ratio, f32[8,32,256]{2,1,0:T(8,128)S(1)} %collective-permute-done.8.ratio_far, f32[8,32,256]{2,1,0:T(8,128)S(1)} %collective-permute-done.9.ratio_near, ...), custom_call_target="tpu_custom_call" | custom-call | flops 1073741824 | bytes 1048576 | tf_op jit(solution)/shard_map/pallas_call | solution.py:403
  46.6 0.7 %collective-permute-start.10 = (f32[8,16,256]{2,1,0:T(8,128)S(1)}, f32[8,16,256]{2,1,0:T(8,128)S(1)}, u32[]{:S(2)}, u32[]{:S(2)}) collective-permute-start(f32[8,16,256]{2,1,0:T(8,128)S(1)} %get-tuple-element.57), channel_id=1, source_target_pairs={{4,8},{8,4},{12,24},{24,12},{28,16},{16,28},{20,17},{17,20},{21,25... | collective-permute-start | bytes 393224 | tf_op jit(solution)/shard_map/ppermute | solution.py:349
  47.3 3.9 %collective-permute-start.11 = (f32[8,16,256]{2,1,0:T(8,128)S(1)}, f32[8,16,256]{2,1,0:T(8,128)S(1)}, u32[]{:S(2)}, u32[]{:S(2)}) collective-permute-start(f32[8,16,256]{2,1,0:T(8,128)S(1)} %get-tuple-element.58), channel_id=1, source_target_pairs={{0,4},{4,0},{8,12},{12,8},{24,28},{28,24},{16,20},{20,16},{17,21},... | collective-permute-start | bytes 393224 | tf_op jit(solution)/shard_map/ppermute | solution.py:350
  51.2 1.1 %shard_map.65 = (bf16[9,256,256]{2,1,0:T(8,128)(2,1)S(1)}, bf16[9,256,256]{2,1,0:T(8,128)(2,1)S(1)}, bf16[64,128]{1,0:T(8,128)(2,1)S(1)}) custom-call(f32[3,2,33]{2,1,0:T(2,128)S(1)} %bitcast.17, f32[8,32,256]{2,1,0:T(8,128)S(1)} %get-tuple-element.56._.ratio), custom_call_target="tpu_custom_call" | custom-call | flops 1073741824 | bytes 1048576 | tf_op jit(solution)/shard_map/pallas_call | solution.py:389
  52.3 0.9 %shard_map.66 = (f32[4,32,256]{2,1,0:T(8,128)S(1)}, f32[4,32,256]{2,1,0:T(8,128)S(1)}) custom-call(f32[8,32,256]{2,1,0:T(8,128)S(1)} %get-tuple-element.56._.ratio, f32[8,16,256]{2,1,0:T(8,128)S(1)} %collective-permute-done.10.far, f32[8,16,256]{2,1,0:T(8,128)S(1)} %collective-permute-done.11.near, bf16[64,128]{1,0:T(8,128)(2,1)S(1)} %get-tuple-element.59.band, ...), custom_call_target="tpu_custom_call" | custom-call | flops 1073741824 | bytes 1048576 | tf_op jit(solution)/shard_map/pallas_call | solution.py:411
  53.2 3.3 %collective-permute-start.12 = (f32[4,32,256]{2,1,0:T(8,128)S(1)}, f32[4,32,256]{2,1,0:T(8,128)S(1)}, u32[]{:S(2)}, u32[]{:S(2)}) collective-permute-start(f32[4,32,256]{2,1,0:T(8,128)S(1)} %get-tuple-element.64), channel_id=1, source_target_pairs={{0,4},{1,5},{2,6},{3,7},{4,0},{5,1},{6,2},{7,3},{8,12},{9,13},{10,... | collective-permute-start | bytes 393224 | tf_op jit(solution)/shard_map/ppermute | solution.py:418
  56.4 1.0 %collective-permute-done.12.got = f32[4,32,256]{2,1,0:T(8,128)S(1)} collective-permute-done((f32[4,32,256]{2,1,0:T(8,128)S(1)}, f32[4,32,256]{2,1,0:T(8,128)S(1)}, u32[]{:S(2)}, u32[]{:S(2)}) %collective-permute-start.12) | collective-permute-done | bytes 131104 | tf_op jit(solution)/shard_map/ppermute | solution.py:418
  57.4 1.5 %collective-permute-start.13 = (f32[64,256]{1,0:T(8,128)S(1)}, f32[64,256]{1,0:T(8,128)S(1)}, u32[]{:S(2)}, u32[]{:S(2)}) collective-permute-start(f32[64,256]{1,0:T(8,128)S(1)} %get-tuple-element.66), channel_id=1, source_target_pairs={{0,8},{1,9},{2,10},{3,11},{4,12},{5,13},{6,14},{7,15},{8,0},{9,1},... | collective-permute-start | bytes 196616 | tf_op jit(solution)/shard_map/ppermute | solution.py:420
  59.5 1.5 %collective-permute-start.15 = (f32[64,256]{1,0:T(8,128)S(1)}, f32[64,256]{1,0:T(8,128)S(1)}, u32[]{:S(2)}, u32[]{:S(2)}) collective-permute-start(f32[64,256]{1,0:T(8,128)S(1)} %get-tuple-element.68), channel_id=1, source_target_pairs={{0,24},{1,25},{2,26},{3,27},{4,28},{5,29},{6,30},{7,31},{8,16},{9,... | collective-permute-start | bytes 196616 | tf_op jit(solution)/shard_map/ppermute | solution.py:420
  61.0 0.9 %collective-permute-done.13.refs_1_ = f32[64,256]{1,0:T(8,128)S(1)} collective-permute-done((f32[64,256]{1,0:T(8,128)S(1)}, f32[64,256]{1,0:T(8,128)S(1)}, u32[]{:S(2)}, u32[]{:S(2)}) %collective-permute-start.13) | collective-permute-done | bytes 65568 | tf_op jit(solution)/shard_map/ppermute | solution.py:420
  61.9 1.8 %collective-permute-done.14.refs_2_ = f32[64,256]{1,0:T(8,128)S(1)} collective-permute-done((f32[64,256]{1,0:T(8,128)S(1)}, f32[64,256]{1,0:T(8,128)S(1)}, u32[]{:S(2)}, u32[]{:S(2)}) %collective-permute-start.14) | collective-permute-done | bytes 65568 | tf_op jit(solution)/shard_map/ppermute | solution.py:420
  63.6 1.1 %collective-permute-done.15.refs_3_ = f32[64,256]{1,0:T(8,128)S(1)} collective-permute-done((f32[64,256]{1,0:T(8,128)S(1)}, f32[64,256]{1,0:T(8,128)S(1)}, u32[]{:S(2)}, u32[]{:S(2)}) %collective-permute-start.15) | collective-permute-done | bytes 65568 | tf_op jit(solution)/shard_map/ppermute | solution.py:420
  64.7 0.9 %shard_map.68 = f32[256,256]{1,0:T(8,128)} custom-call(f32[64,256]{1,0:T(8,128)S(1)} %get-tuple-element.65.refs_0_, f32[64,256]{1,0:T(8,128)S(1)} %collective-permute-done.13.refs_1_, f32[64,256]{1,0:T(8,128)S(1)} %collective-permute-done.14.refs_2_, f32[64,256]{1,0:T(8,128)S(1)} %collective-permute-done.15.refs_3_), custom_call_target="tpu_custom_call" | custom-call | bytes 1048576 | tf_op jit(solution)/shard_map/pallas_call | solution.py:421
  (22 shorter events, 0.9 us)
Async XLA Ops:
  2.5 7.3 %copy-start = (f32[16,16,256]{2,1,0:T(8,128)S(1)}, f32[16,16,256]{2,1,0:T(8,128)}, u32[]{:S(2)}) copy-start(f32[16,16,256]{2,1,0:T(8,128)} %param.5) | copy-start | bytes 786436
  2.5 7.3 %copy-start.1 = (s32[2,1,1,1]{0,3,2,1:T(1,128)S(1)}, s32[2,1,1,1]{0,3,2,1:T(1,128)}, u32[]{:S(2)}) copy-start(s32[2,1,1,1]{0,3,2,1:T(1,128)} %param.9) | copy-start | bytes 28
  2.5 25.3 %copy-start.2 = (f32[2,3,33]{2,0,1:T(2,128)S(1)}, f32[2,3,33]{2,0,1:T(2,128)}, u32[]{:S(2)}) copy-start(f32[2,3,33]{2,0,1:T(2,128)} %param.8) | copy-start | bytes 2380
  2.5 33.0 %all-to-all-start = ((f32[32,1,8448]{2,1,0:T(1,128)}), f32[32,1,8448]{2,1,0:T(1,128)S(1)}, u32[]{:S(2)}, u32[]{:S(2)}) async-start(f32[32,1,8448]{2,1,0:T(1,128)} %bitcast.18), calls=%async_computation | async-start | bytes 2162688 | tf_op jit(solution)/shard_map/all_to_all | solution.py:376
  10.6 9.9 %collective-permute-start = (f32[72,256]{1,0:T(8,128)S(1)}, f32[72,256]{1,0:T(8,128)S(1)}, u32[]{:S(2)}, u32[]{:S(2)}) collective-permute-start(f32[72,256]{1,0:T(8,128)S(1)} %get-tuple-element.38), channel_id=1, source_target_pairs={{0,8},{1,9},{2,10},{3,11},{4,12},{5,13},{6,14},{7,15},{8,0},{9,1},... | collective-permute-start | bytes 221192 | tf_op jit(solution)/shard_map/ppermute | solution.py:356
  12.4 8.9 %collective-permute-start.1 = (f32[72,256]{1,0:T(8,128)S(1)}, f32[72,256]{1,0:T(8,128)S(1)}, u32[]{:S(2)}, u32[]{:S(2)}) collective-permute-start(f32[72,256]{1,0:T(8,128)S(1)} %get-tuple-element.39), channel_id=1, source_target_pairs={{0,16},{1,17},{2,18},{3,19},{4,20},{5,21},{6,22},{7,23},{8,24},{9,... | collective-permute-start | bytes 221192 | tf_op jit(solution)/shard_map/ppermute | solution.py:356
  13.9 12.0 %collective-permute-start.2 = (f32[72,256]{1,0:T(8,128)S(1)}, f32[72,256]{1,0:T(8,128)S(1)}, u32[]{:S(2)}, u32[]{:S(2)}) collective-permute-start(f32[72,256]{1,0:T(8,128)S(1)} %get-tuple-element.40), channel_id=1, source_target_pairs={{0,24},{1,25},{2,26},{3,27},{4,28},{5,29},{6,30},{7,31},{8,16},{9,... | collective-permute-start | bytes 221192 | tf_op jit(solution)/shard_map/ppermute | solution.py:356
  14.1 11.7 %collective-permute-start.3 = (f32[72,256]{1,0:T(8,128)S(1)}, f32[72,256]{1,0:T(8,128)S(1)}, u32[]{:S(2)}, u32[]{:S(2)}) collective-permute-start(f32[72,256]{1,0:T(8,128)S(1)} %get-tuple-element.37.refs_0_), channel_id=1, source_target_pairs={{0,4},{1,5},{2,6},{3,7},{4,0},{5,1},{6,2},{7,3},{8,12},{9,13},{10,... | collective-permute-start | bytes 221192 | tf_op jit(solution)/shard_map/ppermute | solution.py:357
  20.4 5.4 %collective-permute-start.4 = (f32[72,256]{1,0:T(8,128)S(1)}, f32[72,256]{1,0:T(8,128)S(1)}, u32[]{:S(2)}, u32[]{:S(2)}) collective-permute-start(f32[72,256]{1,0:T(8,128)S(1)} %collective-permute-done.refs_1_), channel_id=1, source_target_pairs={{0,4},{1,5},{2,6},{3,7},{4,0},{5,1},{6,2},{7,3},{8,12},{9,13},{10,... | collective-permute-start | bytes 221192 | tf_op jit(solution)/shard_map/ppermute | solution.py:357
  21.3 4.5 %collective-permute-start.5 = (f32[72,256]{1,0:T(8,128)S(1)}, f32[72,256]{1,0:T(8,128)S(1)}, u32[]{:S(2)}, u32[]{:S(2)}) collective-permute-start(f32[72,256]{1,0:T(8,128)S(1)} %collective-permute-done.1.refs_2_), channel_id=1, source_target_pairs={{0,4},{1,5},{2,6},{3,7},{4,0},{5,1},{6,2},{7,3},{8,12},{9,13},{10,... | collective-permute-start | bytes 221192 | tf_op jit(solution)/shard_map/ppermute | solution.py:357
  25.8 1.3 %collective-permute-start.6 = (f32[72,256]{1,0:T(8,128)S(1)}, f32[72,256]{1,0:T(8,128)S(1)}, u32[]{:S(2)}, u32[]{:S(2)}) collective-permute-start(f32[72,256]{1,0:T(8,128)S(1)} %collective-permute-done.2.refs_3_), channel_id=1, source_target_pairs={{0,4},{1,5},{2,6},{3,7},{4,0},{5,1},{6,2},{7,3},{8,12},{9,13},{10,... | collective-permute-start | bytes 221192 | tf_op jit(solution)/shard_map/ppermute | solution.py:357
  27.1 1.9 %collective-permute-start.7 = (f32[8,16,256]{2,1,0:T(8,128)S(1)}, f32[8,16,256]{2,1,0:T(8,128)S(1)}, u32[]{:S(2)}, u32[]{:S(2)}) collective-permute-start(f32[8,16,256]{2,1,0:T(8,128)S(1)} %get-tuple-element.43), channel_id=1, source_target_pairs={{4,8},{8,4},{12,24},{24,12},{28,16},{16,28},{20,17},{17,20},{21,25... | collective-permute-start | bytes 393224 | tf_op jit(solution)/shard_map/ppermute | solution.py:386
  36.4 6.7 %collective-permute-start.8 = (f32[8,32,256]{2,1,0:T(8,128)S(1)}, f32[8,32,256]{2,1,0:T(8,128)S(1)}, u32[]{:S(2)}, u32[]{:S(2)}) collective-permute-start(f32[8,32,256]{2,1,0:T(8,128)S(1)} %shard_map.60.ratio), channel_id=1, source_target_pairs={{4,8},{8,4},{12,24},{24,12},{28,16},{16,28},{20,17},{17,20},{21,25... | collective-permute-start | bytes 786440 | tf_op jit(solution)/shard_map/ppermute | solution.py:349
  37.1 6.0 %collective-permute-start.9 = (f32[8,32,256]{2,1,0:T(8,128)S(1)}, f32[8,32,256]{2,1,0:T(8,128)S(1)}, u32[]{:S(2)}, u32[]{:S(2)}) collective-permute-start(f32[8,32,256]{2,1,0:T(8,128)S(1)} %shard_map.60.ratio), channel_id=1, source_target_pairs={{0,4},{4,0},{8,12},{12,8},{24,28},{28,24},{16,20},{20,16},{17,21},... | collective-permute-start | bytes 786440 | tf_op jit(solution)/shard_map/ppermute | solution.py:350
  46.6 5.6 %collective-permute-start.10 = (f32[8,16,256]{2,1,0:T(8,128)S(1)}, f32[8,16,256]{2,1,0:T(8,128)S(1)}, u32[]{:S(2)}, u32[]{:S(2)}) collective-permute-start(f32[8,16,256]{2,1,0:T(8,128)S(1)} %get-tuple-element.57), channel_id=1, source_target_pairs={{4,8},{8,4},{12,24},{24,12},{28,16},{16,28},{20,17},{17,20},{21,25... | collective-permute-start | bytes 393224 | tf_op jit(solution)/shard_map/ppermute | solution.py:349
  47.3 5.0 %collective-permute-start.11 = (f32[8,16,256]{2,1,0:T(8,128)S(1)}, f32[8,16,256]{2,1,0:T(8,128)S(1)}, u32[]{:S(2)}, u32[]{:S(2)}) collective-permute-start(f32[8,16,256]{2,1,0:T(8,128)S(1)} %get-tuple-element.58), channel_id=1, source_target_pairs={{0,4},{4,0},{8,12},{12,8},{24,28},{28,24},{16,20},{20,16},{17,21},... | collective-permute-start | bytes 393224 | tf_op jit(solution)/shard_map/ppermute | solution.py:350
  53.2 4.3 %collective-permute-start.12 = (f32[4,32,256]{2,1,0:T(8,128)S(1)}, f32[4,32,256]{2,1,0:T(8,128)S(1)}, u32[]{:S(2)}, u32[]{:S(2)}) collective-permute-start(f32[4,32,256]{2,1,0:T(8,128)S(1)} %get-tuple-element.64), channel_id=1, source_target_pairs={{0,4},{1,5},{2,6},{3,7},{4,0},{5,1},{6,2},{7,3},{8,12},{9,13},{10,... | collective-permute-start | bytes 393224 | tf_op jit(solution)/shard_map/ppermute | solution.py:418
  57.4 4.4 %collective-permute-start.13 = (f32[64,256]{1,0:T(8,128)S(1)}, f32[64,256]{1,0:T(8,128)S(1)}, u32[]{:S(2)}, u32[]{:S(2)}) collective-permute-start(f32[64,256]{1,0:T(8,128)S(1)} %get-tuple-element.66), channel_id=1, source_target_pairs={{0,8},{1,9},{2,10},{3,11},{4,12},{5,13},{6,14},{7,15},{8,0},{9,1},... | collective-permute-start | bytes 196616 | tf_op jit(solution)/shard_map/ppermute | solution.py:420
  59.0 4.6 %collective-permute-start.14 = (f32[64,256]{1,0:T(8,128)S(1)}, f32[64,256]{1,0:T(8,128)S(1)}, u32[]{:S(2)}, u32[]{:S(2)}) collective-permute-start(f32[64,256]{1,0:T(8,128)S(1)} %get-tuple-element.67), channel_id=1, source_target_pairs={{0,16},{1,17},{2,18},{3,19},{4,20},{5,21},{6,22},{7,23},{8,24},{9,... | collective-permute-start | bytes 196616 | tf_op jit(solution)/shard_map/ppermute | solution.py:420
  59.5 5.2 %collective-permute-start.15 = (f32[64,256]{1,0:T(8,128)S(1)}, f32[64,256]{1,0:T(8,128)S(1)}, u32[]{:S(2)}, u32[]{:S(2)}) collective-permute-start(f32[64,256]{1,0:T(8,128)S(1)} %get-tuple-element.68), channel_id=1, source_target_pairs={{0,24},{1,25},{2,26},{3,27},{4,28},{5,29},{6,30},{7,31},{8,16},{9,... | collective-permute-start | bytes 196616 | tf_op jit(solution)/shard_map/ppermute | solution.py:420

commit v6 on v5

--- a/solution.py
+++ b/solution.py
@@ -179,16 +179,17 @@
     high, low = (part.astype(F32) for part in split2(toeplitz(along_z[2:3, :], 32)))
     band[0:32, :] = (high + pltpu.roll(high, 64, 1)).astype(BF16)
     band[32:64, :] = low.astype(BF16)
-    tall_x = jnp.broadcast_to(toeplitz(along_xy[0:1, :], 16)[:, None, :], (16, 16, 128)).reshape(256, 128)
-    tall_y = jnp.broadcast_to(toeplitz(along_xy[1:2, :], 16)[None], (16, 16, 128)).reshape(256, 128)
+    small_x, small_y = split3(toeplitz(along_xy[0:1, :], 16)), split3(toeplitz(along_xy[1:2, :], 16))
     from_row = lax.broadcasted_iota(jnp.int32, (128, 256), 0)
     to_lane = lax.broadcasted_iota(jnp.int32, (128, 256), 1)
     wide_x, wide_y = [], []
     for offset in range(3):
         pick_x = (from_row == to_lane // 16 + 16 * offset).astype(BF16)
         pick_y = (from_row == lax.rem(to_lane, 16) + 16 * offset).astype(BF16)
-        wide_x.append(sum(dot_nn(piece, pick_x) for piece in split3(tall_x)))
-        wide_y.append(sum(dot_nn(piece, pick_y) for piece in split3(tall_y)))
+        rows_x = sum(dot_nn(piece, pick_x) for piece in small_x)
+        rows_y = sum(dot_nn(piece, pick_y) for piece in small_y)
+        wide_x.append(jnp.broadcast_to(rows_x[:, None, :], (16, 16, 256)).reshape(256, 256))
+        wide_y.append(jnp.broadcast_to(rows_y[None], (16, 16, 256)).reshape(256, 256))
     for dx in range(3):
         for dy in range(3):
             high, low = split2(wide_x[dx] * wide_y[dy])
@@ -232,11 +233,17 @@
     near[...] = value[:, pl.ds(pl.multiple_of(16 - 16 * upper, 16), 16), :]
 
 
+def at_end(planes):
+    x, y, _, z = coordinates()
+    slab = 2 * place_on_ring(x, y, z) + upper_half()
+    return ((z == 0) & (slab == 0)) | ((z == planes - 1) & (slab == 7))
+
+
 def widened(wide, value, far, near, margin):
     rows, upper = value.shape[1], upper_half()
     wide[:, margin : margin + rows, :] = value[...]
     side = margin + rows
-    wide[:, pl.ds(pl.multiple_of(side * upper, 16), margin), :] = far[...]
+    wide[:, pl.ds(pl.multiple_of(side * upper, 16), margin), :] = far
     wide[:, pl.ds(pl.multiple_of(side - side * upper, 16), margin), :] = near[...]
 
 
@@ -272,7 +279,7 @@
 
 
 def blur_kernel(est, far, near, band, big_high, big_low, blurred, wide, flat):
-    widened(wide, est, far, near, 16)
+    widened(wide, est, far[...], near, 16)
     blurred_into(wide, band, big_high, big_low, flat, blurred)
 
 
@@ -288,31 +295,29 @@
         ratio[column] = 1.0 + cover * (data / blurred[column * 32 : column * 32 + 32, :] - 1.0)
 
 
-def middle_kernel(
-    ratio, ratio_far, ratio_near, est, est_far, est_near, band0, high0, low0, band1, high1, low1,
-    data, cover, new, next_ratio, far, near, wide, tall, flat, total, short,
-):
-    widened(wide, ratio, ratio_far, ratio_near, 32)
-    widened(tall, est, est_far, est_near, 16)
-    blurred_into(wide, band0, high0, low0, flat, total)
+def update_kernel(planes, ratio, ratio_far, ratio_near, est, est_far, est_near, band, high, low, new, wide, flat, total):
+    widened(wide, ratio, jnp.where(at_end(planes), 0.0, ratio_far[...]), ratio_near, 32)
+    widened(new, est, est_far[...], est_near, 16)
+    blurred_into(wide, band, high, low, flat, total)
     for column in range(8):
-        tall[column] = tall[column] * total[column * 64 : column * 64 + 64, :]
-    new[...] = tall[:, 16:48, :]
-    out = total.at[0:256, :]
-    blurred_into(tall, band1, high1, low1, short, out)
-    ratio_from(next_ratio, data, cover, out)
-    payloads(next_ratio, far, near)
+        new[column] = new[column] * total[column * 64 : column * 64 + 64, :]
+
+
+def ratio_kernel(est, band, high, low, data, cover, ratio, far, near, flat, total):
+    blurred_into(est, band, high, low, flat, total)
+    ratio_from(ratio, data, cover, total)
+    payloads(ratio, far, near)
 
 
 def last_kernel(ratio, far, near, band, big_high, big_low, est, keep, give, wide, flat, total):
-    widened(wide, ratio, far, near, 16)
+    widened(wide, ratio, far[...], near, 16)
     blurred_into(wide, band, big_high, big_low, flat, total)
     _, _, core, _ = coordinates()
     for flip, x, y, _ in chips():
         for turn, out in enumerate((keep, give)):
             column = 4 * x + 2 * y + (core if turn == 0 else 1 - core)
             start = pl.multiple_of(column * 32, 32)
-            out[flip] = est[column] * total[pl.ds(start, 32), :]
+            out[flip] = est[column, 16:48, :] * total[pl.ds(start, 32), :]
 
 
 def merge_kernel(keep, got, *pieces):
@@ -343,6 +348,8 @@
 def slab_sweep(planes, estimate, raw_lines, line_index, psf, view_weight):
     far_pairs, near_pairs = chain_pairs(planes)
     to_chips, to_core = swaps(planes)
+    ends = sorted(set(range(8 * planes)) - {source for source, _ in far_pairs})
+    ring_pairs = far_pairs + [tuple(ends), tuple(ends[::-1])]
 
     def exchange(far, near):
         return (
@@ -400,13 +407,16 @@
     )(est, est_far, est_near, *matrices(0, 0, est))
     ratio = call(scatter_ratio_kernel, full, [VMEM] * 3, flops=1 << 30)(slots, weights, blurred)
     data, cover = call(scatter_kernel, (full, shape(8, 8, 256)), [VMEM] * 2, flops=1 << 30)(slots, weights)
-    est, ratio, far, near = call(
-        middle_kernel,
-        (full, full, half, half),
-        [VMEM] * 14,
-        [work(8, 96, 256), work(8, 64, 256), work(512, 256), work(512, 256), work(256, 256)],
+    est = call(
+        functools.partial(update_kernel, planes),
+        shape(8, 64, 256),
+        [VMEM] * 9,
+        [work(8, 96, 256), work(512, 256), work(512, 256)],
         flops=1 << 30,
-    )(ratio, *exchange(ratio, ratio), est, est_far, est_near, *matrices(0, 1, slots), *matrices(1, 0, slots), data, cover)
+    )(ratio, lax.ppermute(ratio, ALL, ring_pairs), lax.ppermute(ratio, ALL, near_pairs), est, est_far, est_near, *matrices(0, 1, slots))
+    ratio, far, near = call(
+        ratio_kernel, (full, half, half), [VMEM] * 6, [work(256, 256), work(256, 256)], flops=1 << 30
+    )(est, *matrices(1, 0, slots), data, cover)
     quarter = shape(4, 32, 256)
     keep, give = call(
         last_kernel,

time: 65.8 us -> 63.4 us (0.964)
  starting transfers between devices: 26.5 us -> 22.4 us
  waiting for transfers between devices: 23.3 us -> 26.9 us
  Pallas kernels: 15.5 us -> 13.5 us
    ppermute x2 -> x1, starting transfers between devices: 6.78 us -> 1.31 us  [exchange(): lax.ppermute(near, ALL, near_pairs)]
    ppermute x0 -> x2, waiting for transfers between devices: none -> 3.21 us  [the longest x1 3.21 us: slab_sweep(): lax.ppermute(ratio, ALL, ring_pairs)]
    ppermute x0 -> x2, starting transfers between devices: none -> 1.94 us  [the longest x1 1.94 us: slab_sweep(): lax.ppermute(ratio, ALL, ring_pairs)]
    pallas_call x1 -> x2, Pallas kernels: 3.47 us -> 2.41 us  [the longest x1 1.52 us: slab_sweep(): call(functools.partial(update_kernel, planes), shape(8, 64, 256), [VMEM]...]
    pallas_call x4, Pallas kernels: 4.49 us -> 3.48 us  [matrices(): call(functools.partial(taps_kernel, view, way), (big, big, shape(64, 128,...]
    ppermute x2 -> x1, starting transfers between devices: 1.35 us -> 0.67 us  [exchange(): lax.ppermute(far, ALL, far_pairs)]
  transfers between devices with their start and end apart: 17 -> 17, of which waited for: 9 -> 11; matrix products, arithmetic and copies ran while one was open for 0% -> 0% of each run, Pallas kernels for 11% -> 9%
where the time goes in v6:
time: 63.4 us; the launch traced here: 62.9 us
  waiting for transfers between devices  26.9 us (42%)
  starting transfers between devices  22.4 us (35%)
  Pallas kernels  13.5 us (21%)
    ppermute x6, waiting for transfers between devices, slab_sweep(): lax.ppermute(piece, ALL, pairs)  15.3 us
    all_to_all x1, starting transfers between devices, slab_sweep(): slots = lax.all_to_all(slots, ALL, split_axis=0, concat_axis=0, tiled=True)  7.3 us
    ppermute x6, starting transfers between devices, slab_sweep(): lax.ppermute(piece, ALL, pairs)  7.12 us
    all_to_all x1, waiting for transfers between devices, slab_sweep(): slots = lax.all_to_all(slots, ALL, split_axis=0, concat_axis=0, tiled=True)  5.91 us
    pallas_call x4, Pallas kernels, matrices(): call(functools.partial(taps_kernel, view, way), (big, big, shape(64, 128,...  3.48 us
    ppermute x1, starting transfers between devices, slab_sweep(): got = lax.ppermute(give, ALL, to_core)  3.38 us
    ppermute x1, waiting for transfers between devices, slab_sweep(): lax.ppermute(ratio, ALL, ring_pairs)  3.21 us
    pallas_call x1, Pallas kernels, slab_sweep(): call(functools.partial(lines_kernel, planes), shape(8, 66 * planes, 128),...  2.46 us
  transfers between devices with their start and end apart: 17, of which 11 were waited for; matrix products, arithmetic and copies ran while one was open for 0% of the time, Pallas kernels for 9%

profile of v6, /device:TPU:0, one launch (start us, length us, event | category | flops | bytes accessed | tf_op | source)
XLA Modules:
  0.0 62.9 jit_solution(4680410204175113133)
XLA Ops:
  0.0 2.5 %shard_map.55 = f32[8,264,128]{2,1,0:T(8,128)} custom-call(f32[2,4,4,32,256]{4,3,2,1,0:T(8,128)} %bitcast.19, s32[8,128]{1,0:T(8,128)} %bitcast.20), custom_call_target="tpu_custom_call" | custom-call | bytes 1048576 | tf_op jit(solution)/shard_map/pallas_call | solution.py:367
  2.5 7.3 %all-to-all-start = ((f32[32,1,8448]{2,1,0:T(1,128)}), f32[32,1,8448]{2,1,0:T(1,128)S(1)}, u32[]{:S(2)}, u32[]{:S(2)}) async-start(f32[32,1,8448]{2,1,0:T(1,128)} %bitcast.18), calls=%async_computation | async-start | bytes 2162688 | tf_op jit(solution)/shard_map/all_to_all | solution.py:383
  9.8 0.7 %shard_map.56 = (f32[72,256]{1,0:T(8,128)S(1)}, f32[72,256]{1,0:T(8,128)S(1)}, f32[72,256]{1,0:T(8,128)S(1)}, f32[72,256]{1,0:T(8,128)S(1)}) custom-call(s32[2]{0:T(128)S(1)} %bitcast.13, f32[256,256]{1,0:T(8,128)S(1)} %bitcast.12), custom_call_target="tpu_custom_call" | custom-call | bytes 1048576 | tf_op jit(solution)/shard_map/pallas_call | solution.py:360
  10.6 1.8 %collective-permute-start = (f32[72,256]{1,0:T(8,128)S(1)}, f32[72,256]{1,0:T(8,128)S(1)}, u32[]{:S(2)}, u32[]{:S(2)}) collective-permute-start(f32[72,256]{1,0:T(8,128)S(1)} %get-tuple-element.37), channel_id=1, source_target_pairs={{0,8},{1,9},{2,10},{3,11},{4,12},{5,13},{6,14},{7,15},{8,0},{9,1},... | collective-permute-start | bytes 221192 | tf_op jit(solution)/shard_map/ppermute | solution.py:363
  12.4 1.5 %collective-permute-start.1 = (f32[72,256]{1,0:T(8,128)S(1)}, f32[72,256]{1,0:T(8,128)S(1)}, u32[]{:S(2)}, u32[]{:S(2)}) collective-permute-start(f32[72,256]{1,0:T(8,128)S(1)} %get-tuple-element.38), channel_id=1, source_target_pairs={{0,16},{1,17},{2,18},{3,19},{4,20},{5,21},{6,22},{7,23},{8,24},{9,... | collective-permute-start | bytes 221192 | tf_op jit(solution)/shard_map/ppermute | solution.py:363
  14.1 6.3 %collective-permute-done.refs_1_ = f32[72,256]{1,0:T(8,128)S(1)} collective-permute-done((f32[72,256]{1,0:T(8,128)S(1)}, f32[72,256]{1,0:T(8,128)S(1)}, u32[]{:S(2)}, u32[]{:S(2)}) %collective-permute-start) | collective-permute-done | bytes 73760 | tf_op jit(solution)/shard_map/ppermute | solution.py:363
  20.4 0.9 %collective-permute-done.1.refs_2_ = f32[72,256]{1,0:T(8,128)S(1)} collective-permute-done((f32[72,256]{1,0:T(8,128)S(1)}, f32[72,256]{1,0:T(8,128)S(1)}, u32[]{:S(2)}, u32[]{:S(2)}) %collective-permute-start.1) | collective-permute-done | bytes 73760 | tf_op jit(solution)/shard_map/ppermute | solution.py:363
  21.3 4.5 %collective-permute-done.2.refs_3_ = f32[72,256]{1,0:T(8,128)S(1)} collective-permute-done((f32[72,256]{1,0:T(8,128)S(1)}, f32[72,256]{1,0:T(8,128)S(1)}, u32[]{:S(2)}, u32[]{:S(2)}) %collective-permute-start.2) | collective-permute-done | bytes 73760 | tf_op jit(solution)/shard_map/ppermute | solution.py:363
  25.8 1.2 %collective-permute-done.6.refs_7_ = f32[72,256]{1,0:T(8,128)S(1)} collective-permute-done((f32[72,256]{1,0:T(8,128)S(1)}, f32[72,256]{1,0:T(8,128)S(1)}, u32[]{:S(2)}, u32[]{:S(2)}) %collective-permute-start.6) | collective-permute-done | bytes 73760 | tf_op jit(solution)/shard_map/ppermute | solution.py:364
  27.1 0.7 %collective-permute-start.7 = (f32[8,16,256]{2,1,0:T(8,128)S(1)}, f32[8,16,256]{2,1,0:T(8,128)S(1)}, u32[]{:S(2)}, u32[]{:S(2)}) collective-permute-start(f32[8,16,256]{2,1,0:T(8,128)S(1)} %get-tuple-element.42), channel_id=1, source_target_pairs={{4,8},{8,4},{12,24},{24,12},{28,16},{16,28},{20,17},{17,20},{21,25... | collective-permute-start | bytes 393224 | tf_op jit(solution)/shard_map/ppermute | solution.py:393
  27.8 0.9 %shard_map.58 = (bf16[9,256,256]{2,1,0:T(8,128)(2,1)S(1)}, bf16[9,256,256]{2,1,0:T(8,128)(2,1)S(1)}, bf16[64,128]{1,0:T(8,128)(2,1)S(1)}) custom-call(f32[3,2,33]{2,1,0:T(2,128)S(1)} %bitcast.14, f32[8,32,256]{2,1,0:T(8,128)S(1)} %get-tuple-element.41._.est), custom_call_target="tpu_custom_call" | custom-call | flops 1073741824 | bytes 1048576 | tf_op jit(solution)/shard_map/pallas_call | solution.py:396
  28.8 0.9 %shard_map.59.blurred = f32[256,256]{1,0:T(8,128)S(1)} custom-call(f32[8,32,256]{2,1,0:T(8,128)S(1)} %get-tuple-element.41._.est, f32[8,16,256]{2,1,0:T(8,128)S(1)} %collective-permute-done.7.far.est_far, f32[8,16,256]{2,1,0:T(8,128)S(1)} %get-tuple-element.43.near.est_near, bf16[64,128]{1,0:T(8,128)(2,1)S(1)} %get-tuple-element.44.band, ...), custom_call_target="tpu_custom_call" | custom-call | flops 1073741824 | bytes 1048576 | tf_op jit(solution)/shard_map/pallas_call | solution.py:405
  29.6 5.9 %all-to-all-done = f32[32,1,8448]{2,1,0:T(1,128)S(1)} async-done(((f32[32,1,8448]{2,1,0:T(1,128)}), f32[32,1,8448]{2,1,0:T(1,128)S(1)}, u32[]{:S(2)}, u32[]{:S(2)}) %all-to-all-start) | async-done | bytes 1081376 | tf_op jit(solution)/shard_map/all_to_all | solution.py:383
  35.6 0.9 %shard_map.60.ratio = f32[8,32,256]{2,1,0:T(8,128)S(1)} custom-call(f32[8,264,128]{2,1,0:T(8,128)S(1)} %bitcast.8, f32[8,8,256]{2,1,0:T(8,128)S(1)} %get-tuple-element.40.weights, f32[256,256]{1,0:T(8,128)S(1)} %shard_map.59.blurred), custom_call_target="tpu_custom_call" | custom-call | flops 1073741824 | bytes 1048576 | tf_op jit(solution)/shard_map/pallas_call | solution.py:408
  36.4 1.9 %collective-permute-start.8 = (f32[8,32,256]{2,1,0:T(8,128)S(1)}, f32[8,32,256]{2,1,0:T(8,128)S(1)}, u32[]{:S(2)}, u32[]{:S(2)}) collective-permute-start(f32[8,32,256]{2,1,0:T(8,128)S(1)} %shard_map.60.ratio), channel_id=1, source_target_pairs={{4,8},{8,4},{12,24},{24,12},{28,16},{16,28},{20,17},{17,20},{21,25... | collective-permute-start | bytes 786440 | tf_op jit(solution)/shard_map/ppermute | solution.py:416
  38.4 0.8 %shard_map.61 = (bf16[9,256,256]{2,1,0:T(8,128)(2,1)S(1)}, bf16[9,256,256]{2,1,0:T(8,128)(2,1)S(1)}, bf16[64,128]{1,0:T(8,128)(2,1)S(1)}) custom-call(f32[3,2,33]{2,1,0:T(2,128)S(1)} %bitcast.15, f32[8,264,128]{2,1,0:T(8,128)S(1)} %bitcast.9), custom_call_target="tpu_custom_call" | custom-call | flops 1073741824 | bytes 1048576 | tf_op jit(solution)/shard_map/pallas_call | solution.py:396
  39.2 0.8 %shard_map.64 = (f32[8,32,256]{2,1,0:T(8,128)S(1)}, f32[8,8,256]{2,1,0:T(8,128)S(1)}) custom-call(f32[8,264,128]{2,1,0:T(8,128)S(1)} %bitcast.10, f32[8,8,256]{2,1,0:T(8,128)S(1)} %get-tuple-element.40.weights), custom_call_target="tpu_custom_call" | custom-call | flops 1073741824 | bytes 1048576 | tf_op jit(solution)/shard_map/pallas_call | solution.py:409
  40.0 0.9 %shard_map.63 = (bf16[9,256,256]{2,1,0:T(8,128)(2,1)S(1)}, bf16[9,256,256]{2,1,0:T(8,128)(2,1)S(1)}, bf16[64,128]{1,0:T(8,128)(2,1)S(1)}) custom-call(f32[3,2,33]{2,1,0:T(2,128)S(1)} %bitcast.16, f32[8,264,128]{2,1,0:T(8,128)S(1)} %bitcast.11), custom_call_target="tpu_custom_call" | custom-call | flops 1073741824 | bytes 1048576 | tf_op jit(solution)/shard_map/pallas_call | solution.py:396
  41.0 3.2 %collective-permute-done.8.ratio_far = f32[8,32,256]{2,1,0:T(8,128)S(1)} collective-permute-done((f32[8,32,256]{2,1,0:T(8,128)S(1)}, f32[8,32,256]{2,1,0:T(8,128)S(1)}, u32[]{:S(2)}, u32[]{:S(2)}) %collective-permute-start.8) | collective-permute-done | bytes 262176 | tf_op jit(solution)/shard_map/ppermute | solution.py:416
  44.2 1.5 %shard_map.62.est = f32[8,64,256]{2,1,0:T(8,128)S(1)} custom-call(f32[8,32,256]{2,1,0:T(8,128)S(1)} %shard_map.60.ratio, f32[8,32,256]{2,1,0:T(8,128)S(1)} %collective-permute-done.8.ratio_far, f32[8,32,256]{2,1,0:T(8,128)S(1)} %collective-permute-done.9.ratio_near, f32[8,32,256]{2,1,0:T(8,128)S(1)} %get-tuple-element.41._.est, ...), custom_call_target="tpu_custom_call" | custom-call | flops 1073741824 | bytes 1048576 | tf_op jit(solution)/shard_map/pallas_call | solution.py:410
  45.7 0.9 %shard_map.65 = (f32[8,32,256]{2,1,0:T(8,128)S(1)}, f32[8,16,256]{2,1,0:T(8,128)S(1)}, f32[8,16,256]{2,1,0:T(8,128)S(1)}) custom-call(f32[8,64,256]{2,1,0:T(8,128)S(1)} %shard_map.62.est, bf16[64,128]{1,0:T(8,128)(2,1)S(1)} %get-tuple-element.50.band, bf16[9,256,256]{2,1,0:T(8,128)(2,1)S(1)} %get-tuple-element.51.high, ...), custom_call_target="tpu_custom_call" | custom-call | flops 1073741824 | bytes 1048576 | tf_op jit(solution)/shard_map/pallas_call | solution.py:417
  47.3 1.3 %collective-permute-start.11 = (f32[8,16,256]{2,1,0:T(8,128)S(1)}, f32[8,16,256]{2,1,0:T(8,128)S(1)}, u32[]{:S(2)}, u32[]{:S(2)}) collective-permute-start(f32[8,16,256]{2,1,0:T(8,128)S(1)} %get-tuple-element.57), channel_id=1, source_target_pairs={{0,4},{4,0},{8,12},{12,8},{24,28},{28,24},{16,20},{20,16},{17,21},... | collective-permute-start | bytes 393224 | tf_op jit(solution)/shard_map/ppermute | solution.py:357
  48.6 0.8 %shard_map.66 = (bf16[9,256,256]{2,1,0:T(8,128)(2,1)S(1)}, bf16[9,256,256]{2,1,0:T(8,128)(2,1)S(1)}, bf16[64,128]{1,0:T(8,128)(2,1)S(1)}) custom-call(f32[3,2,33]{2,1,0:T(2,128)S(1)} %bitcast.17, f32[8,32,256]{2,1,0:T(8,128)S(1)} %get-tuple-element.55._.ratio), custom_call_target="tpu_custom_call" | custom-call | flops 1073741824 | bytes 1048576 | tf_op jit(solution)/shard_map/pallas_call | solution.py:396
  49.6 0.9 %shard_map.67 = (f32[4,32,256]{2,1,0:T(8,128)S(1)}, f32[4,32,256]{2,1,0:T(8,128)S(1)}) custom-call(f32[8,32,256]{2,1,0:T(8,128)S(1)} %get-tuple-element.55._.ratio, f32[8,16,256]{2,1,0:T(8,128)S(1)} %collective-permute-done.10.far, f32[8,16,256]{2,1,0:T(8,128)S(1)} %collective-permute-done.11.near, bf16[64,128]{1,0:T(8,128)(2,1)S(1)} %get-tuple-element.58.band, ...), custom_call_target="tpu_custom_call" | custom-call | flops 1073741824 | bytes 1048576 | tf_op jit(solution)/shard_map/pallas_call | solution.py:421
  50.5 3.4 %collective-permute-start.12 = (f32[4,32,256]{2,1,0:T(8,128)S(1)}, f32[4,32,256]{2,1,0:T(8,128)S(1)}, u32[]{:S(2)}, u32[]{:S(2)}) collective-permute-start(f32[4,32,256]{2,1,0:T(8,128)S(1)} %get-tuple-element.62), channel_id=1, source_target_pairs={{0,4},{1,5},{2,6},{3,7},{4,0},{5,1},{6,2},{7,3},{8,12},{9,13},{10,... | collective-permute-start | bytes 393224 | tf_op jit(solution)/shard_map/ppermute | solution.py:428
  53.9 1.0 %collective-permute-done.12.got = f32[4,32,256]{2,1,0:T(8,128)S(1)} collective-permute-done((f32[4,32,256]{2,1,0:T(8,128)S(1)}, f32[4,32,256]{2,1,0:T(8,128)S(1)}, u32[]{:S(2)}, u32[]{:S(2)}) %collective-permute-start.12) | collective-permute-done | bytes 131104 | tf_op jit(solution)/shard_map/ppermute | solution.py:428
  54.9 1.3 %collective-permute-start.13 = (f32[64,256]{1,0:T(8,128)S(1)}, f32[64,256]{1,0:T(8,128)S(1)}, u32[]{:S(2)}, u32[]{:S(2)}) collective-permute-start(f32[64,256]{1,0:T(8,128)S(1)} %get-tuple-element.64), channel_id=1, source_target_pairs={{0,8},{1,9},{2,10},{3,11},{4,12},{5,13},{6,14},{7,15},{8,0},{9,1},... | collective-permute-start | bytes 196616 | tf_op jit(solution)/shard_map/ppermute | solution.py:430
  56.7 1.8 %collective-permute-start.15 = (f32[64,256]{1,0:T(8,128)S(1)}, f32[64,256]{1,0:T(8,128)S(1)}, u32[]{:S(2)}, u32[]{:S(2)}) collective-permute-start(f32[64,256]{1,0:T(8,128)S(1)} %get-tuple-element.66), channel_id=1, source_target_pairs={{0,24},{1,25},{2,26},{3,27},{4,28},{5,29},{6,30},{7,31},{8,16},{9,... | collective-permute-start | bytes 196616 | tf_op jit(solution)/shard_map/ppermute | solution.py:430
  58.5 0.9 %collective-permute-done.13.refs_1_ = f32[64,256]{1,0:T(8,128)S(1)} collective-permute-done((f32[64,256]{1,0:T(8,128)S(1)}, f32[64,256]{1,0:T(8,128)S(1)}, u32[]{:S(2)}, u32[]{:S(2)}) %collective-permute-start.13) | collective-permute-done | bytes 65568 | tf_op jit(solution)/shard_map/ppermute | solution.py:430
  59.3 1.5 %collective-permute-done.14.refs_2_ = f32[64,256]{1,0:T(8,128)S(1)} collective-permute-done((f32[64,256]{1,0:T(8,128)S(1)}, f32[64,256]{1,0:T(8,128)S(1)}, u32[]{:S(2)}, u32[]{:S(2)}) %collective-permute-start.14) | collective-permute-done | bytes 65568 | tf_op jit(solution)/shard_map/ppermute | solution.py:430
  60.8 1.3 %collective-permute-done.15.refs_3_ = f32[64,256]{1,0:T(8,128)S(1)} collective-permute-done((f32[64,256]{1,0:T(8,128)S(1)}, f32[64,256]{1,0:T(8,128)S(1)}, u32[]{:S(2)}, u32[]{:S(2)}) %collective-permute-start.15) | collective-permute-done | bytes 65568 | tf_op jit(solution)/shard_map/ppermute | solution.py:430
  62.1 0.9 %shard_map.69 = f32[256,256]{1,0:T(8,128)} custom-call(f32[64,256]{1,0:T(8,128)S(1)} %get-tuple-element.63.refs_0_, f32[64,256]{1,0:T(8,128)S(1)} %collective-permute-done.13.refs_1_, f32[64,256]{1,0:T(8,128)S(1)} %collective-permute-done.14.refs_2_, f32[64,256]{1,0:T(8,128)S(1)} %collective-permute-done.15.refs_3_), custom_call_target="tpu_custom_call" | custom-call | bytes 1048576 | tf_op jit(solution)/shard_map/pallas_call | solution.py:431
  (23 shorter events, 1.8 us)
Async XLA Ops:
  2.5 7.3 %copy-start = (f32[16,16,256]{2,1,0:T(8,128)S(1)}, f32[16,16,256]{2,1,0:T(8,128)}, u32[]{:S(2)}) copy-start(f32[16,16,256]{2,1,0:T(8,128)} %param.5) | copy-start | bytes 786436
  2.5 7.3 %copy-start.1 = (s32[2,1,1,1]{0,3,2,1:T(1,128)S(1)}, s32[2,1,1,1]{0,3,2,1:T(1,128)}, u32[]{:S(2)}) copy-start(s32[2,1,1,1]{0,3,2,1:T(1,128)} %param.9) | copy-start | bytes 28
  2.5 25.3 %copy-start.2 = (f32[2,3,33]{2,0,1:T(2,128)S(1)}, f32[2,3,33]{2,0,1:T(2,128)}, u32[]{:S(2)}) copy-start(f32[2,3,33]{2,0,1:T(2,128)} %param.8) | copy-start | bytes 2380
  2.5 33.0 %all-to-all-start = ((f32[32,1,8448]{2,1,0:T(1,128)}), f32[32,1,8448]{2,1,0:T(1,128)S(1)}, u32[]{:S(2)}, u32[]{:S(2)}) async-start(f32[32,1,8448]{2,1,0:T(1,128)} %bitcast.18), calls=%async_computation | async-start | bytes 2162688 | tf_op jit(solution)/shard_map/all_to_all | solution.py:383
  10.6 9.9 %collective-permute-start = (f32[72,256]{1,0:T(8,128)S(1)}, f32[72,256]{1,0:T(8,128)S(1)}, u32[]{:S(2)}, u32[]{:S(2)}) collective-permute-start(f32[72,256]{1,0:T(8,128)S(1)} %get-tuple-element.37), channel_id=1, source_target_pairs={{0,8},{1,9},{2,10},{3,11},{4,12},{5,13},{6,14},{7,15},{8,0},{9,1},... | collective-permute-start | bytes 221192 | tf_op jit(solution)/shard_map/ppermute | solution.py:363
  12.4 8.9 %collective-permute-start.1 = (f32[72,256]{1,0:T(8,128)S(1)}, f32[72,256]{1,0:T(8,128)S(1)}, u32[]{:S(2)}, u32[]{:S(2)}) collective-permute-start(f32[72,256]{1,0:T(8,128)S(1)} %get-tuple-element.38), channel_id=1, source_target_pairs={{0,16},{1,17},{2,18},{3,19},{4,20},{5,21},{6,22},{7,23},{8,24},{9,... | collective-permute-start | bytes 221192 | tf_op jit(solution)/shard_map/ppermute | solution.py:363
  13.9 12.0 %collective-permute-start.2 = (f32[72,256]{1,0:T(8,128)S(1)}, f32[72,256]{1,0:T(8,128)S(1)}, u32[]{:S(2)}, u32[]{:S(2)}) collective-permute-start(f32[72,256]{1,0:T(8,128)S(1)} %get-tuple-element.39), channel_id=1, source_target_pairs={{0,24},{1,25},{2,26},{3,27},{4,28},{5,29},{6,30},{7,31},{8,16},{9,... | collective-permute-start | bytes 221192 | tf_op jit(solution)/shard_map/ppermute | solution.py:363
  14.1 11.7 %collective-permute-start.3 = (f32[72,256]{1,0:T(8,128)S(1)}, f32[72,256]{1,0:T(8,128)S(1)}, u32[]{:S(2)}, u32[]{:S(2)}) collective-permute-start(f32[72,256]{1,0:T(8,128)S(1)} %get-tuple-element.36.refs_0_), channel_id=1, source_target_pairs={{0,4},{1,5},{2,6},{3,7},{4,0},{5,1},{6,2},{7,3},{8,12},{9,13},{10,... | collective-permute-start | bytes 221192 | tf_op jit(solution)/shard_map/ppermute | solution.py:364
  20.4 5.4 %collective-permute-start.4 = (f32[72,256]{1,0:T(8,128)S(1)}, f32[72,256]{1,0:T(8,128)S(1)}, u32[]{:S(2)}, u32[]{:S(2)}) collective-permute-start(f32[72,256]{1,0:T(8,128)S(1)} %collective-permute-done.refs_1_), channel_id=1, source_target_pairs={{0,4},{1,5},{2,6},{3,7},{4,0},{5,1},{6,2},{7,3},{8,12},{9,13},{10,... | collective-permute-start | bytes 221192 | tf_op jit(solution)/shard_map/ppermute | solution.py:364
  21.3 4.5 %collective-permute-start.5 = (f32[72,256]{1,0:T(8,128)S(1)}, f32[72,256]{1,0:T(8,128)S(1)}, u32[]{:S(2)}, u32[]{:S(2)}) collective-permute-start(f32[72,256]{1,0:T(8,128)S(1)} %collective-permute-done.1.refs_2_), channel_id=1, source_target_pairs={{0,4},{1,5},{2,6},{3,7},{4,0},{5,1},{6,2},{7,3},{8,12},{9,13},{10,... | collective-permute-start | bytes 221192 | tf_op jit(solution)/shard_map/ppermute | solution.py:364
  25.8 1.3 %collective-permute-start.6 = (f32[72,256]{1,0:T(8,128)S(1)}, f32[72,256]{1,0:T(8,128)S(1)}, u32[]{:S(2)}, u32[]{:S(2)}) collective-permute-start(f32[72,256]{1,0:T(8,128)S(1)} %collective-permute-done.2.refs_3_), channel_id=1, source_target_pairs={{0,4},{1,5},{2,6},{3,7},{4,0},{5,1},{6,2},{7,3},{8,12},{9,13},{10,... | collective-permute-start | bytes 221192 | tf_op jit(solution)/shard_map/ppermute | solution.py:364
  27.1 1.6 %collective-permute-start.7 = (f32[8,16,256]{2,1,0:T(8,128)S(1)}, f32[8,16,256]{2,1,0:T(8,128)S(1)}, u32[]{:S(2)}, u32[]{:S(2)}) collective-permute-start(f32[8,16,256]{2,1,0:T(8,128)S(1)} %get-tuple-element.42), channel_id=1, source_target_pairs={{4,8},{8,4},{12,24},{24,12},{28,16},{16,28},{20,17},{17,20},{21,25... | collective-permute-start | bytes 393224 | tf_op jit(solution)/shard_map/ppermute | solution.py:393
  36.4 7.8 %collective-permute-start.8 = (f32[8,32,256]{2,1,0:T(8,128)S(1)}, f32[8,32,256]{2,1,0:T(8,128)S(1)}, u32[]{:S(2)}, u32[]{:S(2)}) collective-permute-start(f32[8,32,256]{2,1,0:T(8,128)S(1)} %shard_map.60.ratio), channel_id=1, source_target_pairs={{4,8},{8,4},{12,24},{24,12},{28,16},{16,28},{20,17},{17,20},{21,25... | collective-permute-start | bytes 786440 | tf_op jit(solution)/shard_map/ppermute | solution.py:416
  38.4 5.8 %collective-permute-start.9 = (f32[8,32,256]{2,1,0:T(8,128)S(1)}, f32[8,32,256]{2,1,0:T(8,128)S(1)}, u32[]{:S(2)}, u32[]{:S(2)}) collective-permute-start(f32[8,32,256]{2,1,0:T(8,128)S(1)} %shard_map.60.ratio), channel_id=1, source_target_pairs={{0,4},{4,0},{8,12},{12,8},{24,28},{28,24},{16,20},{20,16},{17,21},... | collective-permute-start | bytes 786440 | tf_op jit(solution)/shard_map/ppermute | solution.py:416
  46.6 2.8 %collective-permute-start.10 = (f32[8,16,256]{2,1,0:T(8,128)S(1)}, f32[8,16,256]{2,1,0:T(8,128)S(1)}, u32[]{:S(2)}, u32[]{:S(2)}) collective-permute-start(f32[8,16,256]{2,1,0:T(8,128)S(1)} %get-tuple-element.56), channel_id=1, source_target_pairs={{4,8},{8,4},{12,24},{24,12},{28,16},{16,28},{20,17},{17,20},{21,25... | collective-permute-start | bytes 393224 | tf_op jit(solution)/shard_map/ppermute | solution.py:356
  47.3 2.3 %collective-permute-start.11 = (f32[8,16,256]{2,1,0:T(8,128)S(1)}, f32[8,16,256]{2,1,0:T(8,128)S(1)}, u32[]{:S(2)}, u32[]{:S(2)}) collective-permute-start(f32[8,16,256]{2,1,0:T(8,128)S(1)} %get-tuple-element.57), channel_id=1, source_target_pairs={{0,4},{4,0},{8,12},{12,8},{24,28},{28,24},{16,20},{20,16},{17,21},... | collective-permute-start | bytes 393224 | tf_op jit(solution)/shard_map/ppermute | solution.py:357
  50.5 4.4 %collective-permute-start.12 = (f32[4,32,256]{2,1,0:T(8,128)S(1)}, f32[4,32,256]{2,1,0:T(8,128)S(1)}, u32[]{:S(2)}, u32[]{:S(2)}) collective-permute-start(f32[4,32,256]{2,1,0:T(8,128)S(1)} %get-tuple-element.62), channel_id=1, source_target_pairs={{0,4},{1,5},{2,6},{3,7},{4,0},{5,1},{6,2},{7,3},{8,12},{9,13},{10,... | collective-permute-start | bytes 393224 | tf_op jit(solution)/shard_map/ppermute | solution.py:428
  54.9 4.4 %collective-permute-start.13 = (f32[64,256]{1,0:T(8,128)S(1)}, f32[64,256]{1,0:T(8,128)S(1)}, u32[]{:S(2)}, u32[]{:S(2)}) collective-permute-start(f32[64,256]{1,0:T(8,128)S(1)} %get-tuple-element.64), channel_id=1, source_target_pairs={{0,8},{1,9},{2,10},{3,11},{4,12},{5,13},{6,14},{7,15},{8,0},{9,1},... | collective-permute-start | bytes 196616 | tf_op jit(solution)/shard_map/ppermute | solution.py:430
  56.1 4.7 %collective-permute-start.14 = (f32[64,256]{1,0:T(8,128)S(1)}, f32[64,256]{1,0:T(8,128)S(1)}, u32[]{:S(2)}, u32[]{:S(2)}) collective-permute-start(f32[64,256]{1,0:T(8,128)S(1)} %get-tuple-element.65), channel_id=1, source_target_pairs={{0,16},{1,17},{2,18},{3,19},{4,20},{5,21},{6,22},{7,23},{8,24},{9,... | collective-permute-start | bytes 196616 | tf_op jit(solution)/shard_map/ppermute | solution.py:430
  56.7 5.4 %collective-permute-start.15 = (f32[64,256]{1,0:T(8,128)S(1)}, f32[64,256]{1,0:T(8,128)S(1)}, u32[]{:S(2)}, u32[]{:S(2)}) collective-permute-start(f32[64,256]{1,0:T(8,128)S(1)} %get-tuple-element.66), channel_id=1, source_target_pairs={{0,24},{1,25},{2,26},{3,27},{4,28},{5,29},{6,30},{7,31},{8,16},{9,... | collective-permute-start | bytes 196616 | tf_op jit(solution)/shard_map/ppermute | solution.py:430

commit v7 on v6

--- a/solution.py
+++ b/solution.py
@@ -93,7 +93,8 @@
 
 def est_kernel(weight, est, *refs):
     pieces, turned = refs[:4], refs[4]
-    turned[...] = est[...].T
+    for half in range(2):
+        turned[:, 128 * half : 128 * half + 128] = est[:, half].reshape(128, 256).T
     rows = lax.broadcasted_iota(jnp.int32, (8, 256), 0)
     weights = jnp.where(
         rows == 0,
@@ -112,11 +113,14 @@
     for flip, x, y, _ in chips():
         for turn in range(2):
             piece = pieces[4 * turn + flip]
-            column = 4 * x + 2 * y + (core if turn == 0 else 1 - core)
-            slab[column] = piece[pl.ds(pl.multiple_of(32 * upper, 32), 32), :]
-            weights[column] = piece[64:72, :]
-            far[column] = piece[pl.ds(pl.multiple_of(48 * upper, 16), 16), :]
-            near[column] = piece[pl.ds(pl.multiple_of(32 - 16 * upper, 16), 16), :]
+            block = 4 * y + 2 * (core if turn == 0 else 1 - core)
+            lanes = pl.ds(pl.multiple_of(128 * x, 128), 128)
+            for half in range(2):
+                part = piece.at[:, 128 * half : 128 * half + 128]
+                slab[block + half, :, lanes] = part[pl.ds(pl.multiple_of(32 * upper, 32), 32), :]
+                weights[block + half, :, lanes] = part[64:72, :]
+                far[block + half, :, lanes] = part[pl.ds(pl.multiple_of(48 * upper, 16), 16), :]
+                near[block + half, :, lanes] = part[pl.ds(pl.multiple_of(32 - 16 * upper, 16), 16), :]
 
 
 def lines_kernel(planes, raw, index, out, held, numbers, made, arrived, numbered, left):
@@ -179,27 +183,23 @@
     high, low = (part.astype(F32) for part in split2(toeplitz(along_z[2:3, :], 32)))
     band[0:32, :] = (high + pltpu.roll(high, 64, 1)).astype(BF16)
     band[32:64, :] = low.astype(BF16)
-    small_x, small_y = split3(toeplitz(along_xy[0:1, :], 16)), split3(toeplitz(along_xy[1:2, :], 16))
     from_row = lax.broadcasted_iota(jnp.int32, (128, 256), 0)
     to_lane = lax.broadcasted_iota(jnp.int32, (128, 256), 1)
-    wide_x, wide_y = [], []
-    for offset in range(3):
-        pick_x = (from_row == to_lane // 16 + 16 * offset).astype(BF16)
-        pick_y = (from_row == lax.rem(to_lane, 16) + 16 * offset).astype(BF16)
-        rows_x = sum(dot_nn(piece, pick_x) for piece in small_x)
-        rows_y = sum(dot_nn(piece, pick_y) for piece in small_y)
-        wide_x.append(jnp.broadcast_to(rows_x[:, None, :], (16, 16, 256)).reshape(256, 256))
-        wide_y.append(jnp.broadcast_to(rows_y[None], (16, 16, 256)).reshape(256, 256))
-    for dx in range(3):
-        for dy in range(3):
-            high, low = split2(wide_x[dx] * wide_y[dy])
-            big_high[8 - dx * 3 - dy] = high
-            big_low[8 - dx * 3 - dy] = low
+    pick = (from_row == to_lane // 8 + 16).astype(BF16)
+    rows_x = sum(dot_nn(piece, pick) for piece in split3(toeplitz(along_xy[0:1, :], 32)))
+    wide_x = jnp.broadcast_to(rows_x[:, None, :], (32, 8, 256)).reshape(256, 256)
+    small_y = split3(toeplitz(along_xy[1:2, :], 8))
+    for offset in range(-2, 3):
+        pick = (from_row == lax.rem(to_lane, 8) + 16 - 8 * offset).astype(BF16)
+        rows_y = sum(dot_nn(piece, pick) for piece in small_y)
+        wide_y = jnp.broadcast_to(rows_y[None], (32, 8, 256)).reshape(256, 256)
+        big_high[offset + 2], big_low[offset + 2] = split2(wide_x * wide_y)
 
 
 def scattered(view, slots, weights, column):
     chunk = lax.broadcasted_iota(jnp.int32, (32, 128), 1) // 32
-    line = lax.broadcasted_iota(jnp.int32, (256, 512), 0).astype(F32)
+    at = lax.broadcasted_iota(jnp.int32, (256, 512), 0)
+    line = (lax.rem(at, 128) // 8 * 16 + at // 128 * 8 + lax.rem(at, 8)).astype(F32)
     x, block = column // 4, column % 4
     numbers, values = [], []
     for t in range(4):
@@ -218,13 +218,18 @@
     left = jnp.concatenate([*split3(value), jnp.ones((16, 512), BF16)], axis=0)
     result = dot_nt(left, hot)
     data = result[0:32] + result[32:64] + result[64:96]
-    return data, result[96:97] * weights[column, view : view + 1, :]
+    for half in range(2):
+        lanes = slice(128 * half, 128 * half + 128)
+        to = slice(128 * x, 128 * x + 128)
+        weight = weights[2 * block + half, view : view + 1, to]
+        yield 2 * block + half, to, data[:, lanes], result[96:97, lanes] * weight
 
 
 def scatter_kernel(slots, weights, data, cover):
     for column in range(8):
-        data[column], row = scattered(1, slots, weights, column)
-        cover[column] = jnp.broadcast_to(row, (8, 256))
+        for block, lanes, values, covered in scattered(1, slots, weights, column):
+            data[block, :, lanes] = values
+            cover[block, :, lanes] = jnp.broadcast_to(covered, (8, 128))
 
 
 def payloads(value, far, near):
@@ -258,24 +263,17 @@
             flat[at : at + 32, :] = both[0:32] + both[32:64]
     high, low = split2(flat[...])
 
-    def product(start, stop, dx, dy):
-        at = (dx + 1) * 3 + dy + 1
+    for offset in (0, -2, -1, 1, 2):
+        first, last = max(0, -offset), min(8, 8 - offset)
+        start, stop = (first + offset) * rows, (last + offset) * rows
         size = stop - start
-        both = dot_nn(jnp.concatenate([high[start:stop], low[start:stop]], axis=0), big_high[at])
-        return both[:size] + both[size:] + dot_nn(high[start:stop], big_low[at])
-
-    total[...] = product(0, 8 * rows, 0, 0)
-    for dx in (-1, 0, 1):
-        for dy in (-1, 0, 1):
-            if dx == 0 and dy == 0:
-                continue
-            for x in range(2):
-                if not 0 <= x + dx < 2:
-                    continue
-                first, last = max(0, -dy), min(4, 4 - dy)
-                start, stop = (x * 4 + first) * rows, (x * 4 + last) * rows
-                shift = (dx * 4 + dy) * rows
-                total[start:stop, :] += product(start + shift, stop + shift, dx, dy)
+        both = jnp.concatenate([high[start:stop], low[start:stop]], axis=0)
+        both = dot_nn(both, big_high[offset + 2])
+        part = both[:size] + both[size:] + dot_nn(high[start:stop], big_low[offset + 2])
+        if offset == 0:
+            total[...] = part
+        else:
+            total[first * rows : last * rows, :] += part
 
 
 def blur_kernel(est, far, near, band, big_high, big_low, blurred, wide, flat):
@@ -291,8 +289,9 @@
 
 def scatter_ratio_kernel(slots, weights, blurred, ratio):
     for column in range(8):
-        data, cover = scattered(0, slots, weights, column)
-        ratio[column] = 1.0 + cover * (data / blurred[column * 32 : column * 32 + 32, :] - 1.0)
+        for block, lanes, values, covered in scattered(0, slots, weights, column):
+            here = blurred[32 * block : 32 * block + 32, lanes]
+            ratio[block, :, lanes] = 1.0 + covered * (values / here - 1.0)
 
 
 def update_kernel(planes, ratio, ratio_far, ratio_near, est, est_far, est_near, band, high, low, new, wide, flat, total):
@@ -309,29 +308,45 @@
     payloads(ratio, far, near)
 
 
-def last_kernel(ratio, far, near, band, big_high, big_low, est, keep, give, wide, flat, total):
+def last_kernel(ratio, far, near, band, big_high, big_low, est, *refs):
+    (mine, other), pieces, (wide, flat, total) = refs[:2], refs[2:5], refs[5:]
     widened(wide, ratio, far[...], near, 16)
     blurred_into(wide, band, big_high, big_low, flat, total)
     _, _, core, _ = coordinates()
     for flip, x, y, _ in chips():
-        for turn, out in enumerate((keep, give)):
-            column = 4 * x + 2 * y + (core if turn == 0 else 1 - core)
-            start = pl.multiple_of(column * 32, 32)
-            out[flip] = est[column, 16:48, :] * total[pl.ds(start, 32), :]
-
-
-def merge_kernel(keep, got, *pieces):
+        for turn in range(2):
+            block = 4 * y + 2 * (core if turn == 0 else 1 - core)
+            lanes = pl.ds(pl.multiple_of(128 * x, 128), 128)
+            new = jnp.concatenate(
+                [
+                    est[block + half, 16:48, lanes]
+                    * total[pl.ds(pl.multiple_of(32 * (block + half), 32), 32), lanes]
+                    for half in range(2)
+                ],
+                axis=1,
+            )
+            if flip == 0:
+                (mine, other)[turn][...] = new
+            else:
+                pieces[flip - 1][turn] = new
+
+
+def join_kernel(*refs):
+    pieces, others, (out, held, turned, left) = refs[:4], refs[4:8], refs[8:]
     upper = upper_half()
-    for flip in range(4):
-        pieces[flip][pl.ds(pl.multiple_of(32 * upper, 32), 32), :] = keep[flip]
-        pieces[flip][pl.ds(pl.multiple_of(32 - 32 * upper, 32), 32), :] = got[flip]
-
-
-def join_kernel(*refs):
-    pieces, (out, held) = refs[:4], refs[4:]
     for flip, _, _, place in chips():
-        held[pl.ds(pl.multiple_of(64 * place, 64), 64), :] = pieces[flip][...]
-    out[...] = held[...].T
+        mine = pieces[flip][...] if flip == 0 else pieces[flip][0]
+        held[pl.ds(pl.multiple_of(64 * place + 32 * upper, 32), 32), :] = mine
+        held[pl.ds(pl.multiple_of(64 * place + 32 - 32 * upper, 32), 32), :] = others[flip][...]
+
+    def store(part):
+        return pltpu.make_async_copy(turned.at[:, part], out.at[:, part], left.at[part])
+
+    for part in range(2):
+        turned[:, part] = held[:, 128 * part : 128 * part + 128].T.reshape(16, 8, 256)
+        store(part).start()
+    for part in range(2):
+        store(part).wait()
 
 
 def shape(*dims, dtype=F32):
@@ -359,7 +374,7 @@
 
     own, *away = call(
         est_kernel, (shape(72, 256),) * 4, [SMEM, VMEM], [pltpu.VMEM((256, 256), F32)]
-    )(view_weight.reshape(2), estimate.reshape(256, 256))
+    )(view_weight.reshape(2), estimate.reshape(16, 2, 8, 256))
     here = [own] + [lax.ppermute(piece, ALL, pairs) for piece, pairs in zip(away, to_chips)]
     there = [lax.ppermute(piece, ALL, to_core) for piece in here]
 
@@ -392,7 +407,7 @@
     )
     est_far = lax.ppermute(est_far, ALL, far_pairs)
     def matrices(view, way, after):
-        big = shape(9, 256, 256, dtype=BF16)
+        big = shape(5, 256, 256, dtype=BF16)
         big_high, big_low, band = call(
             functools.partial(taps_kernel, view, way),
             (big, big, shape(64, 128, dtype=BF16)),
@@ -417,18 +432,23 @@
     ratio, far, near = call(
         ratio_kernel, (full, half, half), [VMEM] * 6, [work(256, 256), work(256, 256)], flops=1 << 30
     )(est, *matrices(1, 0, slots), data, cover)
-    quarter = shape(4, 32, 256)
-    keep, give = call(
+    column, pair = shape(32, 256), shape(2, 32, 256)
+    mine, other, *away = call(
         last_kernel,
-        (quarter, quarter),
+        (column, column, pair, pair, pair),
         [VMEM] * 7,
         [work(8, 64, 256), work(256, 256), work(256, 256)],
         flops=1 << 30,
     )(ratio, *exchange(far, near), *matrices(1, 1, ratio), est)
-    got = lax.ppermute(give, ALL, to_core)
-    own, *away = call(merge_kernel, (shape(64, 256),) * 4, [VMEM] * 2)(keep, got)
-    parts = [own] + [lax.ppermute(piece, ALL, pairs) for piece, pairs in zip(away, to_chips)]
-    out = call(join_kernel, shape(256, 256), [VMEM] * 4, [pltpu.VMEM((256, 256), F32)])(*parts)
+    away = [lax.ppermute(piece, ALL, pairs) for piece, pairs in zip(away, to_chips)]
+    others = [lax.ppermute(piece, ALL, to_core) for piece in [other] + [piece[1] for piece in away]]
+    out = call(
+        join_kernel,
+        shape(16, 2, 8, 256),
+        [VMEM] * 8,
+        [work(256, 256), work(16, 2, 8, 256), pltpu.SemaphoreType.DMA((2,))],
+        out_specs=anywhere,
+    )(mine, *away, *others)
     return out.reshape(16, 16, 256)
 
 

time: 63.4 us -> 62.8 us (level)
  Pallas kernels: 13.5 us -> 12.1 us
    ppermute x1 -> x4, starting transfers between devices: 3.38 us -> 1.79 us  [slab_sweep(): lax.ppermute(piece, ALL, to_core)]
    ppermute x6, starting transfers between devices: 7.12 us -> 8.37 us  [slab_sweep(): lax.ppermute(piece, ALL, pairs)]
    pallas_call x4, Pallas kernels: 3.48 us -> 2.62 us  [matrices(): call(functools.partial(taps_kernel, view, way), (big, big, shape(64, 128,...]
    pallas_call x3 -> x2, Pallas kernels: 1.78 us -> 1.64 us  [the longest x1 0.86 us: slab_sweep(): call(join_kernel, shape(16, 2, 8, 256), [VMEM] * 8, [work(256, 256), work...]
  transfers between devices with their start and end apart: 17 -> 20, of which waited for: 11 -> 10; matrix products, arithmetic and copies ran while one was open for 0% -> 0% of each run, Pallas kernels for 9% -> 8%
where the time goes in v7:
time: 62.8 us; the launch traced here: 61.8 us
  waiting for transfers between devices  27.4 us (44%)
  starting transfers between devices  22 us (35%)
  Pallas kernels  12.1 us (19%)
    ppermute x6, waiting for transfers between devices, slab_sweep(): lax.ppermute(piece, ALL, pairs)  14.7 us
    ppermute x6, starting transfers between devices, slab_sweep(): lax.ppermute(piece, ALL, pairs)  8.37 us
    all_to_all x1, starting transfers between devices, slab_sweep(): slots = lax.all_to_all(slots, ALL, split_axis=0, concat_axis=0, tiled=True)  7.3 us
    all_to_all x1, waiting for transfers between devices, slab_sweep(): slots = lax.all_to_all(slots, ALL, split_axis=0, concat_axis=0, tiled=True)  6.23 us
    ppermute x1, waiting for transfers between devices, slab_sweep(): lax.ppermute(ratio, ALL, ring_pairs)  3.66 us
    pallas_call x4, Pallas kernels, matrices(): call(functools.partial(taps_kernel, view, way), (big, big, shape(64, 128,...  2.62 us
    pallas_call x1, Pallas kernels, slab_sweep(): call(functools.partial(lines_kernel, planes), shape(8, 66 * planes, 128),...  2.49 us
    ppermute x1, starting transfers between devices, slab_sweep(): lax.ppermute(ratio, ALL, ring_pairs)  1.93 us
  transfers between devices with their start and end apart: 20, of which 10 were waited for; matrix products, arithmetic and copies ran while one was open for 0% of the time, Pallas kernels for 8%

profile of v7, /device:TPU:0, one launch (start us, length us, event | category | flops | bytes accessed | tf_op | source)
XLA Modules:
  0.0 61.8 jit_solution(16494962059935061869)
XLA Ops:
  0.0 2.5 %shard_map.55 = f32[8,264,128]{2,1,0:T(8,128)} custom-call(f32[2,4,4,32,256]{4,3,2,1,0:T(8,128)} %bitcast.25, s32[8,128]{1,0:T(8,128)} %bitcast.26), custom_call_target="tpu_custom_call" | custom-call | bytes 1048576 | tf_op jit(solution)/shard_map/pallas_call | solution.py:382
  2.5 7.3 %all-to-all-start = ((f32[32,1,8448]{2,1,0:T(1,128)}), f32[32,1,8448]{2,1,0:T(1,128)S(1)}, u32[]{:S(2)}, u32[]{:S(2)}) async-start(f32[32,1,8448]{2,1,0:T(1,128)} %bitcast.24), calls=%async_computation | async-start | bytes 2162688 | tf_op jit(solution)/shard_map/all_to_all | solution.py:398
  9.9 0.7 %shard_map.56 = (f32[72,256]{1,0:T(8,128)S(1)}, f32[72,256]{1,0:T(8,128)S(1)}, f32[72,256]{1,0:T(8,128)S(1)}, f32[72,256]{1,0:T(8,128)S(1)}) custom-call(s32[2]{0:T(128)S(1)} %bitcast.19, f32[16,2,8,256]{3,2,1,0:T(8,128)S(1)} %bitcast.18), custom_call_target="tpu_custom_call" | custom-call | bytes 1048576 | tf_op jit(solution)/shard_map/pallas_call | solution.py:375
  10.6 1.8 %collective-permute-start = (f32[72,256]{1,0:T(8,128)S(1)}, f32[72,256]{1,0:T(8,128)S(1)}, u32[]{:S(2)}, u32[]{:S(2)}) collective-permute-start(f32[72,256]{1,0:T(8,128)S(1)} %get-tuple-element.36), channel_id=1, source_target_pairs={{0,8},{1,9},{2,10},{3,11},{4,12},{5,13},{6,14},{7,15},{8,0},{9,1},... | collective-permute-start | bytes 221192 | tf_op jit(solution)/shard_map/ppermute | solution.py:378
  12.4 1.5 %collective-permute-start.1 = (f32[72,256]{1,0:T(8,128)S(1)}, f32[72,256]{1,0:T(8,128)S(1)}, u32[]{:S(2)}, u32[]{:S(2)}) collective-permute-start(f32[72,256]{1,0:T(8,128)S(1)} %get-tuple-element.37), channel_id=1, source_target_pairs={{0,16},{1,17},{2,18},{3,19},{4,20},{5,21},{6,22},{7,23},{8,24},{9,... | collective-permute-start | bytes 221192 | tf_op jit(solution)/shard_map/ppermute | solution.py:378
  14.1 6.3 %collective-permute-done.refs_1_ = f32[72,256]{1,0:T(8,128)S(1)} collective-permute-done((f32[72,256]{1,0:T(8,128)S(1)}, f32[72,256]{1,0:T(8,128)S(1)}, u32[]{:S(2)}, u32[]{:S(2)}) %collective-permute-start) | collective-permute-done | bytes 73760 | tf_op jit(solution)/shard_map/ppermute | solution.py:378
  20.4 0.9 %collective-permute-done.1.refs_2_ = f32[72,256]{1,0:T(8,128)S(1)} collective-permute-done((f32[72,256]{1,0:T(8,128)S(1)}, f32[72,256]{1,0:T(8,128)S(1)}, u32[]{:S(2)}, u32[]{:S(2)}) %collective-permute-start.1) | collective-permute-done | bytes 73760 | tf_op jit(solution)/shard_map/ppermute | solution.py:378
  21.3 4.5 %collective-permute-done.2.refs_3_ = f32[72,256]{1,0:T(8,128)S(1)} collective-permute-done((f32[72,256]{1,0:T(8,128)S(1)}, f32[72,256]{1,0:T(8,128)S(1)}, u32[]{:S(2)}, u32[]{:S(2)}) %collective-permute-start.2) | collective-permute-done | bytes 73760 | tf_op jit(solution)/shard_map/ppermute | solution.py:378
  25.9 1.2 %collective-permute-done.6.refs_7_ = f32[72,256]{1,0:T(8,128)S(1)} collective-permute-done((f32[72,256]{1,0:T(8,128)S(1)}, f32[72,256]{1,0:T(8,128)S(1)}, u32[]{:S(2)}, u32[]{:S(2)}) %collective-permute-start.6) | collective-permute-done | bytes 73760 | tf_op jit(solution)/shard_map/ppermute | solution.py:379
  27.2 0.7 %collective-permute-start.7 = (f32[8,16,256]{2,1,0:T(8,128)S(1)}, f32[8,16,256]{2,1,0:T(8,128)S(1)}, u32[]{:S(2)}, u32[]{:S(2)}) collective-permute-start(f32[8,16,256]{2,1,0:T(8,128)S(1)} %get-tuple-element.41), channel_id=1, source_target_pairs={{4,8},{8,4},{12,24},{24,12},{28,16},{16,28},{20,17},{17,20},{21,25... | collective-permute-start | bytes 393224 | tf_op jit(solution)/shard_map/ppermute | solution.py:408
  27.9 0.7 %shard_map.58 = (bf16[5,256,256]{2,1,0:T(8,128)(2,1)S(1)}, bf16[5,256,256]{2,1,0:T(8,128)(2,1)S(1)}, bf16[64,128]{1,0:T(8,128)(2,1)S(1)}) custom-call(f32[3,2,33]{2,1,0:T(2,128)S(1)} %bitcast.20, f32[8,32,256]{2,1,0:T(8,128)S(1)} %get-tuple-element.40._.est), custom_call_target="tpu_custom_call" | custom-call | flops 1073741824 | bytes 1048576 | tf_op jit(solution)/shard_map/pallas_call | solution.py:411
  28.6 0.8 %shard_map.59.blurred = f32[256,256]{1,0:T(8,128)S(1)} custom-call(f32[8,32,256]{2,1,0:T(8,128)S(1)} %get-tuple-element.40._.est, f32[8,16,256]{2,1,0:T(8,128)S(1)} %collective-permute-done.7.far.est_far, f32[8,16,256]{2,1,0:T(8,128)S(1)} %get-tuple-element.42.near.est_near, bf16[64,128]{1,0:T(8,128)(2,1)S(1)} %get-tuple-element.43.band, ...), custom_call_target="tpu_custom_call" | custom-call | flops 1073741824 | bytes 1048576 | tf_op jit(solution)/shard_map/pallas_call | solution.py:420
  29.4 6.2 %all-to-all-done = f32[32,1,8448]{2,1,0:T(1,128)S(1)} async-done(((f32[32,1,8448]{2,1,0:T(1,128)}), f32[32,1,8448]{2,1,0:T(1,128)S(1)}, u32[]{:S(2)}, u32[]{:S(2)}) %all-to-all-start) | async-done | bytes 1081376 | tf_op jit(solution)/shard_map/all_to_all | solution.py:398
  35.6 0.9 %shard_map.60.ratio = f32[8,32,256]{2,1,0:T(8,128)S(1)} custom-call(f32[8,264,128]{2,1,0:T(8,128)S(1)} %bitcast.14, f32[8,8,256]{2,1,0:T(8,128)S(1)} %get-tuple-element.39.weights, f32[256,256]{1,0:T(8,128)S(1)} %shard_map.59.blurred), custom_call_target="tpu_custom_call" | custom-call | flops 1073741824 | bytes 1048576 | tf_op jit(solution)/shard_map/pallas_call | solution.py:423
  36.5 1.9 %collective-permute-start.8 = (f32[8,32,256]{2,1,0:T(8,128)S(1)}, f32[8,32,256]{2,1,0:T(8,128)S(1)}, u32[]{:S(2)}, u32[]{:S(2)}) collective-permute-start(f32[8,32,256]{2,1,0:T(8,128)S(1)} %shard_map.60.ratio), channel_id=1, source_target_pairs={{4,8},{8,4},{12,24},{24,12},{28,16},{16,28},{20,17},{17,20},{21,25... | collective-permute-start | bytes 786440 | tf_op jit(solution)/shard_map/ppermute | solution.py:431
  38.4 0.6 shard_map.61
  39.0 0.8 %shard_map.64 = (f32[8,32,256]{2,1,0:T(8,128)S(1)}, f32[8,8,256]{2,1,0:T(8,128)S(1)}) custom-call(f32[8,264,128]{2,1,0:T(8,128)S(1)} %bitcast.16, f32[8,8,256]{2,1,0:T(8,128)S(1)} %get-tuple-element.39.weights), custom_call_target="tpu_custom_call" | custom-call | flops 1073741824 | bytes 1048576 | tf_op jit(solution)/shard_map/pallas_call | solution.py:424
  39.8 0.7 %shard_map.63 = (bf16[5,256,256]{2,1,0:T(8,128)(2,1)S(1)}, bf16[5,256,256]{2,1,0:T(8,128)(2,1)S(1)}, bf16[64,128]{1,0:T(8,128)(2,1)S(1)}) custom-call(f32[3,2,33]{2,1,0:T(2,128)S(1)} %bitcast.22, f32[8,264,128]{2,1,0:T(8,128)S(1)} %bitcast.17), custom_call_target="tpu_custom_call" | custom-call | flops 1073741824 | bytes 1048576 | tf_op jit(solution)/shard_map/pallas_call | solution.py:411
  40.6 3.7 %collective-permute-done.8.ratio_far = f32[8,32,256]{2,1,0:T(8,128)S(1)} collective-permute-done((f32[8,32,256]{2,1,0:T(8,128)S(1)}, f32[8,32,256]{2,1,0:T(8,128)S(1)}, u32[]{:S(2)}, u32[]{:S(2)}) %collective-permute-start.8) | collective-permute-done | bytes 262176 | tf_op jit(solution)/shard_map/ppermute | solution.py:431
  44.2 1.3 %shard_map.62.est = f32[8,64,256]{2,1,0:T(8,128)S(1)} custom-call(f32[8,32,256]{2,1,0:T(8,128)S(1)} %shard_map.60.ratio, f32[8,32,256]{2,1,0:T(8,128)S(1)} %collective-permute-done.8.ratio_far, f32[8,32,256]{2,1,0:T(8,128)S(1)} %collective-permute-done.9.ratio_near, f32[8,32,256]{2,1,0:T(8,128)S(1)} %get-tuple-element.40._.est, ...), custom_call_target="tpu_custom_call" | custom-call | flops 1073741824 | bytes 1048576 | tf_op jit(solution)/shard_map/pallas_call | solution.py:425
  45.6 0.8 %shard_map.65 = (f32[8,32,256]{2,1,0:T(8,128)S(1)}, f32[8,16,256]{2,1,0:T(8,128)S(1)}, f32[8,16,256]{2,1,0:T(8,128)S(1)}) custom-call(f32[8,64,256]{2,1,0:T(8,128)S(1)} %shard_map.62.est, bf16[64,128]{1,0:T(8,128)(2,1)S(1)} %get-tuple-element.49.band, bf16[5,256,256]{2,1,0:T(8,128)(2,1)S(1)} %get-tuple-element.50.high, ...), custom_call_target="tpu_custom_call" | custom-call | flops 1073741824 | bytes 1048576 | tf_op jit(solution)/shard_map/pallas_call | solution.py:432
  46.4 0.7 %collective-permute-start.10 = (f32[8,16,256]{2,1,0:T(8,128)S(1)}, f32[8,16,256]{2,1,0:T(8,128)S(1)}, u32[]{:S(2)}, u32[]{:S(2)}) collective-permute-start(f32[8,16,256]{2,1,0:T(8,128)S(1)} %get-tuple-element.55), channel_id=1, source_target_pairs={{4,8},{8,4},{12,24},{24,12},{28,16},{16,28},{20,17},{17,20},{21,25... | collective-permute-start | bytes 393224 | tf_op jit(solution)/shard_map/ppermute | solution.py:371
  47.1 1.3 %collective-permute-start.11 = (f32[8,16,256]{2,1,0:T(8,128)S(1)}, f32[8,16,256]{2,1,0:T(8,128)S(1)}, u32[]{:S(2)}, u32[]{:S(2)}) collective-permute-start(f32[8,16,256]{2,1,0:T(8,128)S(1)} %get-tuple-element.56), channel_id=1, source_target_pairs={{0,4},{4,0},{8,12},{12,8},{24,28},{28,24},{16,20},{20,16},{17,21},... | collective-permute-start | bytes 393224 | tf_op jit(solution)/shard_map/ppermute | solution.py:372
  48.4 0.6 shard_map.66
  49.3 0.8 %shard_map.67 = (f32[32,256]{1,0:T(8,128)S(1)}, f32[32,256]{1,0:T(8,128)S(1)}, f32[2,32,256]{2,1,0:T(8,128)S(1)}, f32[2,32,256]{2,1,0:T(8,128)S(1)}, f32[2,32,256]{2,1,0:T(8,128)S(1)}) custom-call(f32[8,32,256]{2,1,0:T(8,128)S(1)} %get-tuple-element.54._.ratio, f32[8,16,256]{2,1,0:T(8,128)S(1)} %collective-permute-done.10.far, ...), custom_call_target="tpu_custom_call" | custom-call | flops 1073741824 | bytes 1048576 | tf_op jit(solution)/shard_map/pallas_call | solution.py:436
  50.1 3.3 %collective-permute-start.12 = (f32[2,32,256]{2,1,0:T(8,128)S(1)}, f32[2,32,256]{2,1,0:T(8,128)S(1)}, u32[]{:S(2)}, u32[]{:S(2)}) collective-permute-start(f32[2,32,256]{2,1,0:T(8,128)S(1)} %get-tuple-element.61), channel_id=1, source_target_pairs={{0,8},{1,9},{2,10},{3,11},{4,12},{5,13},{6,14},{7,15},{8,0},{9,1},... | collective-permute-start | bytes 196616 | tf_op jit(solution)/shard_map/ppermute | solution.py:443
  53.4 1.2 %collective-permute-start.13 = (f32[2,32,256]{2,1,0:T(8,128)S(1)}, f32[2,32,256]{2,1,0:T(8,128)S(1)}, u32[]{:S(2)}, u32[]{:S(2)}) collective-permute-start(f32[2,32,256]{2,1,0:T(8,128)S(1)} %get-tuple-element.62), channel_id=1, source_target_pairs={{0,16},{1,17},{2,18},{3,19},{4,20},{5,21},{6,22},{7,23},{8,24},{9,... | collective-permute-start | bytes 196616 | tf_op jit(solution)/shard_map/ppermute | solution.py:443
  54.9 1.2 %collective-permute-start.15 = (f32[32,256]{1,0:T(8,128)S(1)}, f32[32,256]{1,0:T(8,128)S(1)}, u32[]{:S(2)}, u32[]{:S(2)}) collective-permute-start(f32[32,256]{1,0:T(8,128)S(1)} %get-tuple-element.64), channel_id=1, source_target_pairs={{0,4},{1,5},{2,6},{3,7},{4,0},{5,1},{6,2},{7,3},{8,12},{9,13},{10,... | collective-permute-start | bytes 98312 | tf_op jit(solution)/shard_map/ppermute | solution.py:444
  56.6 1.7 %collective-permute-done.13.refs_2_ = f32[2,32,256]{2,1,0:T(8,128)S(1)} collective-permute-done((f32[2,32,256]{2,1,0:T(8,128)S(1)}, f32[2,32,256]{2,1,0:T(8,128)S(1)}, u32[]{:S(2)}, u32[]{:S(2)}) %collective-permute-start.13) | collective-permute-done | bytes 65568 | tf_op jit(solution)/shard_map/ppermute | solution.py:443
  58.5 1.3 %collective-permute-done.14.refs_3_ = f32[2,32,256]{2,1,0:T(8,128)S(1)} collective-permute-done((f32[2,32,256]{2,1,0:T(8,128)S(1)}, f32[2,32,256]{2,1,0:T(8,128)S(1)}, u32[]{:S(2)}, u32[]{:S(2)}) %collective-permute-start.14) | collective-permute-done | bytes 65568 | tf_op jit(solution)/shard_map/ppermute | solution.py:443
  59.8 1.2 %collective-permute-done.18.refs_7_ = f32[32,256]{1,0:T(8,128)S(1)} collective-permute-done((f32[32,256]{1,0:T(8,128)S(1)}, f32[32,256]{1,0:T(8,128)S(1)}, u32[]{:S(2)}, u32[]{:S(2)}) %collective-permute-start.18) | collective-permute-done | bytes 32800 | tf_op jit(solution)/shard_map/ppermute | solution.py:444
  61.0 0.9 %shard_map.68 = f32[16,2,8,256]{3,2,1,0:T(8,128)} custom-call(f32[32,256]{1,0:T(8,128)S(1)} %get-tuple-element.60.refs_0_, f32[2,32,256]{2,1,0:T(8,128)S(1)} %collective-permute-done.12.refs_1_, f32[2,32,256]{2,1,0:T(8,128)S(1)} %collective-permute-done.13.refs_2_, f32[2,32,256]{2,1,0:T(8,128)S(1)} %collective-permute-done.14.refs_3_, ...), custom_call_target="tpu_custom_call" | custom-call | bytes 1048576 | tf_op jit(solution)/shard_map/pallas_call | solution.py:445
  (31 shorter events, 1.7 us)
Async XLA Ops:
  2.5 7.3 %copy-start = (f32[16,16,256]{2,1,0:T(8,128)S(1)}, f32[16,16,256]{2,1,0:T(8,128)}, u32[]{:S(2)}) copy-start(f32[16,16,256]{2,1,0:T(8,128)} %param.5) | copy-start | bytes 786436
  2.5 7.3 %copy-start.1 = (s32[2,1,1,1]{0,3,2,1:T(1,128)S(1)}, s32[2,1,1,1]{0,3,2,1:T(1,128)}, u32[]{:S(2)}) copy-start(s32[2,1,1,1]{0,3,2,1:T(1,128)} %param.9) | copy-start | bytes 28
  2.5 25.3 %copy-start.2 = (f32[2,3,33]{2,0,1:T(2,128)S(1)}, f32[2,3,33]{2,0,1:T(2,128)}, u32[]{:S(2)}) copy-start(f32[2,3,33]{2,0,1:T(2,128)} %param.8) | copy-start | bytes 2380
  2.5 33.0 %all-to-all-start = ((f32[32,1,8448]{2,1,0:T(1,128)}), f32[32,1,8448]{2,1,0:T(1,128)S(1)}, u32[]{:S(2)}, u32[]{:S(2)}) async-start(f32[32,1,8448]{2,1,0:T(1,128)} %bitcast.24), calls=%async_computation | async-start | bytes 2162688 | tf_op jit(solution)/shard_map/all_to_all | solution.py:398
  10.6 9.9 %collective-permute-start = (f32[72,256]{1,0:T(8,128)S(1)}, f32[72,256]{1,0:T(8,128)S(1)}, u32[]{:S(2)}, u32[]{:S(2)}) collective-permute-start(f32[72,256]{1,0:T(8,128)S(1)} %get-tuple-element.36), channel_id=1, source_target_pairs={{0,8},{1,9},{2,10},{3,11},{4,12},{5,13},{6,14},{7,15},{8,0},{9,1},... | collective-permute-start | bytes 221192 | tf_op jit(solution)/shard_map/ppermute | solution.py:378
  12.4 8.9 %collective-permute-start.1 = (f32[72,256]{1,0:T(8,128)S(1)}, f32[72,256]{1,0:T(8,128)S(1)}, u32[]{:S(2)}, u32[]{:S(2)}) collective-permute-start(f32[72,256]{1,0:T(8,128)S(1)} %get-tuple-element.37), channel_id=1, source_target_pairs={{0,16},{1,17},{2,18},{3,19},{4,20},{5,21},{6,22},{7,23},{8,24},{9,... | collective-permute-start | bytes 221192 | tf_op jit(solution)/shard_map/ppermute | solution.py:378
  13.9 12.0 %collective-permute-start.2 = (f32[72,256]{1,0:T(8,128)S(1)}, f32[72,256]{1,0:T(8,128)S(1)}, u32[]{:S(2)}, u32[]{:S(2)}) collective-permute-start(f32[72,256]{1,0:T(8,128)S(1)} %get-tuple-element.38), channel_id=1, source_target_pairs={{0,24},{1,25},{2,26},{3,27},{4,28},{5,29},{6,30},{7,31},{8,16},{9,... | collective-permute-start | bytes 221192 | tf_op jit(solution)/shard_map/ppermute | solution.py:378
  14.1 11.7 %collective-permute-start.3 = (f32[72,256]{1,0:T(8,128)S(1)}, f32[72,256]{1,0:T(8,128)S(1)}, u32[]{:S(2)}, u32[]{:S(2)}) collective-permute-start(f32[72,256]{1,0:T(8,128)S(1)} %get-tuple-element.35.refs_0_), channel_id=1, source_target_pairs={{0,4},{1,5},{2,6},{3,7},{4,0},{5,1},{6,2},{7,3},{8,12},{9,13},{10,... | collective-permute-start | bytes 221192 | tf_op jit(solution)/shard_map/ppermute | solution.py:379
  20.4 5.4 %collective-permute-start.4 = (f32[72,256]{1,0:T(8,128)S(1)}, f32[72,256]{1,0:T(8,128)S(1)}, u32[]{:S(2)}, u32[]{:S(2)}) collective-permute-start(f32[72,256]{1,0:T(8,128)S(1)} %collective-permute-done.refs_1_), channel_id=1, source_target_pairs={{0,4},{1,5},{2,6},{3,7},{4,0},{5,1},{6,2},{7,3},{8,12},{9,13},{10,... | collective-permute-start | bytes 221192 | tf_op jit(solution)/shard_map/ppermute | solution.py:379
  21.3 4.5 %collective-permute-start.5 = (f32[72,256]{1,0:T(8,128)S(1)}, f32[72,256]{1,0:T(8,128)S(1)}, u32[]{:S(2)}, u32[]{:S(2)}) collective-permute-start(f32[72,256]{1,0:T(8,128)S(1)} %collective-permute-done.1.refs_2_), channel_id=1, source_target_pairs={{0,4},{1,5},{2,6},{3,7},{4,0},{5,1},{6,2},{7,3},{8,12},{9,13},{10,... | collective-permute-start | bytes 221192 | tf_op jit(solution)/shard_map/ppermute | solution.py:379
  25.8 1.3 %collective-permute-start.6 = (f32[72,256]{1,0:T(8,128)S(1)}, f32[72,256]{1,0:T(8,128)S(1)}, u32[]{:S(2)}, u32[]{:S(2)}) collective-permute-start(f32[72,256]{1,0:T(8,128)S(1)} %collective-permute-done.2.refs_3_), channel_id=1, source_target_pairs={{0,4},{1,5},{2,6},{3,7},{4,0},{5,1},{6,2},{7,3},{8,12},{9,13},{10,... | collective-permute-start | bytes 221192 | tf_op jit(solution)/shard_map/ppermute | solution.py:379
  27.2 1.4 %collective-permute-start.7 = (f32[8,16,256]{2,1,0:T(8,128)S(1)}, f32[8,16,256]{2,1,0:T(8,128)S(1)}, u32[]{:S(2)}, u32[]{:S(2)}) collective-permute-start(f32[8,16,256]{2,1,0:T(8,128)S(1)} %get-tuple-element.41), channel_id=1, source_target_pairs={{4,8},{8,4},{12,24},{24,12},{28,16},{16,28},{20,17},{17,20},{21,25... | collective-permute-start | bytes 393224 | tf_op jit(solution)/shard_map/ppermute | solution.py:408
  36.5 7.8 %collective-permute-start.8 = (f32[8,32,256]{2,1,0:T(8,128)S(1)}, f32[8,32,256]{2,1,0:T(8,128)S(1)}, u32[]{:S(2)}, u32[]{:S(2)}) collective-permute-start(f32[8,32,256]{2,1,0:T(8,128)S(1)} %shard_map.60.ratio), channel_id=1, source_target_pairs={{4,8},{8,4},{12,24},{24,12},{28,16},{16,28},{20,17},{17,20},{21,25... | collective-permute-start | bytes 786440 | tf_op jit(solution)/shard_map/ppermute | solution.py:431
  38.4 5.8 %collective-permute-start.9 = (f32[8,32,256]{2,1,0:T(8,128)S(1)}, f32[8,32,256]{2,1,0:T(8,128)S(1)}, u32[]{:S(2)}, u32[]{:S(2)}) collective-permute-start(f32[8,32,256]{2,1,0:T(8,128)S(1)} %shard_map.60.ratio), channel_id=1, source_target_pairs={{0,4},{4,0},{8,12},{12,8},{24,28},{28,24},{16,20},{20,16},{17,21},... | collective-permute-start | bytes 786440 | tf_op jit(solution)/shard_map/ppermute | solution.py:431
  46.4 2.6 %collective-permute-start.10 = (f32[8,16,256]{2,1,0:T(8,128)S(1)}, f32[8,16,256]{2,1,0:T(8,128)S(1)}, u32[]{:S(2)}, u32[]{:S(2)}) collective-permute-start(f32[8,16,256]{2,1,0:T(8,128)S(1)} %get-tuple-element.55), channel_id=1, source_target_pairs={{4,8},{8,4},{12,24},{24,12},{28,16},{16,28},{20,17},{17,20},{21,25... | collective-permute-start | bytes 393224 | tf_op jit(solution)/shard_map/ppermute | solution.py:371
  47.1 2.3 %collective-permute-start.11 = (f32[8,16,256]{2,1,0:T(8,128)S(1)}, f32[8,16,256]{2,1,0:T(8,128)S(1)}, u32[]{:S(2)}, u32[]{:S(2)}) collective-permute-start(f32[8,16,256]{2,1,0:T(8,128)S(1)} %get-tuple-element.56), channel_id=1, source_target_pairs={{0,4},{4,0},{8,12},{12,8},{24,28},{28,24},{16,20},{20,16},{17,21},... | collective-permute-start | bytes 393224 | tf_op jit(solution)/shard_map/ppermute | solution.py:372
  50.1 6.0 %collective-permute-start.12 = (f32[2,32,256]{2,1,0:T(8,128)S(1)}, f32[2,32,256]{2,1,0:T(8,128)S(1)}, u32[]{:S(2)}, u32[]{:S(2)}) collective-permute-start(f32[2,32,256]{2,1,0:T(8,128)S(1)} %get-tuple-element.61), channel_id=1, source_target_pairs={{0,8},{1,9},{2,10},{3,11},{4,12},{5,13},{6,14},{7,15},{8,0},{9,1},... | collective-permute-start | bytes 196616 | tf_op jit(solution)/shard_map/ppermute | solution.py:443
  53.4 5.0 %collective-permute-start.13 = (f32[2,32,256]{2,1,0:T(8,128)S(1)}, f32[2,32,256]{2,1,0:T(8,128)S(1)}, u32[]{:S(2)}, u32[]{:S(2)}) collective-permute-start(f32[2,32,256]{2,1,0:T(8,128)S(1)} %get-tuple-element.62), channel_id=1, source_target_pairs={{0,16},{1,17},{2,18},{3,19},{4,20},{5,21},{6,22},{7,23},{8,24},{9,... | collective-permute-start | bytes 196616 | tf_op jit(solution)/shard_map/ppermute | solution.py:443
  54.6 5.2 %collective-permute-start.14 = (f32[2,32,256]{2,1,0:T(8,128)S(1)}, f32[2,32,256]{2,1,0:T(8,128)S(1)}, u32[]{:S(2)}, u32[]{:S(2)}) collective-permute-start(f32[2,32,256]{2,1,0:T(8,128)S(1)} %get-tuple-element.63), channel_id=1, source_target_pairs={{0,24},{1,25},{2,26},{3,27},{4,28},{5,29},{6,30},{7,31},{8,16},{9,... | collective-permute-start | bytes 196616 | tf_op jit(solution)/shard_map/ppermute | solution.py:443
  54.9 4.8 %collective-permute-start.15 = (f32[32,256]{1,0:T(8,128)S(1)}, f32[32,256]{1,0:T(8,128)S(1)}, u32[]{:S(2)}, u32[]{:S(2)}) collective-permute-start(f32[32,256]{1,0:T(8,128)S(1)} %get-tuple-element.64), channel_id=1, source_target_pairs={{0,4},{1,5},{2,6},{3,7},{4,0},{5,1},{6,2},{7,3},{8,12},{9,13},{10,... | collective-permute-start | bytes 98312 | tf_op jit(solution)/shard_map/ppermute | solution.py:444
  56.2 3.6 %collective-permute-start.16 = (f32[32,256]{1,0:T(8,128)S(1)}, f32[32,256]{1,0:T(8,128)S(1)}, u32[]{:S(2)}, u32[]{:S(2)}) collective-permute-start(f32[32,256]{1,0:T(8,128)S(1)} %slice_bitcast_fusion.2), channel_id=1, source_target_pairs={{0,4},{1,5},{2,6},{3,7},{4,0},{5,1},{6,2},{7,3},{8,12},{9,13},{10,... | collective-permute-start | bytes 98312 | tf_op jit(solution)/shard_map/ppermute | solution.py:444
  58.4 1.4 %collective-permute-start.17 = (f32[32,256]{1,0:T(8,128)S(1)}, f32[32,256]{1,0:T(8,128)S(1)}, u32[]{:S(2)}, u32[]{:S(2)}) collective-permute-start(f32[32,256]{1,0:T(8,128)S(1)} %slice_bitcast_fusion.1), channel_id=1, source_target_pairs={{0,4},{1,5},{2,6},{3,7},{4,0},{5,1},{6,2},{7,3},{8,12},{9,13},{10,... | collective-permute-start | bytes 98312 | tf_op jit(solution)/shard_map/ppermute | solution.py:444
  59.8 1.2 %collective-permute-start.18 = (f32[32,256]{1,0:T(8,128)S(1)}, f32[32,256]{1,0:T(8,128)S(1)}, u32[]{:S(2)}, u32[]{:S(2)}) collective-permute-start(f32[32,256]{1,0:T(8,128)S(1)} %slice_bitcast_fusion), channel_id=1, source_target_pairs={{0,4},{1,5},{2,6},{3,7},{4,0},{5,1},{6,2},{7,3},{8,12},{9,13},{10,... | collective-permute-start | bytes 98312 | tf_op jit(solution)/shard_map/ppermute | solution.py:444

commit v8 on v7

--- a/solution.py
+++ b/solution.py
@@ -308,9 +308,9 @@
     payloads(ratio, far, near)
 
 
-def last_kernel(ratio, far, near, band, big_high, big_low, est, *refs):
+def last_kernel(planes, ratio, far, near, band, big_high, big_low, est, *refs):
     (mine, other), pieces, (wide, flat, total) = refs[:2], refs[2:5], refs[5:]
-    widened(wide, ratio, far[...], near, 16)
+    widened(wide, ratio, jnp.where(at_end(planes), 0.0, far[...]), near, 16)
     blurred_into(wide, band, big_high, big_low, flat, total)
     _, _, core, _ = coordinates()
     for flip, x, y, _ in chips():
@@ -428,18 +428,18 @@
         [VMEM] * 9,
         [work(8, 96, 256), work(512, 256), work(512, 256)],
         flops=1 << 30,
-    )(ratio, lax.ppermute(ratio, ALL, ring_pairs), lax.ppermute(ratio, ALL, near_pairs), est, est_far, est_near, *matrices(0, 1, slots))
+    )(ratio, lax.ppermute(ratio, ALL, far_pairs), lax.ppermute(ratio, ALL, near_pairs), est, est_far, est_near, *matrices(0, 1, slots))
     ratio, far, near = call(
         ratio_kernel, (full, half, half), [VMEM] * 6, [work(256, 256), work(256, 256)], flops=1 << 30
     )(est, *matrices(1, 0, slots), data, cover)
     column, pair = shape(32, 256), shape(2, 32, 256)
     mine, other, *away = call(
-        last_kernel,
+        functools.partial(last_kernel, planes),
         (column, column, pair, pair, pair),
         [VMEM] * 7,
         [work(8, 64, 256), work(256, 256), work(256, 256)],
         flops=1 << 30,
-    )(ratio, *exchange(far, near), *matrices(1, 1, ratio), est)
+    )(ratio, lax.ppermute(far, ALL, ring_pairs), lax.ppermute(near, ALL, near_pairs), *matrices(1, 1, ratio), est)
     away = [lax.ppermute(piece, ALL, pairs) for piece, pairs in zip(away, to_chips)]
     others = [lax.ppermute(piece, ALL, to_core) for piece in [other] + [piece[1] for piece in away]]
     out = call(

time: 62.8 us -> 62.1 us (0.989); the launches traced: 61.8 us -> 61.9 us
  starting transfers between devices: 22 us -> 23.8 us
  waiting for transfers between devices: 27.4 us -> 25.7 us
    ppermute x1, starting transfers between devices: 0.01 us -> 2.89 us  [slab_sweep(): lax.ppermute(ratio, ALL, near_pairs)]
    ppermute x3, waiting for transfers between devices: 4.03 us -> 2.01 us  [the longest x1 2 us: slab_sweep(): lax.ppermute(far, ALL, ring_pairs)]
    ppermute x6, starting transfers between devices: 8.37 us -> 7.11 us  [slab_sweep(): lax.ppermute(piece, ALL, pairs)]
  transfers between devices with their start and end apart: 20 -> 20, of which waited for: 10 -> 9; matrix products, arithmetic and copies ran while one was open for 0% -> 0% of each run, Pallas kernels for 8% -> 8%
where the time goes in v8:
time: 62.1 us; the launch traced here: 61.9 us
  waiting for transfers between devices  25.7 us (41%)
  starting transfers between devices  23.8 us (38%)
  Pallas kernels  12.2 us (20%)
    ppermute x6, waiting for transfers between devices, slab_sweep(): lax.ppermute(piece, ALL, pairs)  15 us
    all_to_all x1, starting transfers between devices, slab_sweep(): slots = lax.all_to_all(slots, ALL, split_axis=0, concat_axis=0, tiled=True)  7.3 us
    ppermute x6, starting transfers between devices, slab_sweep(): lax.ppermute(piece, ALL, pairs)  7.11 us
    all_to_all x1, waiting for transfers between devices, slab_sweep(): slots = lax.all_to_all(slots, ALL, split_axis=0, concat_axis=0, tiled=True)  6.23 us
    ppermute x1, starting transfers between devices, slab_sweep(): lax.ppermute(ratio, ALL, near_pairs)  2.89 us
    pallas_call x4, Pallas kernels, matrices(): call(functools.partial(taps_kernel, view, way), (big, big, shape(64, 128,...  2.62 us
    pallas_call x1, Pallas kernels, slab_sweep(): call(functools.partial(lines_kernel, planes), shape(8, 66 * planes, 128),...  2.49 us
    ppermute x1, starting transfers between devices, slab_sweep(): lax.ppermute(far, ALL, ring_pairs)  2.32 us
  transfers between devices with their start and end apart: 20, of which 9 were waited for; matrix products, arithmetic and copies ran while one was open for 0% of the time, Pallas kernels for 8%

profile of v8, /device:TPU:0, one launch (start us, length us, event | category | flops | bytes accessed | tf_op | source)
XLA Modules:
  0.0 61.9 jit_solution(16996031680872869224)
XLA Ops:
  0.0 2.5 %shard_map.55 = f32[8,264,128]{2,1,0:T(8,128)} custom-call(f32[2,4,4,32,256]{4,3,2,1,0:T(8,128)} %bitcast.25, s32[8,128]{1,0:T(8,128)} %bitcast.26), custom_call_target="tpu_custom_call" | custom-call | bytes 1048576 | tf_op jit(solution)/shard_map/pallas_call | solution.py:382
  2.5 7.3 %all-to-all-start = ((f32[32,1,8448]{2,1,0:T(1,128)}), f32[32,1,8448]{2,1,0:T(1,128)S(1)}, u32[]{:S(2)}, u32[]{:S(2)}) async-start(f32[32,1,8448]{2,1,0:T(1,128)} %bitcast.24), calls=%async_computation | async-start | bytes 2162688 | tf_op jit(solution)/shard_map/all_to_all | solution.py:398
  9.9 0.7 %shard_map.56 = (f32[72,256]{1,0:T(8,128)S(1)}, f32[72,256]{1,0:T(8,128)S(1)}, f32[72,256]{1,0:T(8,128)S(1)}, f32[72,256]{1,0:T(8,128)S(1)}) custom-call(s32[2]{0:T(128)S(1)} %bitcast.19, f32[16,2,8,256]{3,2,1,0:T(8,128)S(1)} %bitcast.18), custom_call_target="tpu_custom_call" | custom-call | bytes 1048576 | tf_op jit(solution)/shard_map/pallas_call | solution.py:375
  10.6 1.8 %collective-permute-start = (f32[72,256]{1,0:T(8,128)S(1)}, f32[72,256]{1,0:T(8,128)S(1)}, u32[]{:S(2)}, u32[]{:S(2)}) collective-permute-start(f32[72,256]{1,0:T(8,128)S(1)} %get-tuple-element.36), channel_id=1, source_target_pairs={{0,8},{1,9},{2,10},{3,11},{4,12},{5,13},{6,14},{7,15},{8,0},{9,1},... | collective-permute-start | bytes 221192 | tf_op jit(solution)/shard_map/ppermute | solution.py:378
  12.4 1.5 %collective-permute-start.1 = (f32[72,256]{1,0:T(8,128)S(1)}, f32[72,256]{1,0:T(8,128)S(1)}, u32[]{:S(2)}, u32[]{:S(2)}) collective-permute-start(f32[72,256]{1,0:T(8,128)S(1)} %get-tuple-element.37), channel_id=1, source_target_pairs={{0,16},{1,17},{2,18},{3,19},{4,20},{5,21},{6,22},{7,23},{8,24},{9,... | collective-permute-start | bytes 221192 | tf_op jit(solution)/shard_map/ppermute | solution.py:378
  14.1 6.3 %collective-permute-done.refs_1_ = f32[72,256]{1,0:T(8,128)S(1)} collective-permute-done((f32[72,256]{1,0:T(8,128)S(1)}, f32[72,256]{1,0:T(8,128)S(1)}, u32[]{:S(2)}, u32[]{:S(2)}) %collective-permute-start) | collective-permute-done | bytes 73760 | tf_op jit(solution)/shard_map/ppermute | solution.py:378
  20.4 0.9 %collective-permute-done.1.refs_2_ = f32[72,256]{1,0:T(8,128)S(1)} collective-permute-done((f32[72,256]{1,0:T(8,128)S(1)}, f32[72,256]{1,0:T(8,128)S(1)}, u32[]{:S(2)}, u32[]{:S(2)}) %collective-permute-start.1) | collective-permute-done | bytes 73760 | tf_op jit(solution)/shard_map/ppermute | solution.py:378
  21.3 4.5 %collective-permute-done.2.refs_3_ = f32[72,256]{1,0:T(8,128)S(1)} collective-permute-done((f32[72,256]{1,0:T(8,128)S(1)}, f32[72,256]{1,0:T(8,128)S(1)}, u32[]{:S(2)}, u32[]{:S(2)}) %collective-permute-start.2) | collective-permute-done | bytes 73760 | tf_op jit(solution)/shard_map/ppermute | solution.py:378
  25.9 1.2 %collective-permute-done.6.refs_7_ = f32[72,256]{1,0:T(8,128)S(1)} collective-permute-done((f32[72,256]{1,0:T(8,128)S(1)}, f32[72,256]{1,0:T(8,128)S(1)}, u32[]{:S(2)}, u32[]{:S(2)}) %collective-permute-start.6) | collective-permute-done | bytes 73760 | tf_op jit(solution)/shard_map/ppermute | solution.py:379
  27.2 0.7 %collective-permute-start.7 = (f32[8,16,256]{2,1,0:T(8,128)S(1)}, f32[8,16,256]{2,1,0:T(8,128)S(1)}, u32[]{:S(2)}, u32[]{:S(2)}) collective-permute-start(f32[8,16,256]{2,1,0:T(8,128)S(1)} %get-tuple-element.41), channel_id=1, source_target_pairs={{4,8},{8,4},{12,24},{24,12},{28,16},{16,28},{20,17},{17,20},{21,25... | collective-permute-start | bytes 393224 | tf_op jit(solution)/shard_map/ppermute | solution.py:408
  27.9 0.7 %shard_map.58 = (bf16[5,256,256]{2,1,0:T(8,128)(2,1)S(1)}, bf16[5,256,256]{2,1,0:T(8,128)(2,1)S(1)}, bf16[64,128]{1,0:T(8,128)(2,1)S(1)}) custom-call(f32[3,2,33]{2,1,0:T(2,128)S(1)} %bitcast.20, f32[8,32,256]{2,1,0:T(8,128)S(1)} %get-tuple-element.40._.est), custom_call_target="tpu_custom_call" | custom-call | flops 1073741824 | bytes 1048576 | tf_op jit(solution)/shard_map/pallas_call | solution.py:411
  28.6 0.8 %shard_map.59.blurred = f32[256,256]{1,0:T(8,128)S(1)} custom-call(f32[8,32,256]{2,1,0:T(8,128)S(1)} %get-tuple-element.40._.est, f32[8,16,256]{2,1,0:T(8,128)S(1)} %collective-permute-done.7.far.est_far, f32[8,16,256]{2,1,0:T(8,128)S(1)} %get-tuple-element.42.near.est_near, bf16[64,128]{1,0:T(8,128)(2,1)S(1)} %get-tuple-element.43.band, ...), custom_call_target="tpu_custom_call" | custom-call | flops 1073741824 | bytes 1048576 | tf_op jit(solution)/shard_map/pallas_call | solution.py:420
  29.4 6.2 %all-to-all-done = f32[32,1,8448]{2,1,0:T(1,128)S(1)} async-done(((f32[32,1,8448]{2,1,0:T(1,128)}), f32[32,1,8448]{2,1,0:T(1,128)S(1)}, u32[]{:S(2)}, u32[]{:S(2)}) %all-to-all-start) | async-done | bytes 1081376 | tf_op jit(solution)/shard_map/all_to_all | solution.py:398
  35.6 0.9 %shard_map.60.ratio = f32[8,32,256]{2,1,0:T(8,128)S(1)} custom-call(f32[8,264,128]{2,1,0:T(8,128)S(1)} %bitcast.14, f32[8,8,256]{2,1,0:T(8,128)S(1)} %get-tuple-element.39.weights, f32[256,256]{1,0:T(8,128)S(1)} %shard_map.59.blurred), custom_call_target="tpu_custom_call" | custom-call | flops 1073741824 | bytes 1048576 | tf_op jit(solution)/shard_map/pallas_call | solution.py:423
  36.5 0.7 %collective-permute-start.8 = (f32[8,32,256]{2,1,0:T(8,128)S(1)}, f32[8,32,256]{2,1,0:T(8,128)S(1)}, u32[]{:S(2)}, u32[]{:S(2)}) collective-permute-start(f32[8,32,256]{2,1,0:T(8,128)S(1)} %shard_map.60.ratio), channel_id=1, source_target_pairs={{4,8},{8,4},{12,24},{24,12},{28,16},{16,28},{20,17},{17,20},{21,25... | collective-permute-start | bytes 786440 | tf_op jit(solution)/shard_map/ppermute | solution.py:431
  37.1 2.9 %collective-permute-start.9 = (f32[8,32,256]{2,1,0:T(8,128)S(1)}, f32[8,32,256]{2,1,0:T(8,128)S(1)}, u32[]{:S(2)}, u32[]{:S(2)}) collective-permute-start(f32[8,32,256]{2,1,0:T(8,128)S(1)} %shard_map.60.ratio), channel_id=1, source_target_pairs={{0,4},{4,0},{8,12},{12,8},{24,28},{28,24},{16,20},{20,16},{17,21},... | collective-permute-start | bytes 786440 | tf_op jit(solution)/shard_map/ppermute | solution.py:431
  40.0 0.6 shard_map.61
  40.6 0.8 %shard_map.64 = (f32[8,32,256]{2,1,0:T(8,128)S(1)}, f32[8,8,256]{2,1,0:T(8,128)S(1)}) custom-call(f32[8,264,128]{2,1,0:T(8,128)S(1)} %bitcast.16, f32[8,8,256]{2,1,0:T(8,128)S(1)} %get-tuple-element.39.weights), custom_call_target="tpu_custom_call" | custom-call | flops 1073741824 | bytes 1048576 | tf_op jit(solution)/shard_map/pallas_call | solution.py:424
  41.5 0.7 %shard_map.63 = (bf16[5,256,256]{2,1,0:T(8,128)(2,1)S(1)}, bf16[5,256,256]{2,1,0:T(8,128)(2,1)S(1)}, bf16[64,128]{1,0:T(8,128)(2,1)S(1)}) custom-call(f32[3,2,33]{2,1,0:T(2,128)S(1)} %bitcast.22, f32[8,264,128]{2,1,0:T(8,128)S(1)} %bitcast.17), custom_call_target="tpu_custom_call" | custom-call | flops 1073741824 | bytes 1048576 | tf_op jit(solution)/shard_map/pallas_call | solution.py:411
  42.2 1.4 %shard_map.62.est = f32[8,64,256]{2,1,0:T(8,128)S(1)} custom-call(f32[8,32,256]{2,1,0:T(8,128)S(1)} %shard_map.60.ratio, f32[8,32,256]{2,1,0:T(8,128)S(1)} %collective-permute-done.8.ratio_far, f32[8,32,256]{2,1,0:T(8,128)S(1)} %collective-permute-done.9.ratio_near, f32[8,32,256]{2,1,0:T(8,128)S(1)} %get-tuple-element.40._.est, ...), custom_call_target="tpu_custom_call" | custom-call | flops 1073741824 | bytes 1048576 | tf_op jit(solution)/shard_map/pallas_call | solution.py:425
  43.6 0.8 %shard_map.65 = (f32[8,32,256]{2,1,0:T(8,128)S(1)}, f32[8,16,256]{2,1,0:T(8,128)S(1)}, f32[8,16,256]{2,1,0:T(8,128)S(1)}) custom-call(f32[8,64,256]{2,1,0:T(8,128)S(1)} %shard_map.62.est, bf16[64,128]{1,0:T(8,128)(2,1)S(1)} %get-tuple-element.49.band, bf16[5,256,256]{2,1,0:T(8,128)(2,1)S(1)} %get-tuple-element.50.high, ...), custom_call_target="tpu_custom_call" | custom-call | flops 1073741824 | bytes 1048576 | tf_op jit(solution)/shard_map/pallas_call | solution.py:432
  44.4 2.3 %collective-permute-start.10 = (f32[8,16,256]{2,1,0:T(8,128)S(1)}, f32[8,16,256]{2,1,0:T(8,128)S(1)}, u32[]{:S(2)}, u32[]{:S(2)}) collective-permute-start(f32[8,16,256]{2,1,0:T(8,128)S(1)} %get-tuple-element.55), channel_id=1, source_target_pairs={{4,8},{8,4},{12,24},{24,12},{28,16},{16,28},{20,17},{17,20},{21,25... | collective-permute-start | bytes 393224 | tf_op jit(solution)/shard_map/ppermute | solution.py:442
  46.7 1.3 %collective-permute-start.11 = (f32[8,16,256]{2,1,0:T(8,128)S(1)}, f32[8,16,256]{2,1,0:T(8,128)S(1)}, u32[]{:S(2)}, u32[]{:S(2)}) collective-permute-start(f32[8,16,256]{2,1,0:T(8,128)S(1)} %get-tuple-element.56), channel_id=1, source_target_pairs={{0,4},{4,0},{8,12},{12,8},{24,28},{28,24},{16,20},{20,16},{17,21},... | collective-permute-start | bytes 393224 | tf_op jit(solution)/shard_map/ppermute | solution.py:442
  48.6 2.0 %collective-permute-done.10.far = f32[8,16,256]{2,1,0:T(8,128)S(1)} collective-permute-done((f32[8,16,256]{2,1,0:T(8,128)S(1)}, f32[8,16,256]{2,1,0:T(8,128)S(1)}, u32[]{:S(2)}, u32[]{:S(2)}) %collective-permute-start.10) | collective-permute-done | bytes 131104 | tf_op jit(solution)/shard_map/ppermute | solution.py:442
  50.6 0.8 %shard_map.67 = (f32[32,256]{1,0:T(8,128)S(1)}, f32[32,256]{1,0:T(8,128)S(1)}, f32[2,32,256]{2,1,0:T(8,128)S(1)}, f32[2,32,256]{2,1,0:T(8,128)S(1)}, f32[2,32,256]{2,1,0:T(8,128)S(1)}) custom-call(f32[8,32,256]{2,1,0:T(8,128)S(1)} %get-tuple-element.54._.ratio, f32[8,16,256]{2,1,0:T(8,128)S(1)} %collective-permute-done.10.far, ...), custom_call_target="tpu_custom_call" | custom-call | flops 1073741824 | bytes 1048576 | tf_op jit(solution)/shard_map/pallas_call | solution.py:436
  51.5 1.7 %collective-permute-start.12 = (f32[2,32,256]{2,1,0:T(8,128)S(1)}, f32[2,32,256]{2,1,0:T(8,128)S(1)}, u32[]{:S(2)}, u32[]{:S(2)}) collective-permute-start(f32[2,32,256]{2,1,0:T(8,128)S(1)} %get-tuple-element.61), channel_id=1, source_target_pairs={{0,8},{1,9},{2,10},{3,11},{4,12},{5,13},{6,14},{7,15},{8,0},{9,1},... | collective-permute-start | bytes 196616 | tf_op jit(solution)/shard_map/ppermute | solution.py:443
  53.2 1.5 %collective-permute-start.13 = (f32[2,32,256]{2,1,0:T(8,128)S(1)}, f32[2,32,256]{2,1,0:T(8,128)S(1)}, u32[]{:S(2)}, u32[]{:S(2)}) collective-permute-start(f32[2,32,256]{2,1,0:T(8,128)S(1)} %get-tuple-element.62), channel_id=1, source_target_pairs={{0,16},{1,17},{2,18},{3,19},{4,20},{5,21},{6,22},{7,23},{8,24},{9,... | collective-permute-start | bytes 196616 | tf_op jit(solution)/shard_map/ppermute | solution.py:443
  55.1 0.9 %collective-permute-start.15 = (f32[32,256]{1,0:T(8,128)S(1)}, f32[32,256]{1,0:T(8,128)S(1)}, u32[]{:S(2)}, u32[]{:S(2)}) collective-permute-start(f32[32,256]{1,0:T(8,128)S(1)} %get-tuple-element.64), channel_id=1, source_target_pairs={{0,4},{1,5},{2,6},{3,7},{4,0},{5,1},{6,2},{7,3},{8,12},{9,13},{10,... | collective-permute-start | bytes 98312 | tf_op jit(solution)/shard_map/ppermute | solution.py:444
  56.4 1.4 %collective-permute-done.13.refs_2_ = f32[2,32,256]{2,1,0:T(8,128)S(1)} collective-permute-done((f32[2,32,256]{2,1,0:T(8,128)S(1)}, f32[2,32,256]{2,1,0:T(8,128)S(1)}, u32[]{:S(2)}, u32[]{:S(2)}) %collective-permute-start.13) | collective-permute-done | bytes 65568 | tf_op jit(solution)/shard_map/ppermute | solution.py:443
  58.0 1.9 %collective-permute-done.14.refs_3_ = f32[2,32,256]{2,1,0:T(8,128)S(1)} collective-permute-done((f32[2,32,256]{2,1,0:T(8,128)S(1)}, f32[2,32,256]{2,1,0:T(8,128)S(1)}, u32[]{:S(2)}, u32[]{:S(2)}) %collective-permute-start.14) | collective-permute-done | bytes 65568 | tf_op jit(solution)/shard_map/ppermute | solution.py:443
  59.9 1.2 %collective-permute-done.18.refs_7_ = f32[32,256]{1,0:T(8,128)S(1)} collective-permute-done((f32[32,256]{1,0:T(8,128)S(1)}, f32[32,256]{1,0:T(8,128)S(1)}, u32[]{:S(2)}, u32[]{:S(2)}) %collective-permute-start.18) | collective-permute-done | bytes 32800 | tf_op jit(solution)/shard_map/ppermute | solution.py:444
  61.0 0.9 %shard_map.68 = f32[16,2,8,256]{3,2,1,0:T(8,128)} custom-call(f32[32,256]{1,0:T(8,128)S(1)} %get-tuple-element.60.refs_0_, f32[2,32,256]{2,1,0:T(8,128)S(1)} %collective-permute-done.12.refs_1_, f32[2,32,256]{2,1,0:T(8,128)S(1)} %collective-permute-done.13.refs_2_, f32[2,32,256]{2,1,0:T(8,128)S(1)} %collective-permute-done.14.refs_3_, ...), custom_call_target="tpu_custom_call" | custom-call | bytes 1048576 | tf_op jit(solution)/shard_map/pallas_call | solution.py:445
  (31 shorter events, 2.0 us)
Async XLA Ops:
  2.5 7.3 %copy-start = (f32[16,16,256]{2,1,0:T(8,128)S(1)}, f32[16,16,256]{2,1,0:T(8,128)}, u32[]{:S(2)}) copy-start(f32[16,16,256]{2,1,0:T(8,128)} %param.5) | copy-start | bytes 786436
  2.5 7.3 %copy-start.1 = (s32[2,1,1,1]{0,3,2,1:T(1,128)S(1)}, s32[2,1,1,1]{0,3,2,1:T(1,128)}, u32[]{:S(2)}) copy-start(s32[2,1,1,1]{0,3,2,1:T(1,128)} %param.9) | copy-start | bytes 28
  2.5 25.3 %copy-start.2 = (f32[2,3,33]{2,0,1:T(2,128)S(1)}, f32[2,3,33]{2,0,1:T(2,128)}, u32[]{:S(2)}) copy-start(f32[2,3,33]{2,0,1:T(2,128)} %param.8) | copy-start | bytes 2380
  2.5 33.0 %all-to-all-start = ((f32[32,1,8448]{2,1,0:T(1,128)}), f32[32,1,8448]{2,1,0:T(1,128)S(1)}, u32[]{:S(2)}, u32[]{:S(2)}) async-start(f32[32,1,8448]{2,1,0:T(1,128)} %bitcast.24), calls=%async_computation | async-start | bytes 2162688 | tf_op jit(solution)/shard_map/all_to_all | solution.py:398
  10.6 9.9 %collective-permute-start = (f32[72,256]{1,0:T(8,128)S(1)}, f32[72,256]{1,0:T(8,128)S(1)}, u32[]{:S(2)}, u32[]{:S(2)}) collective-permute-start(f32[72,256]{1,0:T(8,128)S(1)} %get-tuple-element.36), channel_id=1, source_target_pairs={{0,8},{1,9},{2,10},{3,11},{4,12},{5,13},{6,14},{7,15},{8,0},{9,1},... | collective-permute-start | bytes 221192 | tf_op jit(solution)/shard_map/ppermute | solution.py:378
  12.4 8.9 %collective-permute-start.1 = (f32[72,256]{1,0:T(8,128)S(1)}, f32[72,256]{1,0:T(8,128)S(1)}, u32[]{:S(2)}, u32[]{:S(2)}) collective-permute-start(f32[72,256]{1,0:T(8,128)S(1)} %get-tuple-element.37), channel_id=1, source_target_pairs={{0,16},{1,17},{2,18},{3,19},{4,20},{5,21},{6,22},{7,23},{8,24},{9,... | collective-permute-start | bytes 221192 | tf_op jit(solution)/shard_map/ppermute | solution.py:378
  13.9 12.0 %collective-permute-start.2 = (f32[72,256]{1,0:T(8,128)S(1)}, f32[72,256]{1,0:T(8,128)S(1)}, u32[]{:S(2)}, u32[]{:S(2)}) collective-permute-start(f32[72,256]{1,0:T(8,128)S(1)} %get-tuple-element.38), channel_id=1, source_target_pairs={{0,24},{1,25},{2,26},{3,27},{4,28},{5,29},{6,30},{7,31},{8,16},{9,... | collective-permute-start | bytes 221192 | tf_op jit(solution)/shard_map/ppermute | solution.py:378
  14.1 11.7 %collective-permute-start.3 = (f32[72,256]{1,0:T(8,128)S(1)}, f32[72,256]{1,0:T(8,128)S(1)}, u32[]{:S(2)}, u32[]{:S(2)}) collective-permute-start(f32[72,256]{1,0:T(8,128)S(1)} %get-tuple-element.35.refs_0_), channel_id=1, source_target_pairs={{0,4},{1,5},{2,6},{3,7},{4,0},{5,1},{6,2},{7,3},{8,12},{9,13},{10,... | collective-permute-start | bytes 221192 | tf_op jit(solution)/shard_map/ppermute | solution.py:379
  20.4 5.4 %collective-permute-start.4 = (f32[72,256]{1,0:T(8,128)S(1)}, f32[72,256]{1,0:T(8,128)S(1)}, u32[]{:S(2)}, u32[]{:S(2)}) collective-permute-start(f32[72,256]{1,0:T(8,128)S(1)} %collective-permute-done.refs_1_), channel_id=1, source_target_pairs={{0,4},{1,5},{2,6},{3,7},{4,0},{5,1},{6,2},{7,3},{8,12},{9,13},{10,... | collective-permute-start | bytes 221192 | tf_op jit(solution)/shard_map/ppermute | solution.py:379
  21.3 4.5 %collective-permute-start.5 = (f32[72,256]{1,0:T(8,128)S(1)}, f32[72,256]{1,0:T(8,128)S(1)}, u32[]{:S(2)}, u32[]{:S(2)}) collective-permute-start(f32[72,256]{1,0:T(8,128)S(1)} %collective-permute-done.1.refs_2_), channel_id=1, source_target_pairs={{0,4},{1,5},{2,6},{3,7},{4,0},{5,1},{6,2},{7,3},{8,12},{9,13},{10,... | collective-permute-start | bytes 221192 | tf_op jit(solution)/shard_map/ppermute | solution.py:379
  25.8 1.3 %collective-permute-start.6 = (f32[72,256]{1,0:T(8,128)S(1)}, f32[72,256]{1,0:T(8,128)S(1)}, u32[]{:S(2)}, u32[]{:S(2)}) collective-permute-start(f32[72,256]{1,0:T(8,128)S(1)} %collective-permute-done.2.refs_3_), channel_id=1, source_target_pairs={{0,4},{1,5},{2,6},{3,7},{4,0},{5,1},{6,2},{7,3},{8,12},{9,13},{10,... | collective-permute-start | bytes 221192 | tf_op jit(solution)/shard_map/ppermute | solution.py:379
  27.2 1.4 %collective-permute-start.7 = (f32[8,16,256]{2,1,0:T(8,128)S(1)}, f32[8,16,256]{2,1,0:T(8,128)S(1)}, u32[]{:S(2)}, u32[]{:S(2)}) collective-permute-start(f32[8,16,256]{2,1,0:T(8,128)S(1)} %get-tuple-element.41), channel_id=1, source_target_pairs={{4,8},{8,4},{12,24},{24,12},{28,16},{16,28},{20,17},{17,20},{21,25... | collective-permute-start | bytes 393224 | tf_op jit(solution)/shard_map/ppermute | solution.py:408
  36.5 5.7 %collective-permute-start.8 = (f32[8,32,256]{2,1,0:T(8,128)S(1)}, f32[8,32,256]{2,1,0:T(8,128)S(1)}, u32[]{:S(2)}, u32[]{:S(2)}) collective-permute-start(f32[8,32,256]{2,1,0:T(8,128)S(1)} %shard_map.60.ratio), channel_id=1, source_target_pairs={{4,8},{8,4},{12,24},{24,12},{28,16},{16,28},{20,17},{17,20},{21,25... | collective-permute-start | bytes 786440 | tf_op jit(solution)/shard_map/ppermute | solution.py:431
  37.1 5.1 %collective-permute-start.9 = (f32[8,32,256]{2,1,0:T(8,128)S(1)}, f32[8,32,256]{2,1,0:T(8,128)S(1)}, u32[]{:S(2)}, u32[]{:S(2)}) collective-permute-start(f32[8,32,256]{2,1,0:T(8,128)S(1)} %shard_map.60.ratio), channel_id=1, source_target_pairs={{0,4},{4,0},{8,12},{12,8},{24,28},{28,24},{16,20},{20,16},{17,21},... | collective-permute-start | bytes 786440 | tf_op jit(solution)/shard_map/ppermute | solution.py:431
  44.4 6.3 %collective-permute-start.10 = (f32[8,16,256]{2,1,0:T(8,128)S(1)}, f32[8,16,256]{2,1,0:T(8,128)S(1)}, u32[]{:S(2)}, u32[]{:S(2)}) collective-permute-start(f32[8,16,256]{2,1,0:T(8,128)S(1)} %get-tuple-element.55), channel_id=1, source_target_pairs={{4,8},{8,4},{12,24},{24,12},{28,16},{16,28},{20,17},{17,20},{21,25... | collective-permute-start | bytes 393224 | tf_op jit(solution)/shard_map/ppermute | solution.py:442
  46.7 3.9 %collective-permute-start.11 = (f32[8,16,256]{2,1,0:T(8,128)S(1)}, f32[8,16,256]{2,1,0:T(8,128)S(1)}, u32[]{:S(2)}, u32[]{:S(2)}) collective-permute-start(f32[8,16,256]{2,1,0:T(8,128)S(1)} %get-tuple-element.56), channel_id=1, source_target_pairs={{0,4},{4,0},{8,12},{12,8},{24,28},{28,24},{16,20},{20,16},{17,21},... | collective-permute-start | bytes 393224 | tf_op jit(solution)/shard_map/ppermute | solution.py:442
  51.5 4.4 %collective-permute-start.12 = (f32[2,32,256]{2,1,0:T(8,128)S(1)}, f32[2,32,256]{2,1,0:T(8,128)S(1)}, u32[]{:S(2)}, u32[]{:S(2)}) collective-permute-start(f32[2,32,256]{2,1,0:T(8,128)S(1)} %get-tuple-element.61), channel_id=1, source_target_pairs={{0,8},{1,9},{2,10},{3,11},{4,12},{5,13},{6,14},{7,15},{8,0},{9,1},... | collective-permute-start | bytes 196616 | tf_op jit(solution)/shard_map/ppermute | solution.py:443
  53.2 4.7 %collective-permute-start.13 = (f32[2,32,256]{2,1,0:T(8,128)S(1)}, f32[2,32,256]{2,1,0:T(8,128)S(1)}, u32[]{:S(2)}, u32[]{:S(2)}) collective-permute-start(f32[2,32,256]{2,1,0:T(8,128)S(1)} %get-tuple-element.62), channel_id=1, source_target_pairs={{0,16},{1,17},{2,18},{3,19},{4,20},{5,21},{6,22},{7,23},{8,24},{9,... | collective-permute-start | bytes 196616 | tf_op jit(solution)/shard_map/ppermute | solution.py:443
  54.7 5.2 %collective-permute-start.14 = (f32[2,32,256]{2,1,0:T(8,128)S(1)}, f32[2,32,256]{2,1,0:T(8,128)S(1)}, u32[]{:S(2)}, u32[]{:S(2)}) collective-permute-start(f32[2,32,256]{2,1,0:T(8,128)S(1)} %get-tuple-element.63), channel_id=1, source_target_pairs={{0,24},{1,25},{2,26},{3,27},{4,28},{5,29},{6,30},{7,31},{8,16},{9,... | collective-permute-start | bytes 196616 | tf_op jit(solution)/shard_map/ppermute | solution.py:443
  55.1 4.8 %collective-permute-start.15 = (f32[32,256]{1,0:T(8,128)S(1)}, f32[32,256]{1,0:T(8,128)S(1)}, u32[]{:S(2)}, u32[]{:S(2)}) collective-permute-start(f32[32,256]{1,0:T(8,128)S(1)} %get-tuple-element.64), channel_id=1, source_target_pairs={{0,4},{1,5},{2,6},{3,7},{4,0},{5,1},{6,2},{7,3},{8,12},{9,13},{10,... | collective-permute-start | bytes 98312 | tf_op jit(solution)/shard_map/ppermute | solution.py:444
  55.9 3.9 %collective-permute-start.16 = (f32[32,256]{1,0:T(8,128)S(1)}, f32[32,256]{1,0:T(8,128)S(1)}, u32[]{:S(2)}, u32[]{:S(2)}) collective-permute-start(f32[32,256]{1,0:T(8,128)S(1)} %slice_bitcast_fusion.2), channel_id=1, source_target_pairs={{0,4},{1,5},{2,6},{3,7},{4,0},{5,1},{6,2},{7,3},{8,12},{9,13},{10,... | collective-permute-start | bytes 98312 | tf_op jit(solution)/shard_map/ppermute | solution.py:444
  57.8 2.0 %collective-permute-start.17 = (f32[32,256]{1,0:T(8,128)S(1)}, f32[32,256]{1,0:T(8,128)S(1)}, u32[]{:S(2)}, u32[]{:S(2)}) collective-permute-start(f32[32,256]{1,0:T(8,128)S(1)} %slice_bitcast_fusion.1), channel_id=1, source_target_pairs={{0,4},{1,5},{2,6},{3,7},{4,0},{5,1},{6,2},{7,3},{8,12},{9,13},{10,... | collective-permute-start | bytes 98312 | tf_op jit(solution)/shard_map/ppermute | solution.py:444
  59.8 1.2 %collective-permute-start.18 = (f32[32,256]{1,0:T(8,128)S(1)}, f32[32,256]{1,0:T(8,128)S(1)}, u32[]{:S(2)}, u32[]{:S(2)}) collective-permute-start(f32[32,256]{1,0:T(8,128)S(1)} %slice_bitcast_fusion), channel_id=1, source_target_pairs={{0,4},{1,5},{2,6},{3,7},{4,0},{5,1},{6,2},{7,3},{8,12},{9,13},{10,... | collective-permute-start | bytes 98312 | tf_op jit(solution)/shard_map/ppermute | solution.py:444

commit v9 on v8

--- a/solution.py
+++ b/solution.py
@@ -309,7 +309,7 @@
 
 
 def last_kernel(planes, ratio, far, near, band, big_high, big_low, est, *refs):
-    (mine, other), pieces, (wide, flat, total) = refs[:2], refs[2:5], refs[5:]
+    (mine, other), pieces, (wide, flat, total) = refs[:2], refs[2:6], refs[6:]
     widened(wide, ratio, jnp.where(at_end(planes), 0.0, far[...]), near, 16)
     blurred_into(wide, band, big_high, big_low, flat, total)
     _, _, core, _ = coordinates()
@@ -327,6 +327,8 @@
             )
             if flip == 0:
                 (mine, other)[turn][...] = new
+            elif flip == 3:
+                pieces[2 + turn][...] = new
             else:
                 pieces[flip - 1][turn] = new
 
@@ -335,7 +337,7 @@
     pieces, others, (out, held, turned, left) = refs[:4], refs[4:8], refs[8:]
     upper = upper_half()
     for flip, _, _, place in chips():
-        mine = pieces[flip][...] if flip == 0 else pieces[flip][0]
+        mine = pieces[flip][0] if flip in (1, 2) else pieces[flip][...]
         held[pl.ds(pl.multiple_of(64 * place + 32 * upper, 32), 32), :] = mine
         held[pl.ds(pl.multiple_of(64 * place + 32 - 32 * upper, 32), 32), :] = others[flip][...]
 
@@ -357,12 +359,12 @@
     def flipped(by):
         return [(d * planes + z, (d ^ by) * planes + z) for d in range(8) for z in range(planes)]
 
-    return [flipped(by) for by in (2, 4, 6)], flipped(1)
+    return [flipped(by) for by in (2, 4, 6)], flipped(7), flipped(1)
 
 
 def slab_sweep(planes, estimate, raw_lines, line_index, psf, view_weight):
     far_pairs, near_pairs = chain_pairs(planes)
-    to_chips, to_core = swaps(planes)
+    to_chips, to_far_core, to_core = swaps(planes)
     ends = sorted(set(range(8 * planes)) - {source for source, _ in far_pairs})
     ring_pairs = far_pairs + [tuple(ends), tuple(ends[::-1])]
 
@@ -435,13 +437,14 @@
     column, pair = shape(32, 256), shape(2, 32, 256)
     mine, other, *away = call(
         functools.partial(last_kernel, planes),
-        (column, column, pair, pair, pair),
+        (column, column, pair, pair, column, column),
         [VMEM] * 7,
         [work(8, 64, 256), work(256, 256), work(256, 256)],
         flops=1 << 30,
     )(ratio, lax.ppermute(far, ALL, ring_pairs), lax.ppermute(near, ALL, near_pairs), *matrices(1, 1, ratio), est)
-    away = [lax.ppermute(piece, ALL, pairs) for piece, pairs in zip(away, to_chips)]
-    others = [lax.ppermute(piece, ALL, to_core) for piece in [other] + [piece[1] for piece in away]]
+    *away, last = [lax.ppermute(piece, ALL, pairs) for piece, pairs in zip(away, to_chips + [to_far_core])]
+    others = [lax.ppermute(piece, ALL, to_core) for piece in [other] + [piece[1] for piece in away[:2]]]
+    others.append(last)
     out = call(
         join_kernel,
         shape(16, 2, 8, 256),

time: 62.1 us -> 61.4 us (0.989)
  waiting for transfers between devices: 25.7 us -> 23.4 us
  starting transfers between devices: 23.8 us -> 25.4 us
    ppermute x6 -> x7, starting transfers between devices: 7.11 us -> 8.89 us  [slab_sweep(): lax.ppermute(piece, ALL, pairs)]
    ppermute x4 -> x3, waiting for transfers between devices: 1.19 us -> 0.01 us  [slab_sweep(): lax.ppermute(piece, ALL, to_core)]
    ppermute x6 -> x7, waiting for transfers between devices: 15 us -> 13.9 us  [slab_sweep(): lax.ppermute(piece, ALL, pairs)]
    ppermute x4 -> x3, starting transfers between devices: 1.46 us -> 1.27 us  [slab_sweep(): lax.ppermute(piece, ALL, to_core)]
where the time goes in v9:
time: 61.4 us; the launch traced here: 61.2 us
  starting transfers between devices  25.4 us (41%)
  waiting for transfers between devices  23.4 us (38%)
  Pallas kernels  12.2 us (20%)
    ppermute x7, waiting for transfers between devices, slab_sweep(): lax.ppermute(piece, ALL, pairs)  13.9 us
    ppermute x7, starting transfers between devices, slab_sweep(): lax.ppermute(piece, ALL, pairs)  8.89 us
    all_to_all x1, starting transfers between devices, slab_sweep(): slots = lax.all_to_all(slots, ALL, split_axis=0, concat_axis=0, tiled=True)  7.3 us
    all_to_all x1, waiting for transfers between devices, slab_sweep(): slots = lax.all_to_all(slots, ALL, split_axis=0, concat_axis=0, tiled=True)  6.23 us
    ppermute x1, starting transfers between devices, slab_sweep(): lax.ppermute(ratio, ALL, near_pairs)  2.89 us
    pallas_call x4, Pallas kernels, matrices(): call(functools.partial(taps_kernel, view, way), (big, big, shape(64, 128,...  2.62 us
    pallas_call x1, Pallas kernels, slab_sweep(): call(functools.partial(lines_kernel, planes), shape(8, 66 * planes, 128),...  2.49 us
    ppermute x1, starting transfers between devices, slab_sweep(): lax.ppermute(far, ALL, ring_pairs)  2.32 us
  transfers between devices with their start and end apart: 20, of which 9 were waited for; matrix products, arithmetic and copies ran while one was open for 0% of the time, Pallas kernels for 8%

profile of v9, /device:TPU:0, one launch (start us, length us, event | category | flops | bytes accessed | tf_op | source)
XLA Modules:
  0.0 61.2 jit_solution(14729724180918725005)
XLA Ops:
  0.0 2.5 %shard_map.55 = f32[8,264,128]{2,1,0:T(8,128)} custom-call(f32[2,4,4,32,256]{4,3,2,1,0:T(8,128)} %bitcast.23, s32[8,128]{1,0:T(8,128)} %bitcast.24), custom_call_target="tpu_custom_call" | custom-call | bytes 1048576 | tf_op jit(solution)/shard_map/pallas_call | solution.py:384
  2.5 7.3 %all-to-all-start = ((f32[32,1,8448]{2,1,0:T(1,128)}), f32[32,1,8448]{2,1,0:T(1,128)S(1)}, u32[]{:S(2)}, u32[]{:S(2)}) async-start(f32[32,1,8448]{2,1,0:T(1,128)} %bitcast.22), calls=%async_computation | async-start | bytes 2162688 | tf_op jit(solution)/shard_map/all_to_all | solution.py:400
  9.9 0.7 %shard_map.56 = (f32[72,256]{1,0:T(8,128)S(1)}, f32[72,256]{1,0:T(8,128)S(1)}, f32[72,256]{1,0:T(8,128)S(1)}, f32[72,256]{1,0:T(8,128)S(1)}) custom-call(s32[2]{0:T(128)S(1)} %bitcast.17, f32[16,2,8,256]{3,2,1,0:T(8,128)S(1)} %bitcast.16), custom_call_target="tpu_custom_call" | custom-call | bytes 1048576 | tf_op jit(solution)/shard_map/pallas_call | solution.py:377
  10.6 1.8 %collective-permute-start = (f32[72,256]{1,0:T(8,128)S(1)}, f32[72,256]{1,0:T(8,128)S(1)}, u32[]{:S(2)}, u32[]{:S(2)}) collective-permute-start(f32[72,256]{1,0:T(8,128)S(1)} %get-tuple-element.37), channel_id=1, source_target_pairs={{0,8},{1,9},{2,10},{3,11},{4,12},{5,13},{6,14},{7,15},{8,0},{9,1},... | collective-permute-start | bytes 221192 | tf_op jit(solution)/shard_map/ppermute | solution.py:380
  12.4 1.5 %collective-permute-start.1 = (f32[72,256]{1,0:T(8,128)S(1)}, f32[72,256]{1,0:T(8,128)S(1)}, u32[]{:S(2)}, u32[]{:S(2)}) collective-permute-start(f32[72,256]{1,0:T(8,128)S(1)} %get-tuple-element.38), channel_id=1, source_target_pairs={{0,16},{1,17},{2,18},{3,19},{4,20},{5,21},{6,22},{7,23},{8,24},{9,... | collective-permute-start | bytes 221192 | tf_op jit(solution)/shard_map/ppermute | solution.py:380
  14.1 6.3 %collective-permute-done.refs_1_ = f32[72,256]{1,0:T(8,128)S(1)} collective-permute-done((f32[72,256]{1,0:T(8,128)S(1)}, f32[72,256]{1,0:T(8,128)S(1)}, u32[]{:S(2)}, u32[]{:S(2)}) %collective-permute-start) | collective-permute-done | bytes 73760 | tf_op jit(solution)/shard_map/ppermute | solution.py:380
  20.4 0.9 %collective-permute-done.1.refs_2_ = f32[72,256]{1,0:T(8,128)S(1)} collective-permute-done((f32[72,256]{1,0:T(8,128)S(1)}, f32[72,256]{1,0:T(8,128)S(1)}, u32[]{:S(2)}, u32[]{:S(2)}) %collective-permute-start.1) | collective-permute-done | bytes 73760 | tf_op jit(solution)/shard_map/ppermute | solution.py:380
  21.3 4.5 %collective-permute-done.2.refs_3_ = f32[72,256]{1,0:T(8,128)S(1)} collective-permute-done((f32[72,256]{1,0:T(8,128)S(1)}, f32[72,256]{1,0:T(8,128)S(1)}, u32[]{:S(2)}, u32[]{:S(2)}) %collective-permute-start.2) | collective-permute-done | bytes 73760 | tf_op jit(solution)/shard_map/ppermute | solution.py:380
  25.9 1.2 %collective-permute-done.6.refs_7_ = f32[72,256]{1,0:T(8,128)S(1)} collective-permute-done((f32[72,256]{1,0:T(8,128)S(1)}, f32[72,256]{1,0:T(8,128)S(1)}, u32[]{:S(2)}, u32[]{:S(2)}) %collective-permute-start.6) | collective-permute-done | bytes 73760 | tf_op jit(solution)/shard_map/ppermute | solution.py:381
  27.2 0.7 %collective-permute-start.7 = (f32[8,16,256]{2,1,0:T(8,128)S(1)}, f32[8,16,256]{2,1,0:T(8,128)S(1)}, u32[]{:S(2)}, u32[]{:S(2)}) collective-permute-start(f32[8,16,256]{2,1,0:T(8,128)S(1)} %get-tuple-element.42), channel_id=1, source_target_pairs={{4,8},{8,4},{12,24},{24,12},{28,16},{16,28},{20,17},{17,20},{21,25... | collective-permute-start | bytes 393224 | tf_op jit(solution)/shard_map/ppermute | solution.py:410
  27.9 0.7 %shard_map.58 = (bf16[5,256,256]{2,1,0:T(8,128)(2,1)S(1)}, bf16[5,256,256]{2,1,0:T(8,128)(2,1)S(1)}, bf16[64,128]{1,0:T(8,128)(2,1)S(1)}) custom-call(f32[3,2,33]{2,1,0:T(2,128)S(1)} %bitcast.18, f32[8,32,256]{2,1,0:T(8,128)S(1)} %get-tuple-element.41._.est), custom_call_target="tpu_custom_call" | custom-call | flops 1073741824 | bytes 1048576 | tf_op jit(solution)/shard_map/pallas_call | solution.py:413
  28.6 0.8 %shard_map.59.blurred = f32[256,256]{1,0:T(8,128)S(1)} custom-call(f32[8,32,256]{2,1,0:T(8,128)S(1)} %get-tuple-element.41._.est, f32[8,16,256]{2,1,0:T(8,128)S(1)} %collective-permute-done.7.far.est_far, f32[8,16,256]{2,1,0:T(8,128)S(1)} %get-tuple-element.43.near.est_near, bf16[64,128]{1,0:T(8,128)(2,1)S(1)} %get-tuple-element.44.band, ...), custom_call_target="tpu_custom_call" | custom-call | flops 1073741824 | bytes 1048576 | tf_op jit(solution)/shard_map/pallas_call | solution.py:422
  29.4 6.2 %all-to-all-done = f32[32,1,8448]{2,1,0:T(1,128)S(1)} async-done(((f32[32,1,8448]{2,1,0:T(1,128)}), f32[32,1,8448]{2,1,0:T(1,128)S(1)}, u32[]{:S(2)}, u32[]{:S(2)}) %all-to-all-start) | async-done | bytes 1081376 | tf_op jit(solution)/shard_map/all_to_all | solution.py:400
  35.6 0.9 %shard_map.60.ratio = f32[8,32,256]{2,1,0:T(8,128)S(1)} custom-call(f32[8,264,128]{2,1,0:T(8,128)S(1)} %bitcast.12, f32[8,8,256]{2,1,0:T(8,128)S(1)} %get-tuple-element.40.weights, f32[256,256]{1,0:T(8,128)S(1)} %shard_map.59.blurred), custom_call_target="tpu_custom_call" | custom-call | flops 1073741824 | bytes 1048576 | tf_op jit(solution)/shard_map/pallas_call | solution.py:425
  36.5 0.7 %collective-permute-start.8 = (f32[8,32,256]{2,1,0:T(8,128)S(1)}, f32[8,32,256]{2,1,0:T(8,128)S(1)}, u32[]{:S(2)}, u32[]{:S(2)}) collective-permute-start(f32[8,32,256]{2,1,0:T(8,128)S(1)} %shard_map.60.ratio), channel_id=1, source_target_pairs={{4,8},{8,4},{12,24},{24,12},{28,16},{16,28},{20,17},{17,20},{21,25... | collective-permute-start | bytes 786440 | tf_op jit(solution)/shard_map/ppermute | solution.py:433
  37.1 2.9 %collective-permute-start.9 = (f32[8,32,256]{2,1,0:T(8,128)S(1)}, f32[8,32,256]{2,1,0:T(8,128)S(1)}, u32[]{:S(2)}, u32[]{:S(2)}) collective-permute-start(f32[8,32,256]{2,1,0:T(8,128)S(1)} %shard_map.60.ratio), channel_id=1, source_target_pairs={{0,4},{4,0},{8,12},{12,8},{24,28},{28,24},{16,20},{20,16},{17,21},... | collective-permute-start | bytes 786440 | tf_op jit(solution)/shard_map/ppermute | solution.py:433
  40.6 0.8 %shard_map.64 = (f32[8,32,256]{2,1,0:T(8,128)S(1)}, f32[8,8,256]{2,1,0:T(8,128)S(1)}) custom-call(f32[8,264,128]{2,1,0:T(8,128)S(1)} %bitcast.14, f32[8,8,256]{2,1,0:T(8,128)S(1)} %get-tuple-element.40.weights), custom_call_target="tpu_custom_call" | custom-call | flops 1073741824 | bytes 1048576 | tf_op jit(solution)/shard_map/pallas_call | solution.py:426
  41.5 0.7 %shard_map.63 = (bf16[5,256,256]{2,1,0:T(8,128)(2,1)S(1)}, bf16[5,256,256]{2,1,0:T(8,128)(2,1)S(1)}, bf16[64,128]{1,0:T(8,128)(2,1)S(1)}) custom-call(f32[3,2,33]{2,1,0:T(2,128)S(1)} %bitcast.20, f32[8,264,128]{2,1,0:T(8,128)S(1)} %bitcast.15), custom_call_target="tpu_custom_call" | custom-call | flops 1073741824 | bytes 1048576 | tf_op jit(solution)/shard_map/pallas_call | solution.py:413
  42.2 1.4 %shard_map.62.est = f32[8,64,256]{2,1,0:T(8,128)S(1)} custom-call(f32[8,32,256]{2,1,0:T(8,128)S(1)} %shard_map.60.ratio, f32[8,32,256]{2,1,0:T(8,128)S(1)} %collective-permute-done.8.ratio_far, f32[8,32,256]{2,1,0:T(8,128)S(1)} %collective-permute-done.9.ratio_near, f32[8,32,256]{2,1,0:T(8,128)S(1)} %get-tuple-element.41._.est, ...), custom_call_target="tpu_custom_call" | custom-call | flops 1073741824 | bytes 1048576 | tf_op jit(solution)/shard_map/pallas_call | solution.py:427
  43.6 0.8 %shard_map.65 = (f32[8,32,256]{2,1,0:T(8,128)S(1)}, f32[8,16,256]{2,1,0:T(8,128)S(1)}, f32[8,16,256]{2,1,0:T(8,128)S(1)}) custom-call(f32[8,64,256]{2,1,0:T(8,128)S(1)} %shard_map.62.est, bf16[64,128]{1,0:T(8,128)(2,1)S(1)} %get-tuple-element.50.band, bf16[5,256,256]{2,1,0:T(8,128)(2,1)S(1)} %get-tuple-element.51.high, ...), custom_call_target="tpu_custom_call" | custom-call | flops 1073741824 | bytes 1048576 | tf_op jit(solution)/shard_map/pallas_call | solution.py:434
  44.4 2.3 %collective-permute-start.10 = (f32[8,16,256]{2,1,0:T(8,128)S(1)}, f32[8,16,256]{2,1,0:T(8,128)S(1)}, u32[]{:S(2)}, u32[]{:S(2)}) collective-permute-start(f32[8,16,256]{2,1,0:T(8,128)S(1)} %get-tuple-element.56), channel_id=1, source_target_pairs={{4,8},{8,4},{12,24},{24,12},{28,16},{16,28},{20,17},{17,20},{21,25... | collective-permute-start | bytes 393224 | tf_op jit(solution)/shard_map/ppermute | solution.py:444
  46.7 1.3 %collective-permute-start.11 = (f32[8,16,256]{2,1,0:T(8,128)S(1)}, f32[8,16,256]{2,1,0:T(8,128)S(1)}, u32[]{:S(2)}, u32[]{:S(2)}) collective-permute-start(f32[8,16,256]{2,1,0:T(8,128)S(1)} %get-tuple-element.57), channel_id=1, source_target_pairs={{0,4},{4,0},{8,12},{12,8},{24,28},{28,24},{16,20},{20,16},{17,21},... | collective-permute-start | bytes 393224 | tf_op jit(solution)/shard_map/ppermute | solution.py:444
  48.0 0.6 shard_map.66
  48.6 2.0 %collective-permute-done.10.far = f32[8,16,256]{2,1,0:T(8,128)S(1)} collective-permute-done((f32[8,16,256]{2,1,0:T(8,128)S(1)}, f32[8,16,256]{2,1,0:T(8,128)S(1)}, u32[]{:S(2)}, u32[]{:S(2)}) %collective-permute-start.10) | collective-permute-done | bytes 131104 | tf_op jit(solution)/shard_map/ppermute | solution.py:444
  50.6 0.8 %shard_map.67 = (f32[32,256]{1,0:T(8,128)S(1)}, f32[32,256]{1,0:T(8,128)S(1)}, f32[2,32,256]{2,1,0:T(8,128)S(1)}, f32[2,32,256]{2,1,0:T(8,128)S(1)}, f32[32,256]{1,0:T(8,128)S(1)}, /*index=5*/f32[32,256]{1,0:T(8,128)S(1)}) custom-call(f32[8,32,256]{2,1,0:T(8,128)S(1)} %get-tuple-element.55._.ratio, f32[8,16,256]{2,1,0:T(8,128)S(1)} %collective-permute-done.10.far, ...), custom_call_target="tpu_custom_call" | custom-call | flops 1073741824 | bytes 1048576 | tf_op jit(solution)/shard_map/pallas_call | solution.py:438
  51.5 1.7 %collective-permute-start.12 = (f32[2,32,256]{2,1,0:T(8,128)S(1)}, f32[2,32,256]{2,1,0:T(8,128)S(1)}, u32[]{:S(2)}, u32[]{:S(2)}) collective-permute-start(f32[2,32,256]{2,1,0:T(8,128)S(1)} %get-tuple-element.62), channel_id=1, source_target_pairs={{0,8},{1,9},{2,10},{3,11},{4,12},{5,13},{6,14},{7,15},{8,0},{9,1},... | collective-permute-start | bytes 196616 | tf_op jit(solution)/shard_map/ppermute | solution.py:445
  53.2 1.5 %collective-permute-start.13 = (f32[2,32,256]{2,1,0:T(8,128)S(1)}, f32[2,32,256]{2,1,0:T(8,128)S(1)}, u32[]{:S(2)}, u32[]{:S(2)}) collective-permute-start(f32[2,32,256]{2,1,0:T(8,128)S(1)} %get-tuple-element.63), channel_id=1, source_target_pairs={{0,16},{1,17},{2,18},{3,19},{4,20},{5,21},{6,22},{7,23},{8,24},{9,... | collective-permute-start | bytes 196616 | tf_op jit(solution)/shard_map/ppermute | solution.py:445
  55.1 0.9 %collective-permute-start.15 = (f32[32,256]{1,0:T(8,128)S(1)}, f32[32,256]{1,0:T(8,128)S(1)}, u32[]{:S(2)}, u32[]{:S(2)}) collective-permute-start(f32[32,256]{1,0:T(8,128)S(1)} %get-tuple-element.65), channel_id=1, source_target_pairs={{0,4},{1,5},{2,6},{3,7},{4,0},{5,1},{6,2},{7,3},{8,12},{9,13},{10,... | collective-permute-start | bytes 98312 | tf_op jit(solution)/shard_map/ppermute | solution.py:446
  55.9 1.8 %collective-permute-start.18 = (f32[32,256]{1,0:T(8,128)S(1)}, f32[32,256]{1,0:T(8,128)S(1)}, u32[]{:S(2)}, u32[]{:S(2)}) collective-permute-start(f32[32,256]{1,0:T(8,128)S(1)} %get-tuple-element.66), channel_id=1, source_target_pairs={{0,28},{1,29},{2,30},{3,31},{4,24},{5,25},{6,26},{7,27},{8,20},{9,... | collective-permute-start | bytes 98312 | tf_op jit(solution)/shard_map/ppermute | solution.py:445
  58.2 1.2 %collective-permute-done.14.refs_3_ = f32[32,256]{1,0:T(8,128)S(1)} collective-permute-done((f32[32,256]{1,0:T(8,128)S(1)}, f32[32,256]{1,0:T(8,128)S(1)}, u32[]{:S(2)}, u32[]{:S(2)}) %collective-permute-start.14) | collective-permute-done | bytes 32800 | tf_op jit(solution)/shard_map/ppermute | solution.py:445
  59.5 0.8 %collective-permute-done.18.refs_7_ = f32[32,256]{1,0:T(8,128)S(1)} collective-permute-done((f32[32,256]{1,0:T(8,128)S(1)}, f32[32,256]{1,0:T(8,128)S(1)}, u32[]{:S(2)}, u32[]{:S(2)}) %collective-permute-start.18) | collective-permute-done | bytes 32800 | tf_op jit(solution)/shard_map/ppermute | solution.py:445
  60.3 0.9 %shard_map.68 = f32[16,2,8,256]{3,2,1,0:T(8,128)} custom-call(f32[32,256]{1,0:T(8,128)S(1)} %get-tuple-element.61.refs_0_, f32[2,32,256]{2,1,0:T(8,128)S(1)} %collective-permute-done.12.refs_1_, f32[2,32,256]{2,1,0:T(8,128)S(1)} %collective-permute-done.13.refs_2_, f32[32,256]{1,0:T(8,128)S(1)} %collective-permute-done.14.refs_3_, ...), custom_call_target="tpu_custom_call" | custom-call | bytes 1048576 | tf_op jit(solution)/shard_map/pallas_call | solution.py:448
  (30 shorter events, 1.9 us)
Async XLA Ops:
  2.5 7.3 %copy-start = (f32[16,16,256]{2,1,0:T(8,128)S(1)}, f32[16,16,256]{2,1,0:T(8,128)}, u32[]{:S(2)}) copy-start(f32[16,16,256]{2,1,0:T(8,128)} %param.5) | copy-start | bytes 786436
  2.5 7.3 %copy-start.1 = (s32[2,1,1,1]{0,3,2,1:T(1,128)S(1)}, s32[2,1,1,1]{0,3,2,1:T(1,128)}, u32[]{:S(2)}) copy-start(s32[2,1,1,1]{0,3,2,1:T(1,128)} %param.9) | copy-start | bytes 28
  2.5 25.3 %copy-start.2 = (f32[2,3,33]{2,0,1:T(2,128)S(1)}, f32[2,3,33]{2,0,1:T(2,128)}, u32[]{:S(2)}) copy-start(f32[2,3,33]{2,0,1:T(2,128)} %param.8) | copy-start | bytes 2380
  2.5 33.0 %all-to-all-start = ((f32[32,1,8448]{2,1,0:T(1,128)}), f32[32,1,8448]{2,1,0:T(1,128)S(1)}, u32[]{:S(2)}, u32[]{:S(2)}) async-start(f32[32,1,8448]{2,1,0:T(1,128)} %bitcast.22), calls=%async_computation | async-start | bytes 2162688 | tf_op jit(solution)/shard_map/all_to_all | solution.py:400
  10.6 9.9 %collective-permute-start = (f32[72,256]{1,0:T(8,128)S(1)}, f32[72,256]{1,0:T(8,128)S(1)}, u32[]{:S(2)}, u32[]{:S(2)}) collective-permute-start(f32[72,256]{1,0:T(8,128)S(1)} %get-tuple-element.37), channel_id=1, source_target_pairs={{0,8},{1,9},{2,10},{3,11},{4,12},{5,13},{6,14},{7,15},{8,0},{9,1},... | collective-permute-start | bytes 221192 | tf_op jit(solution)/shard_map/ppermute | solution.py:380
  12.4 8.9 %collective-permute-start.1 = (f32[72,256]{1,0:T(8,128)S(1)}, f32[72,256]{1,0:T(8,128)S(1)}, u32[]{:S(2)}, u32[]{:S(2)}) collective-permute-start(f32[72,256]{1,0:T(8,128)S(1)} %get-tuple-element.38), channel_id=1, source_target_pairs={{0,16},{1,17},{2,18},{3,19},{4,20},{5,21},{6,22},{7,23},{8,24},{9,... | collective-permute-start | bytes 221192 | tf_op jit(solution)/shard_map/ppermute | solution.py:380
  13.9 12.0 %collective-permute-start.2 = (f32[72,256]{1,0:T(8,128)S(1)}, f32[72,256]{1,0:T(8,128)S(1)}, u32[]{:S(2)}, u32[]{:S(2)}) collective-permute-start(f32[72,256]{1,0:T(8,128)S(1)} %get-tuple-element.39), channel_id=1, source_target_pairs={{0,24},{1,25},{2,26},{3,27},{4,28},{5,29},{6,30},{7,31},{8,16},{9,... | collective-permute-start | bytes 221192 | tf_op jit(solution)/shard_map/ppermute | solution.py:380
  14.1 11.7 %collective-permute-start.3 = (f32[72,256]{1,0:T(8,128)S(1)}, f32[72,256]{1,0:T(8,128)S(1)}, u32[]{:S(2)}, u32[]{:S(2)}) collective-permute-start(f32[72,256]{1,0:T(8,128)S(1)} %get-tuple-element.36.refs_0_), channel_id=1, source_target_pairs={{0,4},{1,5},{2,6},{3,7},{4,0},{5,1},{6,2},{7,3},{8,12},{9,13},{10,... | collective-permute-start | bytes 221192 | tf_op jit(solution)/shard_map/ppermute | solution.py:381
  20.4 5.4 %collective-permute-start.4 = (f32[72,256]{1,0:T(8,128)S(1)}, f32[72,256]{1,0:T(8,128)S(1)}, u32[]{:S(2)}, u32[]{:S(2)}) collective-permute-start(f32[72,256]{1,0:T(8,128)S(1)} %collective-permute-done.refs_1_), channel_id=1, source_target_pairs={{0,4},{1,5},{2,6},{3,7},{4,0},{5,1},{6,2},{7,3},{8,12},{9,13},{10,... | collective-permute-start | bytes 221192 | tf_op jit(solution)/shard_map/ppermute | solution.py:381
  21.3 4.5 %collective-permute-start.5 = (f32[72,256]{1,0:T(8,128)S(1)}, f32[72,256]{1,0:T(8,128)S(1)}, u32[]{:S(2)}, u32[]{:S(2)}) collective-permute-start(f32[72,256]{1,0:T(8,128)S(1)} %collective-permute-done.1.refs_2_), channel_id=1, source_target_pairs={{0,4},{1,5},{2,6},{3,7},{4,0},{5,1},{6,2},{7,3},{8,12},{9,13},{10,... | collective-permute-start | bytes 221192 | tf_op jit(solution)/shard_map/ppermute | solution.py:381
  25.8 1.3 %collective-permute-start.6 = (f32[72,256]{1,0:T(8,128)S(1)}, f32[72,256]{1,0:T(8,128)S(1)}, u32[]{:S(2)}, u32[]{:S(2)}) collective-permute-start(f32[72,256]{1,0:T(8,128)S(1)} %collective-permute-done.2.refs_3_), channel_id=1, source_target_pairs={{0,4},{1,5},{2,6},{3,7},{4,0},{5,1},{6,2},{7,3},{8,12},{9,13},{10,... | collective-permute-start | bytes 221192 | tf_op jit(solution)/shard_map/ppermute | solution.py:381
  27.2 1.4 %collective-permute-start.7 = (f32[8,16,256]{2,1,0:T(8,128)S(1)}, f32[8,16,256]{2,1,0:T(8,128)S(1)}, u32[]{:S(2)}, u32[]{:S(2)}) collective-permute-start(f32[8,16,256]{2,1,0:T(8,128)S(1)} %get-tuple-element.42), channel_id=1, source_target_pairs={{4,8},{8,4},{12,24},{24,12},{28,16},{16,28},{20,17},{17,20},{21,25... | collective-permute-start | bytes 393224 | tf_op jit(solution)/shard_map/ppermute | solution.py:410
  36.5 5.7 %collective-permute-start.8 = (f32[8,32,256]{2,1,0:T(8,128)S(1)}, f32[8,32,256]{2,1,0:T(8,128)S(1)}, u32[]{:S(2)}, u32[]{:S(2)}) collective-permute-start(f32[8,32,256]{2,1,0:T(8,128)S(1)} %shard_map.60.ratio), channel_id=1, source_target_pairs={{4,8},{8,4},{12,24},{24,12},{28,16},{16,28},{20,17},{17,20},{21,25... | collective-permute-start | bytes 786440 | tf_op jit(solution)/shard_map/ppermute | solution.py:433
  37.1 5.1 %collective-permute-start.9 = (f32[8,32,256]{2,1,0:T(8,128)S(1)}, f32[8,32,256]{2,1,0:T(8,128)S(1)}, u32[]{:S(2)}, u32[]{:S(2)}) collective-permute-start(f32[8,32,256]{2,1,0:T(8,128)S(1)} %shard_map.60.ratio), channel_id=1, source_target_pairs={{0,4},{4,0},{8,12},{12,8},{24,28},{28,24},{16,20},{20,16},{17,21},... | collective-permute-start | bytes 786440 | tf_op jit(solution)/shard_map/ppermute | solution.py:433
  44.4 6.3 %collective-permute-start.10 = (f32[8,16,256]{2,1,0:T(8,128)S(1)}, f32[8,16,256]{2,1,0:T(8,128)S(1)}, u32[]{:S(2)}, u32[]{:S(2)}) collective-permute-start(f32[8,16,256]{2,1,0:T(8,128)S(1)} %get-tuple-element.56), channel_id=1, source_target_pairs={{4,8},{8,4},{12,24},{24,12},{28,16},{16,28},{20,17},{17,20},{21,25... | collective-permute-start | bytes 393224 | tf_op jit(solution)/shard_map/ppermute | solution.py:444
  46.7 3.9 %collective-permute-start.11 = (f32[8,16,256]{2,1,0:T(8,128)S(1)}, f32[8,16,256]{2,1,0:T(8,128)S(1)}, u32[]{:S(2)}, u32[]{:S(2)}) collective-permute-start(f32[8,16,256]{2,1,0:T(8,128)S(1)} %get-tuple-element.57), channel_id=1, source_target_pairs={{0,4},{4,0},{8,12},{12,8},{24,28},{28,24},{16,20},{20,16},{17,21},... | collective-permute-start | bytes 393224 | tf_op jit(solution)/shard_map/ppermute | solution.py:444
  51.5 6.2 %collective-permute-start.12 = (f32[2,32,256]{2,1,0:T(8,128)S(1)}, f32[2,32,256]{2,1,0:T(8,128)S(1)}, u32[]{:S(2)}, u32[]{:S(2)}) collective-permute-start(f32[2,32,256]{2,1,0:T(8,128)S(1)} %get-tuple-element.62), channel_id=1, source_target_pairs={{0,8},{1,9},{2,10},{3,11},{4,12},{5,13},{6,14},{7,15},{8,0},{9,1},... | collective-permute-start | bytes 196616 | tf_op jit(solution)/shard_map/ppermute | solution.py:445
  53.2 4.7 %collective-permute-start.13 = (f32[2,32,256]{2,1,0:T(8,128)S(1)}, f32[2,32,256]{2,1,0:T(8,128)S(1)}, u32[]{:S(2)}, u32[]{:S(2)}) collective-permute-start(f32[2,32,256]{2,1,0:T(8,128)S(1)} %get-tuple-element.63), channel_id=1, source_target_pairs={{0,16},{1,17},{2,18},{3,19},{4,20},{5,21},{6,22},{7,23},{8,24},{9,... | collective-permute-start | bytes 196616 | tf_op jit(solution)/shard_map/ppermute | solution.py:445
  54.7 4.8 %collective-permute-start.14 = (f32[32,256]{1,0:T(8,128)S(1)}, f32[32,256]{1,0:T(8,128)S(1)}, u32[]{:S(2)}, u32[]{:S(2)}) collective-permute-start(f32[32,256]{1,0:T(8,128)S(1)} %get-tuple-element.64), channel_id=1, source_target_pairs={{0,24},{1,25},{2,26},{3,27},{4,28},{5,29},{6,30},{7,31},{8,16},{9,... | collective-permute-start | bytes 98312 | tf_op jit(solution)/shard_map/ppermute | solution.py:445
  55.1 4.4 %collective-permute-start.15 = (f32[32,256]{1,0:T(8,128)S(1)}, f32[32,256]{1,0:T(8,128)S(1)}, u32[]{:S(2)}, u32[]{:S(2)}) collective-permute-start(f32[32,256]{1,0:T(8,128)S(1)} %get-tuple-element.65), channel_id=1, source_target_pairs={{0,4},{1,5},{2,6},{3,7},{4,0},{5,1},{6,2},{7,3},{8,12},{9,13},{10,... | collective-permute-start | bytes 98312 | tf_op jit(solution)/shard_map/ppermute | solution.py:446
  55.9 4.4 %collective-permute-start.18 = (f32[32,256]{1,0:T(8,128)S(1)}, f32[32,256]{1,0:T(8,128)S(1)}, u32[]{:S(2)}, u32[]{:S(2)}) collective-permute-start(f32[32,256]{1,0:T(8,128)S(1)} %get-tuple-element.66), channel_id=1, source_target_pairs={{0,28},{1,29},{2,30},{3,31},{4,24},{5,25},{6,26},{7,27},{8,20},{9,... | collective-permute-start | bytes 98312 | tf_op jit(solution)/shard_map/ppermute | solution.py:445
  57.7 2.6 %collective-permute-start.16 = (f32[32,256]{1,0:T(8,128)S(1)}, f32[32,256]{1,0:T(8,128)S(1)}, u32[]{:S(2)}, u32[]{:S(2)}) collective-permute-start(f32[32,256]{1,0:T(8,128)S(1)} %slice_bitcast_fusion.1), channel_id=1, source_target_pairs={{0,4},{1,5},{2,6},{3,7},{4,0},{5,1},{6,2},{7,3},{8,12},{9,13},{10,... | collective-permute-start | bytes 98312 | tf_op jit(solution)/shard_map/ppermute | solution.py:446
  57.8 2.5 %collective-permute-start.17 = (f32[32,256]{1,0:T(8,128)S(1)}, f32[32,256]{1,0:T(8,128)S(1)}, u32[]{:S(2)}, u32[]{:S(2)}) collective-permute-start(f32[32,256]{1,0:T(8,128)S(1)} %slice_bitcast_fusion), channel_id=1, source_target_pairs={{0,4},{1,5},{2,6},{3,7},{4,0},{5,1},{6,2},{7,3},{8,12},{9,13},{10,... | collective-permute-start | bytes 98312 | tf_op jit(solution)/shard_map/ppermute | solution.py:446

commit v10 on v9

--- a/solution.py
+++ b/solution.py
@@ -443,8 +443,8 @@
         flops=1 << 30,
     )(ratio, lax.ppermute(far, ALL, ring_pairs), lax.ppermute(near, ALL, near_pairs), *matrices(1, 1, ratio), est)
     *away, last = [lax.ppermute(piece, ALL, pairs) for piece, pairs in zip(away, to_chips + [to_far_core])]
-    others = [lax.ppermute(piece, ALL, to_core) for piece in [other] + [piece[1] for piece in away[:2]]]
-    others.append(last)
+    first = lax.ppermute(jnp.stack([other, away[0][1]]), ALL, to_core)
+    others = [first[0], first[1], lax.ppermute(away[1][1], ALL, to_core), last]
     out = call(
         join_kernel,
         shape(16, 2, 8, 256),

time: 61.4 us -> 61 us (level)
    ppermute x7, waiting for transfers between devices: 13.9 us -> 12.7 us  [slab_sweep(): lax.ppermute(piece, ALL, pairs)]
    ppermute x3 -> x2, waiting for transfers between devices: 0.01 us -> 0.73 us  [the longest x1 0.73 us: slab_sweep(): first = lax.ppermute(jnp.stack([other, away[0][1]]), ALL, to_core)]
    ppermute x3 -> x2, starting transfers between devices: 1.27 us -> 0.92 us  [the longest x1 0.79 us: slab_sweep(): first = lax.ppermute(jnp.stack([other, away[0][1]]), ALL, to_core)]
  transfers between devices with their start and end apart: 20 -> 19, of which waited for: 9 -> 8; matrix products, arithmetic and copies ran while one was open for 0% -> 0% of each run, Pallas kernels for 8% -> 8%
where the time goes in v10:
time: 61 us; the launch traced here: 60.5 us
  starting transfers between devices  25.2 us (41%)
  waiting for transfers between devices  22.9 us (38%)
  Pallas kernels  12.2 us (20%)
    ppermute x7, waiting for transfers between devices, slab_sweep(): lax.ppermute(piece, ALL, pairs)  12.7 us
    ppermute x7, starting transfers between devices, slab_sweep(): lax.ppermute(piece, ALL, pairs)  9.03 us
    all_to_all x1, starting transfers between devices, slab_sweep(): slots = lax.all_to_all(slots, ALL, split_axis=0, concat_axis=0, tiled=True)  7.3 us
    all_to_all x1, waiting for transfers between devices, slab_sweep(): slots = lax.all_to_all(slots, ALL, split_axis=0, concat_axis=0, tiled=True)  6.23 us
    ppermute x1, starting transfers between devices, slab_sweep(): lax.ppermute(ratio, ALL, near_pairs)  2.89 us
    pallas_call x4, Pallas kernels, matrices(): call(functools.partial(taps_kernel, view, way), (big, big, shape(64, 128,...  2.62 us
    pallas_call x1, Pallas kernels, slab_sweep(): call(functools.partial(lines_kernel, planes), shape(8, 66 * planes, 128),...  2.49 us
    ppermute x1, starting transfers between devices, slab_sweep(): lax.ppermute(far, ALL, ring_pairs)  2.32 us
  transfers between devices with their start and end apart: 19, of which 8 were waited for; matrix products, arithmetic and copies ran while one was open for 0% of the time, Pallas kernels for 8%

profile of v10, /device:TPU:0, one launch (start us, length us, event | category | flops | bytes accessed | tf_op | source)
XLA Modules:
  0.0 60.5 jit_solution(11998763339920365617)
XLA Ops:
  0.0 2.5 %shard_map.55 = f32[8,264,128]{2,1,0:T(8,128)} custom-call(f32[2,4,4,32,256]{4,3,2,1,0:T(8,128)} %bitcast.27, s32[8,128]{1,0:T(8,128)} %bitcast.28), custom_call_target="tpu_custom_call" | custom-call | bytes 1048576 | tf_op jit(solution)/shard_map/pallas_call | solution.py:384
  2.5 7.3 %all-to-all-start = ((f32[32,1,8448]{2,1,0:T(1,128)}), f32[32,1,8448]{2,1,0:T(1,128)S(1)}, u32[]{:S(2)}, u32[]{:S(2)}) async-start(f32[32,1,8448]{2,1,0:T(1,128)} %bitcast.26), calls=%async_computation | async-start | bytes 2162688 | tf_op jit(solution)/shard_map/all_to_all | solution.py:400
  9.9 0.7 %shard_map.56 = (f32[72,256]{1,0:T(8,128)S(1)}, f32[72,256]{1,0:T(8,128)S(1)}, f32[72,256]{1,0:T(8,128)S(1)}, f32[72,256]{1,0:T(8,128)S(1)}) custom-call(s32[2]{0:T(128)S(1)} %bitcast.21, f32[16,2,8,256]{3,2,1,0:T(8,128)S(1)} %bitcast.19), custom_call_target="tpu_custom_call" | custom-call | bytes 1048576 | tf_op jit(solution)/shard_map/pallas_call | solution.py:377
  10.6 1.8 %collective-permute-start = (f32[72,256]{1,0:T(8,128)S(1)}, f32[72,256]{1,0:T(8,128)S(1)}, u32[]{:S(2)}, u32[]{:S(2)}) collective-permute-start(f32[72,256]{1,0:T(8,128)S(1)} %get-tuple-element.37), channel_id=1, source_target_pairs={{0,8},{1,9},{2,10},{3,11},{4,12},{5,13},{6,14},{7,15},{8,0},{9,1},... | collective-permute-start | bytes 221192 | tf_op jit(solution)/shard_map/ppermute | solution.py:380
  12.4 1.5 %collective-permute-start.1 = (f32[72,256]{1,0:T(8,128)S(1)}, f32[72,256]{1,0:T(8,128)S(1)}, u32[]{:S(2)}, u32[]{:S(2)}) collective-permute-start(f32[72,256]{1,0:T(8,128)S(1)} %get-tuple-element.38), channel_id=1, source_target_pairs={{0,16},{1,17},{2,18},{3,19},{4,20},{5,21},{6,22},{7,23},{8,24},{9,... | collective-permute-start | bytes 221192 | tf_op jit(solution)/shard_map/ppermute | solution.py:380
  14.1 6.3 %collective-permute-done.refs_1_ = f32[72,256]{1,0:T(8,128)S(1)} collective-permute-done((f32[72,256]{1,0:T(8,128)S(1)}, f32[72,256]{1,0:T(8,128)S(1)}, u32[]{:S(2)}, u32[]{:S(2)}) %collective-permute-start) | collective-permute-done | bytes 73760 | tf_op jit(solution)/shard_map/ppermute | solution.py:380
  20.4 0.9 %collective-permute-done.1.refs_2_ = f32[72,256]{1,0:T(8,128)S(1)} collective-permute-done((f32[72,256]{1,0:T(8,128)S(1)}, f32[72,256]{1,0:T(8,128)S(1)}, u32[]{:S(2)}, u32[]{:S(2)}) %collective-permute-start.1) | collective-permute-done | bytes 73760 | tf_op jit(solution)/shard_map/ppermute | solution.py:380
  21.3 4.5 %collective-permute-done.2.refs_3_ = f32[72,256]{1,0:T(8,128)S(1)} collective-permute-done((f32[72,256]{1,0:T(8,128)S(1)}, f32[72,256]{1,0:T(8,128)S(1)}, u32[]{:S(2)}, u32[]{:S(2)}) %collective-permute-start.2) | collective-permute-done | bytes 73760 | tf_op jit(solution)/shard_map/ppermute | solution.py:380
  25.9 1.2 %collective-permute-done.6.refs_7_ = f32[72,256]{1,0:T(8,128)S(1)} collective-permute-done((f32[72,256]{1,0:T(8,128)S(1)}, f32[72,256]{1,0:T(8,128)S(1)}, u32[]{:S(2)}, u32[]{:S(2)}) %collective-permute-start.6) | collective-permute-done | bytes 73760 | tf_op jit(solution)/shard_map/ppermute | solution.py:381
  27.2 0.7 %collective-permute-start.7 = (f32[8,16,256]{2,1,0:T(8,128)S(1)}, f32[8,16,256]{2,1,0:T(8,128)S(1)}, u32[]{:S(2)}, u32[]{:S(2)}) collective-permute-start(f32[8,16,256]{2,1,0:T(8,128)S(1)} %get-tuple-element.42), channel_id=1, source_target_pairs={{4,8},{8,4},{12,24},{24,12},{28,16},{16,28},{20,17},{17,20},{21,25... | collective-permute-start | bytes 393224 | tf_op jit(solution)/shard_map/ppermute | solution.py:410
  27.9 0.7 %shard_map.58 = (bf16[5,256,256]{2,1,0:T(8,128)(2,1)S(1)}, bf16[5,256,256]{2,1,0:T(8,128)(2,1)S(1)}, bf16[64,128]{1,0:T(8,128)(2,1)S(1)}) custom-call(f32[3,2,33]{2,1,0:T(2,128)S(1)} %bitcast.22, f32[8,32,256]{2,1,0:T(8,128)S(1)} %get-tuple-element.41._.est), custom_call_target="tpu_custom_call" | custom-call | flops 1073741824 | bytes 1048576 | tf_op jit(solution)/shard_map/pallas_call | solution.py:413
  28.6 0.8 %shard_map.59.blurred = f32[256,256]{1,0:T(8,128)S(1)} custom-call(f32[8,32,256]{2,1,0:T(8,128)S(1)} %get-tuple-element.41._.est, f32[8,16,256]{2,1,0:T(8,128)S(1)} %collective-permute-done.7.far.est_far, f32[8,16,256]{2,1,0:T(8,128)S(1)} %get-tuple-element.43.near.est_near, bf16[64,128]{1,0:T(8,128)(2,1)S(1)} %get-tuple-element.44.band, ...), custom_call_target="tpu_custom_call" | custom-call | flops 1073741824 | bytes 1048576 | tf_op jit(solution)/shard_map/pallas_call | solution.py:422
  29.4 6.2 %all-to-all-done = f32[32,1,8448]{2,1,0:T(1,128)S(1)} async-done(((f32[32,1,8448]{2,1,0:T(1,128)}), f32[32,1,8448]{2,1,0:T(1,128)S(1)}, u32[]{:S(2)}, u32[]{:S(2)}) %all-to-all-start) | async-done | bytes 1081376 | tf_op jit(solution)/shard_map/all_to_all | solution.py:400
  35.6 0.9 %shard_map.60.ratio = f32[8,32,256]{2,1,0:T(8,128)S(1)} custom-call(f32[8,264,128]{2,1,0:T(8,128)S(1)} %bitcast.15, f32[8,8,256]{2,1,0:T(8,128)S(1)} %get-tuple-element.40.weights, f32[256,256]{1,0:T(8,128)S(1)} %shard_map.59.blurred), custom_call_target="tpu_custom_call" | custom-call | flops 1073741824 | bytes 1048576 | tf_op jit(solution)/shard_map/pallas_call | solution.py:425
  36.5 0.7 %collective-permute-start.8 = (f32[8,32,256]{2,1,0:T(8,128)S(1)}, f32[8,32,256]{2,1,0:T(8,128)S(1)}, u32[]{:S(2)}, u32[]{:S(2)}) collective-permute-start(f32[8,32,256]{2,1,0:T(8,128)S(1)} %shard_map.60.ratio), channel_id=1, source_target_pairs={{4,8},{8,4},{12,24},{24,12},{28,16},{16,28},{20,17},{17,20},{21,25... | collective-permute-start | bytes 786440 | tf_op jit(solution)/shard_map/ppermute | solution.py:433
  37.1 2.9 %collective-permute-start.9 = (f32[8,32,256]{2,1,0:T(8,128)S(1)}, f32[8,32,256]{2,1,0:T(8,128)S(1)}, u32[]{:S(2)}, u32[]{:S(2)}) collective-permute-start(f32[8,32,256]{2,1,0:T(8,128)S(1)} %shard_map.60.ratio), channel_id=1, source_target_pairs={{0,4},{4,0},{8,12},{12,8},{24,28},{28,24},{16,20},{20,16},{17,21},... | collective-permute-start | bytes 786440 | tf_op jit(solution)/shard_map/ppermute | solution.py:433
  40.0 0.6 shard_map.61
  40.6 0.8 %shard_map.64 = (f32[8,32,256]{2,1,0:T(8,128)S(1)}, f32[8,8,256]{2,1,0:T(8,128)S(1)}) custom-call(f32[8,264,128]{2,1,0:T(8,128)S(1)} %bitcast.17, f32[8,8,256]{2,1,0:T(8,128)S(1)} %get-tuple-element.40.weights), custom_call_target="tpu_custom_call" | custom-call | flops 1073741824 | bytes 1048576 | tf_op jit(solution)/shard_map/pallas_call | solution.py:426
  41.5 0.7 %shard_map.63 = (bf16[5,256,256]{2,1,0:T(8,128)(2,1)S(1)}, bf16[5,256,256]{2,1,0:T(8,128)(2,1)S(1)}, bf16[64,128]{1,0:T(8,128)(2,1)S(1)}) custom-call(f32[3,2,33]{2,1,0:T(2,128)S(1)} %bitcast.24, f32[8,264,128]{2,1,0:T(8,128)S(1)} %bitcast.18), custom_call_target="tpu_custom_call" | custom-call | flops 1073741824 | bytes 1048576 | tf_op jit(solution)/shard_map/pallas_call | solution.py:413
  42.2 1.4 %shard_map.62.est = f32[8,64,256]{2,1,0:T(8,128)S(1)} custom-call(f32[8,32,256]{2,1,0:T(8,128)S(1)} %shard_map.60.ratio, f32[8,32,256]{2,1,0:T(8,128)S(1)} %collective-permute-done.8.ratio_far, f32[8,32,256]{2,1,0:T(8,128)S(1)} %collective-permute-done.9.ratio_near, f32[8,32,256]{2,1,0:T(8,128)S(1)} %get-tuple-element.41._.est, ...), custom_call_target="tpu_custom_call" | custom-call | flops 1073741824 | bytes 1048576 | tf_op jit(solution)/shard_map/pallas_call | solution.py:427
  43.6 0.8 %shard_map.65 = (f32[8,32,256]{2,1,0:T(8,128)S(1)}, f32[8,16,256]{2,1,0:T(8,128)S(1)}, f32[8,16,256]{2,1,0:T(8,128)S(1)}) custom-call(f32[8,64,256]{2,1,0:T(8,128)S(1)} %shard_map.62.est, bf16[64,128]{1,0:T(8,128)(2,1)S(1)} %get-tuple-element.50.band, bf16[5,256,256]{2,1,0:T(8,128)(2,1)S(1)} %get-tuple-element.51.high, ...), custom_call_target="tpu_custom_call" | custom-call | flops 1073741824 | bytes 1048576 | tf_op jit(solution)/shard_map/pallas_call | solution.py:434
  44.4 2.3 %collective-permute-start.10 = (f32[8,16,256]{2,1,0:T(8,128)S(1)}, f32[8,16,256]{2,1,0:T(8,128)S(1)}, u32[]{:S(2)}, u32[]{:S(2)}) collective-permute-start(f32[8,16,256]{2,1,0:T(8,128)S(1)} %get-tuple-element.56), channel_id=1, source_target_pairs={{4,8},{8,4},{12,24},{24,12},{28,16},{16,28},{20,17},{17,20},{21,25... | collective-permute-start | bytes 393224 | tf_op jit(solution)/shard_map/ppermute | solution.py:444
  46.7 1.3 %collective-permute-start.11 = (f32[8,16,256]{2,1,0:T(8,128)S(1)}, f32[8,16,256]{2,1,0:T(8,128)S(1)}, u32[]{:S(2)}, u32[]{:S(2)}) collective-permute-start(f32[8,16,256]{2,1,0:T(8,128)S(1)} %get-tuple-element.57), channel_id=1, source_target_pairs={{0,4},{4,0},{8,12},{12,8},{24,28},{28,24},{16,20},{20,16},{17,21},... | collective-permute-start | bytes 393224 | tf_op jit(solution)/shard_map/ppermute | solution.py:444
  48.6 2.0 %collective-permute-done.10.far = f32[8,16,256]{2,1,0:T(8,128)S(1)} collective-permute-done((f32[8,16,256]{2,1,0:T(8,128)S(1)}, f32[8,16,256]{2,1,0:T(8,128)S(1)}, u32[]{:S(2)}, u32[]{:S(2)}) %collective-permute-start.10) | collective-permute-done | bytes 131104 | tf_op jit(solution)/shard_map/ppermute | solution.py:444
  50.6 0.8 %shard_map.67 = (f32[32,256]{1,0:T(8,128)S(1)}, f32[32,256]{1,0:T(8,128)S(1)}, f32[2,32,256]{2,1,0:T(8,128)S(1)}, f32[2,32,256]{2,1,0:T(8,128)S(1)}, f32[32,256]{1,0:T(8,128)S(1)}, /*index=5*/f32[32,256]{1,0:T(8,128)S(1)}) custom-call(f32[8,32,256]{2,1,0:T(8,128)S(1)} %get-tuple-element.55._.ratio, f32[8,16,256]{2,1,0:T(8,128)S(1)} %collective-permute-done.10.far, ...), custom_call_target="tpu_custom_call" | custom-call | flops 1073741824 | bytes 1048576 | tf_op jit(solution)/shard_map/pallas_call | solution.py:438
  51.5 1.7 %collective-permute-start.12 = (f32[2,32,256]{2,1,0:T(8,128)S(1)}, f32[2,32,256]{2,1,0:T(8,128)S(1)}, u32[]{:S(2)}, u32[]{:S(2)}) collective-permute-start(f32[2,32,256]{2,1,0:T(8,128)S(1)} %get-tuple-element.62), channel_id=1, source_target_pairs={{0,8},{1,9},{2,10},{3,11},{4,12},{5,13},{6,14},{7,15},{8,0},{9,1},... | collective-permute-start | bytes 196616 | tf_op jit(solution)/shard_map/ppermute | solution.py:445
  53.2 1.5 %collective-permute-start.13 = (f32[2,32,256]{2,1,0:T(8,128)S(1)}, f32[2,32,256]{2,1,0:T(8,128)S(1)}, u32[]{:S(2)}, u32[]{:S(2)}) collective-permute-start(f32[2,32,256]{2,1,0:T(8,128)S(1)} %get-tuple-element.63), channel_id=1, source_target_pairs={{0,16},{1,17},{2,18},{3,19},{4,20},{5,21},{6,22},{7,23},{8,24},{9,... | collective-permute-start | bytes 196616 | tf_op jit(solution)/shard_map/ppermute | solution.py:445
  55.1 1.9 %collective-permute-start.17 = (f32[32,256]{1,0:T(8,128)S(1)}, f32[32,256]{1,0:T(8,128)S(1)}, u32[]{:S(2)}, u32[]{:S(2)}) collective-permute-start(f32[32,256]{1,0:T(8,128)S(1)} %get-tuple-element.66), channel_id=1, source_target_pairs={{0,28},{1,29},{2,30},{3,31},{4,24},{5,25},{6,26},{7,27},{8,20},{9,... | collective-permute-start | bytes 98312 | tf_op jit(solution)/shard_map/ppermute | solution.py:445
  57.0 0.8 %collective-permute-start.15 = (f32[2,32,256]{2,1,0:T(8,128)S(1)}, f32[2,32,256]{2,1,0:T(8,128)S(1)}, u32[]{:S(2)}, u32[]{:S(2)}) collective-permute-start(f32[2,32,256]{2,1,0:T(8,128)S(1)} %pad_maximum_fusion), channel_id=1, source_target_pairs={{0,4},{1,5},{2,6},{3,7},{4,0},{5,1},{6,2},{7,3},{8,12},{9,13},{10,... | collective-permute-start | bytes 196616 | tf_op jit(solution)/shard_map/ppermute | solution.py:446
  58.0 0.7 %collective-permute-done.15 = f32[2,32,256]{2,1,0:T(8,128)S(1)} collective-permute-done((f32[2,32,256]{2,1,0:T(8,128)S(1)}, f32[2,32,256]{2,1,0:T(8,128)S(1)}, u32[]{:S(2)}, u32[]{:S(2)}) %collective-permute-start.15) | collective-permute-done | bytes 65568 | tf_op jit(solution)/shard_map/ppermute | solution.py:446
  58.7 0.9 %collective-permute-done.14.refs_3_ = f32[32,256]{1,0:T(8,128)S(1)} collective-permute-done((f32[32,256]{1,0:T(8,128)S(1)}, f32[32,256]{1,0:T(8,128)S(1)}, u32[]{:S(2)}, u32[]{:S(2)}) %collective-permute-start.14) | collective-permute-done | bytes 32800 | tf_op jit(solution)/shard_map/ppermute | solution.py:445
  59.6 0.9 %shard_map.68 = f32[16,2,8,256]{3,2,1,0:T(8,128)} custom-call(f32[32,256]{1,0:T(8,128)S(1)} %get-tuple-element.61.refs_0_, f32[2,32,256]{2,1,0:T(8,128)S(1)} %collective-permute-done.12.refs_1_, f32[2,32,256]{2,1,0:T(8,128)S(1)} %collective-permute-done.13.refs_2_, f32[32,256]{1,0:T(8,128)S(1)} %collective-permute-done.14.refs_3_, ...), custom_call_target="tpu_custom_call" | custom-call | bytes 1048576 | tf_op jit(solution)/shard_map/pallas_call | solution.py:448
  (30 shorter events, 1.5 us)
Async XLA Ops:
  2.5 7.3 %copy-start = (f32[16,16,256]{2,1,0:T(8,128)S(1)}, f32[16,16,256]{2,1,0:T(8,128)}, u32[]{:S(2)}) copy-start(f32[16,16,256]{2,1,0:T(8,128)} %param.5) | copy-start | bytes 786436
  2.5 7.3 %copy-start.1 = (s32[2,1,1,1]{0,3,2,1:T(1,128)S(1)}, s32[2,1,1,1]{0,3,2,1:T(1,128)}, u32[]{:S(2)}) copy-start(s32[2,1,1,1]{0,3,2,1:T(1,128)} %param.9) | copy-start | bytes 28
  2.5 25.3 %copy-start.2 = (f32[2,3,33]{2,0,1:T(2,128)S(1)}, f32[2,3,33]{2,0,1:T(2,128)}, u32[]{:S(2)}) copy-start(f32[2,3,33]{2,0,1:T(2,128)} %param.8) | copy-start | bytes 2380
  2.5 33.0 %all-to-all-start = ((f32[32,1,8448]{2,1,0:T(1,128)}), f32[32,1,8448]{2,1,0:T(1,128)S(1)}, u32[]{:S(2)}, u32[]{:S(2)}) async-start(f32[32,1,8448]{2,1,0:T(1,128)} %bitcast.26), calls=%async_computation | async-start | bytes 2162688 | tf_op jit(solution)/shard_map/all_to_all | solution.py:400
  10.6 9.9 %collective-permute-start = (f32[72,256]{1,0:T(8,128)S(1)}, f32[72,256]{1,0:T(8,128)S(1)}, u32[]{:S(2)}, u32[]{:S(2)}) collective-permute-start(f32[72,256]{1,0:T(8,128)S(1)} %get-tuple-element.37), channel_id=1, source_target_pairs={{0,8},{1,9},{2,10},{3,11},{4,12},{5,13},{6,14},{7,15},{8,0},{9,1},... | collective-permute-start | bytes 221192 | tf_op jit(solution)/shard_map/ppermute | solution.py:380
  12.4 8.9 %collective-permute-start.1 = (f32[72,256]{1,0:T(8,128)S(1)}, f32[72,256]{1,0:T(8,128)S(1)}, u32[]{:S(2)}, u32[]{:S(2)}) collective-permute-start(f32[72,256]{1,0:T(8,128)S(1)} %get-tuple-element.38), channel_id=1, source_target_pairs={{0,16},{1,17},{2,18},{3,19},{4,20},{5,21},{6,22},{7,23},{8,24},{9,... | collective-permute-start | bytes 221192 | tf_op jit(solution)/shard_map/ppermute | solution.py:380
  13.9 12.0 %collective-permute-start.2 = (f32[72,256]{1,0:T(8,128)S(1)}, f32[72,256]{1,0:T(8,128)S(1)}, u32[]{:S(2)}, u32[]{:S(2)}) collective-permute-start(f32[72,256]{1,0:T(8,128)S(1)} %get-tuple-element.39), channel_id=1, source_target_pairs={{0,24},{1,25},{2,26},{3,27},{4,28},{5,29},{6,30},{7,31},{8,16},{9,... | collective-permute-start | bytes 221192 | tf_op jit(solution)/shard_map/ppermute | solution.py:380
  14.1 11.7 %collective-permute-start.3 = (f32[72,256]{1,0:T(8,128)S(1)}, f32[72,256]{1,0:T(8,128)S(1)}, u32[]{:S(2)}, u32[]{:S(2)}) collective-permute-start(f32[72,256]{1,0:T(8,128)S(1)} %get-tuple-element.36.refs_0_), channel_id=1, source_target_pairs={{0,4},{1,5},{2,6},{3,7},{4,0},{5,1},{6,2},{7,3},{8,12},{9,13},{10,... | collective-permute-start | bytes 221192 | tf_op jit(solution)/shard_map/ppermute | solution.py:381
  20.4 5.4 %collective-permute-start.4 = (f32[72,256]{1,0:T(8,128)S(1)}, f32[72,256]{1,0:T(8,128)S(1)}, u32[]{:S(2)}, u32[]{:S(2)}) collective-permute-start(f32[72,256]{1,0:T(8,128)S(1)} %collective-permute-done.refs_1_), channel_id=1, source_target_pairs={{0,4},{1,5},{2,6},{3,7},{4,0},{5,1},{6,2},{7,3},{8,12},{9,13},{10,... | collective-permute-start | bytes 221192 | tf_op jit(solution)/shard_map/ppermute | solution.py:381
  21.3 4.5 %collective-permute-start.5 = (f32[72,256]{1,0:T(8,128)S(1)}, f32[72,256]{1,0:T(8,128)S(1)}, u32[]{:S(2)}, u32[]{:S(2)}) collective-permute-start(f32[72,256]{1,0:T(8,128)S(1)} %collective-permute-done.1.refs_2_), channel_id=1, source_target_pairs={{0,4},{1,5},{2,6},{3,7},{4,0},{5,1},{6,2},{7,3},{8,12},{9,13},{10,... | collective-permute-start | bytes 221192 | tf_op jit(solution)/shard_map/ppermute | solution.py:381
  25.8 1.3 %collective-permute-start.6 = (f32[72,256]{1,0:T(8,128)S(1)}, f32[72,256]{1,0:T(8,128)S(1)}, u32[]{:S(2)}, u32[]{:S(2)}) collective-permute-start(f32[72,256]{1,0:T(8,128)S(1)} %collective-permute-done.2.refs_3_), channel_id=1, source_target_pairs={{0,4},{1,5},{2,6},{3,7},{4,0},{5,1},{6,2},{7,3},{8,12},{9,13},{10,... | collective-permute-start | bytes 221192 | tf_op jit(solution)/shard_map/ppermute | solution.py:381
  27.2 1.4 %collective-permute-start.7 = (f32[8,16,256]{2,1,0:T(8,128)S(1)}, f32[8,16,256]{2,1,0:T(8,128)S(1)}, u32[]{:S(2)}, u32[]{:S(2)}) collective-permute-start(f32[8,16,256]{2,1,0:T(8,128)S(1)} %get-tuple-element.42), channel_id=1, source_target_pairs={{4,8},{8,4},{12,24},{24,12},{28,16},{16,28},{20,17},{17,20},{21,25... | collective-permute-start | bytes 393224 | tf_op jit(solution)/shard_map/ppermute | solution.py:410
  36.5 5.7 %collective-permute-start.8 = (f32[8,32,256]{2,1,0:T(8,128)S(1)}, f32[8,32,256]{2,1,0:T(8,128)S(1)}, u32[]{:S(2)}, u32[]{:S(2)}) collective-permute-start(f32[8,32,256]{2,1,0:T(8,128)S(1)} %shard_map.60.ratio), channel_id=1, source_target_pairs={{4,8},{8,4},{12,24},{24,12},{28,16},{16,28},{20,17},{17,20},{21,25... | collective-permute-start | bytes 786440 | tf_op jit(solution)/shard_map/ppermute | solution.py:433
  37.1 5.1 %collective-permute-start.9 = (f32[8,32,256]{2,1,0:T(8,128)S(1)}, f32[8,32,256]{2,1,0:T(8,128)S(1)}, u32[]{:S(2)}, u32[]{:S(2)}) collective-permute-start(f32[8,32,256]{2,1,0:T(8,128)S(1)} %shard_map.60.ratio), channel_id=1, source_target_pairs={{0,4},{4,0},{8,12},{12,8},{24,28},{28,24},{16,20},{20,16},{17,21},... | collective-permute-start | bytes 786440 | tf_op jit(solution)/shard_map/ppermute | solution.py:433
  44.4 6.3 %collective-permute-start.10 = (f32[8,16,256]{2,1,0:T(8,128)S(1)}, f32[8,16,256]{2,1,0:T(8,128)S(1)}, u32[]{:S(2)}, u32[]{:S(2)}) collective-permute-start(f32[8,16,256]{2,1,0:T(8,128)S(1)} %get-tuple-element.56), channel_id=1, source_target_pairs={{4,8},{8,4},{12,24},{24,12},{28,16},{16,28},{20,17},{17,20},{21,25... | collective-permute-start | bytes 393224 | tf_op jit(solution)/shard_map/ppermute | solution.py:444
  46.7 3.9 %collective-permute-start.11 = (f32[8,16,256]{2,1,0:T(8,128)S(1)}, f32[8,16,256]{2,1,0:T(8,128)S(1)}, u32[]{:S(2)}, u32[]{:S(2)}) collective-permute-start(f32[8,16,256]{2,1,0:T(8,128)S(1)} %get-tuple-element.57), channel_id=1, source_target_pairs={{0,4},{4,0},{8,12},{12,8},{24,28},{28,24},{16,20},{20,16},{17,21},... | collective-permute-start | bytes 393224 | tf_op jit(solution)/shard_map/ppermute | solution.py:444
  51.5 5.5 %collective-permute-start.12 = (f32[2,32,256]{2,1,0:T(8,128)S(1)}, f32[2,32,256]{2,1,0:T(8,128)S(1)}, u32[]{:S(2)}, u32[]{:S(2)}) collective-permute-start(f32[2,32,256]{2,1,0:T(8,128)S(1)} %get-tuple-element.62), channel_id=1, source_target_pairs={{0,8},{1,9},{2,10},{3,11},{4,12},{5,13},{6,14},{7,15},{8,0},{9,1},... | collective-permute-start | bytes 196616 | tf_op jit(solution)/shard_map/ppermute | solution.py:445
  53.2 4.7 %collective-permute-start.13 = (f32[2,32,256]{2,1,0:T(8,128)S(1)}, f32[2,32,256]{2,1,0:T(8,128)S(1)}, u32[]{:S(2)}, u32[]{:S(2)}) collective-permute-start(f32[2,32,256]{2,1,0:T(8,128)S(1)} %get-tuple-element.63), channel_id=1, source_target_pairs={{0,16},{1,17},{2,18},{3,19},{4,20},{5,21},{6,22},{7,23},{8,24},{9,... | collective-permute-start | bytes 196616 | tf_op jit(solution)/shard_map/ppermute | solution.py:445
  54.7 5.0 %collective-permute-start.14 = (f32[32,256]{1,0:T(8,128)S(1)}, f32[32,256]{1,0:T(8,128)S(1)}, u32[]{:S(2)}, u32[]{:S(2)}) collective-permute-start(f32[32,256]{1,0:T(8,128)S(1)} %get-tuple-element.64), channel_id=1, source_target_pairs={{0,24},{1,25},{2,26},{3,27},{4,28},{5,29},{6,30},{7,31},{8,16},{9,... | collective-permute-start | bytes 98312 | tf_op jit(solution)/shard_map/ppermute | solution.py:445
  55.1 4.6 %collective-permute-start.17 = (f32[32,256]{1,0:T(8,128)S(1)}, f32[32,256]{1,0:T(8,128)S(1)}, u32[]{:S(2)}, u32[]{:S(2)}) collective-permute-start(f32[32,256]{1,0:T(8,128)S(1)} %get-tuple-element.66), channel_id=1, source_target_pairs={{0,28},{1,29},{2,30},{3,31},{4,24},{5,25},{6,26},{7,27},{8,20},{9,... | collective-permute-start | bytes 98312 | tf_op jit(solution)/shard_map/ppermute | solution.py:445
  57.0 1.7 %collective-permute-start.15 = (f32[2,32,256]{2,1,0:T(8,128)S(1)}, f32[2,32,256]{2,1,0:T(8,128)S(1)}, u32[]{:S(2)}, u32[]{:S(2)}) collective-permute-start(f32[2,32,256]{2,1,0:T(8,128)S(1)} %pad_maximum_fusion), channel_id=1, source_target_pairs={{0,4},{1,5},{2,6},{3,7},{4,0},{5,1},{6,2},{7,3},{8,12},{9,13},{10,... | collective-permute-start | bytes 196616 | tf_op jit(solution)/shard_map/ppermute | solution.py:446
  57.8 1.8 %collective-permute-start.16 = (f32[32,256]{1,0:T(8,128)S(1)}, f32[32,256]{1,0:T(8,128)S(1)}, u32[]{:S(2)}, u32[]{:S(2)}) collective-permute-start(f32[32,256]{1,0:T(8,128)S(1)} %slice_bitcast_fusion), channel_id=1, source_target_pairs={{0,4},{1,5},{2,6},{3,7},{4,0},{5,1},{6,2},{7,3},{8,12},{9,13},{10,... | collective-permute-start | bytes 98312 | tf_op jit(solution)/shard_map/ppermute | solution.py:447

commit v11 on v10

--- a/solution.py
+++ b/solution.py
@@ -130,20 +130,22 @@
     rows = lax.broadcasted_iota(jnp.int32, (8, 128), 0)
 
     def load(z):
-        return pltpu.make_async_copy(raw.at[:, :, z], held.at[z], arrived.at[z])
+        some = pl.ds(0, 1) if z == 0 else pl.ds(1, planes - 1)
+        return pltpu.make_async_copy(raw.at[:, :, some], held.at[:, :, some], arrived.at[z])
 
     def store(z):
         rows = pl.ds(64 * z, 64 if z < planes - 1 else 64 + 2 * planes)
         return pltpu.make_async_copy(made.at[:, rows], out.at[:, rows], left.at[z])
 
     load_numbers = pltpu.make_async_copy(index, numbers, numbered.at[0])
-    for z in range(planes):
-        load(z).start()
+    load(0).start()
+    load(1).start()
     load_numbers.start()
     for z in range(planes):
-        load(z).wait()
+        if z < 2:
+            load(z).wait()
         for view in range(2):
-            lines = jnp.concatenate([held[z, view, block] for block in blocks], axis=0)
+            lines = jnp.concatenate([held[view, block, z] for block in blocks], axis=0)
             turned = lines.T
             for device in range(8):
                 slab = slab_of(device, z)
@@ -199,7 +201,7 @@
 def scattered(view, slots, weights, column):
     chunk = lax.broadcasted_iota(jnp.int32, (32, 128), 1) // 32
     at = lax.broadcasted_iota(jnp.int32, (256, 512), 0)
-    line = (lax.rem(at, 128) // 8 * 16 + at // 128 * 8 + lax.rem(at, 8)).astype(F32)
+    line = (lax.rem(at, 128) // 8 * 16 + at // 128 * 8 + lax.rem(at, 8)).astype(F32).astype(BF16)
     x, block = column // 4, column % 4
     numbers, values = [], []
     for t in range(4):
@@ -214,7 +216,8 @@
         numbers.append(number)
     value = jnp.concatenate(values, axis=1)
     number = jnp.concatenate(numbers, axis=1)
-    hot = (line == number).astype(BF16)
+    one, zero = jnp.ones((), BF16), jnp.zeros((), BF16)
+    hot = jnp.where(line == number.astype(BF16), one, zero)
     left = jnp.concatenate([*split3(value), jnp.ones((16, 512), BF16)], axis=0)
     result = dot_nt(left, hot)
     data = result[0:32] + result[32:64] + result[64:96]
@@ -386,10 +389,10 @@
         shape(8, 66 * planes, 128),
         [anywhere, anywhere],
         [
-            pltpu.VMEM((planes, 2, 4, 32, 256), F32),
+            pltpu.VMEM((2, 4, planes, 32, 256), F32),
             pltpu.VMEM((8, 128), jnp.int32),
             pltpu.VMEM((8, 66 * planes, 128), F32),
-            pltpu.SemaphoreType.DMA((planes,)),
+            pltpu.SemaphoreType.DMA((2,)),
             pltpu.SemaphoreType.DMA((1,)),
             pltpu.SemaphoreType.DMA((planes,)),
         ],

time: 61 us -> 60.8 us (level)
  transfers between devices with their start and end apart: 19 -> 19, of which waited for: 8 -> 9; matrix products, arithmetic and copies ran while one was open for 0% -> 0% of each run, Pallas kernels for 8% -> 8%
where the time goes in v11:
time: 60.8 us; the launch traced here: 60.3 us
  starting transfers between devices  25.2 us (41%)
  waiting for transfers between devices  22.8 us (38%)
  Pallas kernels  12 us (20%)
    ppermute x7, waiting for transfers between devices, slab_sweep(): lax.ppermute(piece, ALL, pairs)  12.7 us
    ppermute x7, starting transfers between devices, slab_sweep(): lax.ppermute(piece, ALL, pairs)  9.07 us
    all_to_all x1, starting transfers between devices, slab_sweep(): slots = lax.all_to_all(slots, ALL, split_axis=0, concat_axis=0, tiled=True)  7.3 us
    all_to_all x1, waiting for transfers between devices, slab_sweep(): slots = lax.all_to_all(slots, ALL, split_axis=0, concat_axis=0, tiled=True)  6.23 us
    ppermute x1, starting transfers between devices, slab_sweep(): lax.ppermute(ratio, ALL, near_pairs)  2.89 us
    pallas_call x4, Pallas kernels, matrices(): call(functools.partial(taps_kernel, view, way), (big, big, shape(64, 128,...  2.64 us
    pallas_call x1, Pallas kernels, slab_sweep(): call(functools.partial(lines_kernel, planes), shape(8, 66 * planes, 128),...  2.4 us
    ppermute x1, starting transfers between devices, slab_sweep(): lax.ppermute(far, ALL, ring_pairs)  2.32 us
  transfers between devices with their start and end apart: 19, of which 9 were waited for; matrix products, arithmetic and copies ran while one was open for 0% of the time, Pallas kernels for 8%

profile of v11, /device:TPU:0, one launch (start us, length us, event | category | flops | bytes accessed | tf_op | source)
XLA Modules:
  0.0 60.3 jit_solution(5676927045703323813)
XLA Ops:
  0.0 2.4 %shard_map.55 = f32[8,264,128]{2,1,0:T(8,128)} custom-call(f32[2,4,4,32,256]{4,3,2,1,0:T(8,128)} %bitcast.27, s32[8,128]{1,0:T(8,128)} %bitcast.28), custom_call_target="tpu_custom_call" | custom-call | bytes 1048576 | tf_op jit(solution)/shard_map/pallas_call | solution.py:387
  2.4 7.3 %all-to-all-start = ((f32[32,1,8448]{2,1,0:T(1,128)}), f32[32,1,8448]{2,1,0:T(1,128)S(1)}, u32[]{:S(2)}, u32[]{:S(2)}) async-start(f32[32,1,8448]{2,1,0:T(1,128)} %bitcast.26), calls=%async_computation | async-start | bytes 2162688 | tf_op jit(solution)/shard_map/all_to_all | solution.py:403
  9.8 0.7 %shard_map.56 = (f32[72,256]{1,0:T(8,128)S(1)}, f32[72,256]{1,0:T(8,128)S(1)}, f32[72,256]{1,0:T(8,128)S(1)}, f32[72,256]{1,0:T(8,128)S(1)}) custom-call(s32[2]{0:T(128)S(1)} %bitcast.21, f32[16,2,8,256]{3,2,1,0:T(8,128)S(1)} %bitcast.19), custom_call_target="tpu_custom_call" | custom-call | bytes 1048576 | tf_op jit(solution)/shard_map/pallas_call | solution.py:380
  10.5 1.8 %collective-permute-start = (f32[72,256]{1,0:T(8,128)S(1)}, f32[72,256]{1,0:T(8,128)S(1)}, u32[]{:S(2)}, u32[]{:S(2)}) collective-permute-start(f32[72,256]{1,0:T(8,128)S(1)} %get-tuple-element.37), channel_id=1, source_target_pairs={{0,8},{1,9},{2,10},{3,11},{4,12},{5,13},{6,14},{7,15},{8,0},{9,1},... | collective-permute-start | bytes 221192 | tf_op jit(solution)/shard_map/ppermute | solution.py:383
  12.3 1.5 %collective-permute-start.1 = (f32[72,256]{1,0:T(8,128)S(1)}, f32[72,256]{1,0:T(8,128)S(1)}, u32[]{:S(2)}, u32[]{:S(2)}) collective-permute-start(f32[72,256]{1,0:T(8,128)S(1)} %get-tuple-element.38), channel_id=1, source_target_pairs={{0,16},{1,17},{2,18},{3,19},{4,20},{5,21},{6,22},{7,23},{8,24},{9,... | collective-permute-start | bytes 221192 | tf_op jit(solution)/shard_map/ppermute | solution.py:383
  14.0 6.3 %collective-permute-done.refs_1_ = f32[72,256]{1,0:T(8,128)S(1)} collective-permute-done((f32[72,256]{1,0:T(8,128)S(1)}, f32[72,256]{1,0:T(8,128)S(1)}, u32[]{:S(2)}, u32[]{:S(2)}) %collective-permute-start) | collective-permute-done | bytes 73760 | tf_op jit(solution)/shard_map/ppermute | solution.py:383
  20.4 0.9 %collective-permute-done.1.refs_2_ = f32[72,256]{1,0:T(8,128)S(1)} collective-permute-done((f32[72,256]{1,0:T(8,128)S(1)}, f32[72,256]{1,0:T(8,128)S(1)}, u32[]{:S(2)}, u32[]{:S(2)}) %collective-permute-start.1) | collective-permute-done | bytes 73760 | tf_op jit(solution)/shard_map/ppermute | solution.py:383
  21.2 4.5 %collective-permute-done.2.refs_3_ = f32[72,256]{1,0:T(8,128)S(1)} collective-permute-done((f32[72,256]{1,0:T(8,128)S(1)}, f32[72,256]{1,0:T(8,128)S(1)}, u32[]{:S(2)}, u32[]{:S(2)}) %collective-permute-start.2) | collective-permute-done | bytes 73760 | tf_op jit(solution)/shard_map/ppermute | solution.py:383
  25.8 1.2 %collective-permute-done.6.refs_7_ = f32[72,256]{1,0:T(8,128)S(1)} collective-permute-done((f32[72,256]{1,0:T(8,128)S(1)}, f32[72,256]{1,0:T(8,128)S(1)}, u32[]{:S(2)}, u32[]{:S(2)}) %collective-permute-start.6) | collective-permute-done | bytes 73760 | tf_op jit(solution)/shard_map/ppermute | solution.py:384
  27.1 0.7 %collective-permute-start.7 = (f32[8,16,256]{2,1,0:T(8,128)S(1)}, f32[8,16,256]{2,1,0:T(8,128)S(1)}, u32[]{:S(2)}, u32[]{:S(2)}) collective-permute-start(f32[8,16,256]{2,1,0:T(8,128)S(1)} %get-tuple-element.42), channel_id=1, source_target_pairs={{4,8},{8,4},{12,24},{24,12},{28,16},{16,28},{20,17},{17,20},{21,25... | collective-permute-start | bytes 393224 | tf_op jit(solution)/shard_map/ppermute | solution.py:413
  27.8 0.7 %shard_map.58 = (bf16[5,256,256]{2,1,0:T(8,128)(2,1)S(1)}, bf16[5,256,256]{2,1,0:T(8,128)(2,1)S(1)}, bf16[64,128]{1,0:T(8,128)(2,1)S(1)}) custom-call(f32[3,2,33]{2,1,0:T(2,128)S(1)} %bitcast.22, f32[8,32,256]{2,1,0:T(8,128)S(1)} %get-tuple-element.41._.est), custom_call_target="tpu_custom_call" | custom-call | flops 1073741824 | bytes 1048576 | tf_op jit(solution)/shard_map/pallas_call | solution.py:416
  28.5 0.8 %shard_map.59.blurred = f32[256,256]{1,0:T(8,128)S(1)} custom-call(f32[8,32,256]{2,1,0:T(8,128)S(1)} %get-tuple-element.41._.est, f32[8,16,256]{2,1,0:T(8,128)S(1)} %collective-permute-done.7.far.est_far, f32[8,16,256]{2,1,0:T(8,128)S(1)} %get-tuple-element.43.near.est_near, bf16[64,128]{1,0:T(8,128)(2,1)S(1)} %get-tuple-element.44.band, ...), custom_call_target="tpu_custom_call" | custom-call | flops 1073741824 | bytes 1048576 | tf_op jit(solution)/shard_map/pallas_call | solution.py:425
  29.3 6.2 %all-to-all-done = f32[32,1,8448]{2,1,0:T(1,128)S(1)} async-done(((f32[32,1,8448]{2,1,0:T(1,128)}), f32[32,1,8448]{2,1,0:T(1,128)S(1)}, u32[]{:S(2)}, u32[]{:S(2)}) %all-to-all-start) | async-done | bytes 1081376 | tf_op jit(solution)/shard_map/all_to_all | solution.py:403
  35.5 0.8 %shard_map.60.ratio = f32[8,32,256]{2,1,0:T(8,128)S(1)} custom-call(f32[8,264,128]{2,1,0:T(8,128)S(1)} %bitcast.15, f32[8,8,256]{2,1,0:T(8,128)S(1)} %get-tuple-element.40.weights, f32[256,256]{1,0:T(8,128)S(1)} %shard_map.59.blurred), custom_call_target="tpu_custom_call" | custom-call | flops 1073741824 | bytes 1048576 | tf_op jit(solution)/shard_map/pallas_call | solution.py:428
  36.3 0.7 %collective-permute-start.8 = (f32[8,32,256]{2,1,0:T(8,128)S(1)}, f32[8,32,256]{2,1,0:T(8,128)S(1)}, u32[]{:S(2)}, u32[]{:S(2)}) collective-permute-start(f32[8,32,256]{2,1,0:T(8,128)S(1)} %shard_map.60.ratio), channel_id=1, source_target_pairs={{4,8},{8,4},{12,24},{24,12},{28,16},{16,28},{20,17},{17,20},{21,25... | collective-permute-start | bytes 786440 | tf_op jit(solution)/shard_map/ppermute | solution.py:436
  37.0 2.9 %collective-permute-start.9 = (f32[8,32,256]{2,1,0:T(8,128)S(1)}, f32[8,32,256]{2,1,0:T(8,128)S(1)}, u32[]{:S(2)}, u32[]{:S(2)}) collective-permute-start(f32[8,32,256]{2,1,0:T(8,128)S(1)} %shard_map.60.ratio), channel_id=1, source_target_pairs={{0,4},{4,0},{8,12},{12,8},{24,28},{28,24},{16,20},{20,16},{17,21},... | collective-permute-start | bytes 786440 | tf_op jit(solution)/shard_map/ppermute | solution.py:436
  39.9 0.6 shard_map.61
  40.5 0.8 %shard_map.64 = (f32[8,32,256]{2,1,0:T(8,128)S(1)}, f32[8,8,256]{2,1,0:T(8,128)S(1)}) custom-call(f32[8,264,128]{2,1,0:T(8,128)S(1)} %bitcast.17, f32[8,8,256]{2,1,0:T(8,128)S(1)} %get-tuple-element.40.weights), custom_call_target="tpu_custom_call" | custom-call | flops 1073741824 | bytes 1048576 | tf_op jit(solution)/shard_map/pallas_call | solution.py:429
  41.3 0.7 %shard_map.63 = (bf16[5,256,256]{2,1,0:T(8,128)(2,1)S(1)}, bf16[5,256,256]{2,1,0:T(8,128)(2,1)S(1)}, bf16[64,128]{1,0:T(8,128)(2,1)S(1)}) custom-call(f32[3,2,33]{2,1,0:T(2,128)S(1)} %bitcast.24, f32[8,264,128]{2,1,0:T(8,128)S(1)} %bitcast.18), custom_call_target="tpu_custom_call" | custom-call | flops 1073741824 | bytes 1048576 | tf_op jit(solution)/shard_map/pallas_call | solution.py:416
  42.0 1.3 %shard_map.62.est = f32[8,64,256]{2,1,0:T(8,128)S(1)} custom-call(f32[8,32,256]{2,1,0:T(8,128)S(1)} %shard_map.60.ratio, f32[8,32,256]{2,1,0:T(8,128)S(1)} %collective-permute-done.8.ratio_far, f32[8,32,256]{2,1,0:T(8,128)S(1)} %collective-permute-done.9.ratio_near, f32[8,32,256]{2,1,0:T(8,128)S(1)} %get-tuple-element.41._.est, ...), custom_call_target="tpu_custom_call" | custom-call | flops 1073741824 | bytes 1048576 | tf_op jit(solution)/shard_map/pallas_call | solution.py:430
  43.4 0.8 %shard_map.65 = (f32[8,32,256]{2,1,0:T(8,128)S(1)}, f32[8,16,256]{2,1,0:T(8,128)S(1)}, f32[8,16,256]{2,1,0:T(8,128)S(1)}) custom-call(f32[8,64,256]{2,1,0:T(8,128)S(1)} %shard_map.62.est, bf16[64,128]{1,0:T(8,128)(2,1)S(1)} %get-tuple-element.50.band, bf16[5,256,256]{2,1,0:T(8,128)(2,1)S(1)} %get-tuple-element.51.high, ...), custom_call_target="tpu_custom_call" | custom-call | flops 1073741824 | bytes 1048576 | tf_op jit(solution)/shard_map/pallas_call | solution.py:437
  44.2 2.3 %collective-permute-start.10 = (f32[8,16,256]{2,1,0:T(8,128)S(1)}, f32[8,16,256]{2,1,0:T(8,128)S(1)}, u32[]{:S(2)}, u32[]{:S(2)}) collective-permute-start(f32[8,16,256]{2,1,0:T(8,128)S(1)} %get-tuple-element.56), channel_id=1, source_target_pairs={{4,8},{8,4},{12,24},{24,12},{28,16},{16,28},{20,17},{17,20},{21,25... | collective-permute-start | bytes 393224 | tf_op jit(solution)/shard_map/ppermute | solution.py:447
  46.5 1.4 %collective-permute-start.11 = (f32[8,16,256]{2,1,0:T(8,128)S(1)}, f32[8,16,256]{2,1,0:T(8,128)S(1)}, u32[]{:S(2)}, u32[]{:S(2)}) collective-permute-start(f32[8,16,256]{2,1,0:T(8,128)S(1)} %get-tuple-element.57), channel_id=1, source_target_pairs={{0,4},{4,0},{8,12},{12,8},{24,28},{28,24},{16,20},{20,16},{17,21},... | collective-permute-start | bytes 393224 | tf_op jit(solution)/shard_map/ppermute | solution.py:447
  48.5 2.0 %collective-permute-done.10.far = f32[8,16,256]{2,1,0:T(8,128)S(1)} collective-permute-done((f32[8,16,256]{2,1,0:T(8,128)S(1)}, f32[8,16,256]{2,1,0:T(8,128)S(1)}, u32[]{:S(2)}, u32[]{:S(2)}) %collective-permute-start.10) | collective-permute-done | bytes 131104 | tf_op jit(solution)/shard_map/ppermute | solution.py:447
  50.4 0.8 %shard_map.67 = (f32[32,256]{1,0:T(8,128)S(1)}, f32[32,256]{1,0:T(8,128)S(1)}, f32[2,32,256]{2,1,0:T(8,128)S(1)}, f32[2,32,256]{2,1,0:T(8,128)S(1)}, f32[32,256]{1,0:T(8,128)S(1)}, /*index=5*/f32[32,256]{1,0:T(8,128)S(1)}) custom-call(f32[8,32,256]{2,1,0:T(8,128)S(1)} %get-tuple-element.55._.ratio, f32[8,16,256]{2,1,0:T(8,128)S(1)} %collective-permute-done.10.far, ...), custom_call_target="tpu_custom_call" | custom-call | flops 1073741824 | bytes 1048576 | tf_op jit(solution)/shard_map/pallas_call | solution.py:441
  51.3 1.7 %collective-permute-start.12 = (f32[2,32,256]{2,1,0:T(8,128)S(1)}, f32[2,32,256]{2,1,0:T(8,128)S(1)}, u32[]{:S(2)}, u32[]{:S(2)}) collective-permute-start(f32[2,32,256]{2,1,0:T(8,128)S(1)} %get-tuple-element.62), channel_id=1, source_target_pairs={{0,8},{1,9},{2,10},{3,11},{4,12},{5,13},{6,14},{7,15},{8,0},{9,1},... | collective-permute-start | bytes 196616 | tf_op jit(solution)/shard_map/ppermute | solution.py:448
  53.0 1.5 %collective-permute-start.13 = (f32[2,32,256]{2,1,0:T(8,128)S(1)}, f32[2,32,256]{2,1,0:T(8,128)S(1)}, u32[]{:S(2)}, u32[]{:S(2)}) collective-permute-start(f32[2,32,256]{2,1,0:T(8,128)S(1)} %get-tuple-element.63), channel_id=1, source_target_pairs={{0,16},{1,17},{2,18},{3,19},{4,20},{5,21},{6,22},{7,23},{8,24},{9,... | collective-permute-start | bytes 196616 | tf_op jit(solution)/shard_map/ppermute | solution.py:448
  54.8 2.0 %collective-permute-start.17 = (f32[32,256]{1,0:T(8,128)S(1)}, f32[32,256]{1,0:T(8,128)S(1)}, u32[]{:S(2)}, u32[]{:S(2)}) collective-permute-start(f32[32,256]{1,0:T(8,128)S(1)} %get-tuple-element.66), channel_id=1, source_target_pairs={{0,28},{1,29},{2,30},{3,31},{4,24},{5,25},{6,26},{7,27},{8,20},{9,... | collective-permute-start | bytes 98312 | tf_op jit(solution)/shard_map/ppermute | solution.py:448
  56.8 0.8 %collective-permute-start.15 = (f32[2,32,256]{2,1,0:T(8,128)S(1)}, f32[2,32,256]{2,1,0:T(8,128)S(1)}, u32[]{:S(2)}, u32[]{:S(2)}) collective-permute-start(f32[2,32,256]{2,1,0:T(8,128)S(1)} %pad_maximum_fusion), channel_id=1, source_target_pairs={{0,4},{1,5},{2,6},{3,7},{4,0},{5,1},{6,2},{7,3},{8,12},{9,13},{10,... | collective-permute-start | bytes 196616 | tf_op jit(solution)/shard_map/ppermute | solution.py:449
  57.8 0.7 %collective-permute-done.15 = f32[2,32,256]{2,1,0:T(8,128)S(1)} collective-permute-done((f32[2,32,256]{2,1,0:T(8,128)S(1)}, f32[2,32,256]{2,1,0:T(8,128)S(1)}, u32[]{:S(2)}, u32[]{:S(2)}) %collective-permute-start.15) | collective-permute-done | bytes 65568 | tf_op jit(solution)/shard_map/ppermute | solution.py:449
  58.5 0.9 %collective-permute-done.14.refs_3_ = f32[32,256]{1,0:T(8,128)S(1)} collective-permute-done((f32[32,256]{1,0:T(8,128)S(1)}, f32[32,256]{1,0:T(8,128)S(1)}, u32[]{:S(2)}, u32[]{:S(2)}) %collective-permute-start.14) | collective-permute-done | bytes 32800 | tf_op jit(solution)/shard_map/ppermute | solution.py:448
  59.4 0.9 %shard_map.68 = f32[16,2,8,256]{3,2,1,0:T(8,128)} custom-call(f32[32,256]{1,0:T(8,128)S(1)} %get-tuple-element.61.refs_0_, f32[2,32,256]{2,1,0:T(8,128)S(1)} %collective-permute-done.12.refs_1_, f32[2,32,256]{2,1,0:T(8,128)S(1)} %collective-permute-done.13.refs_2_, f32[32,256]{1,0:T(8,128)S(1)} %collective-permute-done.14.refs_3_, ...), custom_call_target="tpu_custom_call" | custom-call | bytes 1048576 | tf_op jit(solution)/shard_map/pallas_call | solution.py:451
  (30 shorter events, 1.5 us)
Async XLA Ops:
  2.4 7.3 %copy-start = (f32[16,16,256]{2,1,0:T(8,128)S(1)}, f32[16,16,256]{2,1,0:T(8,128)}, u32[]{:S(2)}) copy-start(f32[16,16,256]{2,1,0:T(8,128)} %param.5) | copy-start | bytes 786436
  2.4 7.3 %copy-start.1 = (s32[2,1,1,1]{0,3,2,1:T(1,128)S(1)}, s32[2,1,1,1]{0,3,2,1:T(1,128)}, u32[]{:S(2)}) copy-start(s32[2,1,1,1]{0,3,2,1:T(1,128)} %param.9) | copy-start | bytes 28
  2.4 25.3 %copy-start.2 = (f32[2,3,33]{2,0,1:T(2,128)S(1)}, f32[2,3,33]{2,0,1:T(2,128)}, u32[]{:S(2)}) copy-start(f32[2,3,33]{2,0,1:T(2,128)} %param.8) | copy-start | bytes 2380
  2.4 33.0 %all-to-all-start = ((f32[32,1,8448]{2,1,0:T(1,128)}), f32[32,1,8448]{2,1,0:T(1,128)S(1)}, u32[]{:S(2)}, u32[]{:S(2)}) async-start(f32[32,1,8448]{2,1,0:T(1,128)} %bitcast.26), calls=%async_computation | async-start | bytes 2162688 | tf_op jit(solution)/shard_map/all_to_all | solution.py:403
  10.5 9.9 %collective-permute-start = (f32[72,256]{1,0:T(8,128)S(1)}, f32[72,256]{1,0:T(8,128)S(1)}, u32[]{:S(2)}, u32[]{:S(2)}) collective-permute-start(f32[72,256]{1,0:T(8,128)S(1)} %get-tuple-element.37), channel_id=1, source_target_pairs={{0,8},{1,9},{2,10},{3,11},{4,12},{5,13},{6,14},{7,15},{8,0},{9,1},... | collective-permute-start | bytes 221192 | tf_op jit(solution)/shard_map/ppermute | solution.py:383
  12.3 8.9 %collective-permute-start.1 = (f32[72,256]{1,0:T(8,128)S(1)}, f32[72,256]{1,0:T(8,128)S(1)}, u32[]{:S(2)}, u32[]{:S(2)}) collective-permute-start(f32[72,256]{1,0:T(8,128)S(1)} %get-tuple-element.38), channel_id=1, source_target_pairs={{0,16},{1,17},{2,18},{3,19},{4,20},{5,21},{6,22},{7,23},{8,24},{9,... | collective-permute-start | bytes 221192 | tf_op jit(solution)/shard_map/ppermute | solution.py:383
  13.8 12.0 %collective-permute-start.2 = (f32[72,256]{1,0:T(8,128)S(1)}, f32[72,256]{1,0:T(8,128)S(1)}, u32[]{:S(2)}, u32[]{:S(2)}) collective-permute-start(f32[72,256]{1,0:T(8,128)S(1)} %get-tuple-element.39), channel_id=1, source_target_pairs={{0,24},{1,25},{2,26},{3,27},{4,28},{5,29},{6,30},{7,31},{8,16},{9,... | collective-permute-start | bytes 221192 | tf_op jit(solution)/shard_map/ppermute | solution.py:383
  14.0 11.7 %collective-permute-start.3 = (f32[72,256]{1,0:T(8,128)S(1)}, f32[72,256]{1,0:T(8,128)S(1)}, u32[]{:S(2)}, u32[]{:S(2)}) collective-permute-start(f32[72,256]{1,0:T(8,128)S(1)} %get-tuple-element.36.refs_0_), channel_id=1, source_target_pairs={{0,4},{1,5},{2,6},{3,7},{4,0},{5,1},{6,2},{7,3},{8,12},{9,13},{10,... | collective-permute-start | bytes 221192 | tf_op jit(solution)/shard_map/ppermute | solution.py:384
  20.4 5.4 %collective-permute-start.4 = (f32[72,256]{1,0:T(8,128)S(1)}, f32[72,256]{1,0:T(8,128)S(1)}, u32[]{:S(2)}, u32[]{:S(2)}) collective-permute-start(f32[72,256]{1,0:T(8,128)S(1)} %collective-permute-done.refs_1_), channel_id=1, source_target_pairs={{0,4},{1,5},{2,6},{3,7},{4,0},{5,1},{6,2},{7,3},{8,12},{9,13},{10,... | collective-permute-start | bytes 221192 | tf_op jit(solution)/shard_map/ppermute | solution.py:384
  21.2 4.5 %collective-permute-start.5 = (f32[72,256]{1,0:T(8,128)S(1)}, f32[72,256]{1,0:T(8,128)S(1)}, u32[]{:S(2)}, u32[]{:S(2)}) collective-permute-start(f32[72,256]{1,0:T(8,128)S(1)} %collective-permute-done.1.refs_2_), channel_id=1, source_target_pairs={{0,4},{1,5},{2,6},{3,7},{4,0},{5,1},{6,2},{7,3},{8,12},{9,13},{10,... | collective-permute-start | bytes 221192 | tf_op jit(solution)/shard_map/ppermute | solution.py:384
  25.8 1.3 %collective-permute-start.6 = (f32[72,256]{1,0:T(8,128)S(1)}, f32[72,256]{1,0:T(8,128)S(1)}, u32[]{:S(2)}, u32[]{:S(2)}) collective-permute-start(f32[72,256]{1,0:T(8,128)S(1)} %collective-permute-done.2.refs_3_), channel_id=1, source_target_pairs={{0,4},{1,5},{2,6},{3,7},{4,0},{5,1},{6,2},{7,3},{8,12},{9,13},{10,... | collective-permute-start | bytes 221192 | tf_op jit(solution)/shard_map/ppermute | solution.py:384
  27.1 1.4 %collective-permute-start.7 = (f32[8,16,256]{2,1,0:T(8,128)S(1)}, f32[8,16,256]{2,1,0:T(8,128)S(1)}, u32[]{:S(2)}, u32[]{:S(2)}) collective-permute-start(f32[8,16,256]{2,1,0:T(8,128)S(1)} %get-tuple-element.42), channel_id=1, source_target_pairs={{4,8},{8,4},{12,24},{24,12},{28,16},{16,28},{20,17},{17,20},{21,25... | collective-permute-start | bytes 393224 | tf_op jit(solution)/shard_map/ppermute | solution.py:413
  36.3 5.7 %collective-permute-start.8 = (f32[8,32,256]{2,1,0:T(8,128)S(1)}, f32[8,32,256]{2,1,0:T(8,128)S(1)}, u32[]{:S(2)}, u32[]{:S(2)}) collective-permute-start(f32[8,32,256]{2,1,0:T(8,128)S(1)} %shard_map.60.ratio), channel_id=1, source_target_pairs={{4,8},{8,4},{12,24},{24,12},{28,16},{16,28},{20,17},{17,20},{21,25... | collective-permute-start | bytes 786440 | tf_op jit(solution)/shard_map/ppermute | solution.py:436
  37.0 5.0 %collective-permute-start.9 = (f32[8,32,256]{2,1,0:T(8,128)S(1)}, f32[8,32,256]{2,1,0:T(8,128)S(1)}, u32[]{:S(2)}, u32[]{:S(2)}) collective-permute-start(f32[8,32,256]{2,1,0:T(8,128)S(1)} %shard_map.60.ratio), channel_id=1, source_target_pairs={{0,4},{4,0},{8,12},{12,8},{24,28},{28,24},{16,20},{20,16},{17,21},... | collective-permute-start | bytes 786440 | tf_op jit(solution)/shard_map/ppermute | solution.py:436
  44.2 6.3 %collective-permute-start.10 = (f32[8,16,256]{2,1,0:T(8,128)S(1)}, f32[8,16,256]{2,1,0:T(8,128)S(1)}, u32[]{:S(2)}, u32[]{:S(2)}) collective-permute-start(f32[8,16,256]{2,1,0:T(8,128)S(1)} %get-tuple-element.56), channel_id=1, source_target_pairs={{4,8},{8,4},{12,24},{24,12},{28,16},{16,28},{20,17},{17,20},{21,25... | collective-permute-start | bytes 393224 | tf_op jit(solution)/shard_map/ppermute | solution.py:447
  46.5 3.9 %collective-permute-start.11 = (f32[8,16,256]{2,1,0:T(8,128)S(1)}, f32[8,16,256]{2,1,0:T(8,128)S(1)}, u32[]{:S(2)}, u32[]{:S(2)}) collective-permute-start(f32[8,16,256]{2,1,0:T(8,128)S(1)} %get-tuple-element.57), channel_id=1, source_target_pairs={{0,4},{4,0},{8,12},{12,8},{24,28},{28,24},{16,20},{20,16},{17,21},... | collective-permute-start | bytes 393224 | tf_op jit(solution)/shard_map/ppermute | solution.py:447
  51.3 5.5 %collective-permute-start.12 = (f32[2,32,256]{2,1,0:T(8,128)S(1)}, f32[2,32,256]{2,1,0:T(8,128)S(1)}, u32[]{:S(2)}, u32[]{:S(2)}) collective-permute-start(f32[2,32,256]{2,1,0:T(8,128)S(1)} %get-tuple-element.62), channel_id=1, source_target_pairs={{0,8},{1,9},{2,10},{3,11},{4,12},{5,13},{6,14},{7,15},{8,0},{9,1},... | collective-permute-start | bytes 196616 | tf_op jit(solution)/shard_map/ppermute | solution.py:448
  53.0 4.7 %collective-permute-start.13 = (f32[2,32,256]{2,1,0:T(8,128)S(1)}, f32[2,32,256]{2,1,0:T(8,128)S(1)}, u32[]{:S(2)}, u32[]{:S(2)}) collective-permute-start(f32[2,32,256]{2,1,0:T(8,128)S(1)} %get-tuple-element.63), channel_id=1, source_target_pairs={{0,16},{1,17},{2,18},{3,19},{4,20},{5,21},{6,22},{7,23},{8,24},{9,... | collective-permute-start | bytes 196616 | tf_op jit(solution)/shard_map/ppermute | solution.py:448
  54.5 4.9 %collective-permute-start.14 = (f32[32,256]{1,0:T(8,128)S(1)}, f32[32,256]{1,0:T(8,128)S(1)}, u32[]{:S(2)}, u32[]{:S(2)}) collective-permute-start(f32[32,256]{1,0:T(8,128)S(1)} %get-tuple-element.64), channel_id=1, source_target_pairs={{0,24},{1,25},{2,26},{3,27},{4,28},{5,29},{6,30},{7,31},{8,16},{9,... | collective-permute-start | bytes 98312 | tf_op jit(solution)/shard_map/ppermute | solution.py:448
  54.8 4.6 %collective-permute-start.17 = (f32[32,256]{1,0:T(8,128)S(1)}, f32[32,256]{1,0:T(8,128)S(1)}, u32[]{:S(2)}, u32[]{:S(2)}) collective-permute-start(f32[32,256]{1,0:T(8,128)S(1)} %get-tuple-element.66), channel_id=1, source_target_pairs={{0,28},{1,29},{2,30},{3,31},{4,24},{5,25},{6,26},{7,27},{8,20},{9,... | collective-permute-start | bytes 98312 | tf_op jit(solution)/shard_map/ppermute | solution.py:448
  56.8 1.7 %collective-permute-start.15 = (f32[2,32,256]{2,1,0:T(8,128)S(1)}, f32[2,32,256]{2,1,0:T(8,128)S(1)}, u32[]{:S(2)}, u32[]{:S(2)}) collective-permute-start(f32[2,32,256]{2,1,0:T(8,128)S(1)} %pad_maximum_fusion), channel_id=1, source_target_pairs={{0,4},{1,5},{2,6},{3,7},{4,0},{5,1},{6,2},{7,3},{8,12},{9,13},{10,... | collective-permute-start | bytes 196616 | tf_op jit(solution)/shard_map/ppermute | solution.py:449
  57.7 1.7 %collective-permute-start.16 = (f32[32,256]{1,0:T(8,128)S(1)}, f32[32,256]{1,0:T(8,128)S(1)}, u32[]{:S(2)}, u32[]{:S(2)}) collective-permute-start(f32[32,256]{1,0:T(8,128)S(1)} %slice_bitcast_fusion), channel_id=1, source_target_pairs={{0,4},{1,5},{2,6},{3,7},{4,0},{5,1},{6,2},{7,3},{8,12},{9,13},{10,... | collective-permute-start | bytes 98312 | tf_op jit(solution)/shard_map/ppermute | solution.py:450
